TPU v7x, 32 devices: a whole 2x2x4 slice. The times are simulated.
32 devices in a mesh: page: 8 (over z, x), pb: 4 (over y, core).
Axes of the slice: x: 2, y: 2, z: 4, core: 2. Of those that a mesh axis runs over, the one named last changes fastest.
Arguments:
- tokens: bfloat16 [24, 512, 768], P('page', 'pb'), may hold values from -6 to 6
- cotangent: bfloat16 [24, 512, 768], P('page', 'pb'), may hold values from -6 to 6
- boxes: int32 [4, 24, 512], P(None, 'page', 'pb'), may hold values from 0 to 3400, as said below
- resolution: int32 [2, 24], P(None, 'page'), may hold values from 600 to 3400, as said below
- padding: int32 [24, 512], P('page', 'pb'), may hold values from 0 to 1, as said below
- query_weight: bfloat16 [768, 768], P(('page', 'pb')), may hold values from -0.21875 to 0.21875
- keys_weight: bfloat16 [768, 768], P(('page', 'pb')), may hold values from -0.21875 to 0.21875
- values_weight: bfloat16 [768, 768], P(('page', 'pb')), may hold values from -0.21875 to 0.21875
- output_weight: bfloat16 [768, 768], P(('page', 'pb')), may hold values from -1.25 to 1.25
- query_place: bfloat16 [768, 768], P(('page', 'pb')), may hold values from -0.5 to 0.5
- keys_place: bfloat16 [768, 768], P(('page', 'pb')), may hold values from -0.5 to 0.5
- inner_weight: bfloat16 [768, 3072], P(('page', 'pb')), may hold values from -0.21875 to 0.21875
- outer_weight: bfloat16 [3072, 768], P(('page', 'pb')), may hold values from -0.109375 to 0.109375
- query_bias: bfloat16 [768], P(('page', 'pb')), may hold values from -3 to 3
- keys_bias: bfloat16 [768], P(('page', 'pb')), may hold values from -3 to 3
- values_bias: bfloat16 [768], P(('page', 'pb')), may hold values from -3 to 3
- output_bias: bfloat16 [768], P(('page', 'pb')), may hold values from -3 to 3
- inner_bias: bfloat16 [3072], P(('page', 'pb')), may hold values from -3 to 3
- outer_bias: bfloat16 [768], P(('page', 'pb')), may hold values from -3 to 3
- first_gain: bfloat16 [768], P(('page', 'pb')), may hold values from 0.25 to 1.75
- first_shift: bfloat16 [768], P(('page', 'pb')), may hold values from -3 to 3
- second_gain: bfloat16 [768], P(('page', 'pb')), may hold values from 0.25 to 1.75
- second_shift: bfloat16 [768], P(('page', 'pb')), may hold values from -3 to 3
Outputs:
- layer_output: bfloat16 [24, 512, 768], P('page', 'pb')
- tokens_grad: float32 [24, 512, 768], P('page', 'pb')
- query_weight_grad: float32 [768, 768], P(('page', 'pb'))
- keys_weight_grad: float32 [768, 768], P(('page', 'pb'))
- values_weight_grad: float32 [768, 768], P(('page', 'pb'))
- output_weight_grad: float32 [768, 768], P(('page', 'pb'))
- query_place_grad: float32 [768, 768], P(('page', 'pb'))
- keys_place_grad: float32 [768, 768], P(('page', 'pb'))
- inner_weight_grad: float32 [768, 3072], P(('page', 'pb'))
- outer_weight_grad: float32 [3072, 768], P(('page', 'pb'))
- query_bias_grad: float32 [768], P(('page', 'pb'))
- keys_bias_grad: float32 [768], P(('page', 'pb'))
- values_bias_grad: float32 [768], P(('page', 'pb'))
- output_bias_grad: float32 [768], P(('page', 'pb'))
- inner_bias_grad: float32 [3072], P(('page', 'pb'))
- outer_bias_grad: float32 [768], P(('page', 'pb'))
- first_gain_grad: float32 [768], P(('page', 'pb'))
- first_shift_grad: float32 [768], P(('page', 'pb'))
- second_gain_grad: float32 [768], P(('page', 'pb'))
- second_shift_grad: float32 [768], P(('page', 'pb'))
Inputs may be any that keep to these rules, and one draw needn't show every extreme that they name: `boxes`: rows hold x0, y0, x1, y1 in pixels with 0 <= x0 <= x1 <= the page's width and 0 <= y0 <= y1 <= its height; each page's first token spans the page's full height. `resolution`: row 0 holds each page's width in pixels, row 1 its height. `padding`: each page's ones form a prefix of 128 or more tokens; among pages k * 3 to (k + 1) * 3 - 1 one page has more than 384 ones.
All inputs are finite; a program needn't handle non-finite values.
Results may differ from a plain program's by a relative error of at most 0.028.
Values may be sent and summed in bfloat16 or wider, within the bound.
No kernel may reach another device: no remote copies, remote signals or barrier semaphores. Data moves between devices by JAX's collectives and lax.ppermute only.
A program may use at most 192 MiB of HBM per device.

v0:
```python
import math

import jax
import jax.numpy as jnp
from jax import lax
from jax.sharding import PartitionSpec as P

HEADS = 12
HD = 64
FREQ = 192


def trig_of(boxes, resolution):
    grid_x = (boxes[0] + boxes[2]) * 500 // resolution[0][:, None]
    grid_y = (boxes[1] + boxes[3]) * 500 // resolution[1][:, None]
    grids = jnp.stack([grid_x, grid_y], axis=-1).astype(jnp.float32)
    rates = jnp.exp(jnp.arange(FREQ).astype(jnp.float32) * (-math.log(10000.0) / FREQ))
    angles = grids[..., None] * rates
    return (jnp.sin(angles), jnp.cos(angles))


def features(first, second):
    stacked = jnp.stack([first, second], axis=-2)
    return stacked.reshape(first.shape[:-2] + (4 * first.shape[-1],))


def split_parts(spread, sines):
    pieces = spread.reshape(spread.shape[:-1] + (2, 2, sines.shape[-1]))
    return (pieces[..., 0, :], pieces[..., 1, :])


def turn_query(spread, sines, cosines):
    sine_part, cosine_part = split_parts(spread, sines)
    turned = jnp.stack(
        [sine_part * cosines + cosine_part * sines, cosine_part * cosines - sine_part * sines],
        axis=-2,
    )
    return turned.reshape(spread.shape)


def turn_key(spread, sines, cosines):
    sine_part, cosine_part = split_parts(spread, sines)
    turned = jnp.stack(
        [sine_part * sines + cosine_part * cosines, cosine_part * sines - sine_part * cosines],
        axis=-2,
    )
    return turned.reshape(spread.shape)


def turn_query_back(gradient, sines, cosines):
    sine_part, cosine_part = split_parts(gradient, sines)
    turned = jnp.stack(
        [sine_part * cosines - cosine_part * sines, sine_part * sines + cosine_part * cosines],
        axis=-2,
    )
    return turned.reshape(gradient.shape)


def turn_key_back(gradient, sines, cosines):
    sine_part, cosine_part = split_parts(gradient, sines)
    turned = jnp.stack(
        [sine_part * sines - cosine_part * cosines, sine_part * cosines + cosine_part * sines],
        axis=-2,
    )
    return turned.reshape(gradient.shape)


def layer_norm(values, gain, shift):
    centred = values - jnp.mean(values, axis=-1, keepdims=True)
    spread = jnp.mean(centred * centred, axis=-1, keepdims=True)
    return centred * lax.rsqrt(spread + 1e-05) * gain + shift


def exact_gelu(values):
    return jax.nn.gelu(values, approximate=False)


def project(values, matrix, offset):
    return jnp.einsum(
        "pnd,de->pne", values, matrix, preferred_element_type=jnp.float32
    ) + offset.astype(jnp.float32)


def weight_of(inputs_low, gradient):
    return jnp.einsum("pnd,pne->de", inputs_low, gradient, preferred_element_type=jnp.float32)


def back_through(gradient, matrix):
    return jnp.einsum("pne,de->pnd", gradient, matrix, preferred_element_type=jnp.float32)


def summed_rows(gradient):
    return jnp.sum(gradient.astype(jnp.float32), axis=(0, 1))


def on_device(
    tokens,
    cotangent,
    boxes,
    resolution,
    padding,
    query_weight,
    keys_weight,
    values_weight,
    output_weight,
    query_place,
    keys_place,
    inner_weight,
    outer_weight,
    query_bias,
    keys_bias,
    values_bias,
    output_bias,
    inner_bias,
    outer_bias,
    first_gain,
    first_shift,
    second_gain,
    second_shift,
):
    shards = (
        query_weight,
        keys_weight,
        values_weight,
        output_weight,
        query_place,
        keys_place,
        inner_weight,
        outer_weight,
        query_bias,
        keys_bias,
        values_bias,
        output_bias,
        inner_bias,
        outer_bias,
        first_gain,
        first_shift,
        second_gain,
        second_shift,
    )
    gathered = (
        lax.all_gather(shards[0], ("page", "pb"), axis=0, tiled=True),
        lax.all_gather(shards[1], ("page", "pb"), axis=0, tiled=True),
        lax.all_gather(shards[2], ("page", "pb"), axis=0, tiled=True),
        lax.all_gather(shards[3], ("page", "pb"), axis=0, tiled=True),
        lax.all_gather(shards[4], ("page", "pb"), axis=0, tiled=True),
        lax.all_gather(shards[5], ("page", "pb"), axis=0, tiled=True),
        lax.all_gather(shards[6], ("page", "pb"), axis=0, tiled=True),
        lax.all_gather(shards[7], ("page", "pb"), axis=0, tiled=True),
        lax.all_gather(shards[8], ("page", "pb"), axis=0, tiled=True),
        lax.all_gather(shards[9], ("page", "pb"), axis=0, tiled=True),
        lax.all_gather(shards[10], ("page", "pb"), axis=0, tiled=True),
        lax.all_gather(shards[11], ("page", "pb"), axis=0, tiled=True),
        lax.all_gather(shards[12], ("page", "pb"), axis=0, tiled=True),
        lax.all_gather(shards[13], ("page", "pb"), axis=0, tiled=True),
        lax.all_gather(shards[14], ("page", "pb"), axis=0, tiled=True),
        lax.all_gather(shards[15], ("page", "pb"), axis=0, tiled=True),
        lax.all_gather(shards[16], ("page", "pb"), axis=0, tiled=True),
        lax.all_gather(shards[17], ("page", "pb"), axis=0, tiled=True),
    )
    (
        matrix_query,
        matrix_keys,
        matrix_values,
        matrix_output,
        place_query,
        place_keys,
        matrix_inner,
        matrix_outer,
        offset_query,
        offset_keys,
        offset_values,
        offset_output,
        offset_inner,
        offset_outer,
        gain_first,
        shift_first,
        gain_second,
        shift_second,
    ) = gathered
    page_count = tokens.shape[0]
    feat_count = place_query.shape[1]
    group_heads = 4
    head_groups = HEADS // group_heads
    scaling = (3.0 * HD) ** (-0.5)

    def split_heads(values):
        count = values.shape[1]
        return values.reshape(page_count, count, head_groups, group_heads, HD).transpose(
            0, 2, 3, 1, 4
        )

    def merge_heads(values):
        count = values.shape[3]
        return values.transpose(0, 3, 1, 2, 4).reshape(page_count, count, HEADS * HD)

    def heads_place(place):
        return place.reshape(head_groups, group_heads, HD, feat_count)

    full_boxes, full_padding = (
        lax.all_gather(boxes, "pb", axis=2, tiled=True),
        lax.all_gather(padding, "pb", axis=1, tiled=True),
    )
    query_sines, query_cosines = trig_of(boxes, resolution)
    keys_sines, keys_cosines = trig_of(full_boxes, resolution)
    key_alive = full_padding == 1
    query_feats = features(query_cosines, query_sines).astype(jnp.bfloat16)
    keys_feats = features(keys_sines, keys_cosines).astype(jnp.bfloat16)
    queries = project(tokens, matrix_query, offset_query).astype(jnp.bfloat16)
    keys_own = project(tokens, matrix_keys, offset_keys).astype(jnp.bfloat16)
    values_own = project(tokens, matrix_values, offset_values).astype(jnp.bfloat16)
    keys_all, values_all = (
        lax.all_gather(keys_own, "pb", axis=1, tiled=True),
        lax.all_gather(values_own, "pb", axis=1, tiled=True),
    )

    def group_scores(group_q, group_k, group_pq, group_pk, page_data):
        q_feats, k_feats, q_sines, q_cosines, k_sines, k_cosines, alive_row = page_data
        spread_q = jnp.einsum("hqd,hde->hqe", group_q, group_pq, preferred_element_type=jnp.float32)
        turned_q = turn_query(spread_q, q_sines, q_cosines).astype(jnp.bfloat16)
        spread_k = jnp.einsum("hkd,hde->hke", group_k, group_pk, preferred_element_type=jnp.float32)
        turned_k = turn_key(spread_k, k_sines, k_cosines).astype(jnp.bfloat16)
        raw = jnp.einsum("hqd,hkd->hqk", group_q, group_k, preferred_element_type=jnp.float32)
        raw = raw + jnp.einsum("hqe,ke->hqk", turned_q, k_feats, preferred_element_type=jnp.float32)
        raw = raw + jnp.einsum("qe,hke->hqk", q_feats, turned_k, preferred_element_type=jnp.float32)
        return jnp.where(alive_row[None, None, :], raw * scaling, -1e30)

    page_items = (
        query_feats,
        keys_feats,
        query_sines,
        query_cosines,
        keys_sines,
        keys_cosines,
        key_alive,
    )
    split_q = split_heads(queries)
    split_k = split_heads(keys_all)
    split_v = split_heads(values_all)
    forward_pq = heads_place(place_query)
    forward_pk = heads_place(place_keys)

    def page_forward(item_set):
        heads_q, heads_k, heads_v = (item_set[0], item_set[1], item_set[2])
        page_data = item_set[3:]

        def group_forward(group):
            group_q, group_k, group_v, group_pq, group_pk = group
            scores = group_scores(group_q, group_k, group_pq, group_pk, page_data)
            row_max = jnp.max(scores, axis=-1, keepdims=True)
            lifted = jnp.exp(scores - row_max)
            row_total = jnp.sum(lifted, axis=-1, keepdims=True)
            attend = (lifted / row_total).astype(jnp.bfloat16)
            context = jnp.einsum(
                "hqk,hkd->hqd", attend, group_v, preferred_element_type=jnp.float32
            )
            return (context, (row_max + jnp.log(row_total))[..., 0])

        return lax.map(group_forward, (heads_q, heads_k, heads_v, forward_pq, forward_pk))

    contexts, log_totals = lax.map(page_forward, (split_q, split_k, split_v) + page_items)
    context = merge_heads(contexts).astype(jnp.bfloat16)
    branch = project(context, matrix_output, offset_output)
    pre_one = tokens.astype(jnp.float32) + branch
    first = layer_norm(pre_one, gain_first.astype(jnp.float32), shift_first.astype(jnp.float32))
    first_low = first.astype(jnp.bfloat16)
    inner = project(first_low, matrix_inner, offset_inner)
    activated = exact_gelu(inner).astype(jnp.bfloat16)
    outer = project(activated, matrix_outer, offset_outer)
    pre_two = first + outer
    output = layer_norm(pre_two, gain_second.astype(jnp.float32), shift_second.astype(jnp.float32))
    gathered = (
        lax.all_gather(shards[0], ("page", "pb"), axis=0, tiled=True),
        lax.all_gather(shards[1], ("page", "pb"), axis=0, tiled=True),
        lax.all_gather(shards[2], ("page", "pb"), axis=0, tiled=True),
        lax.all_gather(shards[3], ("page", "pb"), axis=0, tiled=True),
        lax.all_gather(shards[4], ("page", "pb"), axis=0, tiled=True),
        lax.all_gather(shards[5], ("page", "pb"), axis=0, tiled=True),
        lax.all_gather(shards[6], ("page", "pb"), axis=0, tiled=True),
        lax.all_gather(shards[7], ("page", "pb"), axis=0, tiled=True),
        lax.all_gather(shards[8], ("page", "pb"), axis=0, tiled=True),
        lax.all_gather(shards[9], ("page", "pb"), axis=0, tiled=True),
        lax.all_gather(shards[10], ("page", "pb"), axis=0, tiled=True),
        lax.all_gather(shards[11], ("page", "pb"), axis=0, tiled=True),
        lax.all_gather(shards[12], ("page", "pb"), axis=0, tiled=True),
        lax.all_gather(shards[13], ("page", "pb"), axis=0, tiled=True),
        lax.all_gather(shards[14], ("page", "pb"), axis=0, tiled=True),
        lax.all_gather(shards[15], ("page", "pb"), axis=0, tiled=True),
        lax.all_gather(shards[16], ("page", "pb"), axis=0, tiled=True),
        lax.all_gather(shards[17], ("page", "pb"), axis=0, tiled=True),
    )
    (
        matrix_query,
        matrix_keys,
        matrix_values,
        matrix_output,
        place_query,
        place_keys,
        matrix_inner,
        matrix_outer,
        offset_query,
        offset_keys,
        offset_values,
        offset_output,
        offset_inner,
        offset_outer,
        gain_first,
        shift_first,
        gain_second,
        shift_second,
    ) = gathered
    _, second_back = jax.vjp(
        layer_norm, pre_two, gain_second.astype(jnp.float32), shift_second.astype(jnp.float32)
    )
    pre_two_grad, second_gain_grad, second_shift_grad = second_back(cotangent.astype(jnp.float32))
    outer_grad = pre_two_grad.astype(jnp.bfloat16)
    outer_bias_grad = summed_rows(outer_grad)
    outer_weight_grad = weight_of(activated, outer_grad)
    activated_grad = back_through(outer_grad, matrix_outer)
    _, gelu_back = jax.vjp(exact_gelu, inner)
    inner_grad = gelu_back(activated_grad)[0].astype(jnp.bfloat16)
    inner_bias_grad = summed_rows(inner_grad)
    inner_weight_grad = weight_of(first_low, inner_grad)
    first_grad = pre_two_grad + back_through(inner_grad, matrix_inner)
    _, first_back = jax.vjp(
        layer_norm, pre_one, gain_first.astype(jnp.float32), shift_first.astype(jnp.float32)
    )
    pre_one_grad, first_gain_grad, first_shift_grad = first_back(first_grad)
    branch_grad = pre_one_grad.astype(jnp.bfloat16)
    output_bias_grad = summed_rows(branch_grad)
    output_weight_grad = weight_of(context, branch_grad)
    context_grad = back_through(branch_grad, matrix_output).astype(jnp.bfloat16)
    split_context = split_heads(context_grad)
    backward_pq = heads_place(place_query)
    backward_pk = heads_place(place_keys)

    def page_backward(carry, item_set):
        heads_q, heads_k, heads_v, heads_dc, page_lse = (
            item_set[0],
            item_set[1],
            item_set[2],
            item_set[3],
            item_set[4],
        )
        page_data = item_set[5:]
        q_feats, k_feats, q_sines, q_cosines, k_sines, k_cosines, alive_row = page_data

        def group_backward(group):
            group_q, group_k, group_v, group_dc, group_lse, group_pq, group_pk = group
            scores = group_scores(group_q, group_k, group_pq, group_pk, page_data)
            soft = jnp.exp(scores - group_lse[..., None])
            attend_grad = jnp.einsum(
                "hqd,hkd->hqk", group_dc, group_v, preferred_element_type=jnp.float32
            )
            row_dot = jnp.sum(soft * attend_grad, axis=-1, keepdims=True)
            raw_grad = (soft * (attend_grad - row_dot) * scaling).astype(jnp.bfloat16)
            values_grad = jnp.einsum(
                "hqk,hqd->hkd",
                soft.astype(jnp.bfloat16),
                group_dc,
                preferred_element_type=jnp.float32,
            )
            queries_grad = jnp.einsum(
                "hqk,hkd->hqd", raw_grad, group_k, preferred_element_type=jnp.float32
            )
            turned_q_grad = jnp.einsum(
                "hqk,ke->hqe", raw_grad, k_feats, preferred_element_type=jnp.float32
            )
            spread_q_grad = turn_query_back(turned_q_grad, q_sines, q_cosines).astype(jnp.bfloat16)
            queries_grad = queries_grad + jnp.einsum(
                "hqe,hde->hqd", spread_q_grad, group_pq, preferred_element_type=jnp.float32
            )
            place_q_grad = jnp.einsum(
                "hqd,hqe->hde", group_q, spread_q_grad, preferred_element_type=jnp.float32
            )
            keys_grad = jnp.einsum(
                "hqk,hqd->hkd", raw_grad, group_q, preferred_element_type=jnp.float32
            )
            turned_k_grad = jnp.einsum(
                "hqk,qe->hke", raw_grad, q_feats, preferred_element_type=jnp.float32
            )
            spread_k_grad = turn_key_back(turned_k_grad, k_sines, k_cosines)
            spread_upper = spread_k_grad.astype(jnp.bfloat16)
            spread_lower = (spread_k_grad - spread_upper.astype(jnp.float32)).astype(jnp.bfloat16)
            keys_grad = keys_grad + jnp.einsum(
                "hke,hde->hkd", spread_upper, group_pk, preferred_element_type=jnp.float32
            )
            keys_grad = keys_grad + jnp.einsum(
                "hke,hde->hkd", spread_lower, group_pk, preferred_element_type=jnp.float32
            )
            place_k_grad = jnp.einsum(
                "hkd,hke->hde", group_k, spread_upper, preferred_element_type=jnp.float32
            )
            place_k_grad = place_k_grad + jnp.einsum(
                "hkd,hke->hde", group_k, spread_lower, preferred_element_type=jnp.float32
            )
            return (queries_grad, keys_grad, values_grad, place_q_grad, place_k_grad)

        results = lax.map(
            group_backward,
            (heads_q, heads_k, heads_v, heads_dc, page_lse, backward_pq, backward_pk),
        )
        return (
            (carry[0] + results[3], carry[1] + results[4]),
            (results[0], results[1], results[2]),
        )

    zero_place = jnp.zeros((head_groups, group_heads, HD, feat_count), jnp.float32)
    (place_q_total, place_k_total), (q_grads, k_grads, v_grads) = lax.scan(
        page_backward,
        (zero_place, zero_place),
        (split_q, split_k, split_v, split_context, log_totals) + page_items,
    )
    queries_grad = merge_heads(q_grads).astype(jnp.bfloat16)
    keys_sum, values_sum = (
        lax.psum_scatter(
            merge_heads(k_grads).astype(jnp.bfloat16), "pb", scatter_dimension=1, tiled=True
        ).astype(jnp.float32),
        lax.psum_scatter(
            merge_heads(v_grads).astype(jnp.bfloat16), "pb", scatter_dimension=1, tiled=True
        ).astype(jnp.float32),
    )
    keys_grad = keys_sum.astype(jnp.bfloat16)
    values_grad = values_sum.astype(jnp.bfloat16)
    tokens_grad = pre_one_grad + back_through(queries_grad, matrix_query)
    tokens_grad = (
        tokens_grad
        + back_through(keys_grad, matrix_keys)
        + back_through(values_grad, matrix_values)
    )
    partial_sums = (
        weight_of(tokens, queries_grad),
        weight_of(tokens, keys_grad),
        weight_of(tokens, values_grad),
        output_weight_grad,
        place_q_total.reshape(HEADS * HD, feat_count),
        place_k_total.reshape(HEADS * HD, feat_count),
        inner_weight_grad,
        outer_weight_grad,
        summed_rows(queries_grad),
        summed_rows(keys_grad),
        summed_rows(values_grad),
        output_bias_grad,
        inner_bias_grad,
        outer_bias_grad,
        first_gain_grad,
        first_shift_grad,
        second_gain_grad,
        second_shift_grad,
    )
    totals = (
        lax.psum_scatter(partial_sums[0], ("page", "pb"), scatter_dimension=0, tiled=True),
        lax.psum_scatter(partial_sums[1], ("page", "pb"), scatter_dimension=0, tiled=True),
        lax.psum_scatter(partial_sums[2], ("page", "pb"), scatter_dimension=0, tiled=True),
        lax.psum_scatter(partial_sums[3], ("page", "pb"), scatter_dimension=0, tiled=True),
        lax.psum_scatter(partial_sums[4], ("page", "pb"), scatter_dimension=0, tiled=True),
        lax.psum_scatter(partial_sums[5], ("page", "pb"), scatter_dimension=0, tiled=True),
        lax.psum_scatter(partial_sums[6], ("page", "pb"), scatter_dimension=0, tiled=True),
        lax.psum_scatter(partial_sums[7], ("page", "pb"), scatter_dimension=0, tiled=True),
        lax.psum_scatter(partial_sums[8], ("page", "pb"), scatter_dimension=0, tiled=True),
        lax.psum_scatter(partial_sums[9], ("page", "pb"), scatter_dimension=0, tiled=True),
        lax.psum_scatter(partial_sums[10], ("page", "pb"), scatter_dimension=0, tiled=True),
        lax.psum_scatter(partial_sums[11], ("page", "pb"), scatter_dimension=0, tiled=True),
        lax.psum_scatter(partial_sums[12], ("page", "pb"), scatter_dimension=0, tiled=True),
        lax.psum_scatter(partial_sums[13], ("page", "pb"), scatter_dimension=0, tiled=True),
        lax.psum_scatter(partial_sums[14], ("page", "pb"), scatter_dimension=0, tiled=True),
        lax.psum_scatter(partial_sums[15], ("page", "pb"), scatter_dimension=0, tiled=True),
        lax.psum_scatter(partial_sums[16], ("page", "pb"), scatter_dimension=0, tiled=True),
        lax.psum_scatter(partial_sums[17], ("page", "pb"), scatter_dimension=0, tiled=True),
    )
    return (
        output.astype(jnp.bfloat16),
        tokens_grad,
        totals[0],
        totals[1],
        totals[2],
        totals[3],
        totals[4],
        totals[5],
        totals[6],
        totals[7],
        totals[8],
        totals[9],
        totals[10],
        totals[11],
        totals[12],
        totals[13],
        totals[14],
        totals[15],
        totals[16],
        totals[17],
    )


def solution(mesh):
    in_specs = (
        P("page", "pb", None),
        P("page", "pb", None),
        P(None, "page", "pb"),
        P(None, "page"),
        P("page", "pb"),
        P(("page", "pb"), None),
        P(("page", "pb"), None),
        P(("page", "pb"), None),
        P(("page", "pb"), None),
        P(("page", "pb"), None),
        P(("page", "pb"), None),
        P(("page", "pb"), None),
        P(("page", "pb"), None),
        P(("page", "pb")),
        P(("page", "pb")),
        P(("page", "pb")),
        P(("page", "pb")),
        P(("page", "pb")),
        P(("page", "pb")),
        P(("page", "pb")),
        P(("page", "pb")),
        P(("page", "pb")),
        P(("page", "pb")),
    )
    out_specs = (
        P("page", "pb", None),
        P("page", "pb", None),
        P(("page", "pb"), None),
        P(("page", "pb"), None),
        P(("page", "pb"), None),
        P(("page", "pb"), None),
        P(("page", "pb"), None),
        P(("page", "pb"), None),
        P(("page", "pb"), None),
        P(("page", "pb"), None),
        P(("page", "pb")),
        P(("page", "pb")),
        P(("page", "pb")),
        P(("page", "pb")),
        P(("page", "pb")),
        P(("page", "pb")),
        P(("page", "pb")),
        P(("page", "pb")),
        P(("page", "pb")),
        P(("page", "pb")),
    )
    return jax.shard_map(
        on_device, mesh=mesh, in_specs=in_specs, out_specs=out_specs, check_vma=False
    )
```

profile of v0, /device:TPU:1, one launch (start us, length us, event | category | flops | bytes accessed | tf_op | source)
XLA Modules:
  0.0 2114.4 jit_solution(15429502239535560302)
XLA Ops:
  17.9 41.5 %all-reduce.21 = (bf16[3072]{0:T(1024)(128)(2,1)S(1)}, bf16[768]{0:T(1024)(128)(2,1)S(1)}, bf16[768]{0:T(1024)(128)(2,1)S(1)}, bf16[768]{0:T(1024)(128)(2,1)S(1)...) all-reduce(bf16[3072]{0:T(1024)(128)(2,1)S(1)} %dynamic-update-slic, ...), channel_id=1, replica_groups=mesh['page'=8,'pb'=4] {'page','pb'}, use_global_device_ids=true, to_apply=%add.6 | all-reduce | flops 9984 | bytes 39936
  59.4 8.3 all-gather.17.cloned.1.call-done
  70.7 53.1 %all-gather.13.cloned.1.call-done = bf16[768,768]{1,0:T(8,128)(2,1)} async-done(((bf16[24,768]{1,0:T(8,128)(2,1)}), bf16[768,768]{1,0:T(8,128)(2,1)}) %all-gather.13.cloned.1.call-update) | async-done | bytes 1179664 | tf_op jit(solution)/shard_map/all_gather | solution.py:143
  141.7 9.8 fusion.150
  151.5 9.7 multiply_cosine_fusion.1
  182.8 21.4 %all-gather.19.cloned.1.call-done = bf16[3,512,768]{2,1,0:T(8,128)(2,1)} async-done(((bf16[3,128,768]{2,1,0:T(8,128)(2,1)}), bf16[3,512,768]{2,1,0:T(8,128)(2,1)}) %all-gather.19.cloned.1.call-update) | async-done | bytes 2359312 | tf_op jit(solution)/shard_map/all_gather | solution.py:214
  208.6 21.8 %all-gather.15.cloned.1.call-done = bf16[3,512,768]{2,1,0:T(8,128)(2,1)} async-done(((bf16[3,128,768]{2,1,0:T(8,128)(2,1)}), bf16[3,512,768]{2,1,0:T(8,128)(2,1)}) %all-gather.15.cloned.1.call-update) | async-done | bytes 2359312 | tf_op jit(solution)/shard_map/all_gather | solution.py:213
  234.7 52.6 %all-gather.21.cloned.1.call-done = bf16[768,768]{1,0:T(8,128)(2,1)} async-done(((bf16[24,768]{1,0:T(8,128)(2,1)}), bf16[768,768]{1,0:T(8,128)(2,1)}) %all-gather.21.cloned.1.call-update) | async-done | bytes 1179664 | tf_op jit(solution)/shard_map/all_gather | solution.py:146
  287.2 56.0 %all-gather.23.cloned.1.call-done = bf16[768,768]{1,0:T(8,128)(2,1)} async-done(((bf16[24,768]{1,0:T(8,128)(2,1)}), bf16[768,768]{1,0:T(8,128)(2,1)}) %all-gather.23.cloned.1.call-update) | async-done | bytes 1179664 | tf_op jit(solution)/shard_map/all_gather | solution.py:147
  344.2 128.7 %while.69 = (s32[]{:T(128)}, bf16[3,3,4,128,64]{3,4,2,1,0:T(8,128)(2,1)}, f32[3,3,4,128]{3,2,1,0:T(4,128)}, bf16[3,3,4,128,64]{3,4,2,1,0:T(8,128)(2,1)}, bf16[3,...) while((s32[]{:T(128)}, ...), condition=%wide.region_5.8_spmd.clone, body=%wide.region_0.7_spmd.sunk.clone | while | flops 1136524800 | bytes 55806020 | solution.py:261
  353.6 31.3 %while.68 = (s32[]{:T(128)}, bf16[3,4,128,64]{2,3,1,0:T(8,128)(2,1)}, f32[3,4,128]{2,1,0:T(4,128)S(1)}, pred[512]{0:T(512)(128)(4,1)S(1)}, bf16[3,4,128,64]{2,3,...) while((s32[]{:T(128)}, ...), condition=%wide.region_4.6_spmd, body=%wide.region_1.5_spmd.sunk | while | flops 1136524800 | bytes 45961972 | solution.py:259
  396.5 31.3 %while.68 = (s32[]{:T(128)}, bf16[3,4,128,64]{2,3,1,0:T(8,128)(2,1)}, f32[3,4,128]{2,1,0:T(4,128)S(1)}, pred[512]{0:T(512)(128)(4,1)S(1)}, bf16[3,4,128,64]{2,3,...) while((s32[]{:T(128)}, ...), condition=%wide.region_4.6_spmd, body=%wide.region_1.5_spmd.sunk | while | flops 1136524800 | bytes 45961972 | solution.py:259
  439.4 31.3 %while.68 = (s32[]{:T(128)}, bf16[3,4,128,64]{2,3,1,0:T(8,128)(2,1)}, f32[3,4,128]{2,1,0:T(4,128)S(1)}, pred[512]{0:T(512)(128)(4,1)S(1)}, bf16[3,4,128,64]{2,3,...) while((s32[]{:T(128)}, ...), condition=%wide.region_4.6_spmd, body=%wide.region_1.5_spmd.sunk | while | flops 1136524800 | bytes 45961972 | solution.py:259
  483.6 11.8 multiply_convert_fusion
  495.5 34.5 %all-gather.29.cloned.1.call-done = bf16[3072,768]{1,0:T(8,128)(2,1)} async-done(((bf16[96,768]{1,0:T(8,128)(2,1)}), bf16[3072,768]{1,0:T(8,128)(2,1)}) %all-gather.29.cloned.1.call-update) | async-done | bytes 4718608 | tf_op jit(solution)/shard_map/all_gather | solution.py:149
  538.8 7.1 convert_reduce_fusion
  554.1 571.7 %while.71 = (s32[]{:T(128)}, f32[3,4,64,768]{3,2,1,0:T(8,128)}, f32[3,4,64,768]{3,2,1,0:T(8,128)}, bf16[3,3,4,128,64]{3,4,2,1,0:T(8,128)(2,1)}, bf16[3,3,4,512,6...) while((s32[]{:T(128)}, f32[3,4,64,768]{3,2,1,0:T(8,128)}, ...), condition=%wide.region_18.21_spmd.clone.clone, body=%wide.region_14.20_spmd.clone.sunk.clone | while | flops 2979500032 | bytes 236758768 | solution.py:409
  570.6 165.8 %while.70 = (s32[]{:T(128)}, bf16[3,4,128,64]{2,3,1,0:T(8,128)(2,1)}, bf16[3,4,512,64]{2,3,1,0:T(8,128)(2,1)}, bf16[3,4,512,64]{2,3,1,0:T(8,128)(2,1)}, f32[3,4,...) while((s32[]{:T(128)}, ...), condition=%wide.region_17.19_spmd, body=%wide.region_15.18_spmd.sunk | while | flops 2977140736 | bytes 197410880 | solution.py:399
  760.1 165.8 %while.70 = (s32[]{:T(128)}, bf16[3,4,128,64]{2,3,1,0:T(8,128)(2,1)}, bf16[3,4,512,64]{2,3,1,0:T(8,128)(2,1)}, bf16[3,4,512,64]{2,3,1,0:T(8,128)(2,1)}, f32[3,4,...) while((s32[]{:T(128)}, ...), condition=%wide.region_17.19_spmd, body=%wide.region_15.18_spmd.sunk | while | flops 2977140736 | bytes 197410880 | solution.py:399
  951.0 165.8 %while.70 = (s32[]{:T(128)}, bf16[3,4,128,64]{2,3,1,0:T(8,128)(2,1)}, bf16[3,4,512,64]{2,3,1,0:T(8,128)(2,1)}, bf16[3,4,512,64]{2,3,1,0:T(8,128)(2,1)}, f32[3,4,...) while((s32[]{:T(128)}, ...), condition=%wide.region_17.19_spmd, body=%wide.region_15.18_spmd.sunk | while | flops 2977140736 | bytes 197410880 | solution.py:399
  1145.6 18.5 reduce-scatter.33.cloned.1.call-done
  1170.5 29.2 %reduce-scatter.31.cloned.1.call-done = bf16[128,2304]{1,0:T(8,128)(2,1)} async-done(((bf16[512,2304]{1,0:T(8,128)(2,1)}), bf16[128,2304]{1,0:T(8,128)(2,1)}) %reduce-scatter.31.cloned.1.call-update) | async-done | bytes 589840
  1207.3 6.9 convolution_bitcast_fusion.6
  1226.0 41.1 %all-reduce.20 = (f32[768]{0:T(1024)S(1)}, f32[768]{0:T(1024)S(1)}, f32[768]{0:T(1024)S(1)}, f32[768]{0:T(1024)S(1)}, f32[3072]{0:T(1024)S(1)}, /*index=5*/f32[7...) all-reduce(f32[768]{0:T(1024)S(1)} %reduce_sum.196, ...), channel_id=12, replica_groups=mesh['page'=8,'pb'=4] {'page','pb'}, use_global_device_ids=true, to_apply=%region_30.33.clone | all-reduce | flops 9984 | bytes 79872
  1277.1 25.9 %reduce-scatter.23.cloned.1.call-done = f32[24,768]{1,0:T(8,128)} async-done(((f32[768,768]{1,0:T(8,128)}), f32[24,768]{1,0:T(8,128)}) %reduce-scatter.23.cloned.1.call-update) | async-done | bytes 73744 | tf_op jit(solution)/shard_map/reduce_scatter | solution.py:456
  1303.0 104.7 %reduce-scatter.25.cloned.1.call-done = f32[24,768]{1,0:T(8,128)} async-done(((f32[768,768]{1,0:T(8,128)}), f32[24,768]{1,0:T(8,128)}) %reduce-scatter.25.cloned.1.call-update) | async-done | bytes 73744 | tf_op jit(solution)/shard_map/reduce_scatter | solution.py:457
  1407.7 103.7 %reduce-scatter.21.cloned.1.call-done = f32[24,768]{1,0:T(8,128)} async-done(((f32[768,768]{1,0:T(8,128)}), f32[24,768]{1,0:T(8,128)}) %reduce-scatter.21.cloned.1.call-update) | async-done | bytes 73744 | tf_op jit(solution)/shard_map/reduce_scatter | solution.py:455
  1511.4 104.7 %reduce-scatter.35.cloned.1.call-done = f32[24,768]{1,0:T(8,128)} async-done(((f32[768,768]{1,0:T(8,128)}), f32[24,768]{1,0:T(8,128)}) %reduce-scatter.35.cloned.1.call-update) | async-done | bytes 73744
  1616.0 103.7 %reduce-scatter.39.cloned.1.call-done = f32[24,768]{1,0:T(8,128)} async-done(((f32[768,768]{1,0:T(8,128)}), f32[24,768]{1,0:T(8,128)}) %reduce-scatter.39.cloned.1.call-update) | async-done | bytes 73744
  1719.7 104.7 %reduce-scatter.37.cloned.1.call-done = f32[24,768]{1,0:T(8,128)} async-done(((f32[768,768]{1,0:T(8,128)}), f32[24,768]{1,0:T(8,128)}) %reduce-scatter.37.cloned.1.call-update) | async-done | bytes 73744
  1824.4 140.7 %reduce-scatter.27.cloned.1.call-done = f32[24,3072]{1,0:T(8,128)} async-done(((f32[768,3072]{1,0:T(8,128)}), f32[24,3072]{1,0:T(8,128)}) %reduce-scatter.27.cloned.1.call-update) | async-done | bytes 294928 | tf_op jit(solution)/shard_map/reduce_scatter | solution.py:458
  1965.1 142.0 %reduce-scatter.29.cloned.1.call-done = f32[96,768]{1,0:T(8,128)} async-done(((f32[3072,768]{1,0:T(8,128)}), f32[96,768]{1,0:T(8,128)}) %reduce-scatter.29.cloned.1.call-update) | async-done | bytes 294928 | tf_op jit(solution)/shard_map/reduce_scatter | solution.py:459
  (1018 shorter events, 842.5 us)
Async XLA Ops:
  7.2 116.6 %copy-start.23 = (bf16[3,128,768]{2,1,0:T(8,128)(2,1)S(1)}, bf16[3,128,768]{2,1,0:T(8,128)(2,1)}, u32[]{:S(2)}) copy-start(bf16[3,128,768]{2,1,0:T(8,128)(2,1)} %param.35) | copy-start | bytes 1769476
  7.2 60.5 %all-gather.17.cloned.1.call-start = ((), (), s32[]{:S(2)}) async-start(), calls=%async_computation.13 | async-start | bytes 1216512 | tf_op jit(solution)/shard_map/all_gather | solution.py:144
  7.9 115.8 %all-gather.13.cloned.1.call-start = ((), (), s32[]{:S(2)}) async-start(), calls=%async_computation.11 | async-start | bytes 1216512 | tf_op jit(solution)/shard_map/all_gather | solution.py:143
  8.7 171.1 %all-gather.11.cloned.1.call-start = ((), (), s32[]{:S(2)}) async-start(), calls=%async_computation.10 | async-start | bytes 1216512 | tf_op jit(solution)/shard_map/all_gather | solution.py:142
  9.4 194.8 %all-gather.19.cloned.1.call-start = ((), (), s32[]{:S(2)}) async-start(), calls=%async_computation.14 | async-start | bytes 2949120 | tf_op jit(solution)/shard_map/all_gather | solution.py:214
  70.6 59.3 %copy-start.70 = (s32[2,3]{1,0:T(2,128)S(1)}, s32[2,3]{1,0:T(2,128)}, u32[]{:S(2)}) copy-start(s32[2,3]{1,0:T(2,128)} %param.38) | copy-start | bytes 76
  70.6 59.4 %copy-start.67 = (s32[4,3,128]{2,0,1:T(4,128)S(1)}, s32[4,3,128]{2,0,1:T(4,128)}, u32[]{:S(2)}) copy-start(s32[4,3,128]{2,0,1:T(4,128)} %param.37) | copy-start | bytes 18436
  70.7 159.7 %all-gather.15.cloned.1.call-start = ((), (), s32[]{:S(2)}) async-start(), calls=%async_computation.12 | async-start | bytes 2949120 | tf_op jit(solution)/shard_map/all_gather | solution.py:213
  126.5 160.7 %all-gather.21.cloned.1.call-start = ((), (), s32[]{:S(2)}) async-start(), calls=%async_computation.15 | async-start | bytes 1216512 | tf_op jit(solution)/shard_map/all_gather | solution.py:146
  127.1 216.1 %all-gather.23.cloned.1.call-start = ((), (), s32[]{:S(2)}) async-start(), calls=%async_computation.16 | async-start | bytes 1216512 | tf_op jit(solution)/shard_map/all_gather | solution.py:147
  127.8 345.1 %all-gather.25.cloned.1.call-start = ((), (), s32[]{:S(2)}) async-start(), calls=%async_computation.17 | async-start | bytes 1216512 | tf_op jit(solution)/shard_map/all_gather | solution.py:145
  128.6 347.1 %all-gather.27.cloned.1.call-start = ((), (), s32[]{:S(2)}) async-start(), calls=%async_computation.18 | async-start | bytes 4866048 | tf_op jit(solution)/shard_map/all_gather | solution.py:148
  129.3 400.6 %all-gather.29.cloned.1.call-start = ((), (), s32[]{:S(2)}) async-start(), calls=%async_computation.19 | async-start | bytes 4866048 | tf_op jit(solution)/shard_map/all_gather | solution.py:149
  129.9 1034.1 %reduce-scatter.33.cloned.1.call-start = ((), (), s32[]{:S(2)}) async-start(), calls=%async_computation.26 | async-start | bytes 2949120
  151.5 13.9 copy-start.71
  475.3 73.7 %copy-start.16 = (f32[3,128,768]{2,1,0:T(8,128)}, f32[3,128,768]{2,1,0:T(8,128)S(1)}, u32[]{:S(2)}) copy-start(f32[3,128,768]{2,1,0:T(8,128)S(1)} %get-tuple-element.817) | copy-start | bytes 3538948
  475.4 73.7 %copy-start.50 = (f32[3,128]{1,0:T(4,128)}, f32[3,128]{1,0:T(4,128)S(1)}, u32[]{:S(2)}) copy-start(f32[3,128]{1,0:T(4,128)S(1)} %broadcast_multiply_fusion.1) | copy-start | bytes 4612
  495.5 39.1 %copy-start.20 = (bf16[3,128,3072]{2,1,0:T(8,128)(2,1)}, bf16[3,128,3072]{2,1,0:T(8,128)(2,1)S(1)}, u32[]{:S(2)}) copy-start(bf16[3,128,3072]{2,1,0:T(8,128)(2,1)S(1)} %get-tuple-element.771) | copy-start | bytes 7077892
  529.9 8.9 copy-start.34
  536.8 9.1 slice-start
  743.8 8.5 copy-start.35
  934.7 8.5 copy-start.35
  1132.4 67.2 %reduce-scatter.31.cloned.1.call-start = ((), (), s32[]{:S(2)}) async-start(), calls=%async_computation.25 | async-start | bytes 2949120
  1139.1 163.9 %reduce-scatter.23.cloned.1.call-start = ((), (), s32[]{:S(2)}) async-start(), calls=%async_computation.21 | async-start | bytes 2433024 | tf_op jit(solution)/shard_map/reduce_scatter | solution.py:456
  1139.8 267.8 %reduce-scatter.25.cloned.1.call-start = ((), (), s32[]{:S(2)}) async-start(), calls=%async_computation.22 | async-start | bytes 2433024 | tf_op jit(solution)/shard_map/reduce_scatter | solution.py:457
  1140.4 371.0 %reduce-scatter.21.cloned.1.call-start = ((), (), s32[]{:S(2)}) async-start(), calls=%async_computation.20 | async-start | bytes 2433024 | tf_op jit(solution)/shard_map/reduce_scatter | solution.py:455
  1142.7 473.3 %reduce-scatter.35.cloned.1.call-start = ((), (), s32[]{:S(2)}) async-start(), calls=%async_computation.27 | async-start | bytes 2433024
  1145.6 574.2 %reduce-scatter.39.cloned.1.call-start = ((), (), s32[]{:S(2)}) async-start(), calls=%async_computation.29 | async-start | bytes 2433024
  1170.5 653.9 %reduce-scatter.37.cloned.1.call-start = ((), (), s32[]{:S(2)}) async-start(), calls=%async_computation.28 | async-start | bytes 2433024
  1206.1 759.0 %reduce-scatter.27.cloned.1.call-start = ((), (), s32[]{:S(2)}) async-start(), calls=%async_computation.23 | async-start | bytes 9732096 | tf_op jit(solution)/shard_map/reduce_scatter | solution.py:458
  1214.3 892.8 %reduce-scatter.29.cloned.1.call-start = ((), (), s32[]{:S(2)}) async-start(), calls=%async_computation.24 | async-start | bytes 9732096 | tf_op jit(solution)/shard_map/reduce_scatter | solution.py:459
  1225.7 49.6 %copy-start.42 = (bf16[768,768]{1,0:T(8,128)(2,1)S(1)}, bf16[768,768]{1,0:T(8,128)(2,1)}, u32[]{:S(2)}) copy-start(bf16[768,768]{1,0:T(8,128)(2,1)} %all-gather.17.cloned.1.call-done) | copy-start | bytes 3538948
  (196 other events, 693.6 us)
Sparse Core Ops, SparseCore 0:
  10.9 56.7 all-gather.16
  70.6 53.1 all-gather.12
  126.7 53.0 all-gather.10
  181.2 22.9 all-gather.18
  206.2 24.0 all-gather.14
  233.1 54.1 all-gather.20
  290.2 53.0 all-gather.22
  346.1 53.0 all-gather.24
  402.1 62.5 all-gather.26
  467.5 62.4 all-gather.28
  1132.6 31.4 reduce-scatter.32
  1166.6 33.0 reduce-scatter.30
  1205.6 97.3 reduce-scatter.22
  1309.5 98.0 reduce-scatter.24
  1413.4 97.9 reduce-scatter.20
  1517.9 98.0 reduce-scatter.34
  1621.8 97.9 reduce-scatter.38
  1726.3 98.0 reduce-scatter.36
  1830.9 134.1 reduce-scatter.26
  1972.4 134.6 reduce-scatter.28
where the time goes:
time: 2130 us; the launch traced here: 2110 us
  waiting for transfers between devices  1140 us (54%)
  matrix products  438 us (21%)
  local copies, waits for them, and re-layouts  240 us (11%)
  other arithmetic  189 us (9%)
  blocking collectives  93.2 us (4%)
    unnamed x25, waiting for transfers between devices  367 us
    reduce_scatter x1, waiting for transfers between devices, on_device(): lax.psum_scatter(partial_sums[7], ('page', 'pb'), scatter_dimension=0, ti...  142 us
    reduce_scatter x1, waiting for transfers between devices, on_device(): lax.psum_scatter(partial_sums[6], ('page', 'pb'), scatter_dimension=0, ti...  141 us
    reduce_scatter x1, waiting for transfers between devices, on_device(): lax.psum_scatter(partial_sums[5], ('page', 'pb'), scatter_dimension=0, ti...  105 us
    reduce_scatter x1, waiting for transfers between devices, on_device(): lax.psum_scatter(partial_sums[3], ('page', 'pb'), scatter_dimension=0, ti...  104 us
    unnamed x2, blocking collectives  82.6 us
    squeeze x48, local copies, waits for them, and re-layouts, on_device(): lax.map(page_forward, (split_q, split_k, split_v) + page_items)  72.9 us
    reshape x9, local copies, waits for them, and re-layouts, turn_key_back(): return turned.reshape(gradient.shape)  60.5 us
  transfers between devices with their start and end apart: 20, of which 18 were waited for; matrix products, arithmetic and copies ran while one was open for 12% of the time, Pallas kernels for 0%

commit v1 on v0

v1 whole, which is shorter than its diff:
```python
import functools
import math

import jax
import jax.numpy as jnp
from jax import lax
from jax.experimental import pallas as pl
from jax.experimental.pallas import tpu as pltpu
from jax.sharding import PartitionSpec as P

HEADS = 12
HD = 64
FREQ = 192
D = HEADS * HD
SPAN = 2 * FREQ
LOW = jnp.bfloat16
WIDE = jnp.float32
AXES = ("page", "pb")


def dot(a, b):
    return jnp.dot(a, b, preferred_element_type=WIDE)


def dot_nt(a, b):
    return lax.dot_general(a, b, (((1,), (1,)), ((), ())), preferred_element_type=WIDE)


def dot_tn(a, b):
    return lax.dot_general(a, b, (((0,), (0,)), ((), ())), preferred_element_type=WIDE)


def attend_kernel(heads, tok_ref, w_ref, bias_ref, pq_ref, pk_ref, sin_ref, cos_ref, alive_ref,
                  qkv_ref, soft_ref, ctx_ref):
    blocks, rows = tok_ref.shape[0], tok_ref.shape[2]
    count = blocks * rows
    width = heads * HD
    tok = tok_ref[...].reshape(count, D)
    sines, cosines = sin_ref[0], cos_ref[0]
    sines_low, cosines_low = sines.astype(LOW), cosines.astype(LOW)
    key_feats = jnp.concatenate([sines_low, cosines_low], axis=1)
    query_feats = jnp.concatenate([cosines_low, sines_low], axis=1)
    alive = alive_ref[0] > 0
    qkv = (dot(tok, w_ref[...]) + bias_ref[...]).astype(LOW)
    qkv_ref[0] = qkv
    scaling = (3.0 * HD) ** (-0.5)
    pieces = []
    for h in range(heads):
        q = qkv[:, h * HD:(h + 1) * HD]
        k = qkv[:, width + h * HD:width + (h + 1) * HD]
        v = qkv[:, 2 * width + h * HD:2 * width + (h + 1) * HD]
        spread = dot(q, pq_ref[h])
        s, c = spread[:, :SPAN], spread[:, SPAN:]
        turned_q = jnp.concatenate(
            [(s * cosines + c * sines).astype(LOW), (c * cosines - s * sines).astype(LOW)], axis=1)
        spread = dot(k, pk_ref[h])
        s, c = spread[:, :SPAN], spread[:, SPAN:]
        turned_k = jnp.concatenate(
            [(s * sines + c * cosines).astype(LOW), (c * sines - s * cosines).astype(LOW)], axis=1)
        raw = dot_nt(q, k) + dot_nt(turned_q, key_feats) + dot_nt(query_feats, turned_k)
        scores = jnp.where(alive, raw * scaling, -1e30)
        lifted = jnp.exp(scores - jnp.max(scores, axis=1, keepdims=True))
        soft = (lifted / jnp.sum(lifted, axis=1, keepdims=True)).astype(LOW)
        soft_ref[0, h] = soft
        pieces.append(dot(soft, v).astype(LOW))
    ctx = jnp.concatenate(pieces, axis=1)
    ctx_ref[...] = ctx.reshape(blocks, 1, rows, width)


def attend_call(tok_all, w_qkv, bias, place_q, place_k, sines, cosines, alive):
    blocks, pages, rows, _ = tok_all.shape
    heads = place_q.shape[0]
    width = heads * HD
    count = blocks * rows
    const = lambda shape: pl.BlockSpec(shape, lambda p: (0,) * len(shape))
    return pl.pallas_call(
        functools.partial(attend_kernel, heads),
        grid=(pages,),
        in_specs=[
            pl.BlockSpec((blocks, 1, rows, D), lambda p: (0, p, 0, 0)),
            const((D, 3 * width)),
            const((1, 3 * width)),
            const((heads, HD, 2 * SPAN)),
            const((heads, HD, 2 * SPAN)),
            pl.BlockSpec((1, count, SPAN), lambda p: (p, 0, 0)),
            pl.BlockSpec((1, count, SPAN), lambda p: (p, 0, 0)),
            pl.BlockSpec((1, 1, count), lambda p: (p, 0, 0)),
        ],
        out_specs=[
            pl.BlockSpec((1, count, 3 * width), lambda p: (p, 0, 0)),
            pl.BlockSpec((1, heads, count, count), lambda p: (p, 0, 0, 0)),
            pl.BlockSpec((blocks, 1, rows, width), lambda p: (0, p, 0, 0)),
        ],
        out_shape=[
            jax.ShapeDtypeStruct((pages, count, 3 * width), LOW),
            jax.ShapeDtypeStruct((pages, heads, count, count), LOW),
            jax.ShapeDtypeStruct((blocks, pages, rows, width), LOW),
        ],
        compiler_params=pltpu.CompilerParams(vmem_limit_bytes=56 * 1024 * 1024),
        name="attend",
    )(tok_all, w_qkv, bias, place_q, place_k, sines, cosines, alive)


def attend_back_kernel(heads, qkv_ref, soft_ref, dctx_ref, pq_ref, pk_ref, sin_ref, cos_ref,
                       dqkv_ref, dpq_ref, dpk_ref):
    blocks, rows = dctx_ref.shape[0], dctx_ref.shape[2]
    count = blocks * rows
    width = heads * HD
    sines, cosines = sin_ref[0], cos_ref[0]
    sines_low, cosines_low = sines.astype(LOW), cosines.astype(LOW)
    key_feats = jnp.concatenate([sines_low, cosines_low], axis=1)
    query_feats = jnp.concatenate([cosines_low, sines_low], axis=1)
    qkv = qkv_ref[0]
    dctx = dctx_ref[...].reshape(count, width)
    scaling = (3.0 * HD) ** (-0.5)

    @pl.when(pl.program_id(0) == 0)
    def _():
        dpq_ref[...] = jnp.zeros_like(dpq_ref)
        dpk_ref[...] = jnp.zeros_like(dpk_ref)

    d_q, d_k, d_v = [], [], []
    for h in range(heads):
        q = qkv[:, h * HD:(h + 1) * HD]
        k = qkv[:, width + h * HD:width + (h + 1) * HD]
        v = qkv[:, 2 * width + h * HD:2 * width + (h + 1) * HD]
        dc = dctx[:, h * HD:(h + 1) * HD]
        soft = soft_ref[0, h]
        soft_wide = soft.astype(WIDE)
        attend_grad = dot_nt(dc, v)
        row_dot = jnp.sum(soft_wide * attend_grad, axis=1, keepdims=True)
        raw_grad = (soft_wide * (attend_grad - row_dot) * scaling).astype(LOW)
        d_v.append(dot_tn(soft, dc).astype(LOW))
        turned = dot(raw_grad, key_feats)
        s, c = turned[:, :SPAN], turned[:, SPAN:]
        spread_q = jnp.concatenate(
            [(s * cosines - c * sines).astype(LOW), (s * sines + c * cosines).astype(LOW)], axis=1)
        d_q.append((dot(raw_grad, k) + dot_nt(spread_q, pq_ref[h])).astype(LOW))
        dpq_ref[h] += dot_tn(q, spread_q)
        turned = dot_tn(raw_grad, query_feats)
        s, c = turned[:, :SPAN], turned[:, SPAN:]
        spread_k = jnp.concatenate(
            [(s * sines - c * cosines).astype(LOW), (s * cosines + c * sines).astype(LOW)], axis=1)
        d_k.append((dot_tn(raw_grad, q) + dot_nt(spread_k, pk_ref[h])).astype(LOW))
        dpk_ref[h] += dot_tn(k, spread_k)
    dqkv_ref[0] = jnp.concatenate(d_q + d_k + d_v, axis=1)


def attend_back_call(qkv, soft, dctx, place_q, place_k, sines, cosines):
    blocks, pages, rows, width = dctx.shape
    heads = place_q.shape[0]
    count = blocks * rows
    const = lambda shape: pl.BlockSpec(shape, lambda p: (0,) * len(shape))
    return pl.pallas_call(
        functools.partial(attend_back_kernel, heads),
        grid=(pages,),
        in_specs=[
            pl.BlockSpec((1, count, 3 * width), lambda p: (p, 0, 0)),
            pl.BlockSpec((1, heads, count, count), lambda p: (p, 0, 0, 0)),
            pl.BlockSpec((blocks, 1, rows, width), lambda p: (0, p, 0, 0)),
            const((heads, HD, 2 * SPAN)),
            const((heads, HD, 2 * SPAN)),
            pl.BlockSpec((1, count, SPAN), lambda p: (p, 0, 0)),
            pl.BlockSpec((1, count, SPAN), lambda p: (p, 0, 0)),
        ],
        out_specs=[
            pl.BlockSpec((1, count, 3 * width), lambda p: (p, 0, 0)),
            const((heads, HD, 2 * SPAN)),
            const((heads, HD, 2 * SPAN)),
        ],
        out_shape=[
            jax.ShapeDtypeStruct((pages, count, 3 * width), LOW),
            jax.ShapeDtypeStruct((heads, HD, 2 * SPAN), WIDE),
            jax.ShapeDtypeStruct((heads, HD, 2 * SPAN), WIDE),
        ],
        compiler_params=pltpu.CompilerParams(vmem_limit_bytes=56 * 1024 * 1024),
        name="attend_back",
    )(qkv, soft, dctx, place_q, place_k, sines, cosines)


def swap(value, axis, size, bit):
    return lax.ppermute(value, axis, [(i, i ^ bit) for i in range(size)])


def gather_pb(value, size):
    if size != 4:
        return lax.all_gather(value, "pb", axis=0)
    me = lax.axis_index("pb")
    far = swap(value, "pb", 4, 2)
    near = swap(value, "pb", 4, 1)
    corner = swap(far, "pb", 4, 1)
    out = jnp.zeros((4,) + value.shape, value.dtype)
    for j, piece in enumerate((value, near, far, corner)):
        out = lax.dynamic_update_index_in_dim(out, piece, me ^ j, 0)
    return out


def gather_page(value, size):
    if size != 8:
        return lax.all_gather(value, "page", axis=0)
    me = lax.axis_index("page")
    out = jnp.zeros((8,) + value.shape, value.dtype)
    out = lax.dynamic_update_index_in_dim(out, value, me, 0)
    for step in (2, 4, 6):
        piece = swap(value, "page", 8, step)
        out = lax.dynamic_update_index_in_dim(out, piece, me ^ step, 0)
    mine = out.reshape((4, 2) + value.shape)
    half = me & 1
    mine = lax.dynamic_index_in_dim(mine, half, 1, keepdims=False)
    other = swap(mine, "page", 8, 1)
    both = jnp.zeros((4, 2) + value.shape, value.dtype)
    both = lax.dynamic_update_slice_in_dim(both, mine[:, None], half, 1)
    both = lax.dynamic_update_slice_in_dim(both, other[:, None], 1 - half, 1)
    return both.reshape((8,) + value.shape)


def transpose_roles(value, pages, size):
    inner = pages // size
    pairs = []
    for hi in range(size):
        for lo in range(inner):
            for b in range(size):
                pairs.append(((hi * inner + lo) * size + b, (b * inner + lo) * size + hi))
    return lax.ppermute(value, AXES, pairs)


def scatter_pb(partial, size):
    if size != 4:
        moved = lax.all_to_all(partial.astype(LOW), "pb", 0, 0, tiled=True)
        return jnp.sum(moved.astype(WIDE), axis=0)
    me = lax.axis_index("pb")
    core, row = me & 1, me >> 1
    cut = partial.reshape((2, 2) + partial.shape[1:])
    kept = lax.dynamic_index_in_dim(cut, core, 1, keepdims=False)
    sent = lax.dynamic_index_in_dim(cut, 1 - core, 1, keepdims=False)
    total = kept.astype(WIDE) + swap(sent.astype(LOW), "pb", 4, 1).astype(WIDE)
    kept = lax.dynamic_index_in_dim(total, row, 0, keepdims=False)
    sent = lax.dynamic_index_in_dim(total, 1 - row, 0, keepdims=False)
    return kept + swap(sent.astype(LOW), "pb", 4, 2).astype(WIDE)


def layer_norm(values, gain, shift):
    centred = values - jnp.mean(values, axis=-1, keepdims=True)
    spread = jnp.mean(centred * centred, axis=-1, keepdims=True)
    return centred * lax.rsqrt(spread + 1e-05) * gain + shift


def exact_gelu(values):
    return jax.nn.gelu(values, approximate=False)


def summed_rows(gradient):
    return jnp.sum(gradient.astype(WIDE), axis=0)


def to_halves(place):
    cut = place.reshape(place.shape[:-1] + (2, 2, FREQ))
    return jnp.swapaxes(cut, -3, -2).reshape(place.shape)


def on_device(sizes, tokens, cotangent, boxes, resolution, padding,
              query_weight, keys_weight, values_weight, output_weight, query_place, keys_place,
              inner_weight, outer_weight, query_bias, keys_bias, values_bias, output_bias,
              inner_bias, outer_bias, first_gain, first_shift, second_gain, second_shift):
    page_size, pb_size = sizes
    devices = page_size * pb_size
    pages, rows, _ = tokens.shape
    count = rows * pb_size
    heads = HEADS // pb_size
    width = heads * HD
    own = query_weight.shape[0]
    ff_own = outer_weight.shape[0]
    ff = ff_own * devices
    ff_cuts = ff // D

    small = [output_bias, inner_bias, outer_bias, first_gain, first_shift, second_gain, second_shift]
    lengths = [s.shape[0] for s in small]
    small_row = jnp.concatenate(small)
    small_rows = 8
    small_row = jnp.pad(small_row, (0, small_rows * D - small_row.shape[0])).reshape(small_rows, D)
    packed = jnp.concatenate(
        [output_weight]
        + [inner_weight[:, j * D:(j + 1) * D] for j in range(ff_cuts)]
        + [outer_weight, small_row], axis=0)
    late = lax.all_gather(packed, AXES, axis=0)

    tok_all = gather_pb(tokens, pb_size)
    grid_x = (boxes[0] + boxes[2]) * 500 // resolution[0][:, None]
    grid_y = (boxes[1] + boxes[3]) * 500 // resolution[1][:, None]
    places = gather_pb(jnp.stack([grid_x, grid_y, padding]), pb_size)
    places = places.transpose(1, 2, 0, 3).reshape(3, pages, count)
    rates = jnp.exp(jnp.arange(FREQ).astype(WIDE) * (-math.log(10000.0) / FREQ))
    grids = places[:2].astype(WIDE)
    angles = jnp.concatenate(
        [grids[0][..., None] * rates, grids[1][..., None] * rates], axis=-1)
    sines, cosines = jnp.sin(angles), jnp.cos(angles)
    alive = places[2][:, None, :]

    cols = jnp.stack([query_weight, keys_weight, values_weight]).reshape(3, own, pb_size, width)
    cols = cols.transpose(2, 1, 0, 3).reshape(pb_size, own, 3 * width)
    cols = lax.all_to_all(cols, "pb", 0, 0, tiled=True)
    w_qkv = gather_page(cols, page_size).reshape(D, 3 * width)
    bias_row = jnp.concatenate([query_bias, keys_bias, values_bias])
    bias_row = jnp.pad(bias_row, (0, 8 * D - bias_row.shape[0])).reshape(8, D)
    mixed = jnp.concatenate([to_halves(query_place), to_halves(keys_place), bias_row], axis=0)
    mixed = gather_page(transpose_roles(mixed, page_size, pb_size), page_size)
    inner_pages = page_size // pb_size
    mixed = mixed.reshape((pb_size, inner_pages) + mixed.shape[1:]).swapaxes(0, 1)
    mixed = mixed.reshape((page_size,) + mixed.shape[2:])
    place_q = mixed[:, :own].reshape(heads, HD, 2 * SPAN)
    place_k = mixed[:, own:2 * own].reshape(heads, HD, 2 * SPAN)
    bias_qkv = mixed[:, 2 * own, :3 * own].reshape(page_size, 3, own).swapaxes(0, 1)
    bias_qkv = bias_qkv.reshape(1, 3 * width).astype(WIDE)

    qkv, soft, ctx_heads = attend_call(
        tok_all, w_qkv, bias_qkv, place_q, place_k, sines, cosines, alive)

    ctx = lax.all_to_all(ctx_heads, "pb", 0, 0, tiled=True)
    context = ctx.transpose(1, 2, 0, 3).reshape(pages * rows, D)

    at = 0
    matrix_output = late[:, :own].reshape(D, D)
    at = own
    matrix_inner = jnp.concatenate(
        [late[:, at + j * own:at + (j + 1) * own].reshape(D, D) for j in range(ff_cuts)], axis=1)
    at += own * ff_cuts
    matrix_outer = late[:, at:at + ff_own].reshape(ff, D)
    at += ff_own
    flat = late[:, at:].reshape(devices, small_rows * D)
    vectors, at = [], 0
    for length in lengths:
        vectors.append(flat[:, at:at + length].reshape(devices * length).astype(WIDE))
        at += length
    offset_output, offset_inner, offset_outer, gain_one, shift_one, gain_two, shift_two = vectors

    tok = tokens.reshape(pages * rows, D)
    pre_one = tok.astype(WIDE) + (dot(context, matrix_output) + offset_output)
    first, first_back = jax.vjp(layer_norm, pre_one, gain_one, shift_one)
    first_low = first.astype(LOW)
    inner = dot(first_low, matrix_inner) + offset_inner
    activated, gelu_back = jax.vjp(exact_gelu, inner)
    activated = activated.astype(LOW)
    pre_two = first + (dot(activated, matrix_outer) + offset_outer)
    output, second_back = jax.vjp(layer_norm, pre_two, gain_two, shift_two)
    pre_two_grad, gain_two_grad, shift_two_grad = second_back(
        cotangent.reshape(pages * rows, D).astype(WIDE))
    outer_grad = pre_two_grad.astype(LOW)
    outer_weight_grad = dot_tn(activated, outer_grad)
    inner_grad = gelu_back(dot_nt(outer_grad, matrix_outer))[0].astype(LOW)
    inner_weight_grad = dot_tn(first_low, inner_grad)
    first_grad = pre_two_grad + dot_nt(inner_grad, matrix_inner)
    pre_one_grad, gain_one_grad, shift_one_grad = first_back(first_grad)
    branch_grad = pre_one_grad.astype(LOW)
    output_weight_grad = dot_tn(context, branch_grad)
    context_grad = dot_nt(branch_grad, matrix_output).astype(LOW)

    small_grads = [summed_rows(branch_grad), summed_rows(inner_grad), summed_rows(outer_grad),
                   gain_one_grad, shift_one_grad, gain_two_grad, shift_two_grad]
    small_grads = jnp.concatenate([g.reshape(devices, -1) for g in small_grads], axis=1)
    small_grads = jnp.pad(small_grads, ((0, 0), (0, small_rows * D - small_grads.shape[1])))
    packed_grads = jnp.concatenate(
        [output_weight_grad.astype(LOW).reshape(devices, own, D)]
        + [inner_weight_grad[:, j * D:(j + 1) * D].astype(LOW).reshape(devices, own, D)
           for j in range(ff_cuts)]
        + [outer_weight_grad.astype(LOW).reshape(devices, ff_own, D),
           small_grads.astype(LOW).reshape(devices, small_rows, D)], axis=1)
    late_sum = lax.psum_scatter(packed_grads, AXES, scatter_dimension=0, tiled=False)
    late_sum = late_sum.astype(WIDE)

    dctx = context_grad.reshape(pages, rows, pb_size, width).transpose(2, 0, 1, 3)
    dctx = lax.all_to_all(dctx, "pb", 0, 0, tiled=True)
    dqkv, dpq, dpk = attend_back_call(qkv, soft, dctx, place_q, place_k, sines, cosines)

    dqkv_flat = dqkv.reshape(pages, pb_size, rows, 3 * width)
    partial = jnp.einsum("pbne,de->bpnd", dqkv_flat, w_qkv, preferred_element_type=WIDE)
    tokens_grad = pre_one_grad.reshape(pages, rows, D) + scatter_pb(partial, pb_size)
    d_w = jnp.einsum("bpnd,pbne->de", tok_all, dqkv_flat, preferred_element_type=WIDE)
    d_bias = jnp.sum(dqkv.astype(WIDE), axis=(0, 1))

    d_w = d_w.astype(LOW).reshape(page_size, pb_size * own * 3 * width)
    d_mixed = jnp.stack([dpq.reshape(page_size, own, D), dpk.reshape(page_size, own, D)], axis=1)
    d_mixed = d_mixed.astype(LOW).reshape(page_size, 2 * own * D)
    d_bias = d_bias.astype(LOW).reshape(3, page_size, own).swapaxes(0, 1).reshape(page_size, 3 * own)
    d_mixed = jnp.concatenate([d_mixed, d_bias], axis=1)
    d_mixed = d_mixed.reshape((inner_pages, pb_size) + d_mixed.shape[1:]).swapaxes(0, 1)
    d_mixed = d_mixed.reshape((page_size,) + d_mixed.shape[2:])
    joined = jnp.concatenate([d_w, d_mixed], axis=1)
    total = joined.shape[1]
    padded = -total % (8 * 128)
    joined = jnp.pad(joined, ((0, 0), (0, padded))).reshape(page_size, -1, 128)
    joined = lax.all_to_all(joined, "page", 0, 0, tiled=True)
    joined = jnp.sum(joined.astype(WIDE), axis=0).reshape(-1)
    cut = pb_size * own * 3 * width
    d_cols = joined[:cut].astype(LOW).reshape(pb_size, own, 3 * width)
    d_cols = lax.all_to_all(d_cols, "pb", 0, 0, tiled=True).astype(WIDE)
    d_cols = d_cols.reshape(pb_size, own, 3, width).transpose(2, 1, 0, 3).reshape(3, own, D)
    d_mixed = transpose_roles(joined[cut:cut + 2 * own * D + 3 * own], page_size, pb_size)
    d_places = to_halves(d_mixed[:2 * own * D].reshape(2, own, D))
    d_bias = d_mixed[2 * own * D:].reshape(3, own)

    at = own * (1 + ff_cuts)
    small_sum = late_sum[at + ff_own:].reshape(-1)
    vectors, cursor = [], 0
    for length in lengths:
        vectors.append(small_sum[cursor:cursor + length])
        cursor += length
    return (
        output.astype(LOW).reshape(pages, rows, D),
        tokens_grad,
        d_cols[0], d_cols[1], d_cols[2],
        late_sum[:own],
        d_places[0], d_places[1],
        jnp.concatenate([late_sum[own * (1 + j):own * (2 + j)] for j in range(ff_cuts)], axis=1),
        late_sum[at:at + ff_own],
        d_bias[0], d_bias[1], d_bias[2],
        *vectors,
    )


def solution(mesh):
    rows, vector = P(AXES, None), P(AXES)
    token = P("page", "pb", None)
    in_specs = (token, token, P(None, "page", "pb"), P(None, "page"), P("page", "pb"))
    in_specs = in_specs + (rows,) * 8 + (vector,) * 10
    out_specs = (token, token) + (rows,) * 8 + (vector,) * 10
    sizes = (mesh.shape["page"], mesh.shape["pb"])
    return jax.shard_map(
        functools.partial(on_device, sizes), mesh=mesh, in_specs=in_specs, out_specs=out_specs,
        check_vma=False)
```

time: 2130 us -> 434 us (0.20)
  waiting for transfers between devices: 1140 us -> 121 us
  matrix products: 438 us -> 48.2 us
  other arithmetic: 189 us -> 36 us
  local copies, waits for them, and re-layouts: 240 us -> 99.2 us
  blocking collectives: 93.2 us -> 0 us
  starting transfers between devices: 0.79 us -> 55.9 us
  Pallas kernels: 0 us -> 50.8 us
    reduce_scatter x5 -> x1, waiting for transfers between devices: 517 us -> 27.5 us  [on_device(): lax.psum_scatter(packed_grads, AXES, scatter_dimension=0, tiled=False)]
    dot_general x225 -> x11, matrix products: 438 us -> 48.2 us  [the longest x3 21.2 us: dot(): return jnp.dot(a, b, preferred_element_type=WIDE)]
    unnamed x25 -> x2, waiting for transfers between devices: 367 us -> 0.03 us
    all_gather x10 -> x1, waiting for transfers between devices: 251 us -> 0.01 us  [on_device(): late = lax.all_gather(packed, AXES, axis=0)]
    another operation x122 -> x5, other arithmetic: 94.8 us -> 3.99 us
    unnamed x2 -> x0, blocking collectives: 82.6 us -> none
    squeeze x51 -> x7, local copies, waits for them, and re-layouts: 75 us -> 4.66 us  [the longest x2 0.91 us: gather_page(): mine = lax.dynamic_index_in_dim(mine, half, 1, keepdims=False)]
    pallas_call x0 -> x2, Pallas kernels: none -> 50.8 us  [the longest x1 27.5 us: attend_back_call(): pl.pallas_call(functools.partial(attend_back_kernel, heads), grid=(pages,...]
  transfers between devices with their start and end apart: 20 -> 25, of which waited for: 18 -> 12; matrix products, arithmetic and copies ran while one was open for 12% -> 21% of each run, Pallas kernels for 0% -> 12%
where the time goes in v1:
time: 434 us; the launch traced here: 427 us
  waiting for transfers between devices  121 us (28%)
  local copies, waits for them, and re-layouts  99.2 us (23%)
  starting transfers between devices  55.9 us (13%)
  Pallas kernels  50.8 us (12%)
  matrix products  48.2 us (11%)
  other arithmetic  36 us (8%)
  between operations  15.5 us (4%)
    ppermute x16, waiting for transfers between devices, swap(): return lax.ppermute(value, axis, [(i, i ^ bit) for i in range(size)])  42 us
    all_to_all x1, waiting for transfers between devices, on_device(): joined = lax.all_to_all(joined, 'page', 0, 0, tiled=True)  32.4 us
    ppermute x16, starting transfers between devices, swap(): return lax.ppermute(value, axis, [(i, i ^ bit) for i in range(size)])  29.7 us
    pallas_call x1, Pallas kernels, attend_back_call(): pl.pallas_call(functools.partial(attend_back_kernel, heads), grid=(pages,...  27.5 us
    reduce_scatter x1, waiting for transfers between devices, on_device(): lax.psum_scatter(packed_grads, AXES, scatter_dimension=0, tiled=False)  27.5 us
    pallas_call x1, Pallas kernels, attend_call(): pl.pallas_call(functools.partial(attend_kernel, heads), grid=(pages,), in...  23.3 us
    dot_general x3, matrix products, dot(): return jnp.dot(a, b, preferred_element_type=WIDE)  21.2 us
    unnamed x94, local copies, waits for them, and re-layouts  20 us
  transfers between devices with their start and end apart: 25, of which 12 were waited for; matrix products, arithmetic and copies ran while one was open for 21% of the time, Pallas kernels for 12%

profile of v1, /device:TPU:1, one launch (start us, length us, event | category | flops | bytes accessed | tf_op | source)
XLA Modules:
  0.0 426.7 jit_solution(6929710919376029662)
XLA Ops:
  7.3 4.8 %concatenate.41 = bf16[240]{0:T(256)(128)(2,1)S(1)} concatenate(bf16[24]{0:T(256)(128)(2,1)} %param.41, bf16[96]{0:T(256)(128)(2,1)} %param.42, bf16[24]{0:T(256)(128)(2,1)} %param.43, bf16[24]{0:T(256)(128)(2,1)} %param.44, bf16[24]{0:T(256)(128)(2,1)} %param.45, bf16[24]{0:T(256)(128)(2,1)} %param.46, bf16[24]{0:T(256)(128)(2,1)} %param.47), dimensions={0} | concatenate | bytes 960 | tf_op jit(solution)/shard_map/concatenate | solution.py:278
  21.0 2.7 collective-permute-start.13
  28.2 3.5 all-to-all-start
  32.4 3.4 collective-permute-start.7
  38.4 10.1 %fusion.12 = (f32[3,512,384]{2,1,0:T(8,128)}, f32[3,512,384]{2,1,0:T(8,128)}) fusion(f32[3,512,192]{2,1,0:T(8,128)S(1)} %get-tuple-element.100, f32[3,512,192]{2,1,0:T(8,128)S(1)} %get-tuple-element.99), kind=kLoop, calls=%fused_computation.33 | loop fusion | flops 589824 | bytes 7077888 | tf_op jit(solution)/shard_map/cos | solution.py:296
  49.1 3.2 collective-permute-start.5
  52.9 11.3 %collective-permute-done.8 = bf16[56,768]{1,0:T(8,128)(2,1)S(1)} collective-permute-done((bf16[56,768]{1,0:T(8,128)(2,1)S(1)}, bf16[56,768]{1,0:T(8,128)(2,1)S(1)}, u32[]{:S(2)}, u32[]{:S(2)}) %collective-permute-start.8) | collective-permute-done | bytes 86048 | tf_op jit(solution)/shard_map/ppermute | solution.py:182
  66.1 14.4 %collective-permute-done.9 = bf16[56,768]{1,0:T(8,128)(2,1)S(1)} collective-permute-done((bf16[56,768]{1,0:T(8,128)(2,1)S(1)}, bf16[56,768]{1,0:T(8,128)(2,1)S(1)}, u32[]{:S(2)}, u32[]{:S(2)}) %collective-permute-start.9) | collective-permute-done | bytes 86048 | tf_op jit(solution)/shard_map/ppermute | solution.py:182
  80.5 2.8 collective-permute-start.10
  92.0 11.3 %collective-permute-done.11 = bf16[4,56,768]{2,1,0:T(8,128)(2,1)S(1)} collective-permute-done((bf16[4,56,768]{2,1,0:T(8,128)(2,1)S(1)}, bf16[4,56,768]{2,1,0:T(8,128)(2,1)S(1)}, u32[]{:S(2)}, u32[]{:S(2)}) %collective-permute-start.11) | collective-permute-done | bytes 344096 | tf_op jit(solution)/shard_map/ppermute | solution.py:182
  112.1 15.7 %collective-permute-start.2 = (bf16[3,128,768]{2,1,0:T(8,128)(2,1)}, bf16[3,128,768]{2,1,0:T(8,128)(2,1)S(1)}, u32[]{:S(2)}, u32[]{:S(2)}) collective-permute-start(bf16[3,128,768]{2,1,0:T(8,128)(2,1)} %collective-permute-done.1), channel_id=1, source_target_pairs={{0,1},{1,0},{2,3},{3,2},{4,5},{5,4},{6,7},{7,6},{8,9},{9,8},{10,11... | collective-permute-start | bytes 1769480 | tf_op jit(solution)/shard_map/ppermute | solution.py:182
  132.8 23.3 %attend.1 = (bf16[3,512,576]{2,1,0:T(8,128)(2,1)}, bf16[3,3,512,512]{3,2,1,0:T(8,128)(2,1)}, bf16[4,3,128,192]{3,2,1,0:T(8,128)(2,1)}) custom-call(bf16[4,3,128,768]{3,2,1,0:T(8,128)(2,1)} %copy-done.1, bf16[768,576]{1,0:T(8,128)(2,1)} %bitcast.211, f32[1,576]{1,0:T(1,128)} %reshape.449.bias_ref, bf16[3,64,768]{2,1,0:T(8,128)(2,1)} %bitcast.218, ...), custom_call_target="tpu_custom_call" | custom-call | tf_op jit(solution)/shard_map/attend/pallas_call | solution.py:76
  158.4 3.6 all-to-all-start.1
  162.5 8.3 %all-to-all-done.1 = bf16[4,3,128,192]{2,3,1,0:T(8,128)(2,1)S(1)} async-done(((bf16[4,3,128,192]{2,3,1,0:T(8,128)(2,1)}), bf16[4,3,128,192]{2,3,1,0:T(8,128)(2,1)S(1)}, u32[]{:S(2)}, u32[]{:S(2)}) %all-to-all-start.1) | async-done | bytes 589856 | tf_op jit(solution)/shard_map/all_to_all | solution.py:318
  174.5 5.1 %slice.304 = bf16[32,96,768]{2,1,0:T(8,128)(2,1)} slice(bf16[32,224,768]{2,1,0:T(8,128)(2,1)} %bitcast.195), slice={[0:32], [120:216], [0:768]} | slice | bytes 9437184 | tf_op jit(solution)/shard_map/slice | solution.py:327
  179.6 2.4 fusion.54
  187.8 17.1 %multiply_convert_fusion = (bf16[384,3072]{1,0:T(8,128)(2,1)S(1)}, f32[384,3072]{1,0:T(8,128)S(1)}, f32[384,3072]{1,0:T(8,128)}) fusion(f32[3072]{0:T(1024)S(1)} %copy-done.24, bf16[768,768]{1,0:T(8,128)(2,1)} %bitcast.230, bf16[768,768]{1,0:T(8,128)(2,1)} %bitcast.232, bf16[768,768]{1,0:T(8,128)(2,1)} %bitcast.234, bf16[768,768]{1,0:T(8,128)(2,1)} %bitcast.236, ...), kind=kOutput, calls=%fused_computation.6 | convolution fusion | flops 1910145024 | bytes 17716224 | tf_op jit(solution)/shard_map/dot_general | solution.py:22
  210.6 6.0 %fusion.50 = (bf16[3072]{0:T(1024)(128)(2,1)}, bf16[384,3072]{1,0:T(8,128)(2,1)S(1)}) fusion(f32[384,3072]{1,0:T(8,128)S(1)} %get-tuple-element.49, f32[384,3072]{1,0:T(8,128)} %get-tuple-element.107, bf16[384,768]{1,0:T(8,128)(2,1)S(1)} %get-tuple-element.39, bf16[3072,768]{1,0:T(8,128)(2,1)S(1)} %bitcast.209), kind=kOutput, calls=%fused_computation.173 | convolution fusion | flops 1829630976 | bytes 17111040 | tf_op jit(solution)/shard_map/dot_general | solution.py:26
  216.6 2.9 multiply_reduce_fusion
  219.5 4.8 %convolution_convert_fusion.1 = bf16[768,3072]{1,0:T(8,128)(2,1)} fusion(bf16[384,3072]{1,0:T(8,128)(2,1)S(1)} %get-tuple-element.41, f32[384,768]{1,0:T(8,128)S(1)} %get-tuple-element.106, f32[768]{0:T(1024)S(1)} %copy-done.27, f32[768]{0:T(1024)S(1)} %copy-done.23, f32[384]{0:T(512)S(1)} %fusion.38, f32[384]{0:T(512)S(1)} %broadcast_multiply_fusion.3), kind=kOutput, calls=%fused_computation.2 | convolution fusion | flops 1815773184 | bytes 8266752 | tf_op jit(solution)/shard_map/dot_general | solution.py:30
  224.3 4.3 %convolution_convert_fusion = bf16[3072,768]{1,0:T(8,128)(2,1)} fusion(bf16[384,3072]{1,0:T(8,128)(2,1)S(1)} %get-tuple-element.48, bf16[384,768]{1,0:T(8,128)(2,1)S(1)} %get-tuple-element.39), kind=kOutput, calls=%fused_computation.1 | convolution fusion | flops 1814298624 | bytes 7667712 | tf_op jit(solution)/shard_map/dot_general | solution.py:30
  236.5 2.8 fusion.55
  245.1 2.5 constant_dynamic-update-slice_fusion.4
  251.2 4.7 %all-to-all-start.2 = ((bf16[4,3,128,192]{2,3,1,0:T(8,128)(2,1)}), bf16[4,3,128,192]{2,3,1,0:T(8,128)(2,1)S(1)}, u32[]{:S(2)}, u32[]{:S(2)}) async-start(bf16[4,3,128,192]{2,3,1,0:T(8,128)(2,1)} %copy.138), calls=%async_computation.2 | async-start | bytes 1179648 | tf_op jit(solution)/shard_map/all_to_all | solution.py:371
  256.0 8.6 %all-to-all-done.2 = bf16[4,3,128,192]{2,3,1,0:T(8,128)(2,1)S(1)} async-done(((bf16[4,3,128,192]{2,3,1,0:T(8,128)(2,1)}), bf16[4,3,128,192]{2,3,1,0:T(8,128)(2,1)S(1)}, u32[]{:S(2)}, u32[]{:S(2)}) %all-to-all-start.2) | async-done | bytes 589856 | tf_op jit(solution)/shard_map/all_to_all | solution.py:371
  265.8 27.5 %attend_back.1 = (bf16[3,512,576]{2,1,0:T(8,128)(2,1)}, f32[3,64,768]{2,1,0:T(8,128)}, f32[3,64,768]{2,1,0:T(8,128)}) custom-call(bf16[3,512,576]{2,1,0:T(8,128)(2,1)} %get-tuple-element.28.qkv_ref, bf16[3,3,512,512]{3,2,1,0:T(8,128)(2,1)} %get-tuple-element.29.soft_ref, bf16[4,3,128,192]{3,2,1,0:T(8,128)(2,1)} %copy.139.dctx_ref, ...), custom_call_target="tpu_custom_call" | custom-call | tf_op jit(solution)/shard_map/attend_back/pallas_call | solution.py:154
  297.4 4.1 bitcast_convert_fusion
  312.3 4.3 %all-to-all-start.3 = ((bf16[8,728,128]{2,1,0:T(8,128)(2,1)}), bf16[8,728,128]{2,1,0:T(8,128)(2,1)}, u32[]{:S(2)}, u32[]{:S(2)}) async-start(bf16[8,728,128]{2,1,0:T(8,128)(2,1)} %copy.149), calls=%async_computation.3 | async-start | bytes 2981888 | tf_op jit(solution)/shard_map/all_to_all | solution.py:391
  316.5 3.6 fusion.64
  332.0 32.4 %all-to-all-done.3 = bf16[8,728,128]{2,1,0:T(8,128)(2,1)} async-done(((bf16[8,728,128]{2,1,0:T(8,128)(2,1)}), bf16[8,728,128]{2,1,0:T(8,128)(2,1)}, u32[]{:S(2)}, u32[]{:S(2)}) %all-to-all-start.3) | async-done | bytes 1490976 | tf_op jit(solution)/shard_map/all_to_all | solution.py:391
  369.1 4.6 %all-to-all-start.4 = ((bf16[4,24,576]{2,1,0:T(8,128)(2,1)}), bf16[4,24,576]{2,1,0:T(8,128)(2,1)}, u32[]{:S(2)}, u32[]{:S(2)}) async-start(bf16[4,24,576]{2,1,0:T(8,128)(2,1)} %convert_element_type.238), calls=%async_computation.4 | async-start | bytes 245760 | tf_op jit(solution)/shard_map/all_to_all | solution.py:395
  387.1 27.5 %reduce-scatter.2.cloned.1.call-done = bf16[1,224,768]{2,1,0:T(8,128)(2,1)} async-done(((bf16[32,224,768]{2,1,0:T(8,128)(2,1)}), bf16[1,224,768]{2,1,0:T(8,128)(2,1)}) %reduce-scatter.2.cloned.1.call-update) | async-done | bytes 344080 | tf_op jit(solution)/shard_map/reduce_scatter | solution.py:367
  (294 shorter events, 127.8 us)
Async XLA Ops:
  7.2 24.5 %copy-start.31 = (bf16[24]{0:T(256)(128)(2,1)S(1)}, bf16[24]{0:T(256)(128)(2,1)}, u32[]{:S(2)}) copy-start(bf16[24]{0:T(256)(128)(2,1)} %param.40) | copy-start | bytes 148
  7.2 24.5 %copy-start.32 = (bf16[24]{0:T(256)(128)(2,1)S(1)}, bf16[24]{0:T(256)(128)(2,1)}, u32[]{:S(2)}) copy-start(bf16[24]{0:T(256)(128)(2,1)} %param.39) | copy-start | bytes 148
  7.2 24.5 %copy-start.33 = (bf16[24]{0:T(256)(128)(2,1)S(1)}, bf16[24]{0:T(256)(128)(2,1)}, u32[]{:S(2)}) copy-start(bf16[24]{0:T(256)(128)(2,1)} %param.38) | copy-start | bytes 148
  7.2 24.6 %copy-start.17 = (bf16[24,768]{1,0:T(8,128)(2,1)S(1)}, bf16[24,768]{1,0:T(8,128)(2,1)}, u32[]{:S(2)}) copy-start(bf16[24,768]{1,0:T(8,128)(2,1)} %param.34) | copy-start | bytes 110596
  7.2 24.8 %copy-start.18 = (bf16[24,768]{1,0:T(8,128)(2,1)S(1)}, bf16[24,768]{1,0:T(8,128)(2,1)}, u32[]{:S(2)}) copy-start(bf16[24,768]{1,0:T(8,128)(2,1)} %param.35) | copy-start | bytes 110596
  7.2 165.8 %all-gather.3.cloned.1.call-start = ((), (), s32[]{:S(2)}) async-start(), calls=%async_computation.7 | async-start | bytes 11354112 | tf_op jit(solution)/shard_map/all_gather | solution.py:285
  20.9 15.4 %collective-permute-start.12 = (s32[3,3,128]{2,1,0:T(4,128)S(1)}, s32[3,3,128]{2,1,0:T(4,128)S(1)}, u32[]{:S(2)}, u32[]{:S(2)}) collective-permute-start(s32[3,3,128]{2,1,0:T(4,128)S(1)} %get-tuple-element.93), channel_id=1, source_target_pairs={{0,1},{1,0},{2,3},{3,2},{4,5},{5,4},{6,7},{7,6},{8,9},{9,8},{10,11... | collective-permute-start | bytes 13832 | tf_op jit(solution)/shard_map/ppermute | solution.py:182
  21.0 15.1 %collective-permute-start.13 = (s32[3,3,128]{2,1,0:T(4,128)S(1)}, s32[3,3,128]{2,1,0:T(4,128)S(1)}, u32[]{:S(2)}, u32[]{:S(2)}) collective-permute-start(s32[3,3,128]{2,1,0:T(4,128)S(1)} %get-tuple-element.93), channel_id=1, source_target_pairs={{0,2},{1,3},{2,0},{3,1},{4,6},{5,7},{6,4},{7,5},{8,10},{9,11},{10,... | collective-permute-start | bytes 13832 | tf_op jit(solution)/shard_map/ppermute | solution.py:182
  23.7 88.4 %collective-permute-start.1 = (bf16[3,128,768]{2,1,0:T(8,128)(2,1)}, bf16[3,128,768]{2,1,0:T(8,128)(2,1)}, u32[]{:S(2)}, u32[]{:S(2)}) collective-permute-start(bf16[3,128,768]{2,1,0:T(8,128)(2,1)} %param.25), channel_id=1, source_target_pairs={{0,2},{1,3},{2,0},{3,1},{4,6},{5,7},{6,4},{7,5},{8,10},{9,11},{10,... | collective-permute-start | bytes 1769480 | tf_op jit(solution)/shard_map/ppermute | solution.py:182
  23.7 104.1 %collective-permute-start = (bf16[3,128,768]{2,1,0:T(8,128)(2,1)}, bf16[3,128,768]{2,1,0:T(8,128)(2,1)}, u32[]{:S(2)}, u32[]{:S(2)}) collective-permute-start(bf16[3,128,768]{2,1,0:T(8,128)(2,1)} %param.25), channel_id=1, source_target_pairs={{0,1},{1,0},{2,3},{3,2},{4,5},{5,4},{6,7},{7,6},{8,9},{9,8},{10,11... | collective-permute-start | bytes 1769480 | tf_op jit(solution)/shard_map/ppermute | solution.py:182
  28.2 20.9 %all-to-all-start = ((bf16[4,24,576]{2,1,0:T(8,128)(2,1)}), bf16[4,24,576]{2,1,0:T(8,128)(2,1)S(1)}, u32[]{:S(2)}, u32[]{:S(2)}) async-start(bf16[4,24,576]{2,1,0:T(8,128)(2,1)} %reshape.402), calls=%async_computation | async-start | bytes 245760 | tf_op jit(solution)/shard_map/all_to_all | solution.py:301
  32.4 20.1 %collective-permute-start.7 = (bf16[56,768]{1,0:T(8,128)(2,1)S(1)}, bf16[56,768]{1,0:T(8,128)(2,1)S(1)}, u32[]{:S(2)}, u32[]{:S(2)}) collective-permute-start(bf16[56,768]{1,0:T(8,128)(2,1)S(1)} %pad_maximum_fusion.6), channel_id=1, source_target_pairs={{0,0},{1,8},{2,16},{3,24},{4,4},{5,12},{6,20},{7,28},{8,1},{9,9},{... | collective-permute-start | bytes 258056 | tf_op jit(solution)/shard_map/ppermute | solution.py:224
  36.1 1.2 collective-permute-start.14
  49.1 41.9 %collective-permute-start.5 = (bf16[4,24,576]{2,1,0:T(8,128)(2,1)S(1)}, bf16[4,24,576]{2,1,0:T(8,128)(2,1)S(1)}, u32[]{:S(2)}, u32[]{:S(2)}) collective-permute-start(bf16[4,24,576]{2,1,0:T(8,128)(2,1)S(1)} %all-to-all-done), channel_id=1, source_target_pairs={{0,24},{4,28},{8,16},{12,20},{16,8},{20,12},{24,0},{28,4},{1,25},{... | collective-permute-start | bytes 331784 | tf_op jit(solution)/shard_map/ppermute | solution.py:182
  52.3 38.6 %collective-permute-start.4 = (bf16[4,24,576]{2,1,0:T(8,128)(2,1)S(1)}, bf16[4,24,576]{2,1,0:T(8,128)(2,1)S(1)}, u32[]{:S(2)}, u32[]{:S(2)}) collective-permute-start(bf16[4,24,576]{2,1,0:T(8,128)(2,1)S(1)} %all-to-all-done), channel_id=1, source_target_pairs={{0,16},{4,20},{8,24},{12,28},{16,0},{20,4},{24,8},{28,12},{1,17},{... | collective-permute-start | bytes 331784 | tf_op jit(solution)/shard_map/ppermute | solution.py:182
  52.4 11.8 %collective-permute-start.8 = (bf16[56,768]{1,0:T(8,128)(2,1)S(1)}, bf16[56,768]{1,0:T(8,128)(2,1)S(1)}, u32[]{:S(2)}, u32[]{:S(2)}) collective-permute-start(bf16[56,768]{1,0:T(8,128)(2,1)S(1)} %collective-permute-done.7), channel_id=1, source_target_pairs={{0,8},{4,12},{8,0},{12,4},{16,24},{20,28},{24,16},{28,20},{1,9},{5... | collective-permute-start | bytes 258056 | tf_op jit(solution)/shard_map/ppermute | solution.py:182
  64.2 16.3 %collective-permute-start.9 = (bf16[56,768]{1,0:T(8,128)(2,1)S(1)}, bf16[56,768]{1,0:T(8,128)(2,1)S(1)}, u32[]{:S(2)}, u32[]{:S(2)}) collective-permute-start(bf16[56,768]{1,0:T(8,128)(2,1)S(1)} %collective-permute-done.7), channel_id=1, source_target_pairs={{0,16},{4,20},{8,24},{12,28},{16,0},{20,4},{24,8},{28,12},{1,17},{... | collective-permute-start | bytes 258056 | tf_op jit(solution)/shard_map/ppermute | solution.py:182
  80.5 5.1 %collective-permute-start.10 = (bf16[56,768]{1,0:T(8,128)(2,1)S(1)}, bf16[56,768]{1,0:T(8,128)(2,1)S(1)}, u32[]{:S(2)}, u32[]{:S(2)}) collective-permute-start(bf16[56,768]{1,0:T(8,128)(2,1)S(1)} %collective-permute-done.7), channel_id=1, source_target_pairs={{0,24},{4,28},{8,16},{12,20},{16,8},{20,12},{24,0},{28,4},{1,25},{... | collective-permute-start | bytes 258056 | tf_op jit(solution)/shard_map/ppermute | solution.py:182
  85.6 3.7 collective-permute-start.3
  89.4 13.9 %collective-permute-start.11 = (bf16[4,56,768]{2,1,0:T(8,128)(2,1)S(1)}, bf16[4,56,768]{2,1,0:T(8,128)(2,1)S(1)}, u32[]{:S(2)}, u32[]{:S(2)}) collective-permute-start(bf16[4,56,768]{2,1,0:T(8,128)(2,1)S(1)} %fusion.80), channel_id=1, source_target_pairs={{0,4},{4,0},{8,12},{12,8},{16,20},{20,16},{24,28},{28,24},{1,5},{5... | collective-permute-start | bytes 1032200 | tf_op jit(solution)/shard_map/ppermute | solution.py:182
  92.0 38.0 %collective-permute-start.6 = (bf16[4,4,24,576]{3,2,1,0:T(8,128)(2,1)}, bf16[4,4,24,576]{3,2,1,0:T(8,128)(2,1)}, u32[]{:S(2)}, u32[]{:S(2)}) collective-permute-start(bf16[4,4,24,576]{3,2,1,0:T(8,128)(2,1)} %get-tuple-element.62), channel_id=1, source_target_pairs={{0,4},{4,0},{8,12},{12,8},{16,20},{20,16},{24,28},{28,24},{1,5},{5... | collective-permute-start | bytes 1327112 | tf_op jit(solution)/shard_map/ppermute | solution.py:182
  112.1 19.0 %collective-permute-start.2 = (bf16[3,128,768]{2,1,0:T(8,128)(2,1)}, bf16[3,128,768]{2,1,0:T(8,128)(2,1)S(1)}, u32[]{:S(2)}, u32[]{:S(2)}) collective-permute-start(bf16[3,128,768]{2,1,0:T(8,128)(2,1)} %collective-permute-done.1), channel_id=1, source_target_pairs={{0,1},{1,0},{2,3},{3,2},{4,5},{5,4},{6,7},{7,6},{8,9},{9,8},{10,11... | collective-permute-start | bytes 1769480 | tf_op jit(solution)/shard_map/ppermute | solution.py:182
  158.4 12.3 %all-to-all-start.1 = ((bf16[4,3,128,192]{2,3,1,0:T(8,128)(2,1)}), bf16[4,3,128,192]{2,3,1,0:T(8,128)(2,1)S(1)}, u32[]{:S(2)}, u32[]{:S(2)}) async-start(bf16[4,3,128,192]{2,3,1,0:T(8,128)(2,1)} %copy.136), calls=%async_computation.1 | async-start | bytes 1179648 | tf_op jit(solution)/shard_map/all_to_all | solution.py:318
  162.1 252.5 %reduce-scatter.2.cloned.1.call-start = ((), (), s32[]{:S(2)}) async-start(), calls=%async_computation.6 | async-start | bytes 11354112 | tf_op jit(solution)/shard_map/reduce_scatter | solution.py:367
  185.5 19.4 %slice-start.2 = ((s8[4718592]{0:T(1024)(128)(4,1)}), s8[4194304]{0:T(1024)(128)(4,1)S(1)}, s32[]{:S(2)}) async-start(s8[4718592]{0:T(1024)(128)(4,1)} %bitcast.206), calls=%async_computation.10 | async-start | bytes 8388608
  187.8 31.8 %copy-start.26 = (f32[384]{0:T(512)}, f32[384]{0:T(512)S(1)}, u32[]{:S(2)}) copy-start(f32[384]{0:T(512)S(1)} %fusion.38) | copy-start | bytes 4612
  251.2 13.4 %all-to-all-start.2 = ((bf16[4,3,128,192]{2,3,1,0:T(8,128)(2,1)}), bf16[4,3,128,192]{2,3,1,0:T(8,128)(2,1)S(1)}, u32[]{:S(2)}, u32[]{:S(2)}) async-start(bf16[4,3,128,192]{2,3,1,0:T(8,128)(2,1)} %copy.138), calls=%async_computation.2 | async-start | bytes 1179648 | tf_op jit(solution)/shard_map/all_to_all | solution.py:371
  312.3 52.1 %all-to-all-start.3 = ((bf16[8,728,128]{2,1,0:T(8,128)(2,1)}), bf16[8,728,128]{2,1,0:T(8,128)(2,1)}, u32[]{:S(2)}, u32[]{:S(2)}) async-start(bf16[8,728,128]{2,1,0:T(8,128)(2,1)} %copy.149), calls=%async_computation.3 | async-start | bytes 2981888 | tf_op jit(solution)/shard_map/all_to_all | solution.py:391
  323.8 4.8 %collective-permute-start.15 = (bf16[2,3,128,768]{3,2,1,0:T(8,128)(2,1)}, bf16[2,3,128,768]{3,2,1,0:T(8,128)(2,1)}, u32[]{:S(2)}, u32[]{:S(2)}) collective-permute-start(bf16[2,3,128,768]{3,2,1,0:T(8,128)(2,1)} %bitcast.171), channel_id=1, source_target_pairs={{0,1},{1,0},{2,3},{3,2},{4,5},{5,4},{6,7},{7,6},{8,9},{9,8},{10,11... | collective-permute-start | bytes 3538952 | tf_op jit(solution)/shard_map/ppermute | solution.py:182
  331.8 41.9 %collective-permute-start.16 = (bf16[3,128,768]{2,1,0:T(8,128)(2,1)}, bf16[3,128,768]{2,1,0:T(8,128)(2,1)}, u32[]{:S(2)}, u32[]{:S(2)}) collective-permute-start(bf16[3,128,768]{2,1,0:T(8,128)(2,1)} %fusion.24), channel_id=1, source_target_pairs={{0,2},{1,3},{2,0},{3,1},{4,6},{5,7},{6,4},{7,5},{8,10},{9,11},{10,... | collective-permute-start | bytes 1769480 | tf_op jit(solution)/shard_map/ppermute | solution.py:182
  369.1 10.0 %all-to-all-start.4 = ((bf16[4,24,576]{2,1,0:T(8,128)(2,1)}), bf16[4,24,576]{2,1,0:T(8,128)(2,1)}, u32[]{:S(2)}, u32[]{:S(2)}) async-start(bf16[4,24,576]{2,1,0:T(8,128)(2,1)} %convert_element_type.238), calls=%async_computation.4 | async-start | bytes 245760 | tf_op jit(solution)/shard_map/all_to_all | solution.py:395
  376.9 7.8 %collective-permute-start.17 = (f32[36936]{0:T(1024)S(1)}, f32[36936]{0:T(1024)S(1)}, u32[]{:S(2)}, u32[]{:S(2)}) collective-permute-start(f32[36936]{0:T(1024)S(1)} %slice.317), channel_id=1, source_target_pairs={{0,0},{1,8},{2,16},{3,24},{4,4},{5,12},{6,20},{7,28},{8,1},{9,9},{... | collective-permute-start | bytes 443240 | tf_op jit(solution)/shard_map/ppermute | solution.py:224
  (31 other events, 168.6 us)
Sparse Core Ops, SparseCore 0:
  17.8 118.5 all-gather.2
  248.6 165.9 reduce-scatter.1

commit v2 on v1

v2 whole, which is shorter than its diff:
```python
import functools
import math

import jax
import jax.numpy as jnp
from jax import lax
from jax.experimental import pallas as pl
from jax.experimental.pallas import tpu as pltpu
from jax.sharding import PartitionSpec as P

HEADS = 12
HD = 64
FREQ = 192
D = HEADS * HD
SPAN = 2 * FREQ
SCALING = (3.0 * HD) ** (-0.5)
LOW = jnp.bfloat16
WIDE = jnp.float32
AXES = ("page", "pb")
VMEM_BYTES = 56 * 1024 * 1024


def dot(a, b):
    return jnp.dot(a, b, preferred_element_type=WIDE)


def dot_nt(a, b):
    return lax.dot_general(a, b, (((1,), (1,)), ((), ())), preferred_element_type=WIDE)


def dot_tn(a, b):
    return lax.dot_general(a, b, (((0,), (0,)), ((), ())), preferred_element_type=WIDE)


def whole(shape):
    return pl.BlockSpec(shape, lambda i, *_: (0,) * len(shape))


def cost(flops, bytes_accessed):
    return pl.CostEstimate(flops=int(flops), bytes_accessed=int(bytes_accessed), transcendentals=0)


def lanes_to(rows, length, start):
    lane = lax.broadcasted_iota(jnp.int32, rows.shape, 1)
    rows = jnp.where(lane < length, rows, 0.0)
    padded = jnp.concatenate([rows, jnp.zeros((rows.shape[0], D - rows.shape[1]), WIDE)], axis=1)
    return pltpu.roll(padded, start, 1)


def halves(place):
    cut = [place[:, i * FREQ:(i + 1) * FREQ] for i in (0, 2, 1, 3)]
    return jnp.concatenate(cut, axis=1)


def pack_kernel(size, at_ref, vec_ref, wq_ref, wk_ref, wv_ref, pq_ref, pk_ref, wo_ref, wi_ref, wu_ref,
                late_ref, cols_ref, mixed_ref):
    number, place_at = at_ref[3], at_ref[4]
    own, ff_own = wq_ref.shape[0], wu_ref.shape[0]
    cuts = wi_ref.shape[1] // D
    width = D // size
    vectors = vec_ref[...]
    lanes = lanes_to(vectors[:8], own, number * own)
    row = lax.broadcasted_iota(jnp.int32, lanes.shape, 0)
    first = jnp.where(row < 6, lanes, 0.0)
    inner = lanes_to(vectors[8:16], ff_own, lax.rem(number, D // ff_own) * ff_own)
    spot = lax.div(number, D // ff_own)
    for j in range(cuts):
        hit = (row == (6 + j) % 8) & (spot == j)
        if 6 + j < 8:
            first = first + jnp.where(hit, pltpu.roll(inner, 6 + j, 0), 0.0)
    second = jnp.zeros_like(first)
    for j in range(2, cuts):
        hit = (row == j - 2) & (spot == j)
        second = second + jnp.where(hit, pltpu.roll(inner, j - 2, 0), 0.0)
    wi = wi_ref[...].astype(WIDE)
    late = [wu_ref[...].astype(WIDE)] + [wi[:, j * D:(j + 1) * D] for j in range(cuts)]
    late += [first, second, wo_ref[...].astype(WIDE)]
    late_ref[...] = jnp.concatenate(late, axis=0).astype(LOW)
    cols = jnp.concatenate([ref[...].astype(WIDE) for ref in (wq_ref, wk_ref, wv_ref)], axis=0)
    for b in range(size):
        cols_ref[b] = cols[:, b * width:(b + 1) * width].astype(LOW)
    lanes = lanes_to(vectors[16:24], own, place_at * own)
    bias = jnp.concatenate(
        [lanes[i:i + 1, :width] for i in range(3)] + [jnp.zeros((1, D - 3 * width), WIDE)], axis=1)
    bias = jnp.concatenate([bias, jnp.zeros((7, D), WIDE)], axis=0)
    places = [halves(pq_ref[...].astype(WIDE)), halves(pk_ref[...].astype(WIDE)), bias]
    mixed_ref[...] = jnp.concatenate(places, axis=0).astype(LOW)


def pack_call(at, vectors, *weights):
    own, ff_own = weights[0].shape[0], weights[-1].shape[0]
    size = 4
    rows = ff_own + weights[-2].shape[1] // D * own + 16 + own
    return pl.pallas_call(
        functools.partial(pack_kernel, size),
        out_shape=[
            jax.ShapeDtypeStruct((rows, D), LOW),
            jax.ShapeDtypeStruct((size, 3 * own, D // size), LOW),
            jax.ShapeDtypeStruct((2 * own + 8, D), LOW),
        ],
        in_specs=[pl.BlockSpec(memory_space=pltpu.SMEM)]
        + [pl.BlockSpec(memory_space=pltpu.VMEM)] * (1 + len(weights)),
        compiler_params=pltpu.CompilerParams(vmem_limit_bytes=VMEM_BYTES),
        name="pack",
    )(at, vectors, *weights)


def finish_kernel(cols_ref, mixed_ref, *out_refs):
    own = out_refs[0].shape[0]
    cols = [cols_ref[b].astype(WIDE) for b in range(cols_ref.shape[0])]
    for i in range(3):
        out_refs[i][...] = jnp.concatenate([c[i * own:(i + 1) * own] for c in cols], axis=1)
    mixed = mixed_ref[...].astype(WIDE)
    for i in range(2):
        out_refs[3 + i][...] = halves(mixed[i * own:(i + 1) * own])


def finish_call(cols, mixed):
    own = cols.shape[1] // 3
    return pl.pallas_call(
        finish_kernel,
        out_shape=[jax.ShapeDtypeStruct((own, D), WIDE)] * 5,
        compiler_params=pltpu.CompilerParams(vmem_limit_bytes=VMEM_BYTES),
        name="finish",
    )(cols, mixed)


def assemble_kernel(own, size, at_ref, mine_ref, theirs_ref, w_ref, pq_ref, pk_ref, bias_ref, got):
    pages = got.shape[0]
    inner = pages // size
    width = D // size
    even = (at_ref[1] >> 1) == 0
    for z in range(pages // 2):
        mine, theirs = mine_ref[at_ref[2] ^ z].astype(WIDE), theirs_ref[at_ref[2] ^ z].astype(WIDE)
        got[2 * z] = jnp.where(even, mine, theirs)
        got[2 * z + 1] = jnp.where(even, theirs, mine)
    columns = []
    for part in range(3):
        rows = got[:, pl.ds(part * own, own)]
        cut = [rows[:, :, b * width:(b + 1) * width][:, None] for b in range(size)]
        columns.append(jnp.concatenate(cut, axis=1).reshape(D, width))
    w_ref[...] = jnp.concatenate(columns, axis=1).astype(LOW)
    for start, ref in ((3 * own, pq_ref), (4 * own, pk_ref)):
        order = [b * inner + lo for lo in range(inner) for b in range(size)]
        rows = jnp.concatenate([got[p, pl.ds(start, own)] for p in order], axis=0)
        ref[...] = rows.astype(LOW).reshape(ref.shape)
    bias_ref[...] = jnp.sum(got[:, pl.ds(5 * own, 8)], axis=0)[:1, :3 * width]


def assemble_call(at, mine, theirs, own, size):
    width = D // size
    place = (width // HD, HD, 2 * SPAN)
    return pl.pallas_call(
        functools.partial(assemble_kernel, own, size),
        out_shape=[
            jax.ShapeDtypeStruct((D, 3 * width), LOW),
            jax.ShapeDtypeStruct(place, LOW),
            jax.ShapeDtypeStruct(place, LOW),
            jax.ShapeDtypeStruct((1, 3 * width), WIDE),
        ],
        in_specs=[pl.BlockSpec(memory_space=pltpu.SMEM)] + [pl.BlockSpec(memory_space=pltpu.VMEM)] * 2,
        scratch_shapes=[pltpu.VMEM((2 * mine.shape[0],) + mine.shape[1:], WIDE)],
        compiler_params=pltpu.CompilerParams(vmem_limit_bytes=VMEM_BYTES),
        name="assemble",
    )(at, mine, theirs)


def turn(spread, left, right):
    s, c = spread[:, :SPAN], spread[:, SPAN:]
    return jnp.concatenate(
        [(s * left + c * right).astype(LOW), (c * left - s * right).astype(LOW)], axis=1)


def turn_back(gradient, left, right):
    s, c = gradient[:, :SPAN], gradient[:, SPAN:]
    return jnp.concatenate(
        [(s * left - c * right).astype(LOW), (s * right + c * left).astype(LOW)], axis=1)


def feature_pair(sines, cosines):
    sines, cosines = sines.astype(LOW), cosines.astype(LOW)
    return (jnp.concatenate([sines, cosines], axis=1), jnp.concatenate([cosines, sines], axis=1))


def attend_kernel(heads, blocks, me_ref, *refs):
    tok_refs = refs[:blocks]
    (w_ref, bias_ref, pq_ref, pk_ref, sin_ref, cos_ref, alive_ref,
     qkv_ref, soft_ref, ctx_ref) = refs[blocks:]
    me = me_ref[0]
    rows = tok_refs[0].shape[1]
    width = heads * HD
    tok = jnp.concatenate([ref[0] for ref in tok_refs], axis=0)
    sines, cosines = sin_ref[0], cos_ref[0]
    key_feats, query_feats = feature_pair(sines, cosines)
    alive = alive_ref[0] > 0
    qkv = (dot(tok, w_ref[...]) + bias_ref[...]).astype(LOW)
    qkv_ref[0] = qkv
    pieces = []
    for h in range(heads):
        q = qkv[:, h * HD:(h + 1) * HD]
        k = qkv[:, width + h * HD:width + (h + 1) * HD]
        v = qkv[:, 2 * width + h * HD:2 * width + (h + 1) * HD]
        turned_q = turn(dot(q, pq_ref[h]), cosines, sines)
        turned_k = turn(dot(k, pk_ref[h]), sines, cosines)
        raw = dot_nt(q, k) + dot_nt(turned_q, key_feats) + dot_nt(query_feats, turned_k)
        scores = jnp.where(alive, raw * SCALING, -1e30)
        lifted = jnp.exp(scores - jnp.max(scores, axis=1, keepdims=True))
        soft = (lifted / jnp.sum(lifted, axis=1, keepdims=True)).astype(LOW)
        soft_ref[0, h] = soft
        pieces.append(dot(soft, v).astype(LOW))
    ctx = jnp.concatenate(pieces, axis=1)
    for j in range(blocks):
        ctx_ref[me ^ j, 0] = ctx[j * rows:(j + 1) * rows]


def attend_call(me, toks, w_qkv, bias, place_q, place_k, sines, cosines, alive):
    blocks = len(toks)
    pages, rows, _ = toks[0].shape
    heads = place_q.shape[0]
    width = heads * HD
    count = blocks * rows
    by_page = lambda *shape: pl.BlockSpec((1,) + shape, lambda p, *_: (p,) + (0,) * len(shape))
    return pl.pallas_call(
        functools.partial(attend_kernel, heads, blocks),
        grid_spec=pltpu.PrefetchScalarGridSpec(
            num_scalar_prefetch=1,
            grid=(pages,),
            in_specs=[by_page(rows, D)] * blocks + [
                whole((D, 3 * width)), whole((1, 3 * width)),
                whole((heads, HD, 2 * SPAN)), whole((heads, HD, 2 * SPAN)),
                by_page(count, SPAN), by_page(count, SPAN), by_page(1, count)],
            out_specs=[
                by_page(count, 3 * width), by_page(heads, count, count),
                pl.BlockSpec((blocks, 1, rows, width), lambda p, *_: (0, p, 0, 0))],
        ),
        out_shape=[
            jax.ShapeDtypeStruct((pages, count, 3 * width), LOW),
            jax.ShapeDtypeStruct((pages, heads, count, count), LOW),
            jax.ShapeDtypeStruct((blocks, pages, rows, width), LOW),
        ],
        compiler_params=pltpu.CompilerParams(vmem_limit_bytes=VMEM_BYTES),
        cost_estimate=cost(20e9, 20e6),
        name="attend",
    )(me, *toks, w_qkv, bias, place_q, place_k, sines, cosines, alive)


def joined_grads(own, size, pages, d_w, d_pq, d_pk, d_bias):
    inner = pages // size
    width = D // size
    cut = d_w.reshape(pages, size, own, 3 * width)
    parts = []
    for part in range(3):
        parts.append(jnp.concatenate(
            [cut[:, b, :, part * width:(part + 1) * width] for b in range(size)], axis=2))
    for place in (d_pq, d_pk):
        place = place.reshape(D // size, 2 * SPAN)
        order = [(lo * size + b) * own for b in range(size) for lo in range(inner)]
        parts.append(jnp.concatenate([place[at:at + own][None] for at in order], axis=0))
    row = jnp.concatenate([d_bias, jnp.zeros((1, D - 3 * width), WIDE)], axis=1)
    parts.append(jnp.broadcast_to(row[None], (pages, 8, D)))
    return jnp.concatenate(parts, axis=1).astype(LOW)


def attend_back_kernel(heads, blocks, joined, me_ref, *refs):
    tok_refs = refs[:blocks]
    (w_ref, qkv_ref, soft_ref, dctx_ref, pq_ref, pk_ref, sin_ref, cos_ref,
     part_ref, *out_refs, dw_sum, dpq_sum, dpk_sum, db_sum) = refs[blocks:]
    me = me_ref[0]
    step, last = pl.program_id(0), pl.num_programs(0) - 1
    rows = tok_refs[0].shape[1]
    width = heads * HD
    sines, cosines = sin_ref[0], cos_ref[0]
    key_feats, query_feats = feature_pair(sines, cosines)
    qkv = qkv_ref[0]
    dctx = jnp.concatenate([dctx_ref[me ^ j, 0] for j in range(blocks)], axis=0)

    @pl.when(step == 0)
    def _():
        for ref in (dw_sum, dpq_sum, dpk_sum, db_sum):
            ref[...] = jnp.zeros_like(ref)

    d_q, d_k, d_v = [], [], []
    for h in range(heads):
        q = qkv[:, h * HD:(h + 1) * HD]
        k = qkv[:, width + h * HD:width + (h + 1) * HD]
        v = qkv[:, 2 * width + h * HD:2 * width + (h + 1) * HD]
        dc = dctx[:, h * HD:(h + 1) * HD]
        soft = soft_ref[0, h]
        soft_wide = soft.astype(WIDE)
        attend_grad = dot_nt(dc, v)
        row_dot = jnp.sum(soft_wide * attend_grad, axis=1, keepdims=True)
        raw_grad = (soft_wide * (attend_grad - row_dot) * SCALING).astype(LOW)
        d_v.append(dot_tn(soft, dc).astype(LOW))
        spread_q = turn_back(dot(raw_grad, key_feats), cosines, sines)
        d_q.append((dot(raw_grad, k) + dot_nt(spread_q, pq_ref[h])).astype(LOW))
        dpq_sum[h] += dot_tn(q, spread_q)
        spread_k = turn_back(dot_tn(raw_grad, query_feats), sines, cosines)
        d_k.append((dot_tn(raw_grad, q) + dot_nt(spread_k, pk_ref[h])).astype(LOW))
        dpk_sum[h] += dot_tn(k, spread_k)
    dqkv = jnp.concatenate(d_q + d_k + d_v, axis=1)
    db_sum[...] += jnp.sum(dqkv.astype(WIDE), axis=0, keepdims=True)
    tok = jnp.concatenate([ref[0] for ref in tok_refs], axis=0)
    dw_sum[...] += dot_tn(tok, dqkv)
    part = dot_nt(dqkv, w_ref[...]).astype(LOW)
    for j in range(blocks):
        part_ref[j, 0] = part[j * rows:(j + 1) * rows]

    @pl.when(step == last)
    def _():
        if joined:
            rows = joined_grads(*joined, dw_sum[...], dpq_sum[...], dpk_sum[...], db_sum[...])
            even = me_ref[1] == 0
            for z in range(rows.shape[0] // 2):
                first, second = rows[2 * z], rows[2 * z + 1]
                out_refs[0][me_ref[2] ^ z] = jnp.where(even, first, second)
                out_refs[1][me_ref[2] ^ z] = jnp.where(even, second, first)
        else:
            for ref, total in zip(out_refs, (dw_sum, dpq_sum, dpk_sum, db_sum)):
                ref[...] = total[...].astype(ref.dtype)


def attend_back_call(joined, me, toks, w_qkv, qkv, soft, dctx, place_q, place_k, sines, cosines):
    blocks, pages, rows, width = dctx.shape
    heads = place_q.shape[0]
    count = blocks * rows
    by_page = lambda *shape: pl.BlockSpec((1,) + shape, lambda p, *_: (p,) + (0,) * len(shape))
    place = (heads, HD, 2 * SPAN)
    if joined:
        own, _, owners = joined
        sums = [jax.ShapeDtypeStruct((owners // 2, 5 * own + 8, D), LOW)] * 2
    else:
        sums = [jax.ShapeDtypeStruct((D, 3 * width), LOW), jax.ShapeDtypeStruct(place, LOW),
                jax.ShapeDtypeStruct(place, LOW), jax.ShapeDtypeStruct((1, 3 * width), WIDE)]
    return pl.pallas_call(
        functools.partial(attend_back_kernel, heads, blocks, joined),
        grid_spec=pltpu.PrefetchScalarGridSpec(
            num_scalar_prefetch=1,
            grid=(pages,),
            in_specs=[by_page(rows, D)] * blocks + [
                whole((D, 3 * width)),
                by_page(count, 3 * width), by_page(heads, count, count),
                pl.BlockSpec((blocks, 1, rows, width), lambda p, *_: (0, p, 0, 0)),
                whole(place), whole(place), by_page(count, SPAN), by_page(count, SPAN)],
            out_specs=[
                pl.BlockSpec((blocks, 1, rows, D), lambda p, *_: (0, p, 0, 0)),
                *(whole(item.shape) for item in sums)],
            scratch_shapes=[
                pltpu.VMEM((D, 3 * width), WIDE), pltpu.VMEM(place, WIDE), pltpu.VMEM(place, WIDE),
                pltpu.VMEM((1, 3 * width), WIDE)],
        ),
        out_shape=[jax.ShapeDtypeStruct((blocks, pages, rows, D), LOW), *sums],
        compiler_params=pltpu.CompilerParams(vmem_limit_bytes=VMEM_BYTES),
        cost_estimate=cost(30e9, 20e6),
        name="attend_back",
    )(me, *toks, w_qkv, qkv, soft, dctx, place_q, place_k, sines, cosines)


def normed(values):
    centred = values - jnp.mean(values, axis=1, keepdims=True)
    scale = lax.rsqrt(jnp.mean(centred * centred, axis=1, keepdims=True) + 1e-05)
    return centred * scale, scale


def normed_back(gradient, unit, scale):
    mean = jnp.mean(gradient, axis=1, keepdims=True)
    along = jnp.mean(gradient * unit, axis=1, keepdims=True)
    return scale * (gradient - mean - unit * along)


def summed(values):
    return jnp.sum(values, axis=0, keepdims=True)


def second_half_kernel(cuts, split, at_ref, ctx_ref, tok_ref, cot_ref, wo_ref, vec_ref, wi_ref, *refs):
    n_grads = 4 if split else 2
    wu_ref, out_ref, pre_grad_ref, dctx_ref = refs[:4]
    grad_refs = refs[4:4 + n_grads]
    (small_ref, ctx_all, first, first_low, unit_one, scale_one, act, slope, outer, pre_two_grad,
     outer_grad, first_grad) = refs[4 + n_grads:]
    step = pl.program_id(0)
    core, x_at, y_at, z_at = at_ref[0], at_ref[1] >> 1, at_ref[1] & 1, at_ref[2]
    blocks, _, _, width = ctx_ref.shape
    count = tok_ref.shape[0]
    b_out, b_outer, gain_one, shift_one, gain_two, shift_two = (vec_ref[i:i + 1] for i in range(6))

    w_outer = wu_ref[...].reshape(D, D)

    @pl.when(step == 0)
    def _():
        small_ref[...] = jnp.zeros_like(small_ref)
        ctx = jnp.concatenate([ctx_ref[b].reshape(count, width) for b in range(blocks)], axis=1)
        ctx_all[...] = ctx
        pre = tok_ref[...].astype(WIDE) + (dot(ctx, wo_ref[...]) + b_out)
        unit, scale = normed(pre)
        unit_one[...] = unit
        scale_one[...] = jnp.broadcast_to(scale, scale_one.shape)
        value = unit * gain_one + shift_one
        first[...] = value
        first_low[...] = value.astype(LOW)

    @pl.when(step < cuts)
    def _():
        inner = dot(first_low[...], wi_ref[...]) + vec_ref[pl.ds(6 + step, 1)]
        half = 0.5 + 0.5 * lax.erf(inner * (0.5 ** 0.5))
        slope[step] = half + inner * (jnp.exp(inner * inner * -0.5) * ((0.5 / math.pi) ** 0.5))
        activated = (inner * half).astype(LOW)
        act[step] = activated
        product = dot(activated, w_outer)

        @pl.when(step == 0)
        def _():
            outer[...] = product

        @pl.when(step > 0)
        def _():
            outer[...] += product

    @pl.when(step == cuts - 1)
    def _():
        unit, scale = normed(first[...] + (outer[...] + b_outer))
        out_ref[...] = (unit * gain_two + shift_two).astype(LOW)
        cot = cot_ref[...].astype(WIDE)
        grad = normed_back(cot * gain_two, unit, scale)
        pre_two_grad[...] = grad
        low = grad.astype(LOW)
        outer_grad[...] = low
        small_ref[1:2] = summed(low.astype(WIDE))
        small_ref[4:5] = summed(cot * unit)
        small_ref[5:6] = summed(cot)

    def store_24(grad):
        cut = grad.reshape(4, 2, 2, 2, D // 32, D)
        for z in range(4):
            for x in range(2):
                for y in range(2):
                    slot = (0, y_at ^ y, x_at ^ x, z_at ^ z)
                    first, second = cut[z, x, y, 0], cut[z, x, y, 1]
                    grad_refs[2][slot] = jnp.where(core == 0, first, second).astype(LOW)
                    grad_refs[3][slot] = jnp.where(core == 0, second, first).astype(LOW)

    @pl.when((step >= cuts) & (step < 2 * cuts))
    def _():
        j = 2 * cuts - 1 - step
        low = outer_grad[...]
        d_outer = dot_tn(act[j], low).astype(LOW)
        inner_grad = (dot_nt(low, w_outer) * slope[j]).astype(LOW)
        small_ref[pl.ds(6 + j, 1)] = summed(inner_grad.astype(WIDE))
        d_inner = dot_tn(first_low[...], inner_grad)
        if split:
            cut = d_outer.reshape(2, 2, 2, D // 8, D)
            for x in range(2):
                for y in range(2):
                    slot = (x_at ^ x, y_at ^ y, 0)
                    first, second = cut[x, y, 0], cut[x, y, 1]
                    grad_refs[0][slot] = jnp.where(core == 0, first, second)
                    grad_refs[1][slot] = jnp.where(core == 0, second, first)
            store_24(d_inner)
        else:
            grad_refs[0][...] = d_outer
            grad_refs[1][0] = d_inner.astype(LOW)
        product = dot_nt(inner_grad, wi_ref[...])

        @pl.when(step == cuts)
        def _():
            first_grad[...] = pre_two_grad[...] + product

        @pl.when(step > cuts)
        def _():
            first_grad[...] += product

    @pl.when(step == 2 * cuts)
    def _():
        grad = first_grad[...]
        unit = unit_one[...]
        small_ref[2:3] = summed(grad * unit)
        small_ref[3:4] = summed(grad)
        grad = normed_back(grad * gain_one, unit, scale_one[:, :1])
        pre_grad_ref[...] = grad
        low = grad.astype(LOW)
        small_ref[0:1] = summed(low.astype(WIDE))
        dctx = dot_nt(low, wo_ref[...]).astype(LOW)
        for b in range(blocks):
            dctx_ref[b] = dctx[:, b * width:(b + 1) * width].reshape(dctx_ref.shape[1:])
        d_output = dot_tn(ctx_all[...], low)
        if split:
            store_24(d_output)
        else:
            grad_refs[1][0] = d_output.astype(LOW)


def second_half_call(split, at, ctx, tok, cot, w_output, vectors, w_inner, w_outer):
    blocks, pages, rows, width = ctx.shape
    count = pages * rows
    cuts = w_inner.shape[1] // D
    now = lambda i: jnp.where(i < cuts, i, jnp.maximum(2 * cuts - 1 - i, 0))
    late = lambda i: jnp.where(i < cuts, cuts - 1, jnp.maximum(2 * cuts - 1 - i, 0))
    last = lambda i: jnp.where(i < 2 * cuts, late(i), cuts)
    square, tall = (D, D), (count, D)
    eighth = (2, 2, 1, D // 8, D)
    slots = (1, 2, 2, 4, D // 32, D)
    if split:
        grad_specs = [pl.BlockSpec(eighth, lambda i, at: (0, 0, late(i) ^ at[2], 0, 0))] * 2
        grad_specs += [pl.BlockSpec(slots, lambda i, at: (last(i), 0, 0, 0, 0, 0))] * 2
        grads = [(2, 2, cuts, D // 8, D)] * 2 + [(cuts + 1,) + slots[1:]] * 2
    else:
        grad_specs = [
            pl.BlockSpec(square, lambda i, at: (late(i), 0)),
            pl.BlockSpec((1,) + square, lambda i, at: (last(i), 0, 0))]
        grads = [(cuts * D, D), (cuts + 1,) + square]
    return pl.pallas_call(
        functools.partial(second_half_kernel, cuts, split),
        grid_spec=pltpu.PrefetchScalarGridSpec(
            num_scalar_prefetch=1,
            grid=(2 * cuts + 1,),
            in_specs=[
                whole(ctx.shape), whole(tall), whole(tall), whole(square), whole(vectors.shape),
                pl.BlockSpec(square, lambda i, at: (0, now(i))),
                pl.BlockSpec((8, D // 8, D), lambda i, at: (now(i), 0, 0))],
            out_specs=[whole(tall), whole(tall), whole(ctx.shape), *grad_specs, whole(vectors.shape)],
            scratch_shapes=[
                pltpu.VMEM(tall, LOW), pltpu.VMEM(tall, WIDE), pltpu.VMEM(tall, LOW),
                pltpu.VMEM(tall, WIDE), pltpu.VMEM((count, 128), WIDE), pltpu.VMEM((cuts,) + tall, LOW),
                pltpu.VMEM((cuts,) + tall, WIDE), pltpu.VMEM(tall, WIDE), pltpu.VMEM(tall, WIDE),
                pltpu.VMEM(tall, LOW), pltpu.VMEM(tall, WIDE)],
        ),
        out_shape=[
            jax.ShapeDtypeStruct(tall, LOW),
            jax.ShapeDtypeStruct(tall, WIDE),
            jax.ShapeDtypeStruct(ctx.shape, LOW),
            *(jax.ShapeDtypeStruct(shape, LOW) for shape in grads),
            jax.ShapeDtypeStruct(vectors.shape, WIDE),
        ],
        compiler_params=pltpu.CompilerParams(vmem_limit_bytes=VMEM_BYTES),
        cost_estimate=cost(20e9, 30e6),
        name="second_half",
    )(at, ctx, tok, cot, w_output, vectors, w_inner, w_outer)


def swap(value, axis, size, bit):
    return lax.ppermute(value, axis, [(i, i ^ bit) for i in range(size)])


def gather_slots(value):
    near = swap(value, "pb", 4, 1)
    far = swap(value, "pb", 4, 2)
    return (value, near, far, swap(far, "pb", 4, 1))


def hop(value, devices, bits):
    return lax.ppermute(value, AXES, [(i, i ^ bits) for i in range(devices)])


def added(*terms):
    return sum(term.astype(WIDE) for term in terms)


def sum_along_z(value, devices):
    return added(value[0], *(hop(value[j], devices, j << 3) for j in (1, 2, 3)))


def tie(*values):
    return lax.optimization_barrier(values)


def transpose_roles(value, pages, size):
    inner = pages // size
    pairs = []
    for hi in range(size):
        for lo in range(inner):
            for b in range(size):
                pairs.append(((hi * inner + lo) * size + b, (b * inner + lo) * size + hi))
    return lax.ppermute(value, AXES, pairs)


def sum_slots(partial):
    got = swap(partial[1::2], "pb", 4, 1)
    total = partial[0::2].astype(WIDE) + got.astype(WIDE)
    return total[0] + swap(total[1].astype(LOW), "pb", 4, 2).astype(WIDE)


def to_halves(place):
    cut = place.reshape(place.shape[:-1] + (2, 2, FREQ))
    return jnp.swapaxes(cut, -3, -2).reshape(place.shape)


def on_device(sizes, tokens, cotangent, boxes, resolution, padding,
              query_weight, keys_weight, values_weight, output_weight, query_place, keys_place,
              inner_weight, outer_weight, query_bias, keys_bias, values_bias, output_bias,
              inner_bias, outer_bias, first_gain, first_shift, second_gain, second_shift):
    page_size, pb_size = sizes
    devices = page_size * pb_size
    inner_pages = page_size // pb_size
    pages, rows, _ = tokens.shape
    count = rows * pb_size
    heads = HEADS // pb_size
    width = heads * HD
    own = query_weight.shape[0]
    ff_own = outer_weight.shape[0]
    ff = ff_own * devices
    cuts = ff // D
    me, page = lax.axis_index("pb"), lax.axis_index("page")
    place_at = (page % inner_pages) * pb_size + me
    number = page * pb_size + me
    me_array = me.astype(jnp.int32).reshape(1)
    by_link = (page_size, pb_size, own) == (8, 4, 24)

    at = jnp.stack([number & 1, (number >> 1) & 3, number >> 3, number, place_at]).astype(jnp.int32)
    small_rows = 16
    vectors = [output_bias, outer_bias, first_gain, first_shift, second_gain, second_shift]
    if by_link:
        lines = vectors + [None] * 2 + [inner_bias] + [None] * 7 + [query_bias, keys_bias, values_bias]
        lines = [jnp.zeros((128,), WIDE) if line is None
                 else jnp.pad(line.astype(WIDE), (0, 128 - line.shape[0])) for line in lines]
        lines = jnp.concatenate(lines + [jnp.zeros((5 * 128,), WIDE)]).reshape(24, 128)
        packed, cols, mixed = pack_call(
            at, lines, query_weight, keys_weight, values_weight, query_place, keys_place,
            output_weight, inner_weight, outer_weight)
    else:
        cols = jnp.concatenate([query_weight, keys_weight, values_weight], axis=0)
        cols = cols.reshape(3 * own, pb_size, width).swapaxes(0, 1)
        bias_rows = jnp.zeros((3, width), LOW)
        bias_rows = lax.dynamic_update_slice(
            bias_rows, jnp.stack([query_bias, keys_bias, values_bias]), (0, place_at * own))
        bias_rows = jnp.pad(bias_rows.reshape(1, 3 * width), ((0, 7), (0, D - 3 * width)))
        mixed = jnp.concatenate([to_halves(query_place), to_halves(keys_place), bias_rows], axis=0)
        vectors = lax.dynamic_update_slice(jnp.zeros((6, D), LOW), jnp.stack(vectors), (0, number * own))
        b_inner = lax.dynamic_update_slice(jnp.zeros((ff,), LOW), inner_bias, (number * ff_own,))
        vectors = jnp.concatenate(
            [vectors, b_inner.reshape(cuts, D), jnp.zeros((small_rows - 6 - cuts, D), LOW)], axis=0)
        packed = jnp.concatenate(
            [outer_weight] + [inner_weight[:, j * D:(j + 1) * D] for j in range(cuts)]
            + [vectors, output_weight], axis=0)
    cols = lax.all_to_all(cols, "pb", 0, 0, tiled=True)
    cols = cols.swapaxes(0, 1).reshape(3 * own, D)
    mixed = transpose_roles(mixed, page_size, pb_size)
    mixed = jnp.concatenate([cols, mixed], axis=0)
    late = lax.all_gather(packed, AXES, axis=0)

    grid_x = (boxes[0] + boxes[2]) * 500 // resolution[0][:, None]
    grid_y = (boxes[1] + boxes[3]) * 500 // resolution[1][:, None]
    places = lax.all_gather(jnp.stack([grid_x, grid_y, padding]), "pb", axis=0)
    toks = gather_slots(tokens)

    places = jnp.stack([places[me ^ j] for j in range(pb_size)])
    places = places.transpose(1, 2, 0, 3).reshape(3, pages, count)
    rates = jnp.exp(jnp.arange(FREQ).astype(WIDE) * (-math.log(10000.0) / FREQ))
    grids = places[:2].astype(WIDE)
    angles = jnp.concatenate(
        [grids[0][..., None] * rates, grids[1][..., None] * rates], axis=-1)
    sines, cosines = jnp.sin(angles), jnp.cos(angles)
    alive = places[2][:, None, :]

    if by_link:
        mixed = jnp.stack([mixed] + [hop(mixed, devices, j << 3) for j in (1, 2, 3)])
        w_qkv, place_q, place_k, bias_qkv = assemble_call(
            at, mixed, hop(mixed, devices, 4), own, pb_size)
    else:
        mixed = lax.all_gather(mixed, "page", axis=0)
        w_qkv = mixed[:, :3 * own].reshape(page_size, 3, own, pb_size, width)
        w_qkv = w_qkv.transpose(0, 3, 2, 1, 4).reshape(D, 3 * width)
        bias_qkv = jnp.sum(mixed[:, 5 * own, :3 * width].astype(WIDE), axis=0, keepdims=True)
        mixed = mixed[:, 3 * own:5 * own].reshape(pb_size, inner_pages, 2, own, D)
        mixed = mixed.transpose(2, 1, 0, 3, 4).reshape(2, heads, HD, 2 * SPAN)
        place_q, place_k = mixed[0], mixed[1]

    qkv, soft, ctx_heads = attend_call(
        me_array, toks, w_qkv, bias_qkv, place_q, place_k, sines, cosines, alive)
    ctx = lax.all_to_all(ctx_heads, "pb", 0, 0, tiled=True)

    spot = ff_own
    w_inner = jnp.concatenate(
        [late[:, spot + j * own:spot + (j + 1) * own].reshape(D, D) for j in range(cuts)], axis=1)
    spot += cuts * own
    vectors = jnp.sum(late[:, spot:spot + small_rows].astype(WIDE), axis=0)
    w_output = late[:, spot + small_rows:].reshape(D, D)
    w_outer = late if by_link else late[:, :ff_own].reshape(8 * cuts, D // 8, D)

    tok = tokens.reshape(pages * rows, D)
    output, pre_one_grad, dctx, *grads, small = second_half_call(
        by_link, at, ctx, tok, cotangent.reshape(pages * rows, D), w_output, vectors, w_inner, w_outer)
    dctx = lax.all_to_all(dctx, "pb", 0, 0, tiled=True)

    if by_link:
        outer_kept, outer_sent, inner_kept, inner_sent = grads
        outer_sent, inner_sent = hop(outer_sent, devices, 1), hop(inner_sent, devices, 1)
        outer_far = added(outer_kept[1], outer_sent[1]).astype(LOW)
        inner_far = added(inner_kept[:, 1], inner_sent[:, 1]).astype(LOW)
        outer_kept = added(outer_kept[0], outer_sent[0]).astype(LOW)
        inner_kept = added(inner_kept[:, 0], inner_sent[:, 0]).astype(LOW)
        dctx, outer_far, inner_far, outer_kept, inner_kept = tie(
            dctx, outer_far, inner_far, outer_kept, inner_kept)
        outer_far, inner_far = hop(outer_far, devices, 4), hop(inner_far, devices, 2)
    small = lax.all_gather(small, AXES, axis=0)

    joined = (own, pb_size, page_size) if by_link else None
    me_array = jnp.stack([me, at[1] >> 1, at[2]]).astype(jnp.int32)
    partial, *sums = attend_back_call(
        joined, me_array, toks, w_qkv, qkv, soft, dctx, place_q, place_k, sines, cosines)

    if by_link:
        partial, mixed, mixed_far, outer_kept, outer_far, inner_kept, inner_far = tie(
            partial, *sums, outer_kept, outer_far, inner_kept, inner_far)
        mixed_far = hop(mixed_far, devices, 4)
        near = hop(partial[1::2], devices, 1)
        outer_sent = added(outer_kept[1], outer_far[1]).astype(LOW)
        inner_sent = added(inner_kept[:, 1], inner_far[:, 1]).astype(LOW)
        outer_sent, inner_sent = hop(outer_sent, devices, 2), hop(inner_sent, devices, 4)
        outer_kept, inner_kept = added(outer_kept[0], outer_far[0]), added(inner_kept[:, 0], inner_far[:, 0])
        mixed, mixed_far, partial, near = tie(mixed, mixed_far, partial, near)
        total = added(partial[0::2], near)
        far = hop(total[1].astype(LOW), devices, 2)
        mixed = added(mixed, mixed_far).astype(LOW)
        mixed, outer_kept, outer_sent, inner_kept, inner_sent = tie(
            mixed, outer_kept, outer_sent, inner_kept, inner_sent)
        mixed_z = [hop(mixed[j], devices, j << 3) for j in (1, 2, 3)]
        outer_sum = added(outer_kept, outer_sent).astype(LOW)
        inner_sum = added(inner_kept, inner_sent).astype(LOW).swapaxes(0, 1)
        outer_z = [hop(outer_sum[j], devices, j << 3) for j in (1, 2, 3)]
        inner_z = [hop(inner_sum[j], devices, j << 3) for j in (1, 2, 3)]
        mixed = added(mixed[0], *mixed_z).astype(LOW)
        cols, far, total = tie(
            mixed[:3 * own].reshape(3 * own, pb_size, width).swapaxes(0, 1), far, total[0])
        tokens_grad = pre_one_grad.reshape(pages, rows, D) + added(total, far)
        cols = lax.all_to_all(cols, "pb", 0, 0, tiled=True)
        mixed = transpose_roles(mixed[3 * own:], page_size, pb_size)
        cols, mixed, outer_sum, inner_sum, *got = tie(
            cols, mixed, outer_sum, inner_sum, *outer_z, *inner_z)
        d_outer = added(outer_sum[0], *got[:3])
        inner_sum = added(inner_sum[0], *got[3:])
        d_query, d_keys, d_values, d_place_q, d_place_k = finish_call(cols, mixed)
        d_inner = jnp.concatenate([inner_sum[j] for j in range(cuts)], axis=1)
        d_output = inner_sum[cuts]
    else:
        d_outer = lax.psum_scatter(
            grads[0].reshape(devices, ff_own, D), AXES, scatter_dimension=0, tiled=False).astype(WIDE)
        inner_sum = grads[1].reshape(cuts + 1, devices, own, D).swapaxes(0, 1)
        inner_sum = lax.psum_scatter(inner_sum, AXES, scatter_dimension=0, tiled=False).astype(WIDE)
        d_inner = jnp.concatenate([inner_sum[j] for j in range(cuts)], axis=1)
        d_output = inner_sum[cuts]
        d_w, d_pq, d_pk, d_bias = sums
        d_w = d_w.reshape(page_size, pb_size, own, 3, width).transpose(0, 3, 2, 1, 4)
        d_w = d_w.reshape(page_size, 3 * own, D)
        d_p = jnp.stack([d_pq, d_pk]).reshape(2, inner_pages, pb_size, own, D)
        d_p = d_p.transpose(2, 1, 0, 3, 4).reshape(page_size, 2 * own, D)
        d_bias = jnp.pad(d_bias, ((0, 7), (0, D - 3 * width))).astype(LOW)
        d_bias = jnp.broadcast_to(d_bias[None], (page_size, 8, D))
        mixed = jnp.concatenate([d_w, d_p, d_bias], axis=1)
        mixed = lax.all_to_all(mixed, "page", 0, 0, tiled=True)
        mixed = jnp.sum(mixed.astype(WIDE), axis=0).astype(LOW)
        tokens_grad = pre_one_grad.reshape(pages, rows, D) + sum_slots(partial)
        cols = mixed[:3 * own].reshape(3 * own, pb_size, width).swapaxes(0, 1)
        cols = lax.all_to_all(cols, "pb", 0, 0, tiled=True)
        d_query, d_keys, d_values = cols.swapaxes(0, 1).reshape(3, own, D).astype(WIDE)
        mixed = transpose_roles(mixed[3 * own:], page_size, pb_size)
        d_place_q, d_place_k = to_halves(mixed[:own].astype(WIDE)), to_halves(mixed[own:2 * own].astype(WIDE))
    d_bias = lax.dynamic_slice(
        mixed[2 * own, :3 * width].astype(WIDE).reshape(3, width), (0, place_at * own), (3, own))

    small = jnp.sum(small, axis=0)
    d_b_inner = lax.dynamic_slice(small[6:6 + cuts].reshape(ff), (number * ff_own,), (ff_own,))
    vectors = lax.dynamic_slice(small, (0, number * own), (6, own))
    return (
        output.reshape(pages, rows, D),
        tokens_grad,
        d_query, d_keys, d_values,
        d_output,
        d_place_q, d_place_k,
        d_inner,
        d_outer.reshape(ff_own, D),
        d_bias[0], d_bias[1], d_bias[2],
        vectors[0], d_b_inner, vectors[1], vectors[2], vectors[3], vectors[4], vectors[5],
    )


def solution(mesh):
    rows, vector = P(AXES, None), P(AXES)
    token = P("page", "pb", None)
    in_specs = (token, token, P(None, "page", "pb"), P(None, "page"), P("page", "pb"))
    in_specs = in_specs + (rows,) * 8 + (vector,) * 10
    out_specs = (token, token) + (rows,) * 8 + (vector,) * 10
    sizes = (mesh.shape["page"], mesh.shape["pb"])
    return jax.shard_map(
        functools.partial(on_device, sizes), mesh=mesh, in_specs=in_specs, out_specs=out_specs,
        check_vma=False)
```

time: 434 us -> 330 us (0.76); the launches traced: 427 us -> 329 us
  local copies, waits for them, and re-layouts: 99.2 us -> 24.8 us
  matrix products: 48.2 us -> 0 us
  waiting for transfers between devices: 121 us -> 79.9 us
  Pallas kernels: 50.8 us -> 91.6 us
  blocking collectives: 0 us -> 20.7 us
  other arithmetic: 36 us -> 44.4 us
    ppermute x0 -> x22, waiting for transfers between devices: none -> 72 us  [hop(): return lax.ppermute(value, AXES, [(i, i ^ bits) for i in range(devices)])]
    dot_general x11 -> x0, matrix products: 48.2 us -> none  [the longest x3 21.2 us: dot(): return jnp.dot(a, b, preferred_element_type=WIDE)]
    ppermute x16 -> x3, waiting for transfers between devices: 42 us -> 0.01 us  [swap(): return lax.ppermute(value, axis, [(i, i ^ bit) for i in range(size)])]
    all_to_all x3 -> x0, waiting for transfers between devices: 40.9 us -> none  [the longest x1 32.4 us: on_device(): joined = lax.all_to_all(joined, 'page', 0, 0, tiled=True)]
    pallas_call x2 -> x6, Pallas kernels: 50.8 us -> 91.6 us  [the longest x1 33.6 us: attend_back_call(): pl.pallas_call(functools.partial(attend_back_kernel, heads, blocks, joine...]
    ppermute x0 -> x22, starting transfers between devices: none -> 32.1 us  [hop(): return lax.ppermute(value, AXES, [(i, i ^ bits) for i in range(devices)])]
    reduce_scatter x1 -> x0, waiting for transfers between devices: 27.5 us -> none  [on_device(): lax.psum_scatter(packed_grads, AXES, scatter_dimension=0, tiled=False)]
    ppermute x16 -> x3, starting transfers between devices: 29.7 us -> 3.79 us  [swap(): return lax.ppermute(value, axis, [(i, i ^ bit) for i in range(size)])]
  transfers between devices with their start and end apart: 25 -> 32, of which waited for: 12 -> 12; matrix products, arithmetic and copies ran while one was open for 21% -> 13% of each run, Pallas kernels for 12% -> 18%
where the time goes in v2:
time: 330 us; the launch traced here: 329 us
  Pallas kernels  91.6 us (28%)
  waiting for transfers between devices  79.9 us (24%)
  starting transfers between devices  53.1 us (16%)
  other arithmetic  44.4 us (13%)
  local copies, waits for them, and re-layouts  24.8 us (8%)
  blocking collectives  20.7 us (6%)
  between operations  14.5 us (4%)
    ppermute x22, waiting for transfers between devices, hop(): return lax.ppermute(value, AXES, [(i, i ^ bits) for i in range(devices)])  72 us
    pallas_call x1, Pallas kernels, attend_back_call(): pl.pallas_call(functools.partial(attend_back_kernel, heads, blocks, joine...  33.6 us
    ppermute x22, starting transfers between devices, hop(): return lax.ppermute(value, AXES, [(i, i ^ bits) for i in range(devices)])  32.1 us
    pallas_call x1, Pallas kernels, second_half_call(): pl.pallas_call(functools.partial(second_half_kernel, cuts, split), grid_s...  27.3 us
    pallas_call x1, Pallas kernels, attend_call(): pl.pallas_call(functools.partial(attend_kernel, heads, blocks), grid_spec...  24 us
    all_to_all x1, blocking collectives, on_device(): ctx = lax.all_to_all(ctx_heads, 'pb', 0, 0, tiled=True)  12 us
    cos x1, other arithmetic, on_device(): sines, cosines = (jnp.sin(angles), jnp.cos(angles))  10.1 us
    all_gather x1, blocking collectives, on_device(): places = lax.all_gather(jnp.stack([grid_x, grid_y, padding]), 'pb', axis=0)  8.72 us
  transfers between devices with their start and end apart: 32, of which 12 were waited for; matrix products, arithmetic and copies ran while one was open for 13% of the time, Pallas kernels for 18%

profile of v2, /device:TPU:1, one launch (start us, length us, event | category | flops | bytes accessed | tf_op | source)
XLA Modules:
  0.0 329.1 jit_solution(12888782771239537603)
XLA Ops:
  14.6 2.0 pack.1
  16.6 2.1 collective-permute-start.1
  19.7 3.3 %all-to-all-start = ((bf16[4,72,192]{2,1,0:T(8,128)(2,1)}), bf16[4,72,192]{2,1,0:T(8,128)(2,1)S(1)}, u32[]{:S(2)}, u32[]{:S(2)}) async-start(bf16[4,72,192]{2,1,0:T(8,128)(2,1)} %get-tuple-element.81), calls=%async_computation | async-start | bytes 294912 | tf_op jit(solution)/shard_map/all_to_all | solution.py:633
  23.1 3.1 collective-permute-start.3
  29.5 8.7 %all-gather = s32[12,3,128]{2,1,0:T(4,128)S(1)} all-gather(s32[3,3,128]{2,1,0:T(4,128)S(1)} %pad_add_fusion), channel_id=2, replica_groups=mesh['page'=8,'pb'=4] {'pb'}, dimensions={0}, use_global_device_ids=true | all-gather | bytes 23040 | tf_op jit(solution)/shard_map/all_gather | solution.py:641
  38.6 5.4 %collective-permute-start.6 = (bf16[128,768]{1,0:T(8,128)(2,1)S(1)}, bf16[128,768]{1,0:T(8,128)(2,1)S(1)}, u32[]{:S(2)}, u32[]{:S(2)}) collective-permute-start(bf16[128,768]{1,0:T(8,128)(2,1)S(1)} %constant_dynamic-update-slice_fusion.1), channel_id=1, source_target_pairs={{0,24},{1,25},{2,26},{3,27},{4,28},{5,29},{6,30},{7,31},{8,16},{9,... | collective-permute-start | bytes 589832 | tf_op jit(solution)/shard_map/ppermute | solution.py:550
  44.4 4.8 %collective-permute-done.6 = bf16[128,768]{1,0:T(8,128)(2,1)S(1)} collective-permute-done((bf16[128,768]{1,0:T(8,128)(2,1)S(1)}, bf16[128,768]{1,0:T(8,128)(2,1)S(1)}, u32[]{:S(2)}, u32[]{:S(2)}) %collective-permute-start.6) | collective-permute-done | bytes 196640 | tf_op jit(solution)/shard_map/ppermute | solution.py:550
  49.2 15.8 %collective-permute-done.5 = bf16[128,768]{1,0:T(8,128)(2,1)S(1)} collective-permute-done((bf16[128,768]{1,0:T(8,128)(2,1)S(1)}, bf16[128,768]{1,0:T(8,128)(2,1)S(1)}, u32[]{:S(2)}, u32[]{:S(2)}) %collective-permute-start.5) | collective-permute-done | bytes 196640 | tf_op jit(solution)/shard_map/ppermute | solution.py:550
  68.2 10.1 %fusion = (f32[3,512,384]{2,1,0:T(8,128)}, f32[3,512,384]{2,1,0:T(8,128)}) fusion(f32[3,512,192]{2,1,0:T(8,128)S(1)} %get-tuple-element.186, f32[3,512,192]{2,1,0:T(8,128)S(1)} %get-tuple-element.185), kind=kLoop, calls=%fused_computation.9 | loop fusion | flops 589824 | bytes 7077888 | tf_op jit(solution)/shard_map/cos | solution.py:650
  78.3 7.9 %collective-permute-done.7.theirs_ref = bf16[4,128,768]{2,1,0:T(8,128)(2,1)S(1)} collective-permute-done((bf16[4,128,768]{2,1,0:T(8,128)(2,1)S(1)}, bf16[4,128,768]{2,1,0:T(8,128)(2,1)S(1)}, u32[]{:S(2)}, u32[]{:S(2)}) %collective-permute-start.7) | collective-permute-done | bytes 786464 | tf_op jit(solution)/shard_map/ppermute | solution.py:550
  87.1 2.9 assemble.1
  91.1 24.0 %attend.1 = (bf16[3,512,576]{2,1,0:T(8,128)(2,1)}, bf16[3,3,512,512]{3,2,1,0:T(8,128)(2,1)}, bf16[4,3,128,192]{3,2,1,0:T(8,128)(2,1)}) custom-call(s32[1]{0:T(128)} %bitcast.5.me_ref, bf16[3,128,768]{2,1,0:T(8,128)(2,1)} %refs_0_.3, bf16[3,128,768]{2,1,0:T(8,128)(2,1)} %copy-done.11, bf16[3,128,768]{2,1,0:T(8,128)(2,1)} %copy-done.10, ...), custom_call_target="tpu_custom_call" | custom-call | flops 20000000000 | bytes 20000000 | tf_op jit(solution)/shard_map/attend/pallas_call | solution.py:223
  116.5 12.0 %all_to_all.20 = bf16[4,3,128,192]{2,3,1,0:T(8,128)(2,1)S(1)} all-to-all(bf16[4,3,128,192]{2,3,1,0:T(8,128)(2,1)S(1)} %copy.69), channel_id=1, replica_groups=mesh['page'=8,'pb'=4] {'pb'}, dimensions={0} | all-to-all | bytes 1179648 | tf_op jit(solution)/shard_map/all_to_all | solution.py:668
  131.6 4.1 %fusion.28 = (bf16[32,24,768]{2,1,0:T(8,128)(2,1)S(1)}, bf16[32,24,768]{2,1,0:T(8,128)(2,1)S(1)}, bf16[32,24,768]{2,1,0:T(8,128)(2,1)S(1)}, bf16[32,24,768]{2,1,0:T(8,128)(2,1)S(1)}, bf16[32,24,768]{2,1,0:T(8,128)(2,1)}) fusion(bf16[32,232,768]{2,1,0:T(8,128)(2,1)} %bitcast.163), kind=kLoop, calls=%fused_computation.122 | loop fusion | bytes 11796480 | tf_op jit(solution)/shard_map/slice | solution.py:672
  135.7 2.5 pad_maximum_fusion.wi_ref
  138.1 27.3 %second_half.1 = (bf16[384,768]{1,0:T(8,128)(2,1)}, f32[384,768]{1,0:T(8,128)}, bf16[4,3,128,192]{3,2,1,0:T(8,128)(2,1)}, bf16[2,2,4,96,768]{4,3,2,1,0:T(8,128)(...) custom-call(s32[5]{0:T(128)} %stack.60.at_ref, ...), custom_call_target="tpu_custom_call" | custom-call | flops 20000000000 | bytes 30000000 | tf_op jit(solution)/shard_map/second_half/pallas_call | solution.py:510
  167.0 2.2 copy.71
  169.2 3.9 %all-to-all-start.2 = ((bf16[4,3,128,192]{2,3,1,0:T(8,128)(2,1)}), bf16[4,3,128,192]{2,3,1,0:T(8,128)(2,1)S(1)}, u32[]{:S(2)}, u32[]{:S(2)}) async-start(bf16[4,3,128,192]{2,3,1,0:T(8,128)(2,1)} %copy.71), calls=%async_computation.2 | async-start | bytes 1179648 | tf_op jit(solution)/shard_map/all_to_all | solution.py:681
  176.2 4.2 %fusion.6 = (bf16[2,4,96,768]{3,2,1,0:T(8,128)(2,1)S(1)}, bf16[2,4,96,768]{3,2,1,0:T(8,128)(2,1)}) fusion(bf16[2,2,4,96,768]{4,3,2,1,0:T(8,128)(2,1)} %copy-done.2, bf16[2,2,4,96,768]{4,3,2,1,0:T(8,128)(2,1)} %get-tuple-element.94), kind=kLoop, calls=%fused_computation.18 | loop fusion | flops 4718592 | bytes 7077888 | tf_op jit(solution)/shard_map/convert_element_type | solution.py:688
  182.2 2.9 fusion.2
  186.9 33.6 %attend_back.1 = (bf16[4,3,128,768]{3,2,1,0:T(8,128)(2,1)}, bf16[4,128,768]{2,1,0:T(8,128)(2,1)}, bf16[4,128,768]{2,1,0:T(8,128)(2,1)}) custom-call(s32[3]{0:T(128)} %pad_add_fusion.1.me_ref, bf16[3,128,768]{2,1,0:T(8,128)(2,1)} %refs_0_.3, bf16[3,128,768]{2,1,0:T(8,128)(2,1)} %copy-done.11, bf16[3,128,768]{2,1,0:T(8,128)(2,1)} %copy-done.10, ...), custom_call_target="tpu_custom_call" | custom-call | flops 30000001024 | bytes 20000000 | tf_op jit(solution)/shard_map/attend_back/pallas_call | solution.py:334
  220.5 4.2 %all-gather.8.cloned.1.call-done = f32[512,768]{1,0:T(8,128)} async-done(((f32[16,768]{1,0:T(8,128)}), f32[512,768]{1,0:T(8,128)}) %all-gather.8.cloned.1.call-update) | async-done | bytes 1572880 | tf_op jit(solution)/shard_map/all_gather | solution.py:693
  236.0 12.0 %collective-permute-done.12 = bf16[4,128,768]{2,1,0:T(8,128)(2,1)S(1)} collective-permute-done((bf16[4,128,768]{2,1,0:T(8,128)(2,1)S(1)}, bf16[4,128,768]{2,1,0:T(8,128)(2,1)S(1)}, u32[]{:S(2)}, u32[]{:S(2)}) %collective-permute-start.12) | collective-permute-done | bytes 786464 | tf_op jit(solution)/shard_map/ppermute | solution.py:550
  249.8 14.1 %collective-permute-done.15 = bf16[5,4,24,768]{3,2,1,0:T(8,128)(2,1)S(1)} collective-permute-done((bf16[5,4,24,768]{3,2,1,0:T(8,128)(2,1)S(1)}, bf16[5,4,24,768]{3,2,1,0:T(8,128)(2,1)S(1)}, u32[]{:S(2)}, u32[]{:S(2)}) %collective-permute-start.15) | collective-permute-done | bytes 737312 | tf_op jit(solution)/shard_map/ppermute | solution.py:550
  271.7 6.7 %collective-permute-done.16 = bf16[128,768]{1,0:T(8,128)(2,1)S(1)} collective-permute-done((bf16[128,768]{1,0:T(8,128)(2,1)S(1)}, bf16[128,768]{1,0:T(8,128)(2,1)S(1)}, u32[]{:S(2)}, u32[]{:S(2)}) %collective-permute-start.16) | collective-permute-done | bytes 196640 | tf_op jit(solution)/shard_map/ppermute | solution.py:550
  279.6 9.3 %collective-permute-start.21 = (bf16[96,768]{1,0:T(8,128)(2,1)}, bf16[96,768]{1,0:T(8,128)(2,1)}, u32[]{:S(2)}, u32[]{:S(2)}) collective-permute-start(bf16[96,768]{1,0:T(8,128)(2,1)} %get-tuple-element.160), channel_id=1, source_target_pairs={{0,8},{1,9},{2,10},{3,11},{4,12},{5,13},{6,14},{7,15},{8,0},{9,1},... | collective-permute-start | bytes 442376 | tf_op jit(solution)/shard_map/ppermute | solution.py:550
  288.9 4.0 %collective-permute-done.17 = bf16[128,768]{1,0:T(8,128)(2,1)S(1)} collective-permute-done((bf16[128,768]{1,0:T(8,128)(2,1)S(1)}, bf16[128,768]{1,0:T(8,128)(2,1)S(1)}, u32[]{:S(2)}, u32[]{:S(2)}) %collective-permute-start.17) | collective-permute-done | bytes 196640 | tf_op jit(solution)/shard_map/ppermute | solution.py:550
  296.5 4.9 %all-to-all-start.3 = ((bf16[4,72,192]{2,1,0:T(8,128)(2,1)}), bf16[4,72,192]{2,1,0:T(8,128)(2,1)S(1)}, u32[]{:S(2)}, u32[]{:S(2)}) async-start(bf16[4,72,192]{2,1,0:T(8,128)(2,1)} %bitcast.155), calls=%async_computation.3 | async-start | bytes 294912 | tf_op jit(solution)/shard_map/all_to_all | solution.py:724
  301.4 3.2 collective-permute-start.24
  306.5 2.6 add_add_fusion
  309.1 3.7 %collective-permute-done.25 = bf16[5,24,768]{2,1,0:T(8,128)(2,1)S(1)} collective-permute-done((bf16[5,24,768]{2,1,0:T(8,128)(2,1)}, bf16[5,24,768]{2,1,0:T(8,128)(2,1)S(1)}, u32[]{:S(2)}, u32[]{:S(2)}) %collective-permute-start.25) | collective-permute-done | bytes 184352 | tf_op jit(solution)/shard_map/ppermute | solution.py:550
  312.8 3.6 %collective-permute-done.20.mixed_ref = bf16[56,768]{1,0:T(8,128)(2,1)S(1)} collective-permute-done((bf16[56,768]{1,0:T(8,128)(2,1)}, bf16[56,768]{1,0:T(8,128)(2,1)S(1)}, u32[]{:S(2)}, u32[]{:S(2)}) %collective-permute-start.20) | collective-permute-done | bytes 86048 | tf_op jit(solution)/shard_map/ppermute | solution.py:572
  (153 shorter events, 63.2 us)
Async XLA Ops:
  7.2 122.5 %all-gather.6.cloned.1.call-start = ((), (), s32[]{:S(2)}) async-start(), calls=%async_computation.4 | async-start | bytes 11759616 | tf_op jit(solution)/shard_map/all_gather | solution.py:637
  16.6 49.8 %collective-permute-start.1 = (bf16[3,128,768]{2,1,0:T(8,128)(2,1)}, bf16[3,128,768]{2,1,0:T(8,128)(2,1)S(1)}, u32[]{:S(2)}, u32[]{:S(2)}) collective-permute-start(bf16[3,128,768]{2,1,0:T(8,128)(2,1)} %refs_0_.3), channel_id=1, source_target_pairs={{0,2},{1,3},{2,0},{3,1},{4,6},{5,7},{6,4},{7,5},{8,10},{9,11},{10,... | collective-permute-start | bytes 1769480 | tf_op jit(solution)/shard_map/ppermute | solution.py:540
  18.8 71.2 %collective-permute-start = (bf16[3,128,768]{2,1,0:T(8,128)(2,1)}, bf16[3,128,768]{2,1,0:T(8,128)(2,1)S(1)}, u32[]{:S(2)}, u32[]{:S(2)}) collective-permute-start(bf16[3,128,768]{2,1,0:T(8,128)(2,1)} %refs_0_.3), channel_id=1, source_target_pairs={{0,1},{1,0},{2,3},{3,2},{4,5},{5,4},{6,7},{7,6},{8,9},{9,8},{10,11... | collective-permute-start | bytes 1769480 | tf_op jit(solution)/shard_map/ppermute | solution.py:540
  19.7 18.6 %all-to-all-start = ((bf16[4,72,192]{2,1,0:T(8,128)(2,1)}), bf16[4,72,192]{2,1,0:T(8,128)(2,1)S(1)}, u32[]{:S(2)}, u32[]{:S(2)}) async-start(bf16[4,72,192]{2,1,0:T(8,128)(2,1)} %get-tuple-element.81), calls=%async_computation | async-start | bytes 294912 | tf_op jit(solution)/shard_map/all_to_all | solution.py:633
  23.1 201.7 %all-gather.8.cloned.1.call-start = ((), (), s32[]{:S(2)}) async-start(), calls=%async_computation.5 | async-start | bytes 1622016 | tf_op jit(solution)/shard_map/all_gather | solution.py:693
  23.1 15.4 %collective-permute-start.3 = (bf16[56,768]{1,0:T(8,128)(2,1)}, bf16[56,768]{1,0:T(8,128)(2,1)S(1)}, u32[]{:S(2)}, u32[]{:S(2)}) collective-permute-start(bf16[56,768]{1,0:T(8,128)(2,1)} %get-tuple-element.82), channel_id=1, source_target_pairs={{0,0},{1,8},{2,16},{3,24},{4,4},{5,12},{6,20},{7,28},{8,1},{9,9},{... | collective-permute-start | bytes 258056 | tf_op jit(solution)/shard_map/ppermute | solution.py:572
  38.6 10.6 %collective-permute-start.6 = (bf16[128,768]{1,0:T(8,128)(2,1)S(1)}, bf16[128,768]{1,0:T(8,128)(2,1)S(1)}, u32[]{:S(2)}, u32[]{:S(2)}) collective-permute-start(bf16[128,768]{1,0:T(8,128)(2,1)S(1)} %constant_dynamic-update-slice_fusion.1), channel_id=1, source_target_pairs={{0,24},{1,25},{2,26},{3,27},{4,28},{5,29},{6,30},{7,31},{8,16},{9,... | collective-permute-start | bytes 589832 | tf_op jit(solution)/shard_map/ppermute | solution.py:550
  44.0 21.0 %collective-permute-start.5 = (bf16[128,768]{1,0:T(8,128)(2,1)S(1)}, bf16[128,768]{1,0:T(8,128)(2,1)S(1)}, u32[]{:S(2)}, u32[]{:S(2)}) collective-permute-start(bf16[128,768]{1,0:T(8,128)(2,1)S(1)} %constant_dynamic-update-slice_fusion.1), channel_id=1, source_target_pairs={{0,16},{1,17},{2,18},{3,19},{4,20},{5,21},{6,22},{7,23},{8,24},{9,... | collective-permute-start | bytes 589832 | tf_op jit(solution)/shard_map/ppermute | solution.py:550
  44.0 21.0 %collective-permute-start.4 = (bf16[128,768]{1,0:T(8,128)(2,1)S(1)}, bf16[128,768]{1,0:T(8,128)(2,1)S(1)}, u32[]{:S(2)}, u32[]{:S(2)}) collective-permute-start(bf16[128,768]{1,0:T(8,128)(2,1)S(1)} %constant_dynamic-update-slice_fusion.1), channel_id=1, source_target_pairs={{0,8},{1,9},{2,10},{3,11},{4,12},{5,13},{6,14},{7,15},{8,0},{9,1},... | collective-permute-start | bytes 589832 | tf_op jit(solution)/shard_map/ppermute | solution.py:550
  65.2 21.1 %collective-permute-start.7 = (bf16[4,128,768]{2,1,0:T(8,128)(2,1)S(1)}, bf16[4,128,768]{2,1,0:T(8,128)(2,1)S(1)}, u32[]{:S(2)}, u32[]{:S(2)}) collective-permute-start(bf16[4,128,768]{2,1,0:T(8,128)(2,1)S(1)} %pad_maximum_fusion.2.mine_ref), channel_id=1, source_target_pairs={{0,4},{1,5},{2,6},{3,7},{4,0},{5,1},{6,2},{7,3},{8,12},{9,13},{10,... | collective-permute-start | bytes 2359304 | tf_op jit(solution)/shard_map/ppermute | solution.py:550
  66.4 23.6 %collective-permute-start.2 = (bf16[3,128,768]{2,1,0:T(8,128)(2,1)S(1)}, bf16[3,128,768]{2,1,0:T(8,128)(2,1)S(1)}, u32[]{:S(2)}, u32[]{:S(2)}) collective-permute-start(bf16[3,128,768]{2,1,0:T(8,128)(2,1)S(1)} %collective-permute-done.1.refs_2_), channel_id=1, source_target_pairs={{0,1},{1,0},{2,3},{3,2},{4,5},{5,4},{6,7},{7,6},{8,9},{9,8},{10,11... | collective-permute-start | bytes 1769480 | tf_op jit(solution)/shard_map/ppermute | solution.py:540
  165.5 15.0 %collective-permute-start.9 = (bf16[5,2,2,4,24,768]{5,4,3,2,1,0:T(8,128)(2,1)}, bf16[5,2,2,4,24,768]{5,4,3,2,1,0:T(8,128)(2,1)}, u32[]{:S(2)}, u32[]{:S(2)}) collective-permute-start(bf16[5,2,2,4,24,768]{5,4,3,2,1,0:T(8,128)(2,1)} %get-tuple-element.97), channel_id=1, source_target_pairs={{0,1},{1,0},{2,3},{3,2},{4,5},{5,4},{6,7},{7,6},{8,9},{9,8},{10,11... | collective-permute-start | bytes 8847368 | tf_op jit(solution)/shard_map/ppermute | solution.py:550
  166.3 8.5 %collective-permute-start.8 = (bf16[2,2,4,96,768]{4,3,2,1,0:T(8,128)(2,1)}, bf16[2,2,4,96,768]{4,3,2,1,0:T(8,128)(2,1)S(1)}, u32[]{:S(2)}, u32[]{:S(2)}) collective-permute-start(bf16[2,2,4,96,768]{4,3,2,1,0:T(8,128)(2,1)} %get-tuple-element.95), channel_id=1, source_target_pairs={{0,1},{1,0},{2,3},{3,2},{4,5},{5,4},{6,7},{7,6},{8,9},{9,8},{10,11... | collective-permute-start | bytes 7077896 | tf_op jit(solution)/shard_map/ppermute | solution.py:550
  169.2 15.9 %all-to-all-start.2 = ((bf16[4,3,128,192]{2,3,1,0:T(8,128)(2,1)}), bf16[4,3,128,192]{2,3,1,0:T(8,128)(2,1)S(1)}, u32[]{:S(2)}, u32[]{:S(2)}) async-start(bf16[4,3,128,192]{2,3,1,0:T(8,128)(2,1)} %copy.71), calls=%async_computation.2 | async-start | bytes 1179648 | tf_op jit(solution)/shard_map/all_to_all | solution.py:681
  186.2 40.7 %collective-permute-start.10 = (bf16[2,4,96,768]{3,2,1,0:T(8,128)(2,1)}, bf16[2,4,96,768]{3,2,1,0:T(8,128)(2,1)}, u32[]{:S(2)}, u32[]{:S(2)}) collective-permute-start(bf16[2,4,96,768]{3,2,1,0:T(8,128)(2,1)} %get-tuple-element.103), channel_id=1, source_target_pairs={{0,4},{1,5},{2,6},{3,7},{4,0},{5,1},{6,2},{7,3},{8,12},{9,13},{10,... | collective-permute-start | bytes 3538952 | tf_op jit(solution)/shard_map/ppermute | solution.py:550
  186.8 40.1 %collective-permute-start.11 = (bf16[5,2,4,24,768]{4,3,2,0,1:T(8,128)(2,1)}, bf16[5,2,4,24,768]{4,3,2,0,1:T(8,128)(2,1)}, u32[]{:S(2)}, u32[]{:S(2)}) collective-permute-start(bf16[5,2,4,24,768]{4,3,2,0,1:T(8,128)(2,1)} %fusion.2), channel_id=1, source_target_pairs={{0,2},{1,3},{2,0},{3,1},{4,6},{5,7},{6,4},{7,5},{8,10},{9,11},{10,... | collective-permute-start | bytes 4423688 | tf_op jit(solution)/shard_map/ppermute | solution.py:550
  228.3 19.8 %collective-permute-start.13 = (bf16[2,3,128,768]{3,2,1,0:T(8,128)(2,1)S(1)}, bf16[2,3,128,768]{3,2,1,0:T(8,128)(2,1)S(1)}, u32[]{:S(2)}, u32[]{:S(2)}) collective-permute-start(bf16[2,3,128,768]{3,2,1,0:T(8,128)(2,1)S(1)} %slice.227), channel_id=1, source_target_pairs={{0,1},{1,0},{2,3},{3,2},{4,5},{5,4},{6,7},{7,6},{8,9},{9,8},{10,11... | collective-permute-start | bytes 3538952 | tf_op jit(solution)/shard_map/ppermute | solution.py:550
  229.2 18.9 %collective-permute-start.12 = (bf16[4,128,768]{2,1,0:T(8,128)(2,1)S(1)}, bf16[4,128,768]{2,1,0:T(8,128)(2,1)S(1)}, u32[]{:S(2)}, u32[]{:S(2)}) collective-permute-start(bf16[4,128,768]{2,1,0:T(8,128)(2,1)S(1)} %copy-done.9), channel_id=1, source_target_pairs={{0,4},{1,5},{2,6},{3,7},{4,0},{5,1},{6,2},{7,3},{8,12},{9,13},{10,... | collective-permute-start | bytes 2359304 | tf_op jit(solution)/shard_map/ppermute | solution.py:550
  231.6 32.3 %collective-permute-start.15 = (bf16[5,4,24,768]{3,2,1,0:T(8,128)(2,1)S(1)}, bf16[5,4,24,768]{3,2,1,0:T(8,128)(2,1)S(1)}, u32[]{:S(2)}, u32[]{:S(2)}) collective-permute-start(bf16[5,4,24,768]{3,2,1,0:T(8,128)(2,1)S(1)} %fusion.8), channel_id=1, source_target_pairs={{0,4},{1,5},{2,6},{3,7},{4,0},{5,1},{6,2},{7,3},{8,12},{9,13},{10,... | collective-permute-start | bytes 2211848 | tf_op jit(solution)/shard_map/ppermute | solution.py:550
  233.5 16.2 %collective-permute-start.14 = (bf16[4,96,768]{2,1,0:T(8,128)(2,1)S(1)}, bf16[4,96,768]{2,1,0:T(8,128)(2,1)S(1)}, u32[]{:S(2)}, u32[]{:S(2)}) collective-permute-start(bf16[4,96,768]{2,1,0:T(8,128)(2,1)S(1)} %get-tuple-element.150), channel_id=1, source_target_pairs={{0,2},{1,3},{2,0},{3,1},{4,6},{5,7},{6,4},{7,5},{8,10},{9,11},{10,... | collective-permute-start | bytes 1769480 | tf_op jit(solution)/shard_map/ppermute | solution.py:550
  264.8 36.7 %collective-permute-start.23 = (bf16[96,768]{1,0:T(8,128)(2,1)}, bf16[96,768]{1,0:T(8,128)(2,1)}, u32[]{:S(2)}, u32[]{:S(2)}) collective-permute-start(bf16[96,768]{1,0:T(8,128)(2,1)} %get-tuple-element.158), channel_id=1, source_target_pairs={{0,24},{1,25},{2,26},{3,27},{4,28},{5,29},{6,30},{7,31},{8,16},{9,... | collective-permute-start | bytes 442376 | tf_op jit(solution)/shard_map/ppermute | solution.py:550
  266.8 11.6 %collective-permute-start.16 = (bf16[128,768]{1,0:T(8,128)(2,1)S(1)}, bf16[128,768]{1,0:T(8,128)(2,1)S(1)}, u32[]{:S(2)}, u32[]{:S(2)}) collective-permute-start(bf16[128,768]{1,0:T(8,128)(2,1)S(1)} %get-tuple-element.152), channel_id=1, source_target_pairs={{0,8},{1,9},{2,10},{3,11},{4,12},{5,13},{6,14},{7,15},{8,0},{9,1},... | collective-permute-start | bytes 589832 | tf_op jit(solution)/shard_map/ppermute | solution.py:550
  266.9 12.7 %collective-permute-start.18 = (bf16[128,768]{1,0:T(8,128)(2,1)S(1)}, bf16[128,768]{1,0:T(8,128)(2,1)S(1)}, u32[]{:S(2)}, u32[]{:S(2)}) collective-permute-start(bf16[128,768]{1,0:T(8,128)(2,1)S(1)} %get-tuple-element.153), channel_id=1, source_target_pairs={{0,24},{1,25},{2,26},{3,27},{4,28},{5,29},{6,30},{7,31},{8,16},{9,... | collective-permute-start | bytes 589832 | tf_op jit(solution)/shard_map/ppermute | solution.py:550
  268.2 24.7 %collective-permute-start.17 = (bf16[128,768]{1,0:T(8,128)(2,1)S(1)}, bf16[128,768]{1,0:T(8,128)(2,1)S(1)}, u32[]{:S(2)}, u32[]{:S(2)}) collective-permute-start(bf16[128,768]{1,0:T(8,128)(2,1)S(1)} %get-tuple-element.154), channel_id=1, source_target_pairs={{0,16},{1,17},{2,18},{3,19},{4,20},{5,21},{6,22},{7,23},{8,24},{9,... | collective-permute-start | bytes 589832 | tf_op jit(solution)/shard_map/ppermute | solution.py:550
  269.5 27.0 %collective-permute-start.19 = (bf16[3,128,768]{2,1,0:T(8,128)(2,1)S(1)}, bf16[3,128,768]{2,1,0:T(8,128)(2,1)}, u32[]{:S(2)}, u32[]{:S(2)}) collective-permute-start(bf16[3,128,768]{2,1,0:T(8,128)(2,1)S(1)} %fusion.10), channel_id=1, source_target_pairs={{0,2},{1,3},{2,0},{3,1},{4,6},{5,7},{6,4},{7,5},{8,10},{9,11},{10,... | collective-permute-start | bytes 1769480 | tf_op jit(solution)/shard_map/ppermute | solution.py:550
  278.4 26.2 %collective-permute-start.22 = (bf16[96,768]{1,0:T(8,128)(2,1)}, bf16[96,768]{1,0:T(8,128)(2,1)}, u32[]{:S(2)}, u32[]{:S(2)}) collective-permute-start(bf16[96,768]{1,0:T(8,128)(2,1)} %get-tuple-element.159), channel_id=1, source_target_pairs={{0,16},{1,17},{2,18},{3,19},{4,20},{5,21},{6,22},{7,23},{8,24},{9,... | collective-permute-start | bytes 442376 | tf_op jit(solution)/shard_map/ppermute | solution.py:550
  279.6 29.5 %collective-permute-start.21 = (bf16[96,768]{1,0:T(8,128)(2,1)}, bf16[96,768]{1,0:T(8,128)(2,1)}, u32[]{:S(2)}, u32[]{:S(2)}) collective-permute-start(bf16[96,768]{1,0:T(8,128)(2,1)} %get-tuple-element.160), channel_id=1, source_target_pairs={{0,8},{1,9},{2,10},{3,11},{4,12},{5,13},{6,14},{7,15},{8,0},{9,1},... | collective-permute-start | bytes 442376 | tf_op jit(solution)/shard_map/ppermute | solution.py:550
  292.9 16.2 %collective-permute-start.26 = (bf16[5,24,768]{2,1,0:T(8,128)(2,1)}, bf16[5,24,768]{2,1,0:T(8,128)(2,1)S(1)}, u32[]{:S(2)}, u32[]{:S(2)}) collective-permute-start(bf16[5,24,768]{2,1,0:T(8,128)(2,1)} %get-tuple-element.155), channel_id=1, source_target_pairs={{0,24},{1,25},{2,26},{3,27},{4,28},{5,29},{6,30},{7,31},{8,16},{9,... | collective-permute-start | bytes 552968 | tf_op jit(solution)/shard_map/ppermute | solution.py:550
  296.5 16.4 %collective-permute-start.25 = (bf16[5,24,768]{2,1,0:T(8,128)(2,1)}, bf16[5,24,768]{2,1,0:T(8,128)(2,1)S(1)}, u32[]{:S(2)}, u32[]{:S(2)}) collective-permute-start(bf16[5,24,768]{2,1,0:T(8,128)(2,1)} %get-tuple-element.156), channel_id=1, source_target_pairs={{0,16},{1,17},{2,18},{3,19},{4,20},{5,21},{6,22},{7,23},{8,24},{9,... | collective-permute-start | bytes 552968 | tf_op jit(solution)/shard_map/ppermute | solution.py:550
  296.5 20.0 %all-to-all-start.3 = ((bf16[4,72,192]{2,1,0:T(8,128)(2,1)}), bf16[4,72,192]{2,1,0:T(8,128)(2,1)S(1)}, u32[]{:S(2)}, u32[]{:S(2)}) async-start(bf16[4,72,192]{2,1,0:T(8,128)(2,1)} %bitcast.155), calls=%async_computation.3 | async-start | bytes 294912 | tf_op jit(solution)/shard_map/all_to_all | solution.py:724
  301.4 11.4 %collective-permute-start.24 = (bf16[5,24,768]{2,1,0:T(8,128)(2,1)}, bf16[5,24,768]{2,1,0:T(8,128)(2,1)S(1)}, u32[]{:S(2)}, u32[]{:S(2)}) collective-permute-start(bf16[5,24,768]{2,1,0:T(8,128)(2,1)} %get-tuple-element.157), channel_id=1, source_target_pairs={{0,8},{1,9},{2,10},{3,11},{4,12},{5,13},{6,14},{7,15},{8,0},{9,1},... | collective-permute-start | bytes 552968 | tf_op jit(solution)/shard_map/ppermute | solution.py:550
  304.6 11.9 %collective-permute-start.20 = (bf16[56,768]{1,0:T(8,128)(2,1)}, bf16[56,768]{1,0:T(8,128)(2,1)S(1)}, u32[]{:S(2)}, u32[]{:S(2)}) collective-permute-start(bf16[56,768]{1,0:T(8,128)(2,1)} %slice.288), channel_id=1, source_target_pairs={{0,0},{1,8},{2,16},{3,24},{4,4},{5,12},{6,20},{7,28},{8,1},{9,9},{... | collective-permute-start | bytes 258056 | tf_op jit(solution)/shard_map/ppermute | solution.py:572
  (13 other events, 33.9 us)
Sparse Core Ops, SparseCore 0:
  16.8 110.6 all-gather.5
  167.1 57.6 all-gather.7

commit v3 on v2

--- a/solution.py
+++ b/solution.py
@@ -105,24 +105,39 @@
     )(at, vectors, *weights)
 
 
-def finish_kernel(cols_ref, mixed_ref, *out_refs):
-    own = out_refs[0].shape[0]
-    cols = [cols_ref[b].astype(WIDE) for b in range(cols_ref.shape[0])]
+def finish_kernel(at_ref, cols_ref, mixed_ref, *out_refs):
+    *grad_refs, lines_ref = out_refs
+    number, place_at = at_ref[3], at_ref[4]
+    own = grad_refs[0].shape[0]
+    size, _, width = cols_ref.shape
+    cols = [cols_ref[lax.rem(number, size) ^ b].astype(WIDE) for b in range(size)]
     for i in range(3):
-        out_refs[i][...] = jnp.concatenate([c[i * own:(i + 1) * own] for c in cols], axis=1)
+        grad_refs[i][...] = jnp.concatenate([c[i * own:(i + 1) * own] for c in cols], axis=1)
     mixed = mixed_ref[...].astype(WIDE)
     for i in range(2):
-        out_refs[3 + i][...] = halves(mixed[i * own:(i + 1) * own])
-
-
-def finish_call(cols, mixed):
-    own = cols.shape[1] // 3
+        grad_refs[3 + i][...] = halves(mixed[i * own:(i + 1) * own])
+    total = sum(c[3 * own:] for c in cols)
+    quarters = [total[16 * i:16 * (i + 1)] for i in range(size)]
+    rows = sum(jnp.where(lax.div(number, 8) == i, part, 0.0) for i, part in enumerate(quarters))
+    rows = pltpu.roll(rows, lax.rem(width - lax.rem(number, 8) * own, width), 1)
+    inner = sum(jnp.where(lax.div(lax.rem(number, 8), 2) == i, part, 0.0) for i, part in enumerate(quarters))
+    inner = sum(jnp.where(lax.div(number, 8) == j, inner[6 + j:7 + j], 0.0) for j in range(4))
+    inner = pltpu.roll(jnp.broadcast_to(inner, (8, width)), lax.rem(number, 2) * (width // 2), 1)
+    bias = mixed[2 * own + 8:2 * own + 16]
+    bias = jnp.concatenate([bias[2:3, i * width:(i + 1) * width] for i in range(3)] + [bias[:5, :width]], axis=0)
+    bias = pltpu.roll(bias, lax.rem(width - place_at * own, width), 1)
+    lines_ref[...] = jnp.concatenate([rows[:8, :128], inner[:, :128], bias[:, :128]], axis=0)
+
+
+def finish_call(at, cols, mixed):
+    own = (mixed.shape[0] - 16) // 2
     return pl.pallas_call(
         finish_kernel,
-        out_shape=[jax.ShapeDtypeStruct((own, D), WIDE)] * 5,
+        out_shape=[jax.ShapeDtypeStruct((own, D), WIDE)] * 5 + [jax.ShapeDtypeStruct((24, 128), WIDE)],
+        in_specs=[pl.BlockSpec(memory_space=pltpu.SMEM)] + [pl.BlockSpec(memory_space=pltpu.VMEM)] * 2,
         compiler_params=pltpu.CompilerParams(vmem_limit_bytes=VMEM_BYTES),
         name="finish",
-    )(cols, mixed)
+    )(at, cols, mixed)
 
 
 def assemble_kernel(own, size, at_ref, mine_ref, theirs_ref, w_ref, pq_ref, pk_ref, bias_ref, got):
@@ -165,6 +180,16 @@
     )(at, mine, theirs)
 
 
+def fold(rows):
+    half = rows.shape[0] // 2
+    return jnp.concatenate([rows[:half], rows[half:]], axis=1)
+
+
+def unfold(rows):
+    half = rows.shape[1] // 2
+    return jnp.concatenate([rows[:, :half], rows[:, half:]], axis=0)
+
+
 def turn(spread, left, right):
     s, c = spread[:, :SPAN], spread[:, SPAN:]
     return jnp.concatenate(
@@ -185,14 +210,18 @@
 def attend_kernel(heads, blocks, me_ref, *refs):
     tok_refs = refs[:blocks]
     (w_ref, bias_ref, pq_ref, pk_ref, sin_ref, cos_ref, alive_ref,
-     qkv_ref, soft_ref, ctx_ref) = refs[blocks:]
+     qkv_ref, soft_ref, share_ref, ctx_ref) = refs[blocks:]
     me = me_ref[0]
     rows = tok_refs[0].shape[1]
     width = heads * HD
     tok = jnp.concatenate([ref[0] for ref in tok_refs], axis=0)
     sines, cosines = sin_ref[0], cos_ref[0]
     key_feats, query_feats = feature_pair(sines, cosines)
-    alive = alive_ref[0] > 0
+    count = tok.shape[0]
+    mask = jnp.broadcast_to(jnp.where(alive_ref[0] > 0, 0.0, -1e30), (128, count)).T[:, :HD]
+    lane = lax.broadcasted_iota(jnp.int32, (count, HD), 1)
+    mask = jnp.where(lane == 0, mask, 0.0).astype(LOW)
+    ones = jnp.where(lane == 0, 1.0, 0.0).astype(LOW)
     qkv = (dot(tok, w_ref[...]) + bias_ref[...]).astype(LOW)
     qkv_ref[0] = qkv
     pieces = []
@@ -202,15 +231,17 @@
         v = qkv[:, 2 * width + h * HD:2 * width + (h + 1) * HD]
         turned_q = turn(dot(q, pq_ref[h]), cosines, sines)
         turned_k = turn(dot(k, pk_ref[h]), sines, cosines)
-        raw = dot_nt(q, k) + dot_nt(turned_q, key_feats) + dot_nt(query_feats, turned_k)
-        scores = jnp.where(alive, raw * SCALING, -1e30)
-        lifted = jnp.exp(scores - jnp.max(scores, axis=1, keepdims=True))
-        soft = (lifted / jnp.sum(lifted, axis=1, keepdims=True)).astype(LOW)
-        soft_ref[0, h] = soft
-        pieces.append(dot(soft, v).astype(LOW))
+        raw = dot_nt(jnp.concatenate([turned_q, query_feats, q, ones], axis=1),
+                     jnp.concatenate([key_feats, turned_k, k, mask], axis=1))
+        lifted = jnp.exp2((raw - jnp.max(raw, axis=1, keepdims=True)) * (SCALING * math.log2(math.e)))
+        share = 1.0 / jnp.sum(lifted, axis=1, keepdims=True)
+        share_ref[0, :, h:h + 1] = share
+        lifted = lifted.astype(LOW)
+        soft_ref[0, h] = lifted
+        pieces.append((dot(lifted, v) * share).astype(LOW))
     ctx = jnp.concatenate(pieces, axis=1)
     for j in range(blocks):
-        ctx_ref[me ^ j, 0] = ctx[j * rows:(j + 1) * rows]
+        ctx_ref[me ^ j, 0] = fold(ctx[j * rows:(j + 1) * rows])
 
 
 def attend_call(me, toks, w_qkv, bias, place_q, place_k, sines, cosines, alive):
@@ -230,13 +261,14 @@
                 whole((heads, HD, 2 * SPAN)), whole((heads, HD, 2 * SPAN)),
                 by_page(count, SPAN), by_page(count, SPAN), by_page(1, count)],
             out_specs=[
-                by_page(count, 3 * width), by_page(heads, count, count),
-                pl.BlockSpec((blocks, 1, rows, width), lambda p, *_: (0, p, 0, 0))],
+                by_page(count, 3 * width), by_page(heads, count, count), by_page(count, heads),
+                pl.BlockSpec((blocks, 1, rows // 2, 2 * width), lambda p, *_: (0, p, 0, 0))],
         ),
         out_shape=[
             jax.ShapeDtypeStruct((pages, count, 3 * width), LOW),
             jax.ShapeDtypeStruct((pages, heads, count, count), LOW),
-            jax.ShapeDtypeStruct((blocks, pages, rows, width), LOW),
+            jax.ShapeDtypeStruct((pages, count, heads), WIDE),
+            jax.ShapeDtypeStruct((blocks, pages, rows // 2, 2 * width), LOW),
         ],
         compiler_params=pltpu.CompilerParams(vmem_limit_bytes=VMEM_BYTES),
         cost_estimate=cost(20e9, 20e6),
@@ -244,7 +276,7 @@
     )(me, *toks, w_qkv, bias, place_q, place_k, sines, cosines, alive)
 
 
-def joined_grads(own, size, pages, d_w, d_pq, d_pk, d_bias):
+def joined_grads(own, size, pages, small, d_w, d_pq, d_pk, d_bias):
     inner = pages // size
     width = D // size
     cut = d_w.reshape(pages, size, own, 3 * width)
@@ -257,14 +289,16 @@
         order = [(lo * size + b) * own for b in range(size) for lo in range(inner)]
         parts.append(jnp.concatenate([place[at:at + own][None] for at in order], axis=0))
     row = jnp.concatenate([d_bias, jnp.zeros((1, D - 3 * width), WIDE)], axis=1)
-    parts.append(jnp.broadcast_to(row[None], (pages, 8, D)))
+    at = lax.broadcasted_iota(jnp.int32, small.shape, 0)
+    rows = jnp.where(at == 10, row, jnp.where(at < 10, small, 0.0))
+    parts.append(jnp.broadcast_to(rows[None], (pages,) + rows.shape))
     return jnp.concatenate(parts, axis=1).astype(LOW)
 
 
 def attend_back_kernel(heads, blocks, joined, me_ref, *refs):
     tok_refs = refs[:blocks]
-    (w_ref, qkv_ref, soft_ref, dctx_ref, pq_ref, pk_ref, sin_ref, cos_ref,
-     part_ref, *out_refs, dw_sum, dpq_sum, dpk_sum, db_sum) = refs[blocks:]
+    (w_ref, small_ref, qkv_ref, soft_ref, share_ref, ctx_ref, dctx_ref, pq_ref, pk_ref, sin_ref, cos_ref,
+     kept_ref, sent_ref, *out_refs, dw_sum, dpq_sum, dpk_sum, db_sum) = refs[blocks:]
     me = me_ref[0]
     step, last = pl.program_id(0), pl.num_programs(0) - 1
     rows = tok_refs[0].shape[1]
@@ -272,7 +306,9 @@
     sines, cosines = sin_ref[0], cos_ref[0]
     key_feats, query_feats = feature_pair(sines, cosines)
     qkv = qkv_ref[0]
-    dctx = jnp.concatenate([dctx_ref[me ^ j, 0] for j in range(blocks)], axis=0)
+    dctx = jnp.concatenate([unfold(dctx_ref[me ^ j, 0]) for j in range(blocks)], axis=0)
+    ctx = jnp.concatenate([unfold(ctx_ref[me ^ j, 0]) for j in range(blocks)], axis=0)
+    along = dctx.astype(WIDE) * ctx.astype(WIDE)
 
     @pl.when(step == 0)
     def _():
@@ -285,17 +321,18 @@
         k = qkv[:, width + h * HD:width + (h + 1) * HD]
         v = qkv[:, 2 * width + h * HD:2 * width + (h + 1) * HD]
         dc = dctx[:, h * HD:(h + 1) * HD]
-        soft = soft_ref[0, h]
-        soft_wide = soft.astype(WIDE)
-        attend_grad = dot_nt(dc, v)
-        row_dot = jnp.sum(soft_wide * attend_grad, axis=1, keepdims=True)
-        raw_grad = (soft_wide * (attend_grad - row_dot) * SCALING).astype(LOW)
-        d_v.append(dot_tn(soft, dc).astype(LOW))
-        spread_q = turn_back(dot(raw_grad, key_feats), cosines, sines)
-        d_q.append((dot(raw_grad, k) + dot_nt(spread_q, pq_ref[h])).astype(LOW))
+        share = share_ref[0, :, h:h + 1]
+        lifted = soft_ref[0, h]
+        row_dot = jnp.sum(along[:, h * HD:(h + 1) * HD], axis=1, keepdims=True)
+        raw_grad = ((dot_nt(dc, v) - row_dot) * (share * SCALING) * lifted.astype(WIDE)).astype(LOW)
+        d_v.append(dot_tn(lifted, (dc.astype(WIDE) * share).astype(LOW)).astype(LOW))
+        turned = dot(raw_grad, jnp.concatenate([key_feats, k], axis=1))
+        spread_q = turn_back(turned[:, :2 * SPAN], cosines, sines)
+        d_q.append((turned[:, 2 * SPAN:] + dot_nt(spread_q, pq_ref[h])).astype(LOW))
         dpq_sum[h] += dot_tn(q, spread_q)
-        spread_k = turn_back(dot_tn(raw_grad, query_feats), sines, cosines)
-        d_k.append((dot_tn(raw_grad, q) + dot_nt(spread_k, pk_ref[h])).astype(LOW))
+        turned = dot_tn(raw_grad, jnp.concatenate([query_feats, q], axis=1))
+        spread_k = turn_back(turned[:, :2 * SPAN], sines, cosines)
+        d_k.append((turned[:, 2 * SPAN:] + dot_nt(spread_k, pk_ref[h])).astype(LOW))
         dpk_sum[h] += dot_tn(k, spread_k)
     dqkv = jnp.concatenate(d_q + d_k + d_v, axis=1)
     db_sum[...] += jnp.sum(dqkv.astype(WIDE), axis=0, keepdims=True)
@@ -303,12 +340,12 @@
     dw_sum[...] += dot_tn(tok, dqkv)
     part = dot_nt(dqkv, w_ref[...]).astype(LOW)
     for j in range(blocks):
-        part_ref[j, 0] = part[j * rows:(j + 1) * rows]
+        (sent_ref if j % 2 else kept_ref)[j // 2, 0] = part[j * rows:(j + 1) * rows]
 
     @pl.when(step == last)
     def _():
         if joined:
-            rows = joined_grads(*joined, dw_sum[...], dpq_sum[...], dpk_sum[...], db_sum[...])
+            rows = joined_grads(*joined, small_ref[...], dw_sum[...], dpq_sum[...], dpk_sum[...], db_sum[...])
             even = me_ref[1] == 0
             for z in range(rows.shape[0] // 2):
                 first, second = rows[2 * z], rows[2 * z + 1]
@@ -319,15 +356,16 @@
                 ref[...] = total[...].astype(ref.dtype)
 
 
-def attend_back_call(joined, me, toks, w_qkv, qkv, soft, dctx, place_q, place_k, sines, cosines):
+def attend_back_call(joined, me, toks, w_qkv, small, qkv, soft, share, ctx, dctx, place_q, place_k, sines, cosines):
     blocks, pages, rows, width = dctx.shape
+    rows, width = 2 * rows, width // 2
     heads = place_q.shape[0]
     count = blocks * rows
     by_page = lambda *shape: pl.BlockSpec((1,) + shape, lambda p, *_: (p,) + (0,) * len(shape))
     place = (heads, HD, 2 * SPAN)
     if joined:
         own, _, owners = joined
-        sums = [jax.ShapeDtypeStruct((owners // 2, 5 * own + 8, D), LOW)] * 2
+        sums = [jax.ShapeDtypeStruct((owners // 2, 5 * own + 16, D), LOW)] * 2
     else:
         sums = [jax.ShapeDtypeStruct((D, 3 * width), LOW), jax.ShapeDtypeStruct(place, LOW),
                 jax.ShapeDtypeStruct(place, LOW), jax.ShapeDtypeStruct((1, 3 * width), WIDE)]
@@ -337,22 +375,23 @@
             num_scalar_prefetch=1,
             grid=(pages,),
             in_specs=[by_page(rows, D)] * blocks + [
-                whole((D, 3 * width)),
-                by_page(count, 3 * width), by_page(heads, count, count),
-                pl.BlockSpec((blocks, 1, rows, width), lambda p, *_: (0, p, 0, 0)),
+                whole((D, 3 * width)), whole(small.shape),
+                by_page(count, 3 * width), by_page(heads, count, count), by_page(count, heads),
+                pl.BlockSpec((blocks, 1, rows // 2, 2 * width), lambda p, *_: (0, p, 0, 0)),
+                pl.BlockSpec((blocks, 1, rows // 2, 2 * width), lambda p, *_: (0, p, 0, 0)),
                 whole(place), whole(place), by_page(count, SPAN), by_page(count, SPAN)],
             out_specs=[
-                pl.BlockSpec((blocks, 1, rows, D), lambda p, *_: (0, p, 0, 0)),
+                *[pl.BlockSpec((blocks // 2, 1, rows, D), lambda p, *_: (0, p, 0, 0))] * 2,
                 *(whole(item.shape) for item in sums)],
             scratch_shapes=[
                 pltpu.VMEM((D, 3 * width), WIDE), pltpu.VMEM(place, WIDE), pltpu.VMEM(place, WIDE),
                 pltpu.VMEM((1, 3 * width), WIDE)],
         ),
-        out_shape=[jax.ShapeDtypeStruct((blocks, pages, rows, D), LOW), *sums],
+        out_shape=[*[jax.ShapeDtypeStruct((blocks // 2, pages, rows, D), LOW)] * 2, *sums],
         compiler_params=pltpu.CompilerParams(vmem_limit_bytes=VMEM_BYTES),
         cost_estimate=cost(30e9, 20e6),
         name="attend_back",
-    )(me, *toks, w_qkv, qkv, soft, dctx, place_q, place_k, sines, cosines)
+    )(me, *toks, w_qkv, small, qkv, soft, share, ctx, dctx, place_q, place_k, sines, cosines)
 
 
 def normed(values):
@@ -379,7 +418,8 @@
      outer_grad, first_grad) = refs[4 + n_grads:]
     step = pl.program_id(0)
     core, x_at, y_at, z_at = at_ref[0], at_ref[1] >> 1, at_ref[1] & 1, at_ref[2]
-    blocks, _, _, width = ctx_ref.shape
+    blocks, pages, rows, width = ctx_ref.shape
+    rows, width = 2 * rows, width // 2
     count = tok_ref.shape[0]
     b_out, b_outer, gain_one, shift_one, gain_two, shift_two = (vec_ref[i:i + 1] for i in range(6))
 
@@ -388,7 +428,9 @@
     @pl.when(step == 0)
     def _():
         small_ref[...] = jnp.zeros_like(small_ref)
-        ctx = jnp.concatenate([ctx_ref[b].reshape(count, width) for b in range(blocks)], axis=1)
+        ctx = jnp.concatenate(
+            [jnp.concatenate([unfold(ctx_ref[b, p]) for b in range(blocks)], axis=1)
+             for p in range(pages)], axis=0)
         ctx_all[...] = ctx
         pre = tok_ref[...].astype(WIDE) + (dot(ctx, wo_ref[...]) + b_out)
         unit, scale = normed(pre)
@@ -433,7 +475,7 @@
         for z in range(4):
             for x in range(2):
                 for y in range(2):
-                    slot = (0, y_at ^ y, x_at ^ x, z_at ^ z)
+                    slot = (0, x_at ^ x, y_at ^ y, z_at ^ z)
                     first, second = cut[z, x, y, 0], cut[z, x, y, 1]
                     grad_refs[2][slot] = jnp.where(core == 0, first, second).astype(LOW)
                     grad_refs[3][slot] = jnp.where(core == 0, second, first).astype(LOW)
@@ -450,7 +492,7 @@
             cut = d_outer.reshape(2, 2, 2, D // 8, D)
             for x in range(2):
                 for y in range(2):
-                    slot = (x_at ^ x, y_at ^ y, 0)
+                    slot = (0, x_at ^ x, y_at ^ y)
                     first, second = cut[x, y, 0], cut[x, y, 1]
                     grad_refs[0][slot] = jnp.where(core == 0, first, second)
                     grad_refs[1][slot] = jnp.where(core == 0, second, first)
@@ -480,7 +522,8 @@
         small_ref[0:1] = summed(low.astype(WIDE))
         dctx = dot_nt(low, wo_ref[...]).astype(LOW)
         for b in range(blocks):
-            dctx_ref[b] = dctx[:, b * width:(b + 1) * width].reshape(dctx_ref.shape[1:])
+            for p in range(pages):
+                dctx_ref[b, p] = fold(dctx[p * rows:(p + 1) * rows, b * width:(b + 1) * width])
         d_output = dot_tn(ctx_all[...], low)
         if split:
             store_24(d_output)
@@ -490,18 +533,18 @@
 
 def second_half_call(split, at, ctx, tok, cot, w_output, vectors, w_inner, w_outer):
     blocks, pages, rows, width = ctx.shape
-    count = pages * rows
+    count = 2 * pages * rows
     cuts = w_inner.shape[1] // D
     now = lambda i: jnp.where(i < cuts, i, jnp.maximum(2 * cuts - 1 - i, 0))
     late = lambda i: jnp.where(i < cuts, cuts - 1, jnp.maximum(2 * cuts - 1 - i, 0))
     last = lambda i: jnp.where(i < 2 * cuts, late(i), cuts)
     square, tall = (D, D), (count, D)
-    eighth = (2, 2, 1, D // 8, D)
+    eighth = (1, 2, 2, D // 8, D)
     slots = (1, 2, 2, 4, D // 32, D)
     if split:
-        grad_specs = [pl.BlockSpec(eighth, lambda i, at: (0, 0, late(i) ^ at[2], 0, 0))] * 2
+        grad_specs = [pl.BlockSpec(eighth, lambda i, at: (late(i), 0, 0, 0, 0))] * 2
         grad_specs += [pl.BlockSpec(slots, lambda i, at: (last(i), 0, 0, 0, 0, 0))] * 2
-        grads = [(2, 2, cuts, D // 8, D)] * 2 + [(cuts + 1,) + slots[1:]] * 2
+        grads = [(cuts, 2, 2, D // 8, D)] * 2 + [(cuts + 1,) + slots[1:]] * 2
     else:
         grad_specs = [
             pl.BlockSpec(square, lambda i, at: (late(i), 0)),
@@ -558,6 +601,11 @@
     return added(value[0], *(hop(value[j], devices, j << 3) for j in (1, 2, 3)))
 
 
+def exchange_along_z(value, devices):
+    lines = [[i + 8 * z for z in range(4)] for i in range(8)]
+    return lax.all_to_all(value, AXES, 0, 0, tiled=True, axis_index_groups=lines)
+
+
 def tie(*values):
     return lax.optimization_barrier(values)
 
@@ -572,9 +620,8 @@
     return lax.ppermute(value, AXES, pairs)
 
 
-def sum_slots(partial):
-    got = swap(partial[1::2], "pb", 4, 1)
-    total = partial[0::2].astype(WIDE) + got.astype(WIDE)
+def sum_slots(kept, sent):
+    total = added(kept, swap(sent, "pb", 4, 1))
     return total[0] + swap(total[1].astype(LOW), "pb", 4, 2).astype(WIDE)
 
 
@@ -608,10 +655,9 @@
     small_rows = 16
     vectors = [output_bias, outer_bias, first_gain, first_shift, second_gain, second_shift]
     if by_link:
-        lines = vectors + [None] * 2 + [inner_bias] + [None] * 7 + [query_bias, keys_bias, values_bias]
-        lines = [jnp.zeros((128,), WIDE) if line is None
-                 else jnp.pad(line.astype(WIDE), (0, 128 - line.shape[0])) for line in lines]
-        lines = jnp.concatenate(lines + [jnp.zeros((5 * 128,), WIDE)]).reshape(24, 128)
+        lines = list(enumerate(vectors)) + [(8, inner_bias), (16, query_bias), (17, keys_bias), (18, values_bias)]
+        lines = added(*(jnp.pad(line.astype(WIDE), (128 * i, 128 * (24 - i) - line.shape[0]))
+                        for i, line in lines)).reshape(24, 128)
         packed, cols, mixed = pack_call(
             at, lines, query_weight, keys_weight, values_weight, query_place, keys_place,
             output_weight, inner_weight, outer_weight)
@@ -663,7 +709,7 @@
         mixed = mixed.transpose(2, 1, 0, 3, 4).reshape(2, heads, HD, 2 * SPAN)
         place_q, place_k = mixed[0], mixed[1]
 
-    qkv, soft, ctx_heads = attend_call(
+    qkv, soft, share, ctx_heads = attend_call(
         me_array, toks, w_qkv, bias_qkv, place_q, place_k, sines, cosines, alive)
     ctx = lax.all_to_all(ctx_heads, "pb", 0, 0, tiled=True)
 
@@ -682,52 +728,50 @@
 
     if by_link:
         outer_kept, outer_sent, inner_kept, inner_sent = grads
-        outer_sent, inner_sent = hop(outer_sent, devices, 1), hop(inner_sent, devices, 1)
-        outer_far = added(outer_kept[1], outer_sent[1]).astype(LOW)
-        inner_far = added(inner_kept[:, 1], inner_sent[:, 1]).astype(LOW)
-        outer_kept = added(outer_kept[0], outer_sent[0]).astype(LOW)
-        inner_kept = added(inner_kept[:, 0], inner_sent[:, 0]).astype(LOW)
-        dctx, outer_far, inner_far, outer_kept, inner_kept = tie(
-            dctx, outer_far, inner_far, outer_kept, inner_kept)
-        outer_far, inner_far = hop(outer_far, devices, 4), hop(inner_far, devices, 2)
-    small = lax.all_gather(small, AXES, axis=0)
+        outer_core, inner_core = hop(outer_sent, devices, 1), hop(inner_sent, devices, 1)
+        outer_sum = added(outer_kept, outer_core).astype(LOW)
+        inner_far = added(inner_kept[:, 1], inner_core[:, 1]).astype(LOW)
+        dctx, outer_sum, inner_far = tie(dctx, outer_sum, inner_far)
+        outer_got, inner_far = exchange_along_z(outer_sum, devices), hop(inner_far, devices, 4)
 
     joined = (own, pb_size, page_size) if by_link else None
     me_array = jnp.stack([me, at[1] >> 1, at[2]]).astype(jnp.int32)
-    partial, *sums = attend_back_call(
-        joined, me_array, toks, w_qkv, qkv, soft, dctx, place_q, place_k, sines, cosines)
+    kept, sent, *sums = attend_back_call(
+        joined, me_array, toks, w_qkv, small, qkv, soft, share, ctx_heads, dctx, place_q, place_k, sines, cosines)
 
     if by_link:
-        partial, mixed, mixed_far, outer_kept, outer_far, inner_kept, inner_far = tie(
-            partial, *sums, outer_kept, outer_far, inner_kept, inner_far)
-        mixed_far = hop(mixed_far, devices, 4)
-        near = hop(partial[1::2], devices, 1)
-        outer_sent = added(outer_kept[1], outer_far[1]).astype(LOW)
-        inner_sent = added(inner_kept[:, 1], inner_far[:, 1]).astype(LOW)
-        outer_sent, inner_sent = hop(outer_sent, devices, 2), hop(inner_sent, devices, 4)
-        outer_kept, inner_kept = added(outer_kept[0], outer_far[0]), added(inner_kept[:, 0], inner_far[:, 0])
-        mixed, mixed_far, partial, near = tie(mixed, mixed_far, partial, near)
-        total = added(partial[0::2], near)
-        far = hop(total[1].astype(LOW), devices, 2)
+        kept, sent, mixed, mixed_far, inner_far = tie(kept, sent, *sums, inner_far)
+        mixed_far, sent = hop(mixed_far, devices, 4), hop(sent, devices, 1)
+        inner_sent = added(inner_kept[:, 0, 1], inner_core[:, 0, 1], inner_far[:, 1]).astype(LOW)
+        inner_sent = hop(inner_sent, devices, 2)
+        inner_sum = added(inner_kept[:, 0, 0], inner_core[:, 0, 0], inner_far[:, 0])
+        mixed, mixed_far, kept, sent, inner_sum, inner_sent, outer_got = tie(
+            mixed, mixed_far, kept, sent, inner_sum, inner_sent, outer_got)
         mixed = added(mixed, mixed_far).astype(LOW)
-        mixed, outer_kept, outer_sent, inner_kept, inner_sent = tie(
-            mixed, outer_kept, outer_sent, inner_kept, inner_sent)
+        inner_sum = added(inner_sum, inner_sent).astype(LOW).swapaxes(0, 1).reshape(4, (cuts + 1) * own, D)
+        mixed = jnp.concatenate([mixed, inner_sum], axis=1)
         mixed_z = [hop(mixed[j], devices, j << 3) for j in (1, 2, 3)]
-        outer_sum = added(outer_kept, outer_sent).astype(LOW)
-        inner_sum = added(inner_kept, inner_sent).astype(LOW).swapaxes(0, 1)
-        outer_z = [hop(outer_sum[j], devices, j << 3) for j in (1, 2, 3)]
-        inner_z = [hop(inner_sum[j], devices, j << 3) for j in (1, 2, 3)]
-        mixed = added(mixed[0], *mixed_z).astype(LOW)
-        cols, far, total = tie(
-            mixed[:3 * own].reshape(3 * own, pb_size, width).swapaxes(0, 1), far, total[0])
-        tokens_grad = pre_one_grad.reshape(pages, rows, D) + added(total, far)
-        cols = lax.all_to_all(cols, "pb", 0, 0, tiled=True)
-        mixed = transpose_roles(mixed[3 * own:], page_size, pb_size)
-        cols, mixed, outer_sum, inner_sum, *got = tie(
-            cols, mixed, outer_sum, inner_sum, *outer_z, *inner_z)
-        d_outer = added(outer_sum[0], *got[:3])
-        inner_sum = added(inner_sum[0], *got[3:])
-        d_query, d_keys, d_values, d_place_q, d_place_k = finish_call(cols, mixed)
+        outer_sent = hop(added(*(outer_got[z, 1] for z in range(4))).astype(LOW), devices, 4)
+        far = hop(added(kept[1], sent[1]).astype(LOW), devices, 2)
+        outer_sum = added(*(outer_got[z, 0] for z in range(4)))
+        mixed, kept, sent, far, outer_sum, outer_sent, *mixed_z = tie(
+            mixed, kept, sent, far, outer_sum, outer_sent, *mixed_z)
+        rest = 5 * own + 16
+        inner_sum = added(mixed[0, rest:], *(got[rest:] for got in mixed_z)).reshape(cuts + 1, own, D)
+        mixed = added(mixed[0, :rest], *(got[:rest] for got in mixed_z)).astype(LOW)
+        small = mixed[5 * own:].reshape(16, pb_size, width).swapaxes(0, 1).reshape(1, 16 * pb_size, width)
+        cols = mixed[:3 * own].reshape(3 * own, pb_size, width).swapaxes(0, 1)
+        cols = jnp.concatenate([cols, jnp.broadcast_to(small, (pb_size,) + small.shape[1:])], axis=1)
+        cols = jnp.stack([cols[me]] + [swap(cols[me ^ j], "pb", pb_size, j) for j in (1, 2, 3)])
+        mixed = transpose_roles(mixed[3 * own:5 * own + 16], page_size, pb_size)
+        outer_sum = added(outer_sum, outer_sent)
+        outer_sent = hop(outer_sum[1].astype(LOW), devices, 2)
+        tokens_grad = pre_one_grad.reshape(pages, rows, D) + added(kept[0], sent[0], far)
+        d_outer = added(outer_sum[0], outer_sent)
+        d_query, d_keys, d_values, d_place_q, d_place_k, lines = finish_call(at, cols, mixed)
+        vectors = [lines[i, :own] for i in range(6)]
+        d_b_inner = lines[8, :ff_own]
+        d_bias = [lines[16 + i, :own] for i in range(3)]
         d_inner = jnp.concatenate([inner_sum[j] for j in range(cuts)], axis=1)
         d_output = inner_sum[cuts]
     else:
@@ -747,18 +791,18 @@
         mixed = jnp.concatenate([d_w, d_p, d_bias], axis=1)
         mixed = lax.all_to_all(mixed, "page", 0, 0, tiled=True)
         mixed = jnp.sum(mixed.astype(WIDE), axis=0).astype(LOW)
-        tokens_grad = pre_one_grad.reshape(pages, rows, D) + sum_slots(partial)
+        tokens_grad = pre_one_grad.reshape(pages, rows, D) + sum_slots(kept, sent)
         cols = mixed[:3 * own].reshape(3 * own, pb_size, width).swapaxes(0, 1)
         cols = lax.all_to_all(cols, "pb", 0, 0, tiled=True)
         d_query, d_keys, d_values = cols.swapaxes(0, 1).reshape(3, own, D).astype(WIDE)
         mixed = transpose_roles(mixed[3 * own:], page_size, pb_size)
         d_place_q, d_place_k = to_halves(mixed[:own].astype(WIDE)), to_halves(mixed[own:2 * own].astype(WIDE))
-    d_bias = lax.dynamic_slice(
-        mixed[2 * own, :3 * width].astype(WIDE).reshape(3, width), (0, place_at * own), (3, own))
-
-    small = jnp.sum(small, axis=0)
-    d_b_inner = lax.dynamic_slice(small[6:6 + cuts].reshape(ff), (number * ff_own,), (ff_own,))
-    vectors = lax.dynamic_slice(small, (0, number * own), (6, own))
+        d_bias = lax.dynamic_slice(
+            mixed[2 * own, :3 * width].astype(WIDE).reshape(3, width), (0, place_at * own), (3, own))
+        small = jnp.sum(lax.all_gather(small, AXES, axis=0), axis=0)
+        d_b_inner = lax.dynamic_slice(small[6:6 + cuts].reshape(ff), (number * ff_own,), (ff_own,))
+        vectors = lax.dynamic_slice(small, (0, number * own), (6, own))
+
     return (
         output.reshape(pages, rows, D),
         tokens_grad,

time: 330 us -> 306 us (0.927)
  blocking collectives: 20.7 us -> 8.77 us
  waiting for transfers between devices: 79.9 us -> 91.7 us
  other arithmetic: 44.4 us -> 36.2 us
  local copies, waits for them, and re-layouts: 24.8 us -> 17.3 us
  starting transfers between devices: 53.1 us -> 46.7 us
    ppermute x22 -> x16, starting transfers between devices: 32.1 us -> 19.9 us  [hop(): return lax.ppermute(value, AXES, [(i, i ^ bits) for i in range(devices)])]
    all_to_all x1 -> x0, blocking collectives: 12 us -> none  [on_device(): ctx = lax.all_to_all(ctx_heads, 'pb', 0, 0, tiled=True)]
    all_gather x1, waiting for transfers between devices: 0.01 us -> 9.83 us  [on_device(): late = lax.all_gather(packed, AXES, axis=0)]
    ppermute x22 -> x16, waiting for transfers between devices: 72 us -> 81.8 us  [hop(): return lax.ppermute(value, AXES, [(i, i ^ bits) for i in range(devices)])]
    all_to_all x0 -> x2, starting transfers between devices: none -> 7.72 us  [the longest x1 3.87 us: on_device(): ctx = lax.all_to_all(ctx_heads, 'pb', 0, 0, tiled=True)]
    unnamed x11 -> x0, other arithmetic: 6.63 us -> none
    all_to_all x2 -> x1, starting transfers between devices: 8.27 us -> 3.32 us  [on_device(): cols = lax.all_to_all(cols, 'pb', 0, 0, tiled=True)]
    all_gather x1 -> x0, waiting for transfers between devices: 4.24 us -> none  [on_device(): small = lax.all_gather(small, AXES, axis=0)]
  transfers between devices with their start and end apart: 32 -> 29, of which waited for: 12 -> 11; matrix products, arithmetic and copies ran while one was open for 13% -> 14% of each run, Pallas kernels for 18% -> 20%
where the time goes in v3:
time: 306 us; the launch traced here: 305 us
  waiting for transfers between devices  91.7 us (30%)
  Pallas kernels  89.8 us (29%)
  starting transfers between devices  46.7 us (15%)
  other arithmetic  36.2 us (12%)
  local copies, waits for them, and re-layouts  17.3 us (6%)
  between operations  14.5 us (5%)
  blocking collectives  8.77 us (3%)
    ppermute x16, waiting for transfers between devices, hop(): return lax.ppermute(value, AXES, [(i, i ^ bits) for i in range(devices)])  81.8 us
    pallas_call x1, Pallas kernels, attend_back_call(): pl.pallas_call(functools.partial(attend_back_kernel, heads, blocks, joine...  32.6 us
    pallas_call x1, Pallas kernels, second_half_call(): pl.pallas_call(functools.partial(second_half_kernel, cuts, split), grid_s...  27.2 us
    pallas_call x1, Pallas kernels, attend_call(): pl.pallas_call(functools.partial(attend_kernel, heads, blocks), grid_spec...  23.2 us
    ppermute x16, starting transfers between devices, hop(): return lax.ppermute(value, AXES, [(i, i ^ bits) for i in range(devices)])  19.9 us
    cos x1, other arithmetic, on_device(): sines, cosines = (jnp.sin(angles), jnp.cos(angles))  10.1 us
    all_gather x1, waiting for transfers between devices, on_device(): late = lax.all_gather(packed, AXES, axis=0)  9.83 us
    all_gather x1, blocking collectives, on_device(): places = lax.all_gather(jnp.stack([grid_x, grid_y, padding]), 'pb', axis=0)  8.77 us
  transfers between devices with their start and end apart: 29, of which 11 were waited for; matrix products, arithmetic and copies ran while one was open for 14% of the time, Pallas kernels for 20%

profile of v3, /device:TPU:1, one launch (start us, length us, event | category | flops | bytes accessed | tf_op | source)
XLA Modules:
  0.0 305.0 jit_solution(3594247493136601469)
XLA Ops:
  9.3 2.0 pack.1
  11.3 2.1 collective-permute-start.1
  14.4 3.3 %all-to-all-start = ((bf16[4,72,192]{2,1,0:T(8,128)(2,1)}), bf16[4,72,192]{2,1,0:T(8,128)(2,1)S(1)}, u32[]{:S(2)}, u32[]{:S(2)}) async-start(bf16[4,72,192]{2,1,0:T(8,128)(2,1)} %get-tuple-element.74), calls=%async_computation | async-start | bytes 294912 | tf_op jit(solution)/shard_map/all_to_all | solution.py:679
  17.7 3.1 %collective-permute-start.3 = (bf16[56,768]{1,0:T(8,128)(2,1)}, bf16[56,768]{1,0:T(8,128)(2,1)S(1)}, u32[]{:S(2)}, u32[]{:S(2)}) collective-permute-start(bf16[56,768]{1,0:T(8,128)(2,1)} %get-tuple-element.75), channel_id=1, source_target_pairs={{0,0},{1,8},{2,16},{3,24},{4,4},{5,12},{6,20},{7,28},{8,1},{9,9},{... | collective-permute-start | bytes 258056 | tf_op jit(solution)/shard_map/ppermute | solution.py:620
  24.1 8.8 %all-gather = s32[12,3,128]{2,1,0:T(4,128)S(1)} all-gather(s32[3,3,128]{2,1,0:T(4,128)S(1)} %pad_add_fusion), channel_id=2, replica_groups=mesh['page'=8,'pb'=4] {'pb'}, dimensions={0}, use_global_device_ids=true | all-gather | bytes 23040 | tf_op jit(solution)/shard_map/all_gather | solution.py:687
  33.2 5.4 %collective-permute-start.6 = (bf16[128,768]{1,0:T(8,128)(2,1)S(1)}, bf16[128,768]{1,0:T(8,128)(2,1)S(1)}, u32[]{:S(2)}, u32[]{:S(2)}) collective-permute-start(bf16[128,768]{1,0:T(8,128)(2,1)S(1)} %constant_dynamic-update-slice_fusion), channel_id=1, source_target_pairs={{0,24},{1,25},{2,26},{3,27},{4,28},{5,29},{6,30},{7,31},{8,16},{9,... | collective-permute-start | bytes 589832 | tf_op jit(solution)/shard_map/ppermute | solution.py:593
  39.1 4.8 %collective-permute-done.6 = bf16[128,768]{1,0:T(8,128)(2,1)S(1)} collective-permute-done((bf16[128,768]{1,0:T(8,128)(2,1)S(1)}, bf16[128,768]{1,0:T(8,128)(2,1)S(1)}, u32[]{:S(2)}, u32[]{:S(2)}) %collective-permute-start.6) | collective-permute-done | bytes 196640 | tf_op jit(solution)/shard_map/ppermute | solution.py:593
  43.9 16.5 %collective-permute-done.5 = bf16[128,768]{1,0:T(8,128)(2,1)S(1)} collective-permute-done((bf16[128,768]{1,0:T(8,128)(2,1)S(1)}, bf16[128,768]{1,0:T(8,128)(2,1)S(1)}, u32[]{:S(2)}, u32[]{:S(2)}) %collective-permute-start.5) | collective-permute-done | bytes 196640 | tf_op jit(solution)/shard_map/ppermute | solution.py:593
  63.5 10.1 %fusion = (f32[3,512,384]{2,1,0:T(8,128)}, f32[3,512,384]{2,1,0:T(8,128)}) fusion(f32[3,512,192]{2,1,0:T(8,128)S(1)} %get-tuple-element.170, f32[3,512,192]{2,1,0:T(8,128)S(1)} %get-tuple-element.169), kind=kLoop, calls=%fused_computation.13 | loop fusion | flops 589824 | bytes 7077888 | tf_op jit(solution)/shard_map/cos | solution.py:696
  73.5 7.4 %collective-permute-done.7.theirs_ref = bf16[4,128,768]{2,1,0:T(8,128)(2,1)S(1)} collective-permute-done((bf16[4,128,768]{2,1,0:T(8,128)(2,1)S(1)}, bf16[4,128,768]{2,1,0:T(8,128)(2,1)S(1)}, u32[]{:S(2)}, u32[]{:S(2)}) %collective-permute-start.7) | collective-permute-done | bytes 786464 | tf_op jit(solution)/shard_map/ppermute | solution.py:593
  81.8 2.9 assemble.1
  85.8 23.2 %attend.1 = (bf16[3,512,576]{2,1,0:T(8,128)(2,1)}, bf16[3,3,512,512]{3,2,1,0:T(8,128)(2,1)}, f32[3,512,3]{2,1,0:T(8,128)}, bf16[4,3,64,384]{3,2,1,0:T(8,128)(2,1)}) custom-call(s32[1]{0:T(128)} %bitcast.5.me_ref, bf16[3,128,768]{2,1,0:T(8,128)(2,1)} %refs_0_.3, bf16[3,128,768]{2,1,0:T(8,128)(2,1)} %copy-done.17, bf16[3,128,768]{2,1,0:T(8,128)(2,1)} %copy-done.16, ...), custom_call_target="tpu_custom_call" | custom-call | flops 20000000000 | bytes 20000000 | tf_op jit(solution)/shard_map/attend/pallas_call | solution.py:254
  109.0 3.9 %all-to-all-start.1 = ((bf16[4,3,64,384]{3,2,1,0:T(8,128)(2,1)}), bf16[4,3,64,384]{3,2,1,0:T(8,128)(2,1)S(1)}, u32[]{:S(2)}, u32[]{:S(2)}) async-start(bf16[4,3,64,384]{3,2,1,0:T(8,128)(2,1)} %get-tuple-element.80.refs_9_), calls=%async_computation.1 | async-start | bytes 1179648 | tf_op jit(solution)/shard_map/all_to_all | solution.py:714
  112.9 9.8 %all-gather.4.cloned.1.call-done = bf16[7424,768]{1,0:T(8,128)(2,1)} async-done(((bf16[232,768]{1,0:T(8,128)(2,1)}), bf16[7424,768]{1,0:T(8,128)(2,1)}) %all-gather.4.cloned.1.call-update) | async-done | bytes 11403280 | tf_op jit(solution)/shard_map/all_gather | solution.py:683
  122.7 1.9 convert_reduce_fusion.vec_ref
  124.6 4.1 %fusion.38 = (bf16[32,24,768]{2,1,0:T(8,128)(2,1)S(1)}, bf16[32,24,768]{2,1,0:T(8,128)(2,1)S(1)}, bf16[32,24,768]{2,1,0:T(8,128)(2,1)S(1)}, bf16[32,24,768]{2,1,0:T(8,128)(2,1)S(1)}, bf16[32,24,768]{2,1,0:T(8,128)(2,1)}) fusion(bf16[32,232,768]{2,1,0:T(8,128)(2,1)} %bitcast.158), kind=kLoop, calls=%fused_computation.116 | loop fusion | bytes 11796480 | tf_op jit(solution)/shard_map/slice | solution.py:718
  128.7 2.5 pad_maximum_fusion.wi_ref
  132.0 27.2 %second_half.1 = (bf16[384,768]{1,0:T(8,128)(2,1)}, f32[384,768]{1,0:T(8,128)}, bf16[4,3,64,384]{3,2,1,0:T(8,128)(2,1)}, bf16[4,2,2,96,768]{4,3,2,1,0:T(8,128)(2...) custom-call(s32[5]{0:T(128)} %stack.72.at_ref, ...), custom_call_target="tpu_custom_call" | custom-call | flops 20000000000 | bytes 30000000 | tf_op jit(solution)/shard_map/second_half/pallas_call | solution.py:553
  160.3 3.7 %all-to-all-start.2 = ((bf16[4,3,64,384]{3,2,1,0:T(8,128)(2,1)}), bf16[4,3,64,384]{3,2,1,0:T(8,128)(2,1)S(1)}, u32[]{:S(2)}, u32[]{:S(2)}) async-start(bf16[4,3,64,384]{3,2,1,0:T(8,128)(2,1)} %get-tuple-element.88), calls=%async_computation.2 | async-start | bytes 1179648 | tf_op jit(solution)/shard_map/all_to_all | solution.py:727
  164.0 4.5 %collective-permute-done.8 = bf16[4,2,2,96,768]{4,3,2,1,0:T(8,128)(2,1)} collective-permute-done((bf16[4,2,2,96,768]{4,3,2,1,0:T(8,128)(2,1)}, bf16[4,2,2,96,768]{4,3,2,1,0:T(8,128)(2,1)}, u32[]{:S(2)}, u32[]{:S(2)}) %collective-permute-start.8) | collective-permute-done | bytes 2359328 | tf_op jit(solution)/shard_map/ppermute | solution.py:593
  168.5 4.6 %add_convert_fusion = bf16[4,2,2,96,768]{4,3,2,1,0:T(8,128)(2,1)} fusion(bf16[4,2,2,96,768]{4,3,2,1,0:T(8,128)(2,1)} %collective-permute-done.8, bf16[4,2,2,96,768]{4,3,2,1,0:T(8,128)(2,1)} %get-tuple-element.89), kind=kLoop, calls=%fused_computation.1 | loop fusion | flops 4718592 | bytes 7077888 | tf_op jit(solution)/shard_map/convert_element_type | solution.py:732
  176.0 3.9 %all-to-all-start.3 = ((bf16[4,2,2,96,768]{4,3,2,1,0:T(8,128)(2,1)}), bf16[4,2,2,96,768]{4,3,2,1,0:T(8,128)(2,1)S(1)}, u32[]{:S(2)}, u32[]{:S(2)}) async-start(bf16[4,2,2,96,768]{4,3,2,1,0:T(8,128)(2,1)} %add_convert_fusion), calls=%async_computation.3 | async-start | bytes 4718592 | tf_op jit(solution)/shard_map/all_to_all | solution.py:606
  181.1 32.6 %attend_back.1 = (bf16[2,3,128,768]{3,2,1,0:T(8,128)(2,1)}, bf16[2,3,128,768]{3,2,1,0:T(8,128)(2,1)}, bf16[4,136,768]{2,1,0:T(8,128)(2,1)}, bf16[4,136,768]{2,1,0:T(8,128)(2,1)}) custom-call(s32[3]{0:T(128)} %pad_add_fusion.1.me_ref, bf16[3,128,768]{2,1,0:T(8,128)(2,1)} %refs_0_.3, bf16[3,128,768]{2,1,0:T(8,128)(2,1)} %copy-done.17, ...), custom_call_target="tpu_custom_call" | custom-call | flops 30000001024 | bytes 20000000 | tf_op jit(solution)/shard_map/attend_back/pallas_call | solution.py:372
  216.0 3.0 fusion.3
  219.3 17.5 %collective-permute-done.13 = bf16[5,4,24,768]{3,2,1,0:T(8,128)(2,1)S(1)} collective-permute-done((bf16[5,4,24,768]{3,2,1,0:T(8,128)(2,1)S(1)}, bf16[5,4,24,768]{3,2,1,0:T(8,128)(2,1)S(1)}, u32[]{:S(2)}, u32[]{:S(2)}) %collective-permute-start.13) | collective-permute-done | bytes 737312 | tf_op jit(solution)/shard_map/ppermute | solution.py:593
  242.2 3.0 collective-permute-start.18
  247.3 5.2 %collective-permute-done.15 = bf16[2,96,768]{2,1,0:T(8,128)(2,1)S(1)} collective-permute-done((bf16[2,96,768]{2,1,0:T(8,128)(2,1)S(1)}, bf16[2,96,768]{2,1,0:T(8,128)(2,1)S(1)}, u32[]{:S(2)}, u32[]{:S(2)}) %collective-permute-start.15) | collective-permute-done | bytes 294944 | tf_op jit(solution)/shard_map/ppermute | solution.py:593
  253.5 10.9 %collective-permute-done.16 = bf16[256,768]{1,0:T(8,128)(2,1)S(1)} collective-permute-done((bf16[256,768]{1,0:T(8,128)(2,1)S(1)}, bf16[256,768]{1,0:T(8,128)(2,1)S(1)}, u32[]{:S(2)}, u32[]{:S(2)}) %collective-permute-start.16) | collective-permute-done | bytes 393248 | tf_op jit(solution)/shard_map/ppermute | solution.py:593
  264.4 14.0 %collective-permute-done.17 = bf16[256,768]{1,0:T(8,128)(2,1)S(1)} collective-permute-done((bf16[256,768]{1,0:T(8,128)(2,1)S(1)}, bf16[256,768]{1,0:T(8,128)(2,1)S(1)}, u32[]{:S(2)}, u32[]{:S(2)}) %collective-permute-start.17) | collective-permute-done | bytes 393248 | tf_op jit(solution)/shard_map/ppermute | solution.py:593
  283.0 1.9 collective-permute-start.22
  285.0 3.4 %collective-permute-start.23 = (bf16[96,768]{1,0:T(8,128)(2,1)S(1)}, bf16[96,768]{1,0:T(8,128)(2,1)S(1)}, u32[]{:S(2)}, u32[]{:S(2)}) collective-permute-start(bf16[96,768]{1,0:T(8,128)(2,1)S(1)} %fusion.20), channel_id=1, source_target_pairs={{0,2},{1,3},{2,0},{3,1},{4,6},{5,7},{6,4},{7,5},{8,10},{9,11},{10,... | collective-permute-start | bytes 442376 | tf_op jit(solution)/shard_map/ppermute | solution.py:593
  289.1 2.3 fusion.4
  (132 shorter events, 41.1 us)
Async XLA Ops:
  7.2 115.5 %all-gather.4.cloned.1.call-start = ((), (), s32[]{:S(2)}) async-start(), calls=%async_computation.4 | async-start | bytes 11759616 | tf_op jit(solution)/shard_map/all_gather | solution.py:683
  11.3 50.4 %collective-permute-start.1 = (bf16[3,128,768]{2,1,0:T(8,128)(2,1)}, bf16[3,128,768]{2,1,0:T(8,128)(2,1)S(1)}, u32[]{:S(2)}, u32[]{:S(2)}) collective-permute-start(bf16[3,128,768]{2,1,0:T(8,128)(2,1)} %refs_0_.3), channel_id=1, source_target_pairs={{0,2},{1,3},{2,0},{3,1},{4,6},{5,7},{6,4},{7,5},{8,10},{9,11},{10,... | collective-permute-start | bytes 1769480 | tf_op jit(solution)/shard_map/ppermute | solution.py:583
  13.4 71.2 %collective-permute-start = (bf16[3,128,768]{2,1,0:T(8,128)(2,1)}, bf16[3,128,768]{2,1,0:T(8,128)(2,1)S(1)}, u32[]{:S(2)}, u32[]{:S(2)}) collective-permute-start(bf16[3,128,768]{2,1,0:T(8,128)(2,1)} %refs_0_.3), channel_id=1, source_target_pairs={{0,1},{1,0},{2,3},{3,2},{4,5},{5,4},{6,7},{7,6},{8,9},{9,8},{10,11... | collective-permute-start | bytes 1769480 | tf_op jit(solution)/shard_map/ppermute | solution.py:583
  14.4 18.6 %all-to-all-start = ((bf16[4,72,192]{2,1,0:T(8,128)(2,1)}), bf16[4,72,192]{2,1,0:T(8,128)(2,1)S(1)}, u32[]{:S(2)}, u32[]{:S(2)}) async-start(bf16[4,72,192]{2,1,0:T(8,128)(2,1)} %get-tuple-element.74), calls=%async_computation | async-start | bytes 294912 | tf_op jit(solution)/shard_map/all_to_all | solution.py:679
  17.7 15.5 %collective-permute-start.3 = (bf16[56,768]{1,0:T(8,128)(2,1)}, bf16[56,768]{1,0:T(8,128)(2,1)S(1)}, u32[]{:S(2)}, u32[]{:S(2)}) collective-permute-start(bf16[56,768]{1,0:T(8,128)(2,1)} %get-tuple-element.75), channel_id=1, source_target_pairs={{0,0},{1,8},{2,16},{3,24},{4,4},{5,12},{6,20},{7,28},{8,1},{9,9},{... | collective-permute-start | bytes 258056 | tf_op jit(solution)/shard_map/ppermute | solution.py:620
  33.2 10.6 %collective-permute-start.6 = (bf16[128,768]{1,0:T(8,128)(2,1)S(1)}, bf16[128,768]{1,0:T(8,128)(2,1)S(1)}, u32[]{:S(2)}, u32[]{:S(2)}) collective-permute-start(bf16[128,768]{1,0:T(8,128)(2,1)S(1)} %constant_dynamic-update-slice_fusion), channel_id=1, source_target_pairs={{0,24},{1,25},{2,26},{3,27},{4,28},{5,29},{6,30},{7,31},{8,16},{9,... | collective-permute-start | bytes 589832 | tf_op jit(solution)/shard_map/ppermute | solution.py:593
  38.7 21.7 %collective-permute-start.5 = (bf16[128,768]{1,0:T(8,128)(2,1)S(1)}, bf16[128,768]{1,0:T(8,128)(2,1)S(1)}, u32[]{:S(2)}, u32[]{:S(2)}) collective-permute-start(bf16[128,768]{1,0:T(8,128)(2,1)S(1)} %constant_dynamic-update-slice_fusion), channel_id=1, source_target_pairs={{0,16},{1,17},{2,18},{3,19},{4,20},{5,21},{6,22},{7,23},{8,24},{9,... | collective-permute-start | bytes 589832 | tf_op jit(solution)/shard_map/ppermute | solution.py:593
  38.7 21.7 %collective-permute-start.4 = (bf16[128,768]{1,0:T(8,128)(2,1)S(1)}, bf16[128,768]{1,0:T(8,128)(2,1)S(1)}, u32[]{:S(2)}, u32[]{:S(2)}) collective-permute-start(bf16[128,768]{1,0:T(8,128)(2,1)S(1)} %constant_dynamic-update-slice_fusion), channel_id=1, source_target_pairs={{0,8},{1,9},{2,10},{3,11},{4,12},{5,13},{6,14},{7,15},{8,0},{9,1},... | collective-permute-start | bytes 589832 | tf_op jit(solution)/shard_map/ppermute | solution.py:593
  60.5 20.4 %collective-permute-start.7 = (bf16[4,128,768]{2,1,0:T(8,128)(2,1)S(1)}, bf16[4,128,768]{2,1,0:T(8,128)(2,1)S(1)}, u32[]{:S(2)}, u32[]{:S(2)}) collective-permute-start(bf16[4,128,768]{2,1,0:T(8,128)(2,1)S(1)} %pad_maximum_fusion.3.mine_ref), channel_id=1, source_target_pairs={{0,4},{1,5},{2,6},{3,7},{4,0},{5,1},{6,2},{7,3},{8,12},{9,13},{10,... | collective-permute-start | bytes 2359304 | tf_op jit(solution)/shard_map/ppermute | solution.py:593
  61.7 23.0 %collective-permute-start.2 = (bf16[3,128,768]{2,1,0:T(8,128)(2,1)S(1)}, bf16[3,128,768]{2,1,0:T(8,128)(2,1)S(1)}, u32[]{:S(2)}, u32[]{:S(2)}) collective-permute-start(bf16[3,128,768]{2,1,0:T(8,128)(2,1)S(1)} %collective-permute-done.1.refs_2_), channel_id=1, source_target_pairs={{0,1},{1,0},{2,3},{3,2},{4,5},{5,4},{6,7},{7,6},{8,9},{9,8},{10,11... | collective-permute-start | bytes 1769480 | tf_op jit(solution)/shard_map/ppermute | solution.py:583
  109.0 22.1 %all-to-all-start.1 = ((bf16[4,3,64,384]{3,2,1,0:T(8,128)(2,1)}), bf16[4,3,64,384]{3,2,1,0:T(8,128)(2,1)S(1)}, u32[]{:S(2)}, u32[]{:S(2)}) async-start(bf16[4,3,64,384]{3,2,1,0:T(8,128)(2,1)} %get-tuple-element.80.refs_9_), calls=%async_computation.1 | async-start | bytes 1179648 | tf_op jit(solution)/shard_map/all_to_all | solution.py:714
  159.1 14.0 %collective-permute-start.9 = (bf16[5,2,2,4,24,768]{5,4,3,2,1,0:T(8,128)(2,1)}, bf16[5,2,2,4,24,768]{5,4,3,2,1,0:T(8,128)(2,1)S(1)}, u32[]{:S(2)}, u32[]{:S(2)}) collective-permute-start(bf16[5,2,2,4,24,768]{5,4,3,2,1,0:T(8,128)(2,1)} %get-tuple-element.92), channel_id=1, source_target_pairs={{0,1},{1,0},{2,3},{3,2},{4,5},{5,4},{6,7},{7,6},{8,9},{9,8},{10,11... | collective-permute-start | bytes 8847368 | tf_op jit(solution)/shard_map/ppermute | solution.py:593
  159.4 9.1 %collective-permute-start.8 = (bf16[4,2,2,96,768]{4,3,2,1,0:T(8,128)(2,1)}, bf16[4,2,2,96,768]{4,3,2,1,0:T(8,128)(2,1)}, u32[]{:S(2)}, u32[]{:S(2)}) collective-permute-start(bf16[4,2,2,96,768]{4,3,2,1,0:T(8,128)(2,1)} %get-tuple-element.90), channel_id=1, source_target_pairs={{0,1},{1,0},{2,3},{3,2},{4,5},{5,4},{6,7},{7,6},{8,9},{9,8},{10,11... | collective-permute-start | bytes 7077896 | tf_op jit(solution)/shard_map/ppermute | solution.py:593
  160.3 14.9 %all-to-all-start.2 = ((bf16[4,3,64,384]{3,2,1,0:T(8,128)(2,1)}), bf16[4,3,64,384]{3,2,1,0:T(8,128)(2,1)S(1)}, u32[]{:S(2)}, u32[]{:S(2)}) async-start(bf16[4,3,64,384]{3,2,1,0:T(8,128)(2,1)} %get-tuple-element.88), calls=%async_computation.2 | async-start | bytes 1179648 | tf_op jit(solution)/shard_map/all_to_all | solution.py:727
  176.0 62.6 %all-to-all-start.3 = ((bf16[4,2,2,96,768]{4,3,2,1,0:T(8,128)(2,1)}), bf16[4,2,2,96,768]{4,3,2,1,0:T(8,128)(2,1)S(1)}, u32[]{:S(2)}, u32[]{:S(2)}) async-start(bf16[4,2,2,96,768]{4,3,2,1,0:T(8,128)(2,1)} %add_convert_fusion), calls=%async_computation.3 | async-start | bytes 4718592 | tf_op jit(solution)/shard_map/all_to_all | solution.py:606
  179.9 33.9 %collective-permute-start.10 = (bf16[5,2,4,24,768]{4,3,2,0,1:T(8,128)(2,1)}, bf16[5,2,4,24,768]{4,3,2,0,1:T(8,128)(2,1)S(1)}, u32[]{:S(2)}, u32[]{:S(2)}) collective-permute-start(bf16[5,2,4,24,768]{4,3,2,0,1:T(8,128)(2,1)} %fusion.2), channel_id=1, source_target_pairs={{0,4},{1,5},{2,6},{3,7},{4,0},{5,1},{6,2},{7,3},{8,12},{9,13},{10,... | collective-permute-start | bytes 4423688 | tf_op jit(solution)/shard_map/ppermute | solution.py:593
  181.1 34.9 %copy-start.3 = (bf16[5,2,2,4,24,768]{5,4,3,2,1,0:T(8,128)(2,1)S(1)}, bf16[5,2,2,4,24,768]{5,4,3,2,1,0:T(8,128)(2,1)}, u32[]{:S(2)}) copy-start(bf16[5,2,2,4,24,768]{5,4,3,2,1,0:T(8,128)(2,1)} %get-tuple-element.91) | copy-start | bytes 8847364
  213.8 24.9 %copy-start.5 = (bf16[2,3,128,768]{3,2,1,0:T(8,128)(2,1)S(1)}, bf16[2,3,128,768]{3,2,1,0:T(8,128)(2,1)}, u32[]{:S(2)}) copy-start(bf16[2,3,128,768]{3,2,1,0:T(8,128)(2,1)} %get-tuple-element.112) | copy-start | bytes 3538948
  213.8 24.8 %collective-permute-start.12 = (bf16[2,3,128,768]{3,2,1,0:T(8,128)(2,1)}, bf16[2,3,128,768]{3,2,1,0:T(8,128)(2,1)}, u32[]{:S(2)}, u32[]{:S(2)}) collective-permute-start(bf16[2,3,128,768]{3,2,1,0:T(8,128)(2,1)} %get-tuple-element.102), channel_id=1, source_target_pairs={{0,1},{1,0},{2,3},{3,2},{4,5},{5,4},{6,7},{7,6},{8,9},{9,8},{10,11... | collective-permute-start | bytes 3538952 | tf_op jit(solution)/shard_map/ppermute | solution.py:593
  214.9 22.0 %collective-permute-start.11 = (bf16[4,136,768]{2,1,0:T(8,128)(2,1)}, bf16[4,136,768]{2,1,0:T(8,128)(2,1)S(1)}, u32[]{:S(2)}, u32[]{:S(2)}) collective-permute-start(bf16[4,136,768]{2,1,0:T(8,128)(2,1)} %get-tuple-element.100), channel_id=1, source_target_pairs={{0,4},{1,5},{2,6},{3,7},{4,0},{5,1},{6,2},{7,3},{8,12},{9,13},{10,... | collective-permute-start | bytes 2506760 | tf_op jit(solution)/shard_map/ppermute | solution.py:593
  219.0 17.8 %collective-permute-start.13 = (bf16[5,4,24,768]{3,2,1,0:T(8,128)(2,1)S(1)}, bf16[5,4,24,768]{3,2,1,0:T(8,128)(2,1)S(1)}, u32[]{:S(2)}, u32[]{:S(2)}) collective-permute-start(bf16[5,4,24,768]{3,2,1,0:T(8,128)(2,1)S(1)} %get-tuple-element.132), channel_id=1, source_target_pairs={{0,2},{1,3},{2,0},{3,1},{4,6},{5,7},{6,4},{7,5},{8,10},{9,11},{10,... | collective-permute-start | bytes 2211848 | tf_op jit(solution)/shard_map/ppermute | solution.py:593
  240.0 38.4 %collective-permute-start.14 = (bf16[3,128,768]{2,1,0:T(8,128)(2,1)S(1)}, bf16[3,128,768]{2,1,0:T(8,128)(2,1)S(1)}, u32[]{:S(2)}, u32[]{:S(2)}) collective-permute-start(bf16[3,128,768]{2,1,0:T(8,128)(2,1)S(1)} %fusion.6), channel_id=1, source_target_pairs={{0,2},{1,3},{2,0},{3,1},{4,6},{5,7},{6,4},{7,5},{8,10},{9,11},{10,... | collective-permute-start | bytes 1769480 | tf_op jit(solution)/shard_map/ppermute | solution.py:593
  242.2 11.3 %collective-permute-start.18 = (bf16[256,768]{1,0:T(8,128)(2,1)S(1)}, bf16[256,768]{1,0:T(8,128)(2,1)S(1)}, u32[]{:S(2)}, u32[]{:S(2)}) collective-permute-start(bf16[256,768]{1,0:T(8,128)(2,1)S(1)} %get-tuple-element.138), channel_id=1, source_target_pairs={{0,24},{1,25},{2,26},{3,27},{4,28},{5,29},{6,30},{7,31},{8,16},{9,... | collective-permute-start | bytes 1179656 | tf_op jit(solution)/shard_map/ppermute | solution.py:593
  245.2 19.2 %collective-permute-start.16 = (bf16[256,768]{1,0:T(8,128)(2,1)S(1)}, bf16[256,768]{1,0:T(8,128)(2,1)S(1)}, u32[]{:S(2)}, u32[]{:S(2)}) collective-permute-start(bf16[256,768]{1,0:T(8,128)(2,1)S(1)} %get-tuple-element.139), channel_id=1, source_target_pairs={{0,8},{1,9},{2,10},{3,11},{4,12},{5,13},{6,14},{7,15},{8,0},{9,1},... | collective-permute-start | bytes 1179656 | tf_op jit(solution)/shard_map/ppermute | solution.py:593
  245.2 33.2 %collective-permute-start.17 = (bf16[256,768]{1,0:T(8,128)(2,1)S(1)}, bf16[256,768]{1,0:T(8,128)(2,1)S(1)}, u32[]{:S(2)}, u32[]{:S(2)}) collective-permute-start(bf16[256,768]{1,0:T(8,128)(2,1)S(1)} %get-tuple-element.140), channel_id=1, source_target_pairs={{0,16},{1,17},{2,18},{3,19},{4,20},{5,21},{6,22},{7,23},{8,24},{9,... | collective-permute-start | bytes 1179656 | tf_op jit(solution)/shard_map/ppermute | solution.py:593
  246.1 6.4 %collective-permute-start.15 = (bf16[2,96,768]{2,1,0:T(8,128)(2,1)S(1)}, bf16[2,96,768]{2,1,0:T(8,128)(2,1)S(1)}, u32[]{:S(2)}, u32[]{:S(2)}) collective-permute-start(bf16[2,96,768]{2,1,0:T(8,128)(2,1)S(1)} %get-tuple-element.136), channel_id=1, source_target_pairs={{0,4},{1,5},{2,6},{3,7},{4,0},{5,1},{6,2},{7,3},{8,12},{9,13},{10,... | collective-permute-start | bytes 884744 | tf_op jit(solution)/shard_map/ppermute | solution.py:593
  279.6 9.5 %copy-start.6 = (bf16[2,3,128,768]{3,2,1,0:T(8,128)(2,1)S(1)}, bf16[2,3,128,768]{3,2,1,0:T(8,128)(2,1)}, u32[]{:S(2)}) copy-start(bf16[2,3,128,768]{3,2,1,0:T(8,128)(2,1)} %get-tuple-element.112) | copy-start | bytes 3538948
  279.7 11.7 %collective-permute-start.19 = (bf16[136,192]{1,0:T(8,128)(2,1)S(1)}, bf16[136,192]{1,0:T(8,128)(2,1)S(1)}, u32[]{:S(2)}, u32[]{:S(2)}) collective-permute-start(bf16[136,192]{1,0:T(8,128)(2,1)S(1)} %get-tuple-element.147), channel_id=1, source_target_pairs={{0,1},{1,0},{2,3},{3,2},{4,5},{5,4},{6,7},{7,6},{8,9},{9,8},{10,11... | collective-permute-start | bytes 156680 | tf_op jit(solution)/shard_map/ppermute | solution.py:583
  281.3 10.1 %collective-permute-start.20 = (bf16[136,192]{1,0:T(8,128)(2,1)S(1)}, bf16[136,192]{1,0:T(8,128)(2,1)S(1)}, u32[]{:S(2)}, u32[]{:S(2)}) collective-permute-start(bf16[136,192]{1,0:T(8,128)(2,1)S(1)} %get-tuple-element.148), channel_id=1, source_target_pairs={{0,2},{1,3},{2,0},{3,1},{4,6},{5,7},{6,4},{7,5},{8,10},{9,11},{10,... | collective-permute-start | bytes 156680 | tf_op jit(solution)/shard_map/ppermute | solution.py:583
  282.4 9.1 %collective-permute-start.21 = (bf16[136,192]{1,0:T(8,128)(2,1)S(1)}, bf16[136,192]{1,0:T(8,128)(2,1)S(1)}, u32[]{:S(2)}, u32[]{:S(2)}) collective-permute-start(bf16[136,192]{1,0:T(8,128)(2,1)S(1)} %get-tuple-element.149), channel_id=1, source_target_pairs={{0,3},{1,2},{2,1},{3,0},{4,7},{5,6},{6,5},{7,4},{8,11},{9,10},{10,... | collective-permute-start | bytes 156680 | tf_op jit(solution)/shard_map/ppermute | solution.py:583
  283.0 9.2 %collective-permute-start.22 = (bf16[64,768]{1,0:T(8,128)(2,1)S(1)}, bf16[64,768]{1,0:T(8,128)(2,1)S(1)}, u32[]{:S(2)}, u32[]{:S(2)}) collective-permute-start(bf16[64,768]{1,0:T(8,128)(2,1)S(1)} %slice.301), channel_id=1, source_target_pairs={{0,0},{1,8},{2,16},{3,24},{4,4},{5,12},{6,20},{7,28},{8,1},{9,9},{... | collective-permute-start | bytes 294920 | tf_op jit(solution)/shard_map/ppermute | solution.py:620
  285.0 12.4 %collective-permute-start.23 = (bf16[96,768]{1,0:T(8,128)(2,1)S(1)}, bf16[96,768]{1,0:T(8,128)(2,1)S(1)}, u32[]{:S(2)}, u32[]{:S(2)}) collective-permute-start(bf16[96,768]{1,0:T(8,128)(2,1)S(1)} %fusion.20), channel_id=1, source_target_pairs={{0,2},{1,3},{2,0},{3,1},{4,6},{5,7},{6,4},{7,5},{8,10},{9,11},{10,... | collective-permute-start | bytes 442376 | tf_op jit(solution)/shard_map/ppermute | solution.py:593
  (16 other events, 33.4 us)
Sparse Core Ops, SparseCore 0:
  11.5 111.1 all-gather.3

commit v4 on v3

--- a/solution.py
+++ b/solution.py
@@ -135,7 +135,7 @@
         finish_kernel,
         out_shape=[jax.ShapeDtypeStruct((own, D), WIDE)] * 5 + [jax.ShapeDtypeStruct((24, 128), WIDE)],
         in_specs=[pl.BlockSpec(memory_space=pltpu.SMEM)] + [pl.BlockSpec(memory_space=pltpu.VMEM)] * 2,
-        compiler_params=pltpu.CompilerParams(vmem_limit_bytes=VMEM_BYTES),
+        compiler_params=pltpu.CompilerParams(vmem_limit_bytes=20 * 1024 * 1024),
         name="finish",
     )(at, cols, mixed)
 
@@ -211,7 +211,6 @@
     tok_refs = refs[:blocks]
     (w_ref, bias_ref, pq_ref, pk_ref, sin_ref, cos_ref, alive_ref,
      qkv_ref, soft_ref, share_ref, ctx_ref) = refs[blocks:]
-    me = me_ref[0]
     rows = tok_refs[0].shape[1]
     width = heads * HD
     tok = jnp.concatenate([ref[0] for ref in tok_refs], axis=0)
@@ -241,7 +240,7 @@
         pieces.append((dot(lifted, v) * share).astype(LOW))
     ctx = jnp.concatenate(pieces, axis=1)
     for j in range(blocks):
-        ctx_ref[me ^ j, 0] = fold(ctx[j * rows:(j + 1) * rows])
+        ctx_ref[j, 0] = fold(ctx[j * rows:(j + 1) * rows])
 
 
 def attend_call(me, toks, w_qkv, bias, place_q, place_k, sines, cosines, alive):
@@ -299,15 +298,14 @@
     tok_refs = refs[:blocks]
     (w_ref, small_ref, qkv_ref, soft_ref, share_ref, ctx_ref, dctx_ref, pq_ref, pk_ref, sin_ref, cos_ref,
      kept_ref, sent_ref, *out_refs, dw_sum, dpq_sum, dpk_sum, db_sum) = refs[blocks:]
-    me = me_ref[0]
     step, last = pl.program_id(0), pl.num_programs(0) - 1
     rows = tok_refs[0].shape[1]
     width = heads * HD
     sines, cosines = sin_ref[0], cos_ref[0]
     key_feats, query_feats = feature_pair(sines, cosines)
     qkv = qkv_ref[0]
-    dctx = jnp.concatenate([unfold(dctx_ref[me ^ j, 0]) for j in range(blocks)], axis=0)
-    ctx = jnp.concatenate([unfold(ctx_ref[me ^ j, 0]) for j in range(blocks)], axis=0)
+    dctx = jnp.concatenate([unfold(dctx_ref[me_ref[0] ^ j, 0]) for j in range(blocks)], axis=0)
+    ctx = jnp.concatenate([unfold(ctx_ref[j, 0]) for j in range(blocks)], axis=0)
     along = dctx.astype(WIDE) * ctx.astype(WIDE)
 
     @pl.when(step == 0)
@@ -418,6 +416,7 @@
      outer_grad, first_grad) = refs[4 + n_grads:]
     step = pl.program_id(0)
     core, x_at, y_at, z_at = at_ref[0], at_ref[1] >> 1, at_ref[1] & 1, at_ref[2]
+    here = lax.rem(at_ref[3], ctx_ref.shape[0])
     blocks, pages, rows, width = ctx_ref.shape
     rows, width = 2 * rows, width // 2
     count = tok_ref.shape[0]
@@ -429,7 +428,7 @@
     def _():
         small_ref[...] = jnp.zeros_like(small_ref)
         ctx = jnp.concatenate(
-            [jnp.concatenate([unfold(ctx_ref[b, p]) for b in range(blocks)], axis=1)
+            [jnp.concatenate([unfold(ctx_ref[here ^ b, p]) for b in range(blocks)], axis=1)
              for p in range(pages)], axis=0)
         ctx_all[...] = ctx
         pre = tok_ref[...].astype(WIDE) + (dot(ctx, wo_ref[...]) + b_out)
@@ -442,7 +441,7 @@
 
     @pl.when(step < cuts)
     def _():
-        inner = dot(first_low[...], wi_ref[...]) + vec_ref[pl.ds(6 + step, 1)]
+        inner = dot(first_low[...], wi_ref[0]) + vec_ref[pl.ds(6 + step, 1)]
         half = 0.5 + 0.5 * lax.erf(inner * (0.5 ** 0.5))
         slope[step] = half + inner * (jnp.exp(inner * inner * -0.5) * ((0.5 / math.pi) ** 0.5))
         activated = (inner * half).astype(LOW)
@@ -500,7 +499,7 @@
         else:
             grad_refs[0][...] = d_outer
             grad_refs[1][0] = d_inner.astype(LOW)
-        product = dot_nt(inner_grad, wi_ref[...])
+        product = dot_nt(inner_grad, wi_ref[0])
 
         @pl.when(step == cuts)
         def _():
@@ -534,7 +533,7 @@
 def second_half_call(split, at, ctx, tok, cot, w_output, vectors, w_inner, w_outer):
     blocks, pages, rows, width = ctx.shape
     count = 2 * pages * rows
-    cuts = w_inner.shape[1] // D
+    cuts = w_inner.shape[0]
     now = lambda i: jnp.where(i < cuts, i, jnp.maximum(2 * cuts - 1 - i, 0))
     late = lambda i: jnp.where(i < cuts, cuts - 1, jnp.maximum(2 * cuts - 1 - i, 0))
     last = lambda i: jnp.where(i < 2 * cuts, late(i), cuts)
@@ -542,7 +541,7 @@
     eighth = (1, 2, 2, D // 8, D)
     slots = (1, 2, 2, 4, D // 32, D)
     if split:
-        grad_specs = [pl.BlockSpec(eighth, lambda i, at: (late(i), 0, 0, 0, 0))] * 2
+        grad_specs = [pl.BlockSpec(eighth, lambda i, at: (late(i) ^ at[2], 0, 0, 0, 0))] * 2
         grad_specs += [pl.BlockSpec(slots, lambda i, at: (last(i), 0, 0, 0, 0, 0))] * 2
         grads = [(cuts, 2, 2, D // 8, D)] * 2 + [(cuts + 1,) + slots[1:]] * 2
     else:
@@ -557,7 +556,7 @@
             grid=(2 * cuts + 1,),
             in_specs=[
                 whole(ctx.shape), whole(tall), whole(tall), whole(square), whole(vectors.shape),
-                pl.BlockSpec(square, lambda i, at: (0, now(i))),
+                pl.BlockSpec((1,) + square, lambda i, at: (now(i), 0, 0)),
                 pl.BlockSpec((8, D // 8, D), lambda i, at: (now(i), 0, 0))],
             out_specs=[whole(tall), whole(tall), whole(ctx.shape), *grad_specs, whole(vectors.shape)],
             scratch_shapes=[
@@ -573,7 +572,7 @@
             *(jax.ShapeDtypeStruct(shape, LOW) for shape in grads),
             jax.ShapeDtypeStruct(vectors.shape, WIDE),
         ],
-        compiler_params=pltpu.CompilerParams(vmem_limit_bytes=VMEM_BYTES),
+        compiler_params=pltpu.CompilerParams(vmem_limit_bytes=44 * 1024 * 1024),
         cost_estimate=cost(20e9, 30e6),
         name="second_half",
     )(at, ctx, tok, cot, w_output, vectors, w_inner, w_outer)
@@ -581,6 +580,10 @@
 
 def swap(value, axis, size, bit):
     return lax.ppermute(value, axis, [(i, i ^ bit) for i in range(size)])
+
+
+def exchange_slots(value):
+    return jnp.stack([value[0]] + [swap(value[j], "pb", 4, j) for j in (1, 2, 3)])
 
 
 def gather_slots(value):
@@ -599,11 +602,6 @@
 
 def sum_along_z(value, devices):
     return added(value[0], *(hop(value[j], devices, j << 3) for j in (1, 2, 3)))
-
-
-def exchange_along_z(value, devices):
-    lines = [[i + 8 * z for z in range(4)] for i in range(8)]
-    return lax.all_to_all(value, AXES, 0, 0, tiled=True, axis_index_groups=lines)
 
 
 def tie(*values):
@@ -711,11 +709,11 @@
 
     qkv, soft, share, ctx_heads = attend_call(
         me_array, toks, w_qkv, bias_qkv, place_q, place_k, sines, cosines, alive)
-    ctx = lax.all_to_all(ctx_heads, "pb", 0, 0, tiled=True)
+    ctx = exchange_slots(ctx_heads)
 
     spot = ff_own
-    w_inner = jnp.concatenate(
-        [late[:, spot + j * own:spot + (j + 1) * own].reshape(D, D) for j in range(cuts)], axis=1)
+    w_inner = late[:, spot:spot + cuts * own].reshape(devices, cuts, own, D)
+    w_inner = w_inner.swapaxes(0, 1).reshape(cuts, D, D)
     spot += cuts * own
     vectors = jnp.sum(late[:, spot:spot + small_rows].astype(WIDE), axis=0)
     w_output = late[:, spot + small_rows:].reshape(D, D)
@@ -731,8 +729,9 @@
         outer_core, inner_core = hop(outer_sent, devices, 1), hop(inner_sent, devices, 1)
         outer_sum = added(outer_kept, outer_core).astype(LOW)
         inner_far = added(inner_kept[:, 1], inner_core[:, 1]).astype(LOW)
-        dctx, outer_sum, inner_far = tie(dctx, outer_sum, inner_far)
-        outer_got, inner_far = exchange_along_z(outer_sum, devices), hop(inner_far, devices, 4)
+        outer_got = [outer_sum[0]] + [hop(outer_sum[j], devices, j << 3) for j in (1, 2, 3)]
+        dctx, outer_got[0], far = tie(dctx, outer_got[0], inner_far)
+        inner_far = hop(inner_far, devices, 4)
 
     joined = (own, pb_size, page_size) if by_link else None
     me_array = jnp.stack([me, at[1] >> 1, at[2]]).astype(jnp.int32)
@@ -745,15 +744,15 @@
         inner_sent = added(inner_kept[:, 0, 1], inner_core[:, 0, 1], inner_far[:, 1]).astype(LOW)
         inner_sent = hop(inner_sent, devices, 2)
         inner_sum = added(inner_kept[:, 0, 0], inner_core[:, 0, 0], inner_far[:, 0])
-        mixed, mixed_far, kept, sent, inner_sum, inner_sent, outer_got = tie(
-            mixed, mixed_far, kept, sent, inner_sum, inner_sent, outer_got)
+        mixed, mixed_far, kept, sent, inner_sum, inner_sent, *outer_got = tie(
+            mixed, mixed_far, kept, sent, inner_sum, inner_sent, *outer_got)
         mixed = added(mixed, mixed_far).astype(LOW)
         inner_sum = added(inner_sum, inner_sent).astype(LOW).swapaxes(0, 1).reshape(4, (cuts + 1) * own, D)
         mixed = jnp.concatenate([mixed, inner_sum], axis=1)
         mixed_z = [hop(mixed[j], devices, j << 3) for j in (1, 2, 3)]
-        outer_sent = hop(added(*(outer_got[z, 1] for z in range(4))).astype(LOW), devices, 4)
+        outer_sent = hop(added(*(got[1] for got in outer_got)).astype(LOW), devices, 4)
         far = hop(added(kept[1], sent[1]).astype(LOW), devices, 2)
-        outer_sum = added(*(outer_got[z, 0] for z in range(4)))
+        outer_sum = added(*(got[0] for got in outer_got))
         mixed, kept, sent, far, outer_sum, outer_sent, *mixed_z = tie(
             mixed, kept, sent, far, outer_sum, outer_sent, *mixed_z)
         rest = 5 * own + 16

time: 306 us -> 298 us (0.974)
  other arithmetic: 36.2 us -> 29.9 us
    all_gather x1, waiting for transfers between devices: 9.83 us -> 1.78 us  [on_device(): late = lax.all_gather(packed, AXES, axis=0)]
    all_to_all x2 -> x0, starting transfers between devices: 7.72 us -> none  [the longest x1 3.87 us: on_device(): ctx = lax.all_to_all(ctx_heads, 'pb', 0, 0, tiled=True)]
    ppermute x6 -> x9, waiting for transfers between devices: 0.02 us -> 7.4 us  [swap(): return lax.ppermute(value, axis, [(i, i ^ bit) for i in range(size)])]
    ppermute x6 -> x9, starting transfers between devices: 7.01 us -> 10.2 us  [swap(): return lax.ppermute(value, axis, [(i, i ^ bit) for i in range(size)])]
    ppermute x16 -> x19, starting transfers between devices: 19.9 us -> 23 us  [hop(): return lax.ppermute(value, AXES, [(i, i ^ bits) for i in range(devices)])]
    unnamed x46 -> x48, local copies, waits for them, and re-layouts: 6.46 us -> 4.51 us
    ppermute x16 -> x19, waiting for transfers between devices: 81.8 us -> 83.2 us  [hop(): return lax.ppermute(value, AXES, [(i, i ^ bits) for i in range(devices)])]
  transfers between devices with their start and end apart: 29 -> 33, of which waited for: 11 -> 10; matrix products, arithmetic and copies ran while one was open for 14% -> 11% of each run, Pallas kernels for 20% -> 20%
where the time goes in v4:
time: 298 us; the launch traced here: 297 us
  waiting for transfers between devices  92.5 us (31%)
  Pallas kernels  87.1 us (29%)
  starting transfers between devices  45.9 us (15%)
  other arithmetic  29.9 us (10%)
  local copies, waits for them, and re-layouts  18.6 us (6%)
  between operations  14.6 us (5%)
  blocking collectives  8.77 us (3%)
    ppermute x19, waiting for transfers between devices, hop(): return lax.ppermute(value, AXES, [(i, i ^ bits) for i in range(devices)])  83.2 us
    pallas_call x1, Pallas kernels, attend_back_call(): pl.pallas_call(functools.partial(attend_back_kernel, heads, blocks, joine...  32.7 us
    pallas_call x1, Pallas kernels, second_half_call(): pl.pallas_call(functools.partial(second_half_kernel, cuts, split), grid_s...  25.3 us
    ppermute x19, starting transfers between devices, hop(): return lax.ppermute(value, AXES, [(i, i ^ bits) for i in range(devices)])  23 us
    pallas_call x1, Pallas kernels, attend_call(): pl.pallas_call(functools.partial(attend_kernel, heads, blocks), grid_spec...  22.8 us
    ppermute x9, starting transfers between devices, swap(): return lax.ppermute(value, axis, [(i, i ^ bit) for i in range(size)])  10.2 us
    cos x1, other arithmetic, on_device(): sines, cosines = (jnp.sin(angles), jnp.cos(angles))  10.1 us
    all_gather x1, blocking collectives, on_device(): places = lax.all_gather(jnp.stack([grid_x, grid_y, padding]), 'pb', axis=0)  8.77 us
  transfers between devices with their start and end apart: 33, of which 10 were waited for; matrix products, arithmetic and copies ran while one was open for 11% of the time, Pallas kernels for 20%

profile of v4, /device:TPU:1, one launch (start us, length us, event | category | flops | bytes accessed | tf_op | source)
XLA Modules:
  0.0 297.3 jit_solution(4321859833869601856)
XLA Ops:
  9.3 2.0 pack.1
  11.3 2.1 collective-permute-start.1
  14.4 3.3 %all-to-all-start = ((bf16[4,72,192]{2,1,0:T(8,128)(2,1)}), bf16[4,72,192]{2,1,0:T(8,128)(2,1)S(1)}, u32[]{:S(2)}, u32[]{:S(2)}) async-start(bf16[4,72,192]{2,1,0:T(8,128)(2,1)} %get-tuple-element.76), calls=%async_computation | async-start | bytes 294912 | tf_op jit(solution)/shard_map/all_to_all | solution.py:677
  17.7 3.1 %collective-permute-start.3 = (bf16[56,768]{1,0:T(8,128)(2,1)}, bf16[56,768]{1,0:T(8,128)(2,1)S(1)}, u32[]{:S(2)}, u32[]{:S(2)}) collective-permute-start(bf16[56,768]{1,0:T(8,128)(2,1)} %get-tuple-element.77), channel_id=1, source_target_pairs={{0,0},{1,8},{2,16},{3,24},{4,4},{5,12},{6,20},{7,28},{8,1},{9,9},{... | collective-permute-start | bytes 258056 | tf_op jit(solution)/shard_map/ppermute | solution.py:618
  24.1 8.8 %all-gather = s32[12,3,128]{2,1,0:T(4,128)S(1)} all-gather(s32[3,3,128]{2,1,0:T(4,128)S(1)} %pad_add_fusion), channel_id=2, replica_groups=mesh['page'=8,'pb'=4] {'pb'}, dimensions={0}, use_global_device_ids=true | all-gather | bytes 23040 | tf_op jit(solution)/shard_map/all_gather | solution.py:685
  33.2 5.4 %collective-permute-start.6 = (bf16[128,768]{1,0:T(8,128)(2,1)S(1)}, bf16[128,768]{1,0:T(8,128)(2,1)S(1)}, u32[]{:S(2)}, u32[]{:S(2)}) collective-permute-start(bf16[128,768]{1,0:T(8,128)(2,1)S(1)} %constant_dynamic-update-slice_fusion), channel_id=1, source_target_pairs={{0,24},{1,25},{2,26},{3,27},{4,28},{5,29},{6,30},{7,31},{8,16},{9,... | collective-permute-start | bytes 589832 | tf_op jit(solution)/shard_map/ppermute | solution.py:596
  39.1 4.8 %collective-permute-done.6 = bf16[128,768]{1,0:T(8,128)(2,1)S(1)} collective-permute-done((bf16[128,768]{1,0:T(8,128)(2,1)S(1)}, bf16[128,768]{1,0:T(8,128)(2,1)S(1)}, u32[]{:S(2)}, u32[]{:S(2)}) %collective-permute-start.6) | collective-permute-done | bytes 196640 | tf_op jit(solution)/shard_map/ppermute | solution.py:596
  43.9 15.9 %collective-permute-done.5 = bf16[128,768]{1,0:T(8,128)(2,1)S(1)} collective-permute-done((bf16[128,768]{1,0:T(8,128)(2,1)S(1)}, bf16[128,768]{1,0:T(8,128)(2,1)S(1)}, u32[]{:S(2)}, u32[]{:S(2)}) %collective-permute-start.5) | collective-permute-done | bytes 196640 | tf_op jit(solution)/shard_map/ppermute | solution.py:596
  62.9 10.1 %fusion = (f32[3,512,384]{2,1,0:T(8,128)}, f32[3,512,384]{2,1,0:T(8,128)}) fusion(f32[3,512,192]{2,1,0:T(8,128)S(1)} %get-tuple-element.177, f32[3,512,192]{2,1,0:T(8,128)S(1)} %get-tuple-element.176), kind=kLoop, calls=%fused_computation.12 | loop fusion | flops 589824 | bytes 7077888 | tf_op jit(solution)/shard_map/cos | solution.py:694
  73.0 7.9 %collective-permute-done.7.theirs_ref = bf16[4,128,768]{2,1,0:T(8,128)(2,1)S(1)} collective-permute-done((bf16[4,128,768]{2,1,0:T(8,128)(2,1)S(1)}, bf16[4,128,768]{2,1,0:T(8,128)(2,1)S(1)}, u32[]{:S(2)}, u32[]{:S(2)}) %collective-permute-start.7) | collective-permute-done | bytes 786464 | tf_op jit(solution)/shard_map/ppermute | solution.py:596
  81.8 2.9 assemble.1
  85.8 22.8 %attend.1 = (bf16[3,512,576]{2,1,0:T(8,128)(2,1)}, bf16[3,3,512,512]{3,2,1,0:T(8,128)(2,1)}, f32[3,512,3]{2,1,0:T(8,128)}, bf16[4,3,64,384]{3,2,1,0:T(8,128)(2,1)}) custom-call(s32[1]{0:T(128)} %bitcast.5.me_ref, bf16[3,128,768]{2,1,0:T(8,128)(2,1)} %refs_0_.3, bf16[3,128,768]{2,1,0:T(8,128)(2,1)} %copy-done.18, bf16[3,128,768]{2,1,0:T(8,128)(2,1)} %copy-done.17, ...), custom_call_target="tpu_custom_call" | custom-call | flops 20000000000 | bytes 20000000 | tf_op jit(solution)/shard_map/attend/pallas_call | solution.py:253
  109.8 1.8 collective-permute-start.10
  112.0 4.3 %collective-permute-done.10 = bf16[3,64,384]{2,1,0:T(8,128)(2,1)S(1)} collective-permute-done((bf16[3,64,384]{2,1,0:T(8,128)(2,1)S(1)}, bf16[3,64,384]{2,1,0:T(8,128)(2,1)S(1)}, u32[]{:S(2)}, u32[]{:S(2)}) %collective-permute-start.10) | collective-permute-done | bytes 147488 | tf_op jit(solution)/shard_map/ppermute | solution.py:582
  116.4 3.0 %collective-permute-done.9 = bf16[3,64,384]{2,1,0:T(8,128)(2,1)S(1)} collective-permute-done((bf16[3,64,384]{2,1,0:T(8,128)(2,1)S(1)}, bf16[3,64,384]{2,1,0:T(8,128)(2,1)S(1)}, u32[]{:S(2)}, u32[]{:S(2)}) %collective-permute-start.9) | collective-permute-done | bytes 147488 | tf_op jit(solution)/shard_map/ppermute | solution.py:582
  120.3 1.8 all-gather.4.cloned.1.call-done
  124.7 2.6 slice.304
  127.4 2.4 copy.85
  129.9 25.3 %second_half.1 = (bf16[384,768]{1,0:T(8,128)(2,1)}, f32[384,768]{1,0:T(8,128)S(1)}, bf16[4,3,64,384]{3,2,1,0:T(8,128)(2,1)S(1)}, bf16[4,2,2,96,768]{4,3,2,1,0:T(...) custom-call(s32[5]{0:T(128)S(1)} %copy-done.2, ...), custom_call_target="tpu_custom_call" | custom-call | flops 20000000000 | bytes 30000000 | tf_op jit(solution)/shard_map/second_half/pallas_call | solution.py:552
  157.7 4.4 %all-to-all-start.1 = ((bf16[4,3,64,384]{3,2,1,0:T(8,128)(2,1)}), bf16[4,3,64,384]{3,2,1,0:T(8,128)(2,1)}, u32[]{:S(2)}, u32[]{:S(2)}) async-start(bf16[4,3,64,384]{3,2,1,0:T(8,128)(2,1)} %copy-done), calls=%async_computation.1 | async-start | bytes 1179648 | tf_op jit(solution)/shard_map/all_to_all | solution.py:725
  162.1 2.4 add_convert_fusion
  167.2 2.9 fusion.2
  171.3 32.7 %attend_back.1 = (bf16[2,3,128,768]{3,2,1,0:T(8,128)(2,1)}, bf16[2,3,128,768]{3,2,1,0:T(8,128)(2,1)}, bf16[4,136,768]{2,1,0:T(8,128)(2,1)}, bf16[4,136,768]{2,1,0:T(8,128)(2,1)}) custom-call(s32[3]{0:T(128)} %pad_add_fusion.1.me_ref, bf16[3,128,768]{2,1,0:T(8,128)(2,1)} %refs_0_.3, bf16[3,128,768]{2,1,0:T(8,128)(2,1)} %copy-done.18, ...), custom_call_target="tpu_custom_call" | custom-call | flops 30000001024 | bytes 20000000 | tf_op jit(solution)/shard_map/attend_back/pallas_call | solution.py:370
  206.2 1.9 fusion.3
  211.7 26.3 %collective-permute-done.18 = bf16[2,2,96,768]{3,2,1,0:T(8,128)(2,1)S(1)} collective-permute-done((bf16[2,2,96,768]{3,2,1,0:T(8,128)(2,1)S(1)}, bf16[2,2,96,768]{3,2,1,0:T(8,128)(2,1)S(1)}, u32[]{:S(2)}, u32[]{:S(2)}) %collective-permute-start.18) | collective-permute-done | bytes 589856 | tf_op jit(solution)/shard_map/ppermute | solution.py:596
  240.0 2.1 collective-permute-start.24
  245.4 6.5 %collective-permute-done.21 = bf16[2,96,768]{2,1,0:T(8,128)(2,1)} collective-permute-done((bf16[2,96,768]{2,1,0:T(8,128)(2,1)S(1)}, bf16[2,96,768]{2,1,0:T(8,128)(2,1)}, u32[]{:S(2)}, u32[]{:S(2)}) %collective-permute-start.21) | collective-permute-done | bytes 294944 | tf_op jit(solution)/shard_map/ppermute | solution.py:596
  251.9 12.1 %collective-permute-done.22 = bf16[256,768]{1,0:T(8,128)(2,1)S(1)} collective-permute-done((bf16[256,768]{1,0:T(8,128)(2,1)S(1)}, bf16[256,768]{1,0:T(8,128)(2,1)S(1)}, u32[]{:S(2)}, u32[]{:S(2)}) %collective-permute-start.22) | collective-permute-done | bytes 393248 | tf_op jit(solution)/shard_map/ppermute | solution.py:596
  264.0 9.8 %collective-permute-done.23 = bf16[256,768]{1,0:T(8,128)(2,1)S(1)} collective-permute-done((bf16[256,768]{1,0:T(8,128)(2,1)S(1)}, bf16[256,768]{1,0:T(8,128)(2,1)S(1)}, u32[]{:S(2)}, u32[]{:S(2)}) %collective-permute-start.23) | collective-permute-done | bytes 393248 | tf_op jit(solution)/shard_map/ppermute | solution.py:596
  275.1 2.4 collective-permute-start.25
  279.3 1.9 collective-permute-start.28
  282.3 2.9 collective-permute-start.29
  (146 shorter events, 44.0 us)
Async XLA Ops:
  7.2 114.9 %all-gather.4.cloned.1.call-start = ((), (), s32[]{:S(2)}) async-start(), calls=%async_computation.2 | async-start | bytes 11759616 | tf_op jit(solution)/shard_map/all_gather | solution.py:681
  11.3 49.9 %collective-permute-start.1 = (bf16[3,128,768]{2,1,0:T(8,128)(2,1)}, bf16[3,128,768]{2,1,0:T(8,128)(2,1)S(1)}, u32[]{:S(2)}, u32[]{:S(2)}) collective-permute-start(bf16[3,128,768]{2,1,0:T(8,128)(2,1)} %refs_0_.3), channel_id=1, source_target_pairs={{0,2},{1,3},{2,0},{3,1},{4,6},{5,7},{6,4},{7,5},{8,10},{9,11},{10,... | collective-permute-start | bytes 1769480 | tf_op jit(solution)/shard_map/ppermute | solution.py:582
  13.4 71.3 %collective-permute-start = (bf16[3,128,768]{2,1,0:T(8,128)(2,1)}, bf16[3,128,768]{2,1,0:T(8,128)(2,1)S(1)}, u32[]{:S(2)}, u32[]{:S(2)}) collective-permute-start(bf16[3,128,768]{2,1,0:T(8,128)(2,1)} %refs_0_.3), channel_id=1, source_target_pairs={{0,1},{1,0},{2,3},{3,2},{4,5},{5,4},{6,7},{7,6},{8,9},{9,8},{10,11... | collective-permute-start | bytes 1769480 | tf_op jit(solution)/shard_map/ppermute | solution.py:582
  14.4 18.6 %all-to-all-start = ((bf16[4,72,192]{2,1,0:T(8,128)(2,1)}), bf16[4,72,192]{2,1,0:T(8,128)(2,1)S(1)}, u32[]{:S(2)}, u32[]{:S(2)}) async-start(bf16[4,72,192]{2,1,0:T(8,128)(2,1)} %get-tuple-element.76), calls=%async_computation | async-start | bytes 294912 | tf_op jit(solution)/shard_map/all_to_all | solution.py:677
  17.7 15.5 %collective-permute-start.3 = (bf16[56,768]{1,0:T(8,128)(2,1)}, bf16[56,768]{1,0:T(8,128)(2,1)S(1)}, u32[]{:S(2)}, u32[]{:S(2)}) collective-permute-start(bf16[56,768]{1,0:T(8,128)(2,1)} %get-tuple-element.77), channel_id=1, source_target_pairs={{0,0},{1,8},{2,16},{3,24},{4,4},{5,12},{6,20},{7,28},{8,1},{9,9},{... | collective-permute-start | bytes 258056 | tf_op jit(solution)/shard_map/ppermute | solution.py:618
  33.2 10.6 %collective-permute-start.6 = (bf16[128,768]{1,0:T(8,128)(2,1)S(1)}, bf16[128,768]{1,0:T(8,128)(2,1)S(1)}, u32[]{:S(2)}, u32[]{:S(2)}) collective-permute-start(bf16[128,768]{1,0:T(8,128)(2,1)S(1)} %constant_dynamic-update-slice_fusion), channel_id=1, source_target_pairs={{0,24},{1,25},{2,26},{3,27},{4,28},{5,29},{6,30},{7,31},{8,16},{9,... | collective-permute-start | bytes 589832 | tf_op jit(solution)/shard_map/ppermute | solution.py:596
  38.7 21.0 %collective-permute-start.5 = (bf16[128,768]{1,0:T(8,128)(2,1)S(1)}, bf16[128,768]{1,0:T(8,128)(2,1)S(1)}, u32[]{:S(2)}, u32[]{:S(2)}) collective-permute-start(bf16[128,768]{1,0:T(8,128)(2,1)S(1)} %constant_dynamic-update-slice_fusion), channel_id=1, source_target_pairs={{0,16},{1,17},{2,18},{3,19},{4,20},{5,21},{6,22},{7,23},{8,24},{9,... | collective-permute-start | bytes 589832 | tf_op jit(solution)/shard_map/ppermute | solution.py:596
  38.7 21.0 %collective-permute-start.4 = (bf16[128,768]{1,0:T(8,128)(2,1)S(1)}, bf16[128,768]{1,0:T(8,128)(2,1)S(1)}, u32[]{:S(2)}, u32[]{:S(2)}) collective-permute-start(bf16[128,768]{1,0:T(8,128)(2,1)S(1)} %constant_dynamic-update-slice_fusion), channel_id=1, source_target_pairs={{0,8},{1,9},{2,10},{3,11},{4,12},{5,13},{6,14},{7,15},{8,0},{9,1},... | collective-permute-start | bytes 589832 | tf_op jit(solution)/shard_map/ppermute | solution.py:596
  59.9 21.0 %collective-permute-start.7 = (bf16[4,128,768]{2,1,0:T(8,128)(2,1)S(1)}, bf16[4,128,768]{2,1,0:T(8,128)(2,1)S(1)}, u32[]{:S(2)}, u32[]{:S(2)}) collective-permute-start(bf16[4,128,768]{2,1,0:T(8,128)(2,1)S(1)} %pad_maximum_fusion.2.mine_ref), channel_id=1, source_target_pairs={{0,4},{1,5},{2,6},{3,7},{4,0},{5,1},{6,2},{7,3},{8,12},{9,13},{10,... | collective-permute-start | bytes 2359304 | tf_op jit(solution)/shard_map/ppermute | solution.py:596
  61.2 23.5 %collective-permute-start.2 = (bf16[3,128,768]{2,1,0:T(8,128)(2,1)S(1)}, bf16[3,128,768]{2,1,0:T(8,128)(2,1)S(1)}, u32[]{:S(2)}, u32[]{:S(2)}) collective-permute-start(bf16[3,128,768]{2,1,0:T(8,128)(2,1)S(1)} %collective-permute-done.1.refs_2_), channel_id=1, source_target_pairs={{0,1},{1,0},{2,3},{3,2},{4,5},{5,4},{6,7},{7,6},{8,9},{9,8},{10,11... | collective-permute-start | bytes 1769480 | tf_op jit(solution)/shard_map/ppermute | solution.py:582
  109.8 6.6 %collective-permute-start.10 = (bf16[3,64,384]{2,1,0:T(8,128)(2,1)S(1)}, bf16[3,64,384]{2,1,0:T(8,128)(2,1)S(1)}, u32[]{:S(2)}, u32[]{:S(2)}) collective-permute-start(bf16[3,64,384]{2,1,0:T(8,128)(2,1)S(1)} %get-tuple-element.145), channel_id=1, source_target_pairs={{0,3},{1,2},{2,1},{3,0},{4,7},{5,6},{6,5},{7,4},{8,11},{9,10},{10,... | collective-permute-start | bytes 442376 | tf_op jit(solution)/shard_map/ppermute | solution.py:582
  111.6 7.9 %collective-permute-start.9 = (bf16[3,64,384]{2,1,0:T(8,128)(2,1)S(1)}, bf16[3,64,384]{2,1,0:T(8,128)(2,1)S(1)}, u32[]{:S(2)}, u32[]{:S(2)}) collective-permute-start(bf16[3,64,384]{2,1,0:T(8,128)(2,1)S(1)} %get-tuple-element.146), channel_id=1, source_target_pairs={{0,2},{1,3},{2,0},{3,1},{4,6},{5,7},{6,4},{7,5},{8,10},{9,11},{10,... | collective-permute-start | bytes 442376 | tf_op jit(solution)/shard_map/ppermute | solution.py:582
  111.8 7.6 %collective-permute-start.8 = (bf16[3,64,384]{2,1,0:T(8,128)(2,1)S(1)}, bf16[3,64,384]{2,1,0:T(8,128)(2,1)S(1)}, u32[]{:S(2)}, u32[]{:S(2)}) collective-permute-start(bf16[3,64,384]{2,1,0:T(8,128)(2,1)S(1)} %get-tuple-element.147), channel_id=1, source_target_pairs={{0,1},{1,0},{2,3},{3,2},{4,5},{5,4},{6,7},{7,6},{8,9},{9,8},{10,11... | collective-permute-start | bytes 442376 | tf_op jit(solution)/shard_map/ppermute | solution.py:582
  156.9 10.3 %collective-permute-start.12 = (bf16[5,2,2,4,24,768]{5,4,3,2,1,0:T(8,128)(2,1)}, bf16[5,2,2,4,24,768]{5,4,3,2,1,0:T(8,128)(2,1)}, u32[]{:S(2)}, u32[]{:S(2)}) collective-permute-start(bf16[5,2,2,4,24,768]{5,4,3,2,1,0:T(8,128)(2,1)} %get-tuple-element.94), channel_id=1, source_target_pairs={{0,1},{1,0},{2,3},{3,2},{4,5},{5,4},{6,7},{7,6},{8,9},{9,8},{10,11... | collective-permute-start | bytes 8847368 | tf_op jit(solution)/shard_map/ppermute | solution.py:596
  157.7 13.6 %all-to-all-start.1 = ((bf16[4,3,64,384]{3,2,1,0:T(8,128)(2,1)}), bf16[4,3,64,384]{3,2,1,0:T(8,128)(2,1)}, u32[]{:S(2)}, u32[]{:S(2)}) async-start(bf16[4,3,64,384]{3,2,1,0:T(8,128)(2,1)} %copy-done), calls=%async_computation.1 | async-start | bytes 1179648 | tf_op jit(solution)/shard_map/all_to_all | solution.py:725
  165.9 44.8 %collective-permute-start.19 = (bf16[2,2,96,768]{3,2,1,0:T(8,128)(2,1)}, bf16[2,2,96,768]{3,2,1,0:T(8,128)(2,1)}, u32[]{:S(2)}, u32[]{:S(2)}) collective-permute-start(bf16[2,2,96,768]{3,2,1,0:T(8,128)(2,1)} %get-tuple-element.137), channel_id=1, source_target_pairs={{0,24},{1,25},{2,26},{3,27},{4,28},{5,29},{6,30},{7,31},{8,16},{9,... | collective-permute-start | bytes 1769480 | tf_op jit(solution)/shard_map/ppermute | solution.py:596
  170.2 33.9 %collective-permute-start.13 = (bf16[5,2,4,24,768]{4,3,2,0,1:T(8,128)(2,1)}, bf16[5,2,4,24,768]{4,3,2,0,1:T(8,128)(2,1)S(1)}, u32[]{:S(2)}, u32[]{:S(2)}) collective-permute-start(bf16[5,2,4,24,768]{4,3,2,0,1:T(8,128)(2,1)} %fusion.2), channel_id=1, source_target_pairs={{0,4},{1,5},{2,6},{3,7},{4,0},{5,1},{6,2},{7,3},{8,12},{9,13},{10,... | collective-permute-start | bytes 4423688 | tf_op jit(solution)/shard_map/ppermute | solution.py:596
  204.0 34.0 %collective-permute-start.15 = (bf16[2,3,128,768]{3,2,1,0:T(8,128)(2,1)}, bf16[2,3,128,768]{3,2,1,0:T(8,128)(2,1)S(1)}, u32[]{:S(2)}, u32[]{:S(2)}) collective-permute-start(bf16[2,3,128,768]{3,2,1,0:T(8,128)(2,1)} %get-tuple-element.103), channel_id=1, source_target_pairs={{0,1},{1,0},{2,3},{3,2},{4,5},{5,4},{6,7},{7,6},{8,9},{9,8},{10,11... | collective-permute-start | bytes 3538952 | tf_op jit(solution)/shard_map/ppermute | solution.py:596
  205.1 33.0 %collective-permute-start.14 = (bf16[4,136,768]{2,1,0:T(8,128)(2,1)}, bf16[4,136,768]{2,1,0:T(8,128)(2,1)S(1)}, u32[]{:S(2)}, u32[]{:S(2)}) collective-permute-start(bf16[4,136,768]{2,1,0:T(8,128)(2,1)} %get-tuple-element.101), channel_id=1, source_target_pairs={{0,4},{1,5},{2,6},{3,7},{4,0},{5,1},{6,2},{7,3},{8,12},{9,13},{10,... | collective-permute-start | bytes 2506760 | tf_op jit(solution)/shard_map/ppermute | solution.py:596
  208.1 29.9 %collective-permute-start.16 = (bf16[5,4,24,768]{3,2,1,0:T(8,128)(2,1)S(1)}, bf16[5,4,24,768]{3,2,1,0:T(8,128)(2,1)S(1)}, u32[]{:S(2)}, u32[]{:S(2)}) collective-permute-start(bf16[5,4,24,768]{3,2,1,0:T(8,128)(2,1)S(1)} %get-tuple-element.131), channel_id=1, source_target_pairs={{0,2},{1,3},{2,0},{3,1},{4,6},{5,7},{6,4},{7,5},{8,10},{9,11},{10,... | collective-permute-start | bytes 2211848 | tf_op jit(solution)/shard_map/ppermute | solution.py:596
  209.6 28.5 %collective-permute-start.18 = (bf16[2,2,96,768]{3,2,1,0:T(8,128)(2,1)S(1)}, bf16[2,2,96,768]{3,2,1,0:T(8,128)(2,1)S(1)}, u32[]{:S(2)}, u32[]{:S(2)}) collective-permute-start(bf16[2,2,96,768]{3,2,1,0:T(8,128)(2,1)S(1)} %copy-done.16), channel_id=1, source_target_pairs={{0,16},{1,17},{2,18},{3,19},{4,20},{5,21},{6,22},{7,23},{8,24},{9,... | collective-permute-start | bytes 1769480 | tf_op jit(solution)/shard_map/ppermute | solution.py:596
  210.7 27.3 %collective-permute-start.17 = (bf16[2,2,96,768]{3,2,1,0:T(8,128)(2,1)S(1)}, bf16[2,2,96,768]{3,2,1,0:T(8,128)(2,1)S(1)}, u32[]{:S(2)}, u32[]{:S(2)}) collective-permute-start(bf16[2,2,96,768]{3,2,1,0:T(8,128)(2,1)S(1)} %copy-done.15), channel_id=1, source_target_pairs={{0,8},{1,9},{2,10},{3,11},{4,12},{5,13},{6,14},{7,15},{8,0},{9,1},... | collective-permute-start | bytes 1769480 | tf_op jit(solution)/shard_map/ppermute | solution.py:596
  238.2 35.6 %collective-permute-start.20 = (bf16[3,128,768]{2,1,0:T(8,128)(2,1)S(1)}, bf16[3,128,768]{2,1,0:T(8,128)(2,1)S(1)}, u32[]{:S(2)}, u32[]{:S(2)}) collective-permute-start(bf16[3,128,768]{2,1,0:T(8,128)(2,1)S(1)} %fusion.6), channel_id=1, source_target_pairs={{0,2},{1,3},{2,0},{3,1},{4,6},{5,7},{6,4},{7,5},{8,10},{9,11},{10,... | collective-permute-start | bytes 1769480 | tf_op jit(solution)/shard_map/ppermute | solution.py:596
  240.0 12.0 %collective-permute-start.24 = (bf16[256,768]{1,0:T(8,128)(2,1)S(1)}, bf16[256,768]{1,0:T(8,128)(2,1)S(1)}, u32[]{:S(2)}, u32[]{:S(2)}) collective-permute-start(bf16[256,768]{1,0:T(8,128)(2,1)S(1)} %get-tuple-element.141), channel_id=1, source_target_pairs={{0,24},{1,25},{2,26},{3,27},{4,28},{5,29},{6,30},{7,31},{8,16},{9,... | collective-permute-start | bytes 1179656 | tf_op jit(solution)/shard_map/ppermute | solution.py:596
  242.1 21.9 %collective-permute-start.22 = (bf16[256,768]{1,0:T(8,128)(2,1)S(1)}, bf16[256,768]{1,0:T(8,128)(2,1)S(1)}, u32[]{:S(2)}, u32[]{:S(2)}) collective-permute-start(bf16[256,768]{1,0:T(8,128)(2,1)S(1)} %get-tuple-element.142), channel_id=1, source_target_pairs={{0,8},{1,9},{2,10},{3,11},{4,12},{5,13},{6,14},{7,15},{8,0},{9,1},... | collective-permute-start | bytes 1179656 | tf_op jit(solution)/shard_map/ppermute | solution.py:596
  242.1 31.7 %collective-permute-start.23 = (bf16[256,768]{1,0:T(8,128)(2,1)S(1)}, bf16[256,768]{1,0:T(8,128)(2,1)S(1)}, u32[]{:S(2)}, u32[]{:S(2)}) collective-permute-start(bf16[256,768]{1,0:T(8,128)(2,1)S(1)} %get-tuple-element.143), channel_id=1, source_target_pairs={{0,16},{1,17},{2,18},{3,19},{4,20},{5,21},{6,22},{7,23},{8,24},{9,... | collective-permute-start | bytes 1179656 | tf_op jit(solution)/shard_map/ppermute | solution.py:596
  244.9 7.0 %collective-permute-start.21 = (bf16[2,96,768]{2,1,0:T(8,128)(2,1)S(1)}, bf16[2,96,768]{2,1,0:T(8,128)(2,1)}, u32[]{:S(2)}, u32[]{:S(2)}) collective-permute-start(bf16[2,96,768]{2,1,0:T(8,128)(2,1)S(1)} %get-tuple-element.135), channel_id=1, source_target_pairs={{0,4},{1,5},{2,6},{3,7},{4,0},{5,1},{6,2},{7,3},{8,12},{9,13},{10,... | collective-permute-start | bytes 884744 | tf_op jit(solution)/shard_map/ppermute | solution.py:596
  275.1 12.0 %collective-permute-start.25 = (bf16[136,192]{1,0:T(8,128)(2,1)S(1)}, bf16[136,192]{1,0:T(8,128)(2,1)S(1)}, u32[]{:S(2)}, u32[]{:S(2)}) collective-permute-start(bf16[136,192]{1,0:T(8,128)(2,1)S(1)} %get-tuple-element.154), channel_id=1, source_target_pairs={{0,1},{1,0},{2,3},{3,2},{4,5},{5,4},{6,7},{7,6},{8,9},{9,8},{10,11... | collective-permute-start | bytes 156680 | tf_op jit(solution)/shard_map/ppermute | solution.py:582
  277.6 9.6 %collective-permute-start.26 = (bf16[136,192]{1,0:T(8,128)(2,1)S(1)}, bf16[136,192]{1,0:T(8,128)(2,1)S(1)}, u32[]{:S(2)}, u32[]{:S(2)}) collective-permute-start(bf16[136,192]{1,0:T(8,128)(2,1)S(1)} %get-tuple-element.155), channel_id=1, source_target_pairs={{0,2},{1,3},{2,0},{3,1},{4,6},{5,7},{6,4},{7,5},{8,10},{9,11},{10,... | collective-permute-start | bytes 156680 | tf_op jit(solution)/shard_map/ppermute | solution.py:582
  278.0 9.2 %collective-permute-start.27 = (bf16[136,192]{1,0:T(8,128)(2,1)S(1)}, bf16[136,192]{1,0:T(8,128)(2,1)S(1)}, u32[]{:S(2)}, u32[]{:S(2)}) collective-permute-start(bf16[136,192]{1,0:T(8,128)(2,1)S(1)} %get-tuple-element.156), channel_id=1, source_target_pairs={{0,3},{1,2},{2,1},{3,0},{4,7},{5,6},{6,5},{7,4},{8,11},{9,10},{10,... | collective-permute-start | bytes 156680 | tf_op jit(solution)/shard_map/ppermute | solution.py:582
  279.3 8.0 %collective-permute-start.28 = (bf16[64,768]{1,0:T(8,128)(2,1)S(1)}, bf16[64,768]{1,0:T(8,128)(2,1)S(1)}, u32[]{:S(2)}, u32[]{:S(2)}) collective-permute-start(bf16[64,768]{1,0:T(8,128)(2,1)S(1)} %slice.322), channel_id=1, source_target_pairs={{0,0},{1,8},{2,16},{3,24},{4,4},{5,12},{6,20},{7,28},{8,1},{9,9},{... | collective-permute-start | bytes 294920 | tf_op jit(solution)/shard_map/ppermute | solution.py:618
  282.3 7.5 %collective-permute-start.29 = (bf16[96,768]{1,0:T(8,128)(2,1)S(1)}, bf16[96,768]{1,0:T(8,128)(2,1)S(1)}, u32[]{:S(2)}, u32[]{:S(2)}) collective-permute-start(bf16[96,768]{1,0:T(8,128)(2,1)S(1)} %fusion.20), channel_id=1, source_target_pairs={{0,2},{1,3},{2,0},{3,1},{4,6},{5,7},{6,4},{7,5},{8,10},{9,11},{10,... | collective-permute-start | bytes 442376 | tf_op jit(solution)/shard_map/ppermute | solution.py:596
  (21 other events, 132.4 us)
Sparse Core Ops, SparseCore 0:
  11.4 110.6 all-gather.3

commit v5 on v4

--- a/solution.py
+++ b/solution.py
@@ -106,7 +106,7 @@
 
 
 def finish_kernel(at_ref, cols_ref, mixed_ref, *out_refs):
-    *grad_refs, lines_ref = out_refs
+    grad_refs, line_refs = out_refs[:5], out_refs[5:]
     number, place_at = at_ref[3], at_ref[4]
     own = grad_refs[0].shape[0]
     size, _, width = cols_ref.shape
@@ -126,14 +126,17 @@
     bias = mixed[2 * own + 8:2 * own + 16]
     bias = jnp.concatenate([bias[2:3, i * width:(i + 1) * width] for i in range(3)] + [bias[:5, :width]], axis=0)
     bias = pltpu.roll(bias, lax.rem(width - place_at * own, width), 1)
-    lines_ref[...] = jnp.concatenate([rows[:8, :128], inner[:, :128], bias[:, :128]], axis=0)
-
-
-def finish_call(at, cols, mixed):
+    for i, ref in enumerate(line_refs):
+        source, row = (rows, i) if i < 6 else (inner, 0) if i == 6 else (bias, i - 7)
+        ref[...] = source[row:row + 1, :ref.shape[1]]
+
+
+def finish_call(at, cols, mixed, ff_own):
     own = (mixed.shape[0] - 16) // 2
     return pl.pallas_call(
         finish_kernel,
-        out_shape=[jax.ShapeDtypeStruct((own, D), WIDE)] * 5 + [jax.ShapeDtypeStruct((24, 128), WIDE)],
+        out_shape=[jax.ShapeDtypeStruct((own, D), WIDE)] * 5
+        + [jax.ShapeDtypeStruct((1, ff_own if i == 6 else own), WIDE) for i in range(10)],
         in_specs=[pl.BlockSpec(memory_space=pltpu.SMEM)] + [pl.BlockSpec(memory_space=pltpu.VMEM)] * 2,
         compiler_params=pltpu.CompilerParams(vmem_limit_bytes=20 * 1024 * 1024),
         name="finish",
@@ -415,7 +418,7 @@
     (small_ref, ctx_all, first, first_low, unit_one, scale_one, act, slope, outer, pre_two_grad,
      outer_grad, first_grad) = refs[4 + n_grads:]
     step = pl.program_id(0)
-    core, x_at, y_at, z_at = at_ref[0], at_ref[1] >> 1, at_ref[1] & 1, at_ref[2]
+    core, x_at, y_at = at_ref[0], at_ref[1] >> 1, at_ref[1] & 1
     here = lax.rem(at_ref[3], ctx_ref.shape[0])
     blocks, pages, rows, width = ctx_ref.shape
     rows, width = 2 * rows, width // 2
@@ -474,7 +477,7 @@
         for z in range(4):
             for x in range(2):
                 for y in range(2):
-                    slot = (0, x_at ^ x, y_at ^ y, z_at ^ z)
+                    slot = (0, x_at ^ x, y_at ^ y, z)
                     first, second = cut[z, x, y, 0], cut[z, x, y, 1]
                     grad_refs[2][slot] = jnp.where(core == 0, first, second).astype(LOW)
                     grad_refs[3][slot] = jnp.where(core == 0, second, first).astype(LOW)
@@ -604,6 +607,11 @@
     return added(value[0], *(hop(value[j], devices, j << 3) for j in (1, 2, 3)))
 
 
+def exchange_along_z(value, devices):
+    lines = [[i + 8 * z for z in range(4)] for i in range(8)]
+    return lax.all_to_all(value, AXES, 0, 0, tiled=True, axis_index_groups=lines)
+
+
 def tie(*values):
     return lax.optimization_barrier(values)
 
@@ -712,8 +720,8 @@
     ctx = exchange_slots(ctx_heads)
 
     spot = ff_own
-    w_inner = late[:, spot:spot + cuts * own].reshape(devices, cuts, own, D)
-    w_inner = w_inner.swapaxes(0, 1).reshape(cuts, D, D)
+    w_inner = jnp.stack(
+        [late[:, spot + j * own:spot + (j + 1) * own].reshape(D, D) for j in range(cuts)])
     spot += cuts * own
     vectors = jnp.sum(late[:, spot:spot + small_rows].astype(WIDE), axis=0)
     w_output = late[:, spot + small_rows:].reshape(D, D)
@@ -748,16 +756,14 @@
             mixed, mixed_far, kept, sent, inner_sum, inner_sent, *outer_got)
         mixed = added(mixed, mixed_far).astype(LOW)
         inner_sum = added(inner_sum, inner_sent).astype(LOW).swapaxes(0, 1).reshape(4, (cuts + 1) * own, D)
-        mixed = jnp.concatenate([mixed, inner_sum], axis=1)
+        inner_sum = exchange_along_z(inner_sum, devices)
         mixed_z = [hop(mixed[j], devices, j << 3) for j in (1, 2, 3)]
         outer_sent = hop(added(*(got[1] for got in outer_got)).astype(LOW), devices, 4)
         far = hop(added(kept[1], sent[1]).astype(LOW), devices, 2)
         outer_sum = added(*(got[0] for got in outer_got))
         mixed, kept, sent, far, outer_sum, outer_sent, *mixed_z = tie(
             mixed, kept, sent, far, outer_sum, outer_sent, *mixed_z)
-        rest = 5 * own + 16
-        inner_sum = added(mixed[0, rest:], *(got[rest:] for got in mixed_z)).reshape(cuts + 1, own, D)
-        mixed = added(mixed[0, :rest], *(got[:rest] for got in mixed_z)).astype(LOW)
+        mixed = added(mixed[0], *mixed_z).astype(LOW)
         small = mixed[5 * own:].reshape(16, pb_size, width).swapaxes(0, 1).reshape(1, 16 * pb_size, width)
         cols = mixed[:3 * own].reshape(3 * own, pb_size, width).swapaxes(0, 1)
         cols = jnp.concatenate([cols, jnp.broadcast_to(small, (pb_size,) + small.shape[1:])], axis=1)
@@ -767,10 +773,11 @@
         outer_sent = hop(outer_sum[1].astype(LOW), devices, 2)
         tokens_grad = pre_one_grad.reshape(pages, rows, D) + added(kept[0], sent[0], far)
         d_outer = added(outer_sum[0], outer_sent)
-        d_query, d_keys, d_values, d_place_q, d_place_k, lines = finish_call(at, cols, mixed)
-        vectors = [lines[i, :own] for i in range(6)]
-        d_b_inner = lines[8, :ff_own]
-        d_bias = [lines[16 + i, :own] for i in range(3)]
+        d_query, d_keys, d_values, d_place_q, d_place_k, *lines = finish_call(at, cols, mixed, ff_own)
+        lines = [line.reshape(-1) for line in lines]
+        vectors, d_b_inner, d_bias = lines[:6], lines[6], lines[7:]
+        tokens_grad, d_outer, inner_sum = tie(tokens_grad, d_outer, inner_sum)
+        inner_sum = added(*(inner_sum[z] for z in range(4))).reshape(cuts + 1, own, D)
         d_inner = jnp.concatenate([inner_sum[j] for j in range(cuts)], axis=1)
         d_output = inner_sum[cuts]
     else:

time: 298 us -> 292 us (0.980)
  waiting for transfers between devices: 92.5 us -> 76 us
  starting transfers between devices: 45.9 us -> 53.1 us
  other arithmetic: 29.9 us -> 36.5 us
  local copies, waits for them, and re-layouts: 18.6 us -> 14.7 us
    ppermute x19, waiting for transfers between devices: 83.2 us -> 64.3 us  [hop(): return lax.ppermute(value, AXES, [(i, i ^ bits) for i in range(devices)])]
    ppermute x9, starting transfers between devices: 10.2 us -> 15.3 us  [swap(): return lax.ppermute(value, axis, [(i, i ^ bit) for i in range(size)])]
    all_to_all x0 -> x1, starting transfers between devices: none -> 3.49 us  [exchange_along_z(): lax.all_to_all(value, AXES, 0, 0, tiled=True, axis_index_groups=lines)]
  transfers between devices with their start and end apart: 33 -> 34, of which waited for: 10 -> 9; matrix products, arithmetic and copies ran while one was open for 11% -> 12% of each run, Pallas kernels for 20% -> 21%
where the time goes in v5:
time: 292 us; the launch traced here: 291 us
  Pallas kernels  87 us (30%)
  waiting for transfers between devices  76 us (26%)
  starting transfers between devices  53.1 us (18%)
  other arithmetic  36.5 us (12%)
  local copies, waits for them, and re-layouts  14.7 us (5%)
  between operations  14.6 us (5%)
  blocking collectives  8.77 us (3%)
    ppermute x19, waiting for transfers between devices, hop(): return lax.ppermute(value, AXES, [(i, i ^ bits) for i in range(devices)])  64.3 us
    pallas_call x1, Pallas kernels, attend_back_call(): pl.pallas_call(functools.partial(attend_back_kernel, heads, blocks, joine...  32.6 us
    pallas_call x1, Pallas kernels, second_half_call(): pl.pallas_call(functools.partial(second_half_kernel, cuts, split), grid_s...  25.3 us
    pallas_call x1, Pallas kernels, attend_call(): pl.pallas_call(functools.partial(attend_kernel, heads, blocks), grid_spec...  22.8 us
    ppermute x19, starting transfers between devices, hop(): return lax.ppermute(value, AXES, [(i, i ^ bits) for i in range(devices)])  21.6 us
    ppermute x9, starting transfers between devices, swap(): return lax.ppermute(value, axis, [(i, i ^ bit) for i in range(size)])  15.3 us
    cos x1, other arithmetic, on_device(): sines, cosines = (jnp.sin(angles), jnp.cos(angles))  10 us
    all_gather x1, blocking collectives, on_device(): places = lax.all_gather(jnp.stack([grid_x, grid_y, padding]), 'pb', axis=0)  8.77 us
  transfers between devices with their start and end apart: 34, of which 9 were waited for; matrix products, arithmetic and copies ran while one was open for 12% of the time, Pallas kernels for 21%

profile of v5, /device:TPU:1, one launch (start us, length us, event | category | flops | bytes accessed | tf_op | source)
XLA Modules:
  0.0 290.7 jit_solution(5076112623527385815)
XLA Ops:
  9.3 2.0 pack.1
  11.3 2.1 collective-permute-start.1
  14.4 3.3 %all-to-all-start = ((bf16[4,72,192]{2,1,0:T(8,128)(2,1)}), bf16[4,72,192]{2,1,0:T(8,128)(2,1)S(1)}, u32[]{:S(2)}, u32[]{:S(2)}) async-start(bf16[4,72,192]{2,1,0:T(8,128)(2,1)} %get-tuple-element.88), calls=%async_computation | async-start | bytes 294912 | tf_op jit(solution)/shard_map/all_to_all | solution.py:685
  17.7 3.1 %collective-permute-start.3 = (bf16[56,768]{1,0:T(8,128)(2,1)}, bf16[56,768]{1,0:T(8,128)(2,1)S(1)}, u32[]{:S(2)}, u32[]{:S(2)}) collective-permute-start(bf16[56,768]{1,0:T(8,128)(2,1)} %get-tuple-element.89), channel_id=1, source_target_pairs={{0,0},{1,8},{2,16},{3,24},{4,4},{5,12},{6,20},{7,28},{8,1},{9,9},{... | collective-permute-start | bytes 258056 | tf_op jit(solution)/shard_map/ppermute | solution.py:626
  24.1 8.8 %all-gather = s32[12,3,128]{2,1,0:T(4,128)S(1)} all-gather(s32[3,3,128]{2,1,0:T(4,128)S(1)} %pad_add_fusion), channel_id=2, replica_groups=mesh['page'=8,'pb'=4] {'pb'}, dimensions={0}, use_global_device_ids=true | all-gather | bytes 23040 | tf_op jit(solution)/shard_map/all_gather | solution.py:693
  33.3 5.4 %collective-permute-start.6 = (bf16[128,768]{1,0:T(8,128)(2,1)S(1)}, bf16[128,768]{1,0:T(8,128)(2,1)S(1)}, u32[]{:S(2)}, u32[]{:S(2)}) collective-permute-start(bf16[128,768]{1,0:T(8,128)(2,1)S(1)} %constant_dynamic-update-slice_fusion), channel_id=1, source_target_pairs={{0,24},{1,25},{2,26},{3,27},{4,28},{5,29},{6,30},{7,31},{8,16},{9,... | collective-permute-start | bytes 589832 | tf_op jit(solution)/shard_map/ppermute | solution.py:599
  39.1 4.8 %collective-permute-done.6 = bf16[128,768]{1,0:T(8,128)(2,1)S(1)} collective-permute-done((bf16[128,768]{1,0:T(8,128)(2,1)S(1)}, bf16[128,768]{1,0:T(8,128)(2,1)S(1)}, u32[]{:S(2)}, u32[]{:S(2)}) %collective-permute-start.6) | collective-permute-done | bytes 196640 | tf_op jit(solution)/shard_map/ppermute | solution.py:599
  43.9 15.9 %collective-permute-done.5 = bf16[128,768]{1,0:T(8,128)(2,1)S(1)} collective-permute-done((bf16[128,768]{1,0:T(8,128)(2,1)S(1)}, bf16[128,768]{1,0:T(8,128)(2,1)S(1)}, u32[]{:S(2)}, u32[]{:S(2)}) %collective-permute-start.5) | collective-permute-done | bytes 196640 | tf_op jit(solution)/shard_map/ppermute | solution.py:599
  62.9 10.0 %fusion = (f32[3,512,384]{2,1,0:T(8,128)}, f32[3,512,384]{2,1,0:T(8,128)}) fusion(f32[3,512,192]{2,1,0:T(8,128)S(1)} %get-tuple-element.197, f32[3,512,192]{2,1,0:T(8,128)S(1)} %get-tuple-element.196), kind=kLoop, calls=%fused_computation.6 | loop fusion | flops 589824 | bytes 7077888 | tf_op jit(solution)/shard_map/cos | solution.py:702
  73.0 7.9 %collective-permute-done.7.theirs_ref = bf16[4,128,768]{2,1,0:T(8,128)(2,1)S(1)} collective-permute-done((bf16[4,128,768]{2,1,0:T(8,128)(2,1)S(1)}, bf16[4,128,768]{2,1,0:T(8,128)(2,1)S(1)}, u32[]{:S(2)}, u32[]{:S(2)}) %collective-permute-start.7) | collective-permute-done | bytes 786464 | tf_op jit(solution)/shard_map/ppermute | solution.py:599
  81.8 2.9 assemble.1
  85.8 22.8 %attend.1 = (bf16[3,512,576]{2,1,0:T(8,128)(2,1)}, bf16[3,3,512,512]{3,2,1,0:T(8,128)(2,1)}, f32[3,512,3]{2,1,0:T(8,128)}, bf16[4,3,64,384]{3,2,1,0:T(8,128)(2,1)}) custom-call(s32[1]{0:T(128)} %bitcast.5.me_ref, bf16[3,128,768]{2,1,0:T(8,128)(2,1)} %refs_0_.3, bf16[3,128,768]{2,1,0:T(8,128)(2,1)} %copy-done.17, bf16[3,128,768]{2,1,0:T(8,128)(2,1)} %copy-done.16, ...), custom_call_target="tpu_custom_call" | custom-call | flops 20000000000 | bytes 20000000 | tf_op jit(solution)/shard_map/attend/pallas_call | solution.py:256
  109.8 1.8 collective-permute-start.10
  112.0 4.3 %collective-permute-done.10 = bf16[3,64,384]{2,1,0:T(8,128)(2,1)S(1)} collective-permute-done((bf16[3,64,384]{2,1,0:T(8,128)(2,1)S(1)}, bf16[3,64,384]{2,1,0:T(8,128)(2,1)S(1)}, u32[]{:S(2)}, u32[]{:S(2)}) %collective-permute-start.10) | collective-permute-done | bytes 147488 | tf_op jit(solution)/shard_map/ppermute | solution.py:585
  116.4 3.0 %collective-permute-done.9 = bf16[3,64,384]{2,1,0:T(8,128)(2,1)S(1)} collective-permute-done((bf16[3,64,384]{2,1,0:T(8,128)(2,1)S(1)}, bf16[3,64,384]{2,1,0:T(8,128)(2,1)S(1)}, u32[]{:S(2)}, u32[]{:S(2)}) %collective-permute-start.9) | collective-permute-done | bytes 147488 | tf_op jit(solution)/shard_map/ppermute | solution.py:585
  123.4 3.1 %fusion.30 = (bf16[32,24,768]{2,1,0:T(8,128)(2,1)S(1)}, bf16[32,24,768]{2,1,0:T(8,128)(2,1)S(1)}, bf16[32,24,768]{2,1,0:T(8,128)(2,1)S(1)}, bf16[32,24,768]{2,1,0:T(8,128)(2,1)S(1)}, bf16[32,24,768]{2,1,0:T(8,128)(2,1)S(1)}) fusion(bf16[32,232,768]{2,1,0:T(8,128)(2,1)} %bitcast.174), kind=kLoop, calls=%fused_computation.107 | loop fusion | bytes 11796480 | tf_op jit(solution)/shard_map/slice | solution.py:724
  126.5 2.5 pad_maximum_fusion.wi_ref
  129.0 25.3 %second_half.1 = (bf16[384,768]{1,0:T(8,128)(2,1)}, f32[384,768]{1,0:T(8,128)S(1)}, bf16[4,3,64,384]{3,2,1,0:T(8,128)(2,1)S(1)}, bf16[4,2,2,96,768]{4,3,2,1,0:T(...) custom-call(s32[5]{0:T(128)S(1)} %copy-done.2, ...), custom_call_target="tpu_custom_call" | custom-call | flops 20000000000 | bytes 30000000 | tf_op jit(solution)/shard_map/second_half/pallas_call | solution.py:555
  156.8 4.4 %all-to-all-start.1 = ((bf16[4,3,64,384]{3,2,1,0:T(8,128)(2,1)}), bf16[4,3,64,384]{3,2,1,0:T(8,128)(2,1)}, u32[]{:S(2)}, u32[]{:S(2)}) async-start(bf16[4,3,64,384]{3,2,1,0:T(8,128)(2,1)} %copy-done), calls=%async_computation.1 | async-start | bytes 1179648 | tf_op jit(solution)/shard_map/all_to_all | solution.py:733
  161.2 2.4 add_convert_fusion
  166.2 2.9 %fusion.2 = bf16[5,2,4,24,768]{4,3,2,0,1:T(8,128)(2,1)} fusion(bf16[5,2,2,4,24,768]{5,4,3,2,1,0:T(8,128)(2,1)} %collective-permute-done.12, bf16[5,2,2,4,24,768]{5,4,3,2,1,0:T(8,128)(2,1)S(1)} %copy-done.7), kind=kLoop, calls=%fused_computation.8 | loop fusion | flops 2949120 | bytes 4423680 | tf_op jit(solution)/shard_map/convert_element_type | solution.py:739
  170.2 32.6 %attend_back.1 = (bf16[2,3,128,768]{3,2,1,0:T(8,128)(2,1)}, bf16[2,3,128,768]{3,2,1,0:T(8,128)(2,1)}, bf16[4,136,768]{2,1,0:T(8,128)(2,1)}, bf16[4,136,768]{2,1,0:T(8,128)(2,1)}) custom-call(s32[3]{0:T(128)} %pad_add_fusion.1.me_ref, bf16[3,128,768]{2,1,0:T(8,128)(2,1)} %refs_0_.3, bf16[3,128,768]{2,1,0:T(8,128)(2,1)} %copy-done.17, ...), custom_call_target="tpu_custom_call" | custom-call | flops 30000001024 | bytes 20000000 | tf_op jit(solution)/shard_map/attend_back/pallas_call | solution.py:373
  205.3 2.3 fusion.3
  211.2 26.3 %collective-permute-done.18 = bf16[2,2,96,768]{3,2,1,0:T(8,128)(2,1)S(1)} collective-permute-done((bf16[2,2,96,768]{3,2,1,0:T(8,128)(2,1)S(1)}, bf16[2,2,96,768]{3,2,1,0:T(8,128)(2,1)S(1)}, u32[]{:S(2)}, u32[]{:S(2)}) %collective-permute-start.18) | collective-permute-done | bytes 589856 | tf_op jit(solution)/shard_map/ppermute | solution.py:599
  239.8 2.1 collective-permute-start.24
  243.4 2.1 fusion.10
  246.9 3.5 %all-to-all-start.2 = ((bf16[4,120,768]{2,1,0:T(8,128)(2,1)}), bf16[4,120,768]{2,1,0:T(8,128)(2,1)S(1)}, u32[]{:S(2)}, u32[]{:S(2)}) async-start(bf16[4,120,768]{2,1,0:T(8,128)(2,1)} %bitcast.62), calls=%async_computation.2 | async-start | bytes 1474560 | tf_op jit(solution)/shard_map/all_to_all | solution.py:612
  250.4 9.4 %collective-permute-done.23 = bf16[136,768]{1,0:T(8,128)(2,1)} collective-permute-done((bf16[136,768]{1,0:T(8,128)(2,1)}, bf16[136,768]{1,0:T(8,128)(2,1)}, u32[]{:S(2)}, u32[]{:S(2)}) %collective-permute-start.23) | collective-permute-done | bytes 208928 | tf_op jit(solution)/shard_map/ppermute | solution.py:599
  261.5 7.6 %collective-permute-start.26 = (bf16[136,192]{1,0:T(8,128)(2,1)S(1)}, bf16[136,192]{1,0:T(8,128)(2,1)S(1)}, u32[]{:S(2)}, u32[]{:S(2)}) collective-permute-start(bf16[136,192]{1,0:T(8,128)(2,1)S(1)} %get-tuple-element.183), channel_id=1, source_target_pairs={{0,1},{1,0},{2,3},{3,2},{4,5},{5,4},{6,7},{7,6},{8,9},{9,8},{10,11... | collective-permute-start | bytes 156680 | tf_op jit(solution)/shard_map/ppermute | solution.py:585
  270.8 1.9 collective-permute-start.29
  275.2 2.4 fusion.4
  277.6 2.5 collective-permute-done.29.mixed_ref
  (142 shorter events, 44.7 us)
Async XLA Ops:
  7.2 114.9 %all-gather.4.cloned.1.call-start = ((), (), s32[]{:S(2)}) async-start(), calls=%async_computation.3 | async-start | bytes 11759616 | tf_op jit(solution)/shard_map/all_gather | solution.py:689
  11.3 49.9 %collective-permute-start.1 = (bf16[3,128,768]{2,1,0:T(8,128)(2,1)}, bf16[3,128,768]{2,1,0:T(8,128)(2,1)S(1)}, u32[]{:S(2)}, u32[]{:S(2)}) collective-permute-start(bf16[3,128,768]{2,1,0:T(8,128)(2,1)} %refs_0_.3), channel_id=1, source_target_pairs={{0,2},{1,3},{2,0},{3,1},{4,6},{5,7},{6,4},{7,5},{8,10},{9,11},{10,... | collective-permute-start | bytes 1769480 | tf_op jit(solution)/shard_map/ppermute | solution.py:585
  13.5 71.3 %collective-permute-start = (bf16[3,128,768]{2,1,0:T(8,128)(2,1)}, bf16[3,128,768]{2,1,0:T(8,128)(2,1)S(1)}, u32[]{:S(2)}, u32[]{:S(2)}) collective-permute-start(bf16[3,128,768]{2,1,0:T(8,128)(2,1)} %refs_0_.3), channel_id=1, source_target_pairs={{0,1},{1,0},{2,3},{3,2},{4,5},{5,4},{6,7},{7,6},{8,9},{9,8},{10,11... | collective-permute-start | bytes 1769480 | tf_op jit(solution)/shard_map/ppermute | solution.py:585
  14.4 18.6 %all-to-all-start = ((bf16[4,72,192]{2,1,0:T(8,128)(2,1)}), bf16[4,72,192]{2,1,0:T(8,128)(2,1)S(1)}, u32[]{:S(2)}, u32[]{:S(2)}) async-start(bf16[4,72,192]{2,1,0:T(8,128)(2,1)} %get-tuple-element.88), calls=%async_computation | async-start | bytes 294912 | tf_op jit(solution)/shard_map/all_to_all | solution.py:685
  17.7 15.5 %collective-permute-start.3 = (bf16[56,768]{1,0:T(8,128)(2,1)}, bf16[56,768]{1,0:T(8,128)(2,1)S(1)}, u32[]{:S(2)}, u32[]{:S(2)}) collective-permute-start(bf16[56,768]{1,0:T(8,128)(2,1)} %get-tuple-element.89), channel_id=1, source_target_pairs={{0,0},{1,8},{2,16},{3,24},{4,4},{5,12},{6,20},{7,28},{8,1},{9,9},{... | collective-permute-start | bytes 258056 | tf_op jit(solution)/shard_map/ppermute | solution.py:626
  33.3 10.6 %collective-permute-start.6 = (bf16[128,768]{1,0:T(8,128)(2,1)S(1)}, bf16[128,768]{1,0:T(8,128)(2,1)S(1)}, u32[]{:S(2)}, u32[]{:S(2)}) collective-permute-start(bf16[128,768]{1,0:T(8,128)(2,1)S(1)} %constant_dynamic-update-slice_fusion), channel_id=1, source_target_pairs={{0,24},{1,25},{2,26},{3,27},{4,28},{5,29},{6,30},{7,31},{8,16},{9,... | collective-permute-start | bytes 589832 | tf_op jit(solution)/shard_map/ppermute | solution.py:599
  38.7 21.0 %collective-permute-start.5 = (bf16[128,768]{1,0:T(8,128)(2,1)S(1)}, bf16[128,768]{1,0:T(8,128)(2,1)S(1)}, u32[]{:S(2)}, u32[]{:S(2)}) collective-permute-start(bf16[128,768]{1,0:T(8,128)(2,1)S(1)} %constant_dynamic-update-slice_fusion), channel_id=1, source_target_pairs={{0,16},{1,17},{2,18},{3,19},{4,20},{5,21},{6,22},{7,23},{8,24},{9,... | collective-permute-start | bytes 589832 | tf_op jit(solution)/shard_map/ppermute | solution.py:599
  38.7 21.0 %collective-permute-start.4 = (bf16[128,768]{1,0:T(8,128)(2,1)S(1)}, bf16[128,768]{1,0:T(8,128)(2,1)S(1)}, u32[]{:S(2)}, u32[]{:S(2)}) collective-permute-start(bf16[128,768]{1,0:T(8,128)(2,1)S(1)} %constant_dynamic-update-slice_fusion), channel_id=1, source_target_pairs={{0,8},{1,9},{2,10},{3,11},{4,12},{5,13},{6,14},{7,15},{8,0},{9,1},... | collective-permute-start | bytes 589832 | tf_op jit(solution)/shard_map/ppermute | solution.py:599
  59.9 21.0 %collective-permute-start.7 = (bf16[4,128,768]{2,1,0:T(8,128)(2,1)S(1)}, bf16[4,128,768]{2,1,0:T(8,128)(2,1)S(1)}, u32[]{:S(2)}, u32[]{:S(2)}) collective-permute-start(bf16[4,128,768]{2,1,0:T(8,128)(2,1)S(1)} %pad_maximum_fusion.2.mine_ref), channel_id=1, source_target_pairs={{0,4},{1,5},{2,6},{3,7},{4,0},{5,1},{6,2},{7,3},{8,12},{9,13},{10,... | collective-permute-start | bytes 2359304 | tf_op jit(solution)/shard_map/ppermute | solution.py:599
  61.2 23.5 %collective-permute-start.2 = (bf16[3,128,768]{2,1,0:T(8,128)(2,1)S(1)}, bf16[3,128,768]{2,1,0:T(8,128)(2,1)S(1)}, u32[]{:S(2)}, u32[]{:S(2)}) collective-permute-start(bf16[3,128,768]{2,1,0:T(8,128)(2,1)S(1)} %collective-permute-done.1.refs_2_), channel_id=1, source_target_pairs={{0,1},{1,0},{2,3},{3,2},{4,5},{5,4},{6,7},{7,6},{8,9},{9,8},{10,11... | collective-permute-start | bytes 1769480 | tf_op jit(solution)/shard_map/ppermute | solution.py:585
  111.6 7.9 %collective-permute-start.9 = (bf16[3,64,384]{2,1,0:T(8,128)(2,1)S(1)}, bf16[3,64,384]{2,1,0:T(8,128)(2,1)S(1)}, u32[]{:S(2)}, u32[]{:S(2)}) collective-permute-start(bf16[3,64,384]{2,1,0:T(8,128)(2,1)S(1)} %get-tuple-element.175), channel_id=1, source_target_pairs={{0,2},{1,3},{2,0},{3,1},{4,6},{5,7},{6,4},{7,5},{8,10},{9,11},{10,... | collective-permute-start | bytes 442376 | tf_op jit(solution)/shard_map/ppermute | solution.py:585
  111.8 7.6 %collective-permute-start.8 = (bf16[3,64,384]{2,1,0:T(8,128)(2,1)S(1)}, bf16[3,64,384]{2,1,0:T(8,128)(2,1)S(1)}, u32[]{:S(2)}, u32[]{:S(2)}) collective-permute-start(bf16[3,64,384]{2,1,0:T(8,128)(2,1)S(1)} %get-tuple-element.176), channel_id=1, source_target_pairs={{0,1},{1,0},{2,3},{3,2},{4,5},{5,4},{6,7},{7,6},{8,9},{9,8},{10,11... | collective-permute-start | bytes 442376 | tf_op jit(solution)/shard_map/ppermute | solution.py:585
  156.0 10.2 %collective-permute-start.12 = (bf16[5,2,2,4,24,768]{5,4,3,2,1,0:T(8,128)(2,1)}, bf16[5,2,2,4,24,768]{5,4,3,2,1,0:T(8,128)(2,1)}, u32[]{:S(2)}, u32[]{:S(2)}) collective-permute-start(bf16[5,2,2,4,24,768]{5,4,3,2,1,0:T(8,128)(2,1)} %get-tuple-element.106), channel_id=1, source_target_pairs={{0,1},{1,0},{2,3},{3,2},{4,5},{5,4},{6,7},{7,6},{8,9},{9,8},{10,11... | collective-permute-start | bytes 8847368 | tf_op jit(solution)/shard_map/ppermute | solution.py:599
  156.8 13.4 %all-to-all-start.1 = ((bf16[4,3,64,384]{3,2,1,0:T(8,128)(2,1)}), bf16[4,3,64,384]{3,2,1,0:T(8,128)(2,1)}, u32[]{:S(2)}, u32[]{:S(2)}) async-start(bf16[4,3,64,384]{3,2,1,0:T(8,128)(2,1)} %copy-done), calls=%async_computation.1 | async-start | bytes 1179648 | tf_op jit(solution)/shard_map/all_to_all | solution.py:733
  164.8 45.3 %collective-permute-start.19 = (bf16[2,2,96,768]{3,2,1,0:T(8,128)(2,1)}, bf16[2,2,96,768]{3,2,1,0:T(8,128)(2,1)}, u32[]{:S(2)}, u32[]{:S(2)}) collective-permute-start(bf16[2,2,96,768]{3,2,1,0:T(8,128)(2,1)} %get-tuple-element.166), channel_id=1, source_target_pairs={{0,24},{1,25},{2,26},{3,27},{4,28},{5,29},{6,30},{7,31},{8,16},{9,... | collective-permute-start | bytes 1769480 | tf_op jit(solution)/shard_map/ppermute | solution.py:599
  169.1 33.8 %collective-permute-start.13 = (bf16[5,2,4,24,768]{4,3,2,0,1:T(8,128)(2,1)}, bf16[5,2,4,24,768]{4,3,2,0,1:T(8,128)(2,1)}, u32[]{:S(2)}, u32[]{:S(2)}) collective-permute-start(bf16[5,2,4,24,768]{4,3,2,0,1:T(8,128)(2,1)} %fusion.2), channel_id=1, source_target_pairs={{0,4},{1,5},{2,6},{3,7},{4,0},{5,1},{6,2},{7,3},{8,12},{9,13},{10,... | collective-permute-start | bytes 4423688 | tf_op jit(solution)/shard_map/ppermute | solution.py:599
  202.9 34.6 %collective-permute-start.15 = (bf16[2,3,128,768]{3,2,1,0:T(8,128)(2,1)}, bf16[2,3,128,768]{3,2,1,0:T(8,128)(2,1)S(1)}, u32[]{:S(2)}, u32[]{:S(2)}) collective-permute-start(bf16[2,3,128,768]{3,2,1,0:T(8,128)(2,1)} %get-tuple-element.115), channel_id=1, source_target_pairs={{0,1},{1,0},{2,3},{3,2},{4,5},{5,4},{6,7},{7,6},{8,9},{9,8},{10,11... | collective-permute-start | bytes 3538952 | tf_op jit(solution)/shard_map/ppermute | solution.py:599
  204.1 33.4 %collective-permute-start.14 = (bf16[4,136,768]{2,1,0:T(8,128)(2,1)}, bf16[4,136,768]{2,1,0:T(8,128)(2,1)S(1)}, u32[]{:S(2)}, u32[]{:S(2)}) collective-permute-start(bf16[4,136,768]{2,1,0:T(8,128)(2,1)} %get-tuple-element.113), channel_id=1, source_target_pairs={{0,4},{1,5},{2,6},{3,7},{4,0},{5,1},{6,2},{7,3},{8,12},{9,13},{10,... | collective-permute-start | bytes 2506760 | tf_op jit(solution)/shard_map/ppermute | solution.py:599
  207.6 29.9 %collective-permute-start.16 = (bf16[5,4,24,768]{3,2,1,0:T(8,128)(2,1)S(1)}, bf16[5,4,24,768]{3,2,1,0:T(8,128)(2,1)S(1)}, u32[]{:S(2)}, u32[]{:S(2)}) collective-permute-start(bf16[5,4,24,768]{3,2,1,0:T(8,128)(2,1)S(1)} %get-tuple-element.160), channel_id=1, source_target_pairs={{0,2},{1,3},{2,0},{3,1},{4,6},{5,7},{6,4},{7,5},{8,10},{9,11},{10,... | collective-permute-start | bytes 2211848 | tf_op jit(solution)/shard_map/ppermute | solution.py:599
  209.0 28.5 %collective-permute-start.18 = (bf16[2,2,96,768]{3,2,1,0:T(8,128)(2,1)S(1)}, bf16[2,2,96,768]{3,2,1,0:T(8,128)(2,1)S(1)}, u32[]{:S(2)}, u32[]{:S(2)}) collective-permute-start(bf16[2,2,96,768]{3,2,1,0:T(8,128)(2,1)S(1)} %copy-done.15), channel_id=1, source_target_pairs={{0,16},{1,17},{2,18},{3,19},{4,20},{5,21},{6,22},{7,23},{8,24},{9,... | collective-permute-start | bytes 1769480 | tf_op jit(solution)/shard_map/ppermute | solution.py:599
  210.1 27.4 %collective-permute-start.17 = (bf16[2,2,96,768]{3,2,1,0:T(8,128)(2,1)S(1)}, bf16[2,2,96,768]{3,2,1,0:T(8,128)(2,1)S(1)}, u32[]{:S(2)}, u32[]{:S(2)}) collective-permute-start(bf16[2,2,96,768]{3,2,1,0:T(8,128)(2,1)S(1)} %get-tuple-element.168), channel_id=1, source_target_pairs={{0,8},{1,9},{2,10},{3,11},{4,12},{5,13},{6,14},{7,15},{8,0},{9,1},... | collective-permute-start | bytes 1769480 | tf_op jit(solution)/shard_map/ppermute | solution.py:599
  238.7 21.1 %collective-permute-start.20 = (bf16[3,128,768]{2,1,0:T(8,128)(2,1)}, bf16[3,128,768]{2,1,0:T(8,128)(2,1)}, u32[]{:S(2)}, u32[]{:S(2)}) collective-permute-start(bf16[3,128,768]{2,1,0:T(8,128)(2,1)} %fusion.6), channel_id=1, source_target_pairs={{0,2},{1,3},{2,0},{3,1},{4,6},{5,7},{6,4},{7,5},{8,10},{9,11},{10,... | collective-permute-start | bytes 1769480 | tf_op jit(solution)/shard_map/ppermute | solution.py:599
  239.8 10.6 %collective-permute-start.24 = (bf16[136,768]{1,0:T(8,128)(2,1)}, bf16[136,768]{1,0:T(8,128)(2,1)}, u32[]{:S(2)}, u32[]{:S(2)}) collective-permute-start(bf16[136,768]{1,0:T(8,128)(2,1)} %get-tuple-element.170), channel_id=1, source_target_pairs={{0,24},{1,25},{2,26},{3,27},{4,28},{5,29},{6,30},{7,31},{8,16},{9,... | collective-permute-start | bytes 626696 | tf_op jit(solution)/shard_map/ppermute | solution.py:599
  242.0 17.8 %collective-permute-start.23 = (bf16[136,768]{1,0:T(8,128)(2,1)}, bf16[136,768]{1,0:T(8,128)(2,1)}, u32[]{:S(2)}, u32[]{:S(2)}) collective-permute-start(bf16[136,768]{1,0:T(8,128)(2,1)} %get-tuple-element.171), channel_id=1, source_target_pairs={{0,16},{1,17},{2,18},{3,19},{4,20},{5,21},{6,22},{7,23},{8,24},{9,... | collective-permute-start | bytes 626696 | tf_op jit(solution)/shard_map/ppermute | solution.py:599
  242.0 17.8 %collective-permute-start.22 = (bf16[136,768]{1,0:T(8,128)(2,1)S(1)}, bf16[136,768]{1,0:T(8,128)(2,1)}, u32[]{:S(2)}, u32[]{:S(2)}) collective-permute-start(bf16[136,768]{1,0:T(8,128)(2,1)S(1)} %get-tuple-element.172), channel_id=1, source_target_pairs={{0,8},{1,9},{2,10},{3,11},{4,12},{5,13},{6,14},{7,15},{8,0},{9,1},... | collective-permute-start | bytes 626696 | tf_op jit(solution)/shard_map/ppermute | solution.py:599
  245.5 14.3 %collective-permute-start.21 = (bf16[2,96,768]{2,1,0:T(8,128)(2,1)}, bf16[2,96,768]{2,1,0:T(8,128)(2,1)}, u32[]{:S(2)}, u32[]{:S(2)}) collective-permute-start(bf16[2,96,768]{2,1,0:T(8,128)(2,1)} %get-tuple-element.164), channel_id=1, source_target_pairs={{0,4},{1,5},{2,6},{3,7},{4,0},{5,1},{6,2},{7,3},{8,12},{9,13},{10,... | collective-permute-start | bytes 884744 | tf_op jit(solution)/shard_map/ppermute | solution.py:599
  246.9 35.4 %all-to-all-start.2 = ((bf16[4,120,768]{2,1,0:T(8,128)(2,1)}), bf16[4,120,768]{2,1,0:T(8,128)(2,1)S(1)}, u32[]{:S(2)}, u32[]{:S(2)}) async-start(bf16[4,120,768]{2,1,0:T(8,128)(2,1)} %bitcast.62), calls=%async_computation.2 | async-start | bytes 1474560 | tf_op jit(solution)/shard_map/all_to_all | solution.py:612
  261.5 16.0 %collective-permute-start.26 = (bf16[136,192]{1,0:T(8,128)(2,1)S(1)}, bf16[136,192]{1,0:T(8,128)(2,1)S(1)}, u32[]{:S(2)}, u32[]{:S(2)}) collective-permute-start(bf16[136,192]{1,0:T(8,128)(2,1)S(1)} %get-tuple-element.183), channel_id=1, source_target_pairs={{0,1},{1,0},{2,3},{3,2},{4,5},{5,4},{6,7},{7,6},{8,9},{9,8},{10,11... | collective-permute-start | bytes 156680 | tf_op jit(solution)/shard_map/ppermute | solution.py:585
  269.1 8.5 %collective-permute-start.27 = (bf16[136,192]{1,0:T(8,128)(2,1)S(1)}, bf16[136,192]{1,0:T(8,128)(2,1)S(1)}, u32[]{:S(2)}, u32[]{:S(2)}) collective-permute-start(bf16[136,192]{1,0:T(8,128)(2,1)S(1)} %get-tuple-element.184), channel_id=1, source_target_pairs={{0,2},{1,3},{2,0},{3,1},{4,6},{5,7},{6,4},{7,5},{8,10},{9,11},{10,... | collective-permute-start | bytes 156680 | tf_op jit(solution)/shard_map/ppermute | solution.py:585
  270.5 7.1 %collective-permute-start.28 = (bf16[136,192]{1,0:T(8,128)(2,1)S(1)}, bf16[136,192]{1,0:T(8,128)(2,1)S(1)}, u32[]{:S(2)}, u32[]{:S(2)}) collective-permute-start(bf16[136,192]{1,0:T(8,128)(2,1)S(1)} %get-tuple-element.185), channel_id=1, source_target_pairs={{0,3},{1,2},{2,1},{3,0},{4,7},{5,6},{6,5},{7,4},{8,11},{9,10},{10,... | collective-permute-start | bytes 156680 | tf_op jit(solution)/shard_map/ppermute | solution.py:585
  270.8 9.3 %collective-permute-start.29 = (bf16[64,768]{1,0:T(8,128)(2,1)S(1)}, bf16[64,768]{1,0:T(8,128)(2,1)S(1)}, u32[]{:S(2)}, u32[]{:S(2)}) collective-permute-start(bf16[64,768]{1,0:T(8,128)(2,1)S(1)} %slice.304), channel_id=1, source_target_pairs={{0,0},{1,8},{2,16},{3,24},{4,4},{5,12},{6,20},{7,28},{8,1},{9,9},{... | collective-permute-start | bytes 294920 | tf_op jit(solution)/shard_map/ppermute | solution.py:626
  273.8 7.8 %collective-permute-start.25 = (bf16[96,768]{1,0:T(8,128)(2,1)S(1)}, bf16[96,768]{1,0:T(8,128)(2,1)S(1)}, u32[]{:S(2)}, u32[]{:S(2)}) collective-permute-start(bf16[96,768]{1,0:T(8,128)(2,1)S(1)} %fusion.12), channel_id=1, source_target_pairs={{0,2},{1,3},{2,0},{3,1},{4,6},{5,7},{6,4},{7,5},{8,10},{9,11},{10,... | collective-permute-start | bytes 442376 | tf_op jit(solution)/shard_map/ppermute | solution.py:599
  (21 other events, 169.8 us)
Sparse Core Ops, SparseCore 0:
  11.4 110.6 all-gather.3

commit v6 on v5

--- a/solution.py
+++ b/solution.py
@@ -544,7 +544,7 @@
     eighth = (1, 2, 2, D // 8, D)
     slots = (1, 2, 2, 4, D // 32, D)
     if split:
-        grad_specs = [pl.BlockSpec(eighth, lambda i, at: (late(i) ^ at[2], 0, 0, 0, 0))] * 2
+        grad_specs = [pl.BlockSpec(eighth, lambda i, at: (late(i), 0, 0, 0, 0))] * 2
         grad_specs += [pl.BlockSpec(slots, lambda i, at: (last(i), 0, 0, 0, 0, 0))] * 2
         grads = [(cuts, 2, 2, D // 8, D)] * 2 + [(cuts + 1,) + slots[1:]] * 2
     else:
@@ -737,9 +737,8 @@
         outer_core, inner_core = hop(outer_sent, devices, 1), hop(inner_sent, devices, 1)
         outer_sum = added(outer_kept, outer_core).astype(LOW)
         inner_far = added(inner_kept[:, 1], inner_core[:, 1]).astype(LOW)
-        outer_got = [outer_sum[0]] + [hop(outer_sum[j], devices, j << 3) for j in (1, 2, 3)]
-        dctx, outer_got[0], far = tie(dctx, outer_got[0], inner_far)
-        inner_far = hop(inner_far, devices, 4)
+        dctx, outer_sum, inner_far = tie(dctx, outer_sum, inner_far)
+        outer_got, inner_far = exchange_along_z(outer_sum, devices), hop(inner_far, devices, 4)
 
     joined = (own, pb_size, page_size) if by_link else None
     me_array = jnp.stack([me, at[1] >> 1, at[2]]).astype(jnp.int32)
@@ -752,15 +751,15 @@
         inner_sent = added(inner_kept[:, 0, 1], inner_core[:, 0, 1], inner_far[:, 1]).astype(LOW)
         inner_sent = hop(inner_sent, devices, 2)
         inner_sum = added(inner_kept[:, 0, 0], inner_core[:, 0, 0], inner_far[:, 0])
-        mixed, mixed_far, kept, sent, inner_sum, inner_sent, *outer_got = tie(
-            mixed, mixed_far, kept, sent, inner_sum, inner_sent, *outer_got)
+        mixed, mixed_far, kept, sent, inner_sum, inner_sent = tie(
+            mixed, mixed_far, kept, sent, inner_sum, inner_sent)
         mixed = added(mixed, mixed_far).astype(LOW)
         inner_sum = added(inner_sum, inner_sent).astype(LOW).swapaxes(0, 1).reshape(4, (cuts + 1) * own, D)
         inner_sum = exchange_along_z(inner_sum, devices)
         mixed_z = [hop(mixed[j], devices, j << 3) for j in (1, 2, 3)]
-        outer_sent = hop(added(*(got[1] for got in outer_got)).astype(LOW), devices, 4)
+        outer_sent = hop(added(*(outer_got[z, 1] for z in range(4))).astype(LOW), devices, 4)
         far = hop(added(kept[1], sent[1]).astype(LOW), devices, 2)
-        outer_sum = added(*(got[0] for got in outer_got))
+        outer_sum = added(*(outer_got[z, 0] for z in range(4)))
         mixed, kept, sent, far, outer_sum, outer_sent, *mixed_z = tie(
             mixed, kept, sent, far, outer_sum, outer_sent, *mixed_z)
         mixed = added(mixed[0], *mixed_z).astype(LOW)

time: 292 us -> 290 us (level)
  waiting for transfers between devices: 76 us -> 72.6 us
    all_to_all x1 -> x2, starting transfers between devices: 3.49 us -> 8.06 us  [exchange_along_z(): lax.all_to_all(value, AXES, 0, 0, tiled=True, axis_index_groups=lines)]
    ppermute x19 -> x16, waiting for transfers between devices: 64.3 us -> 63.4 us  [hop(): return lax.ppermute(value, AXES, [(i, i ^ bits) for i in range(devices)])]
    ppermute x19 -> x16, starting transfers between devices: 21.6 us -> 20.6 us  [hop(): return lax.ppermute(value, AXES, [(i, i ^ bits) for i in range(devices)])]
  transfers between devices with their start and end apart: 34 -> 32, of which waited for: 9 -> 9; matrix products, arithmetic and copies ran while one was open for 12% -> 13% of each run, Pallas kernels for 21% -> 21%
where the time goes in v6:
time: 290 us; the launch traced here: 289 us
  Pallas kernels  87 us (30%)
  waiting for transfers between devices  72.6 us (25%)
  starting transfers between devices  55.5 us (19%)
  other arithmetic  36.9 us (13%)
  between operations  14.6 us (5%)
  local copies, waits for them, and re-layouts  13.7 us (5%)
  blocking collectives  8.77 us (3%)
    ppermute x16, waiting for transfers between devices, hop(): return lax.ppermute(value, AXES, [(i, i ^ bits) for i in range(devices)])  63.4 us
    pallas_call x1, Pallas kernels, attend_back_call(): pl.pallas_call(functools.partial(attend_back_kernel, heads, blocks, joine...  32.7 us
    pallas_call x1, Pallas kernels, second_half_call(): pl.pallas_call(functools.partial(second_half_kernel, cuts, split), grid_s...  25.2 us
    pallas_call x1, Pallas kernels, attend_call(): pl.pallas_call(functools.partial(attend_kernel, heads, blocks), grid_spec...  22.8 us
    ppermute x16, starting transfers between devices, hop(): return lax.ppermute(value, AXES, [(i, i ^ bits) for i in range(devices)])  20.6 us
    ppermute x9, starting transfers between devices, swap(): return lax.ppermute(value, axis, [(i, i ^ bit) for i in range(size)])  14 us
    cos x1, other arithmetic, on_device(): sines, cosines = (jnp.sin(angles), jnp.cos(angles))  10.1 us
    all_gather x1, blocking collectives, on_device(): places = lax.all_gather(jnp.stack([grid_x, grid_y, padding]), 'pb', axis=0)  8.77 us
  transfers between devices with their start and end apart: 32, of which 9 were waited for; matrix products, arithmetic and copies ran while one was open for 13% of the time, Pallas kernels for 21%

profile of v6, /device:TPU:1, one launch (start us, length us, event | category | flops | bytes accessed | tf_op | source)
XLA Modules:
  0.0 289.0 jit_solution(2118043796763626199)
XLA Ops:
  9.3 2.0 pack.1
  11.3 2.1 collective-permute-start.1
  14.4 3.3 %all-to-all-start = ((bf16[4,72,192]{2,1,0:T(8,128)(2,1)}), bf16[4,72,192]{2,1,0:T(8,128)(2,1)S(1)}, u32[]{:S(2)}, u32[]{:S(2)}) async-start(bf16[4,72,192]{2,1,0:T(8,128)(2,1)} %get-tuple-element.85), calls=%async_computation | async-start | bytes 294912 | tf_op jit(solution)/shard_map/all_to_all | solution.py:685
  17.7 3.1 %collective-permute-start.3 = (bf16[56,768]{1,0:T(8,128)(2,1)}, bf16[56,768]{1,0:T(8,128)(2,1)S(1)}, u32[]{:S(2)}, u32[]{:S(2)}) collective-permute-start(bf16[56,768]{1,0:T(8,128)(2,1)} %get-tuple-element.86), channel_id=1, source_target_pairs={{0,0},{1,8},{2,16},{3,24},{4,4},{5,12},{6,20},{7,28},{8,1},{9,9},{... | collective-permute-start | bytes 258056 | tf_op jit(solution)/shard_map/ppermute | solution.py:626
  24.1 8.8 %all-gather = s32[12,3,128]{2,1,0:T(4,128)S(1)} all-gather(s32[3,3,128]{2,1,0:T(4,128)S(1)} %pad_add_fusion), channel_id=2, replica_groups=mesh['page'=8,'pb'=4] {'pb'}, dimensions={0}, use_global_device_ids=true | all-gather | bytes 23040 | tf_op jit(solution)/shard_map/all_gather | solution.py:693
  33.3 5.4 %collective-permute-start.6 = (bf16[128,768]{1,0:T(8,128)(2,1)S(1)}, bf16[128,768]{1,0:T(8,128)(2,1)S(1)}, u32[]{:S(2)}, u32[]{:S(2)}) collective-permute-start(bf16[128,768]{1,0:T(8,128)(2,1)S(1)} %constant_dynamic-update-slice_fusion), channel_id=1, source_target_pairs={{0,24},{1,25},{2,26},{3,27},{4,28},{5,29},{6,30},{7,31},{8,16},{9,... | collective-permute-start | bytes 589832 | tf_op jit(solution)/shard_map/ppermute | solution.py:599
  39.1 4.8 %collective-permute-done.6 = bf16[128,768]{1,0:T(8,128)(2,1)S(1)} collective-permute-done((bf16[128,768]{1,0:T(8,128)(2,1)S(1)}, bf16[128,768]{1,0:T(8,128)(2,1)S(1)}, u32[]{:S(2)}, u32[]{:S(2)}) %collective-permute-start.6) | collective-permute-done | bytes 196640 | tf_op jit(solution)/shard_map/ppermute | solution.py:599
  43.9 15.9 %collective-permute-done.5 = bf16[128,768]{1,0:T(8,128)(2,1)S(1)} collective-permute-done((bf16[128,768]{1,0:T(8,128)(2,1)S(1)}, bf16[128,768]{1,0:T(8,128)(2,1)S(1)}, u32[]{:S(2)}, u32[]{:S(2)}) %collective-permute-start.5) | collective-permute-done | bytes 196640 | tf_op jit(solution)/shard_map/ppermute | solution.py:599
  62.9 10.1 %fusion = (f32[3,512,384]{2,1,0:T(8,128)}, f32[3,512,384]{2,1,0:T(8,128)}) fusion(f32[3,512,192]{2,1,0:T(8,128)S(1)} %get-tuple-element.187, f32[3,512,192]{2,1,0:T(8,128)S(1)} %get-tuple-element.186), kind=kLoop, calls=%fused_computation.6 | loop fusion | flops 589824 | bytes 7077888 | tf_op jit(solution)/shard_map/cos | solution.py:702
  73.0 7.9 %collective-permute-done.7.theirs_ref = bf16[4,128,768]{2,1,0:T(8,128)(2,1)S(1)} collective-permute-done((bf16[4,128,768]{2,1,0:T(8,128)(2,1)S(1)}, bf16[4,128,768]{2,1,0:T(8,128)(2,1)S(1)}, u32[]{:S(2)}, u32[]{:S(2)}) %collective-permute-start.7) | collective-permute-done | bytes 786464 | tf_op jit(solution)/shard_map/ppermute | solution.py:599
  81.8 2.9 assemble.1
  85.8 22.8 %attend.1 = (bf16[3,512,576]{2,1,0:T(8,128)(2,1)}, bf16[3,3,512,512]{3,2,1,0:T(8,128)(2,1)}, f32[3,512,3]{2,1,0:T(8,128)}, bf16[4,3,64,384]{3,2,1,0:T(8,128)(2,1)}) custom-call(s32[1]{0:T(128)} %bitcast.5.me_ref, bf16[3,128,768]{2,1,0:T(8,128)(2,1)} %refs_0_.3, bf16[3,128,768]{2,1,0:T(8,128)(2,1)} %copy-done.21, bf16[3,128,768]{2,1,0:T(8,128)(2,1)} %copy-done.20, ...), custom_call_target="tpu_custom_call" | custom-call | flops 20000000000 | bytes 20000000 | tf_op jit(solution)/shard_map/attend/pallas_call | solution.py:256
  112.0 4.3 %collective-permute-done.10 = bf16[3,64,384]{2,1,0:T(8,128)(2,1)S(1)} collective-permute-done((bf16[3,64,384]{2,1,0:T(8,128)(2,1)S(1)}, bf16[3,64,384]{2,1,0:T(8,128)(2,1)S(1)}, u32[]{:S(2)}, u32[]{:S(2)}) %collective-permute-start.10) | collective-permute-done | bytes 147488 | tf_op jit(solution)/shard_map/ppermute | solution.py:585
  116.4 3.0 %collective-permute-done.9 = bf16[3,64,384]{2,1,0:T(8,128)(2,1)S(1)} collective-permute-done((bf16[3,64,384]{2,1,0:T(8,128)(2,1)S(1)}, bf16[3,64,384]{2,1,0:T(8,128)(2,1)S(1)}, u32[]{:S(2)}, u32[]{:S(2)}) %collective-permute-start.9) | collective-permute-done | bytes 147488 | tf_op jit(solution)/shard_map/ppermute | solution.py:585
  123.4 3.1 %fusion.30 = (bf16[32,24,768]{2,1,0:T(8,128)(2,1)S(1)}, bf16[32,24,768]{2,1,0:T(8,128)(2,1)S(1)}, bf16[32,24,768]{2,1,0:T(8,128)(2,1)S(1)}, bf16[32,24,768]{2,1,0:T(8,128)(2,1)S(1)}, bf16[32,24,768]{2,1,0:T(8,128)(2,1)S(1)}) fusion(bf16[32,232,768]{2,1,0:T(8,128)(2,1)} %bitcast.166), kind=kLoop, calls=%fused_computation.103 | loop fusion | bytes 11796480 | tf_op jit(solution)/shard_map/slice | solution.py:724
  126.5 2.5 pad_maximum_fusion.wi_ref
  129.0 25.2 %second_half.1 = (bf16[384,768]{1,0:T(8,128)(2,1)}, f32[384,768]{1,0:T(8,128)S(1)}, bf16[4,3,64,384]{3,2,1,0:T(8,128)(2,1)S(1)}, bf16[4,2,2,96,768]{4,3,2,1,0:T(...) custom-call(s32[5]{0:T(128)S(1)} %copy-done.2, ...), custom_call_target="tpu_custom_call" | custom-call | flops 20000000000 | bytes 30000000 | tf_op jit(solution)/shard_map/second_half/pallas_call | solution.py:555
  156.8 4.4 %all-to-all-start.1 = ((bf16[4,3,64,384]{3,2,1,0:T(8,128)(2,1)}), bf16[4,3,64,384]{3,2,1,0:T(8,128)(2,1)}, u32[]{:S(2)}, u32[]{:S(2)}) async-start(bf16[4,3,64,384]{3,2,1,0:T(8,128)(2,1)} %copy-done), calls=%async_computation.1 | async-start | bytes 1179648 | tf_op jit(solution)/shard_map/all_to_all | solution.py:733
  161.1 3.6 %collective-permute-done.11 = bf16[4,2,2,96,768]{4,3,2,1,0:T(8,128)(2,1)} collective-permute-done((bf16[4,2,2,96,768]{4,3,2,1,0:T(8,128)(2,1)}, bf16[4,2,2,96,768]{4,3,2,1,0:T(8,128)(2,1)}, u32[]{:S(2)}, u32[]{:S(2)}) %collective-permute-start.11) | collective-permute-done | bytes 2359328 | tf_op jit(solution)/shard_map/ppermute | solution.py:599
  164.8 3.9 %add_convert_fusion = bf16[4,2,2,96,768]{4,3,2,1,0:T(8,128)(2,1)} fusion(bf16[4,2,2,96,768]{4,3,2,1,0:T(8,128)(2,1)} %collective-permute-done.11, bf16[4,2,2,96,768]{4,3,2,1,0:T(8,128)(2,1)S(1)} %get-tuple-element.100), kind=kLoop, calls=%fused_computation.1 | loop fusion | flops 4718592 | bytes 7077888 | tf_op jit(solution)/shard_map/convert_element_type | solution.py:738
  168.7 2.9 fusion.2
  171.6 3.9 %all-to-all-start.2 = ((bf16[4,2,2,96,768]{4,3,2,1,0:T(8,128)(2,1)}), bf16[4,2,2,96,768]{4,3,2,1,0:T(8,128)(2,1)S(1)}, u32[]{:S(2)}, u32[]{:S(2)}) async-start(bf16[4,2,2,96,768]{4,3,2,1,0:T(8,128)(2,1)} %add_convert_fusion), calls=%async_computation.2 | async-start | bytes 4718592 | tf_op jit(solution)/shard_map/all_to_all | solution.py:612
  176.7 32.7 %attend_back.1 = (bf16[2,3,128,768]{3,2,1,0:T(8,128)(2,1)}, bf16[2,3,128,768]{3,2,1,0:T(8,128)(2,1)}, bf16[4,136,768]{2,1,0:T(8,128)(2,1)}, bf16[4,136,768]{2,1,0:T(8,128)(2,1)}) custom-call(s32[3]{0:T(128)} %pad_add_fusion.1.me_ref, bf16[3,128,768]{2,1,0:T(8,128)(2,1)} %refs_0_.3, bf16[3,128,768]{2,1,0:T(8,128)(2,1)} %copy-done.21, ...), custom_call_target="tpu_custom_call" | custom-call | flops 30000001024 | bytes 20000000 | tf_op jit(solution)/shard_map/attend_back/pallas_call | solution.py:373
  211.6 3.0 %fusion.3 = (bf16[5,4,24,768]{3,2,1,0:T(8,128)(2,1)S(1)}, f32[5,4,24,768]{3,2,1,0:T(8,128)}) fusion(bf16[5,2,2,4,24,768]{5,4,3,2,1,0:T(8,128)(2,1)} %collective-permute-done.12, bf16[5,2,4,24,768]{4,3,2,0,1:T(8,128)(2,1)S(1)} %collective-permute-done.13, bf16[5,2,2,4,24,768]{5,4,3,2,1,0:T(8,128)(2,1)S(1)} %copy-done.10), kind=kLoop, calls=%fused_computation.10 | loop fusion | flops 4055040 | bytes 6635520 | tf_op jit(solution)/shard_map/convert_element_type | solution.py:751
  214.9 17.5 %collective-permute-done.16 = bf16[5,4,24,768]{3,2,1,0:T(8,128)(2,1)S(1)} collective-permute-done((bf16[5,4,24,768]{3,2,1,0:T(8,128)(2,1)S(1)}, bf16[5,4,24,768]{3,2,1,0:T(8,128)(2,1)S(1)}, u32[]{:S(2)}, u32[]{:S(2)}) %collective-permute-start.16) | collective-permute-done | bytes 737312 | tf_op jit(solution)/shard_map/ppermute | solution.py:599
  235.0 2.9 %collective-permute-start.21 = (bf16[136,768]{1,0:T(8,128)(2,1)}, bf16[136,768]{1,0:T(8,128)(2,1)}, u32[]{:S(2)}, u32[]{:S(2)}) collective-permute-start(bf16[136,768]{1,0:T(8,128)(2,1)} %get-tuple-element.160), channel_id=1, source_target_pairs={{0,24},{1,25},{2,26},{3,27},{4,28},{5,29},{6,30},{7,31},{8,16},{9,... | collective-permute-start | bytes 626696 | tf_op jit(solution)/shard_map/ppermute | solution.py:599
  242.0 4.2 %all-to-all-start.3 = ((bf16[4,120,768]{2,1,0:T(8,128)(2,1)}), bf16[4,120,768]{2,1,0:T(8,128)(2,1)S(1)}, u32[]{:S(2)}, u32[]{:S(2)}) async-start(bf16[4,120,768]{2,1,0:T(8,128)(2,1)} %bitcast.58), calls=%async_computation.3 | async-start | bytes 1474560 | tf_op jit(solution)/shard_map/all_to_all | solution.py:612
  246.3 13.6 %collective-permute-done.20 = bf16[136,768]{1,0:T(8,128)(2,1)} collective-permute-done((bf16[136,768]{1,0:T(8,128)(2,1)}, bf16[136,768]{1,0:T(8,128)(2,1)}, u32[]{:S(2)}, u32[]{:S(2)}) %collective-permute-start.20) | collective-permute-done | bytes 208928 | tf_op jit(solution)/shard_map/ppermute | solution.py:599
  261.7 6.3 %collective-permute-start.23 = (bf16[136,192]{1,0:T(8,128)(2,1)S(1)}, bf16[136,192]{1,0:T(8,128)(2,1)S(1)}, u32[]{:S(2)}, u32[]{:S(2)}) collective-permute-start(bf16[136,192]{1,0:T(8,128)(2,1)S(1)} %get-tuple-element.173), channel_id=1, source_target_pairs={{0,1},{1,0},{2,3},{3,2},{4,5},{5,4},{6,7},{7,6},{8,9},{9,8},{10,11... | collective-permute-start | bytes 156680 | tf_op jit(solution)/shard_map/ppermute | solution.py:585
  269.8 1.9 collective-permute-start.26
  271.8 4.2 %collective-permute-start.22 = (bf16[96,768]{1,0:T(8,128)(2,1)S(1)}, bf16[96,768]{1,0:T(8,128)(2,1)S(1)}, u32[]{:S(2)}, u32[]{:S(2)}) collective-permute-start(bf16[96,768]{1,0:T(8,128)(2,1)S(1)} %fusion.12), channel_id=1, source_target_pairs={{0,2},{1,3},{2,0},{3,1},{4,6},{5,7},{6,4},{7,5},{8,10},{9,11},{10,... | collective-permute-start | bytes 442376 | tf_op jit(solution)/shard_map/ppermute | solution.py:599
  276.0 2.4 fusion.4
  (145 shorter events, 39.8 us)
Async XLA Ops:
  7.2 114.9 %all-gather.4.cloned.1.call-start = ((), (), s32[]{:S(2)}) async-start(), calls=%async_computation.4 | async-start | bytes 11759616 | tf_op jit(solution)/shard_map/all_gather | solution.py:689
  11.3 49.9 %collective-permute-start.1 = (bf16[3,128,768]{2,1,0:T(8,128)(2,1)}, bf16[3,128,768]{2,1,0:T(8,128)(2,1)S(1)}, u32[]{:S(2)}, u32[]{:S(2)}) collective-permute-start(bf16[3,128,768]{2,1,0:T(8,128)(2,1)} %refs_0_.3), channel_id=1, source_target_pairs={{0,2},{1,3},{2,0},{3,1},{4,6},{5,7},{6,4},{7,5},{8,10},{9,11},{10,... | collective-permute-start | bytes 1769480 | tf_op jit(solution)/shard_map/ppermute | solution.py:585
  13.5 71.3 %collective-permute-start = (bf16[3,128,768]{2,1,0:T(8,128)(2,1)}, bf16[3,128,768]{2,1,0:T(8,128)(2,1)S(1)}, u32[]{:S(2)}, u32[]{:S(2)}) collective-permute-start(bf16[3,128,768]{2,1,0:T(8,128)(2,1)} %refs_0_.3), channel_id=1, source_target_pairs={{0,1},{1,0},{2,3},{3,2},{4,5},{5,4},{6,7},{7,6},{8,9},{9,8},{10,11... | collective-permute-start | bytes 1769480 | tf_op jit(solution)/shard_map/ppermute | solution.py:585
  14.4 18.6 %all-to-all-start = ((bf16[4,72,192]{2,1,0:T(8,128)(2,1)}), bf16[4,72,192]{2,1,0:T(8,128)(2,1)S(1)}, u32[]{:S(2)}, u32[]{:S(2)}) async-start(bf16[4,72,192]{2,1,0:T(8,128)(2,1)} %get-tuple-element.85), calls=%async_computation | async-start | bytes 294912 | tf_op jit(solution)/shard_map/all_to_all | solution.py:685
  17.7 15.5 %collective-permute-start.3 = (bf16[56,768]{1,0:T(8,128)(2,1)}, bf16[56,768]{1,0:T(8,128)(2,1)S(1)}, u32[]{:S(2)}, u32[]{:S(2)}) collective-permute-start(bf16[56,768]{1,0:T(8,128)(2,1)} %get-tuple-element.86), channel_id=1, source_target_pairs={{0,0},{1,8},{2,16},{3,24},{4,4},{5,12},{6,20},{7,28},{8,1},{9,9},{... | collective-permute-start | bytes 258056 | tf_op jit(solution)/shard_map/ppermute | solution.py:626
  33.3 10.6 %collective-permute-start.6 = (bf16[128,768]{1,0:T(8,128)(2,1)S(1)}, bf16[128,768]{1,0:T(8,128)(2,1)S(1)}, u32[]{:S(2)}, u32[]{:S(2)}) collective-permute-start(bf16[128,768]{1,0:T(8,128)(2,1)S(1)} %constant_dynamic-update-slice_fusion), channel_id=1, source_target_pairs={{0,24},{1,25},{2,26},{3,27},{4,28},{5,29},{6,30},{7,31},{8,16},{9,... | collective-permute-start | bytes 589832 | tf_op jit(solution)/shard_map/ppermute | solution.py:599
  38.7 21.0 %collective-permute-start.5 = (bf16[128,768]{1,0:T(8,128)(2,1)S(1)}, bf16[128,768]{1,0:T(8,128)(2,1)S(1)}, u32[]{:S(2)}, u32[]{:S(2)}) collective-permute-start(bf16[128,768]{1,0:T(8,128)(2,1)S(1)} %constant_dynamic-update-slice_fusion), channel_id=1, source_target_pairs={{0,16},{1,17},{2,18},{3,19},{4,20},{5,21},{6,22},{7,23},{8,24},{9,... | collective-permute-start | bytes 589832 | tf_op jit(solution)/shard_map/ppermute | solution.py:599
  38.7 21.0 %collective-permute-start.4 = (bf16[128,768]{1,0:T(8,128)(2,1)S(1)}, bf16[128,768]{1,0:T(8,128)(2,1)S(1)}, u32[]{:S(2)}, u32[]{:S(2)}) collective-permute-start(bf16[128,768]{1,0:T(8,128)(2,1)S(1)} %constant_dynamic-update-slice_fusion), channel_id=1, source_target_pairs={{0,8},{1,9},{2,10},{3,11},{4,12},{5,13},{6,14},{7,15},{8,0},{9,1},... | collective-permute-start | bytes 589832 | tf_op jit(solution)/shard_map/ppermute | solution.py:599
  59.9 21.0 %collective-permute-start.7 = (bf16[4,128,768]{2,1,0:T(8,128)(2,1)S(1)}, bf16[4,128,768]{2,1,0:T(8,128)(2,1)S(1)}, u32[]{:S(2)}, u32[]{:S(2)}) collective-permute-start(bf16[4,128,768]{2,1,0:T(8,128)(2,1)S(1)} %pad_maximum_fusion.2.mine_ref), channel_id=1, source_target_pairs={{0,4},{1,5},{2,6},{3,7},{4,0},{5,1},{6,2},{7,3},{8,12},{9,13},{10,... | collective-permute-start | bytes 2359304 | tf_op jit(solution)/shard_map/ppermute | solution.py:599
  61.2 23.5 %collective-permute-start.2 = (bf16[3,128,768]{2,1,0:T(8,128)(2,1)S(1)}, bf16[3,128,768]{2,1,0:T(8,128)(2,1)S(1)}, u32[]{:S(2)}, u32[]{:S(2)}) collective-permute-start(bf16[3,128,768]{2,1,0:T(8,128)(2,1)S(1)} %collective-permute-done.1.refs_2_), channel_id=1, source_target_pairs={{0,1},{1,0},{2,3},{3,2},{4,5},{5,4},{6,7},{7,6},{8,9},{9,8},{10,11... | collective-permute-start | bytes 1769480 | tf_op jit(solution)/shard_map/ppermute | solution.py:585
  109.7 6.6 %collective-permute-start.10 = (bf16[3,64,384]{2,1,0:T(8,128)(2,1)S(1)}, bf16[3,64,384]{2,1,0:T(8,128)(2,1)S(1)}, u32[]{:S(2)}, u32[]{:S(2)}) collective-permute-start(bf16[3,64,384]{2,1,0:T(8,128)(2,1)S(1)} %get-tuple-element.164), channel_id=1, source_target_pairs={{0,3},{1,2},{2,1},{3,0},{4,7},{5,6},{6,5},{7,4},{8,11},{9,10},{10,... | collective-permute-start | bytes 442376 | tf_op jit(solution)/shard_map/ppermute | solution.py:585
  111.5 7.9 %collective-permute-start.9 = (bf16[3,64,384]{2,1,0:T(8,128)(2,1)S(1)}, bf16[3,64,384]{2,1,0:T(8,128)(2,1)S(1)}, u32[]{:S(2)}, u32[]{:S(2)}) collective-permute-start(bf16[3,64,384]{2,1,0:T(8,128)(2,1)S(1)} %get-tuple-element.165), channel_id=1, source_target_pairs={{0,2},{1,3},{2,0},{3,1},{4,6},{5,7},{6,4},{7,5},{8,10},{9,11},{10,... | collective-permute-start | bytes 442376 | tf_op jit(solution)/shard_map/ppermute | solution.py:585
  111.8 7.6 %collective-permute-start.8 = (bf16[3,64,384]{2,1,0:T(8,128)(2,1)S(1)}, bf16[3,64,384]{2,1,0:T(8,128)(2,1)S(1)}, u32[]{:S(2)}, u32[]{:S(2)}) collective-permute-start(bf16[3,64,384]{2,1,0:T(8,128)(2,1)S(1)} %get-tuple-element.166), channel_id=1, source_target_pairs={{0,1},{1,0},{2,3},{3,2},{4,5},{5,4},{6,7},{7,6},{8,9},{9,8},{10,11... | collective-permute-start | bytes 442376 | tf_op jit(solution)/shard_map/ppermute | solution.py:585
  155.7 13.0 %collective-permute-start.12 = (bf16[5,2,2,4,24,768]{5,4,3,2,1,0:T(8,128)(2,1)}, bf16[5,2,2,4,24,768]{5,4,3,2,1,0:T(8,128)(2,1)}, u32[]{:S(2)}, u32[]{:S(2)}) collective-permute-start(bf16[5,2,2,4,24,768]{5,4,3,2,1,0:T(8,128)(2,1)} %get-tuple-element.103), channel_id=1, source_target_pairs={{0,1},{1,0},{2,3},{3,2},{4,5},{5,4},{6,7},{7,6},{8,9},{9,8},{10,11... | collective-permute-start | bytes 8847368 | tf_op jit(solution)/shard_map/ppermute | solution.py:599
  155.9 8.8 %collective-permute-start.11 = (bf16[4,2,2,96,768]{4,3,2,1,0:T(8,128)(2,1)}, bf16[4,2,2,96,768]{4,3,2,1,0:T(8,128)(2,1)}, u32[]{:S(2)}, u32[]{:S(2)}) collective-permute-start(bf16[4,2,2,96,768]{4,3,2,1,0:T(8,128)(2,1)} %get-tuple-element.101), channel_id=1, source_target_pairs={{0,1},{1,0},{2,3},{3,2},{4,5},{5,4},{6,7},{7,6},{8,9},{9,8},{10,11... | collective-permute-start | bytes 7077896 | tf_op jit(solution)/shard_map/ppermute | solution.py:599
  156.8 14.8 %all-to-all-start.1 = ((bf16[4,3,64,384]{3,2,1,0:T(8,128)(2,1)}), bf16[4,3,64,384]{3,2,1,0:T(8,128)(2,1)}, u32[]{:S(2)}, u32[]{:S(2)}) async-start(bf16[4,3,64,384]{3,2,1,0:T(8,128)(2,1)} %copy-done), calls=%async_computation.1 | async-start | bytes 1179648 | tf_op jit(solution)/shard_map/all_to_all | solution.py:733
  171.6 67.0 %all-to-all-start.2 = ((bf16[4,2,2,96,768]{4,3,2,1,0:T(8,128)(2,1)}), bf16[4,2,2,96,768]{4,3,2,1,0:T(8,128)(2,1)S(1)}, u32[]{:S(2)}, u32[]{:S(2)}) async-start(bf16[4,2,2,96,768]{4,3,2,1,0:T(8,128)(2,1)} %add_convert_fusion), calls=%async_computation.2 | async-start | bytes 4718592 | tf_op jit(solution)/shard_map/all_to_all | solution.py:612
  175.4 33.9 %collective-permute-start.13 = (bf16[5,2,4,24,768]{4,3,2,0,1:T(8,128)(2,1)}, bf16[5,2,4,24,768]{4,3,2,0,1:T(8,128)(2,1)S(1)}, u32[]{:S(2)}, u32[]{:S(2)}) collective-permute-start(bf16[5,2,4,24,768]{4,3,2,0,1:T(8,128)(2,1)} %fusion.2), channel_id=1, source_target_pairs={{0,4},{1,5},{2,6},{3,7},{4,0},{5,1},{6,2},{7,3},{8,12},{9,13},{10,... | collective-permute-start | bytes 4423688 | tf_op jit(solution)/shard_map/ppermute | solution.py:599
  209.3 23.0 %collective-permute-start.15 = (bf16[2,3,128,768]{3,2,1,0:T(8,128)(2,1)}, bf16[2,3,128,768]{3,2,1,0:T(8,128)(2,1)S(1)}, u32[]{:S(2)}, u32[]{:S(2)}) collective-permute-start(bf16[2,3,128,768]{3,2,1,0:T(8,128)(2,1)} %get-tuple-element.113), channel_id=1, source_target_pairs={{0,1},{1,0},{2,3},{3,2},{4,5},{5,4},{6,7},{7,6},{8,9},{9,8},{10,11... | collective-permute-start | bytes 3538952 | tf_op jit(solution)/shard_map/ppermute | solution.py:599
  210.4 22.0 %collective-permute-start.14 = (bf16[4,136,768]{2,1,0:T(8,128)(2,1)}, bf16[4,136,768]{2,1,0:T(8,128)(2,1)S(1)}, u32[]{:S(2)}, u32[]{:S(2)}) collective-permute-start(bf16[4,136,768]{2,1,0:T(8,128)(2,1)} %get-tuple-element.111), channel_id=1, source_target_pairs={{0,4},{1,5},{2,6},{3,7},{4,0},{5,1},{6,2},{7,3},{8,12},{9,13},{10,... | collective-permute-start | bytes 2506760 | tf_op jit(solution)/shard_map/ppermute | solution.py:599
  214.6 17.8 %collective-permute-start.16 = (bf16[5,4,24,768]{3,2,1,0:T(8,128)(2,1)S(1)}, bf16[5,4,24,768]{3,2,1,0:T(8,128)(2,1)S(1)}, u32[]{:S(2)}, u32[]{:S(2)}) collective-permute-start(bf16[5,4,24,768]{3,2,1,0:T(8,128)(2,1)S(1)} %get-tuple-element.154), channel_id=1, source_target_pairs={{0,2},{1,3},{2,0},{3,1},{4,6},{5,7},{6,4},{7,5},{8,10},{9,11},{10,... | collective-permute-start | bytes 2211848 | tf_op jit(solution)/shard_map/ppermute | solution.py:599
  233.5 26.4 %collective-permute-start.17 = (bf16[3,128,768]{2,1,0:T(8,128)(2,1)}, bf16[3,128,768]{2,1,0:T(8,128)(2,1)}, u32[]{:S(2)}, u32[]{:S(2)}) collective-permute-start(bf16[3,128,768]{2,1,0:T(8,128)(2,1)} %fusion.6), channel_id=1, source_target_pairs={{0,2},{1,3},{2,0},{3,1},{4,6},{5,7},{6,4},{7,5},{8,10},{9,11},{10,... | collective-permute-start | bytes 1769480 | tf_op jit(solution)/shard_map/ppermute | solution.py:599
  235.0 11.3 %collective-permute-start.21 = (bf16[136,768]{1,0:T(8,128)(2,1)}, bf16[136,768]{1,0:T(8,128)(2,1)}, u32[]{:S(2)}, u32[]{:S(2)}) collective-permute-start(bf16[136,768]{1,0:T(8,128)(2,1)} %get-tuple-element.160), channel_id=1, source_target_pairs={{0,24},{1,25},{2,26},{3,27},{4,28},{5,29},{6,30},{7,31},{8,16},{9,... | collective-permute-start | bytes 626696 | tf_op jit(solution)/shard_map/ppermute | solution.py:599
  237.9 22.0 %collective-permute-start.20 = (bf16[136,768]{1,0:T(8,128)(2,1)}, bf16[136,768]{1,0:T(8,128)(2,1)}, u32[]{:S(2)}, u32[]{:S(2)}) collective-permute-start(bf16[136,768]{1,0:T(8,128)(2,1)} %get-tuple-element.161), channel_id=1, source_target_pairs={{0,16},{1,17},{2,18},{3,19},{4,20},{5,21},{6,22},{7,23},{8,24},{9,... | collective-permute-start | bytes 626696 | tf_op jit(solution)/shard_map/ppermute | solution.py:599
  237.9 22.0 %collective-permute-start.19 = (bf16[136,768]{1,0:T(8,128)(2,1)}, bf16[136,768]{1,0:T(8,128)(2,1)}, u32[]{:S(2)}, u32[]{:S(2)}) collective-permute-start(bf16[136,768]{1,0:T(8,128)(2,1)} %get-tuple-element.162), channel_id=1, source_target_pairs={{0,8},{1,9},{2,10},{3,11},{4,12},{5,13},{6,14},{7,15},{8,0},{9,1},... | collective-permute-start | bytes 626696 | tf_op jit(solution)/shard_map/ppermute | solution.py:599
  239.7 20.2 %collective-permute-start.18 = (bf16[2,96,768]{2,1,0:T(8,128)(2,1)}, bf16[2,96,768]{2,1,0:T(8,128)(2,1)S(1)}, u32[]{:S(2)}, u32[]{:S(2)}) collective-permute-start(bf16[2,96,768]{2,1,0:T(8,128)(2,1)} %get-tuple-element.158), channel_id=1, source_target_pairs={{0,4},{1,5},{2,6},{3,7},{4,0},{5,1},{6,2},{7,3},{8,12},{9,13},{10,... | collective-permute-start | bytes 884744 | tf_op jit(solution)/shard_map/ppermute | solution.py:599
  242.0 38.6 %all-to-all-start.3 = ((bf16[4,120,768]{2,1,0:T(8,128)(2,1)}), bf16[4,120,768]{2,1,0:T(8,128)(2,1)S(1)}, u32[]{:S(2)}, u32[]{:S(2)}) async-start(bf16[4,120,768]{2,1,0:T(8,128)(2,1)} %bitcast.58), calls=%async_computation.3 | async-start | bytes 1474560 | tf_op jit(solution)/shard_map/all_to_all | solution.py:612
  261.7 16.6 %collective-permute-start.23 = (bf16[136,192]{1,0:T(8,128)(2,1)S(1)}, bf16[136,192]{1,0:T(8,128)(2,1)S(1)}, u32[]{:S(2)}, u32[]{:S(2)}) collective-permute-start(bf16[136,192]{1,0:T(8,128)(2,1)S(1)} %get-tuple-element.173), channel_id=1, source_target_pairs={{0,1},{1,0},{2,3},{3,2},{4,5},{5,4},{6,7},{7,6},{8,9},{9,8},{10,11... | collective-permute-start | bytes 156680 | tf_op jit(solution)/shard_map/ppermute | solution.py:585
  268.1 10.3 %collective-permute-start.24 = (bf16[136,192]{1,0:T(8,128)(2,1)S(1)}, bf16[136,192]{1,0:T(8,128)(2,1)S(1)}, u32[]{:S(2)}, u32[]{:S(2)}) collective-permute-start(bf16[136,192]{1,0:T(8,128)(2,1)S(1)} %get-tuple-element.174), channel_id=1, source_target_pairs={{0,2},{1,3},{2,0},{3,1},{4,6},{5,7},{6,4},{7,5},{8,10},{9,11},{10,... | collective-permute-start | bytes 156680 | tf_op jit(solution)/shard_map/ppermute | solution.py:585
  269.2 9.1 %collective-permute-start.25 = (bf16[136,192]{1,0:T(8,128)(2,1)S(1)}, bf16[136,192]{1,0:T(8,128)(2,1)S(1)}, u32[]{:S(2)}, u32[]{:S(2)}) collective-permute-start(bf16[136,192]{1,0:T(8,128)(2,1)S(1)} %get-tuple-element.175), channel_id=1, source_target_pairs={{0,3},{1,2},{2,1},{3,0},{4,7},{5,6},{6,5},{7,4},{8,11},{9,10},{10,... | collective-permute-start | bytes 156680 | tf_op jit(solution)/shard_map/ppermute | solution.py:585
  269.8 8.6 %collective-permute-start.26 = (bf16[64,768]{1,0:T(8,128)(2,1)S(1)}, bf16[64,768]{1,0:T(8,128)(2,1)S(1)}, u32[]{:S(2)}, u32[]{:S(2)}) collective-permute-start(bf16[64,768]{1,0:T(8,128)(2,1)S(1)} %slice.292), channel_id=1, source_target_pairs={{0,0},{1,8},{2,16},{3,24},{4,4},{5,12},{6,20},{7,28},{8,1},{9,9},{... | collective-permute-start | bytes 294920 | tf_op jit(solution)/shard_map/ppermute | solution.py:626
  271.8 8.1 %collective-permute-start.22 = (bf16[96,768]{1,0:T(8,128)(2,1)S(1)}, bf16[96,768]{1,0:T(8,128)(2,1)S(1)}, u32[]{:S(2)}, u32[]{:S(2)}) collective-permute-start(bf16[96,768]{1,0:T(8,128)(2,1)S(1)} %fusion.12), channel_id=1, source_target_pairs={{0,2},{1,3},{2,0},{3,1},{4,6},{5,7},{6,4},{7,5},{8,10},{9,11},{10,... | collective-permute-start | bytes 442376 | tf_op jit(solution)/shard_map/ppermute | solution.py:599
  (23 other events, 166.3 us)
Sparse Core Ops, SparseCore 0:
  11.4 110.6 all-gather.3

commit v7 on v6

--- a/solution.py
+++ b/solution.py
@@ -575,7 +575,7 @@
             *(jax.ShapeDtypeStruct(shape, LOW) for shape in grads),
             jax.ShapeDtypeStruct(vectors.shape, WIDE),
         ],
-        compiler_params=pltpu.CompilerParams(vmem_limit_bytes=44 * 1024 * 1024),
+        compiler_params=pltpu.CompilerParams(vmem_limit_bytes=48 * 1024 * 1024),
         cost_estimate=cost(20e9, 30e6),
         name="second_half",
     )(at, ctx, tok, cot, w_output, vectors, w_inner, w_outer)

time: 290 us -> 290 us (level)
  transfers between devices with their start and end apart: 32 -> 32, of which waited for: 9 -> 10; matrix products, arithmetic and copies ran while one was open for 13% -> 12% of each run, Pallas kernels for 21% -> 21%
where the time goes in v7:
time: 290 us; the launch traced here: 289 us
  Pallas kernels  87.8 us (30%)
  waiting for transfers between devices  74.1 us (26%)
  starting transfers between devices  55.1 us (19%)
  other arithmetic  36.1 us (12%)
  between operations  14.5 us (5%)
  local copies, waits for them, and re-layouts  12.9 us (4%)
  blocking collectives  8.77 us (3%)
    ppermute x16, waiting for transfers between devices, hop(): return lax.ppermute(value, AXES, [(i, i ^ bits) for i in range(devices)])  63.7 us
    pallas_call x1, Pallas kernels, attend_back_call(): pl.pallas_call(functools.partial(attend_back_kernel, heads, blocks, joine...  32.6 us
    pallas_call x1, Pallas kernels, second_half_call(): pl.pallas_call(functools.partial(second_half_kernel, cuts, split), grid_s...  25.7 us
    pallas_call x1, Pallas kernels, attend_call(): pl.pallas_call(functools.partial(attend_kernel, heads, blocks), grid_spec...  23.1 us
    ppermute x16, starting transfers between devices, hop(): return lax.ppermute(value, AXES, [(i, i ^ bits) for i in range(devices)])  20.4 us
    ppermute x9, starting transfers between devices, swap(): return lax.ppermute(value, axis, [(i, i ^ bit) for i in range(size)])  13.9 us
    cos x1, other arithmetic, on_device(): sines, cosines = (jnp.sin(angles), jnp.cos(angles))  10 us
    all_gather x1, blocking collectives, on_device(): places = lax.all_gather(jnp.stack([grid_x, grid_y, padding]), 'pb', axis=0)  8.77 us
  transfers between devices with their start and end apart: 32, of which 10 were waited for; matrix products, arithmetic and copies ran while one was open for 12% of the time, Pallas kernels for 21%

profile of v7, /device:TPU:1, one launch (start us, length us, event | category | flops | bytes accessed | tf_op | source)
XLA Modules:
  0.0 289.2 jit_solution(14757257978699214188)
XLA Ops:
  9.3 2.0 pack.1
  11.3 2.1 collective-permute-start.1
  14.4 3.3 %all-to-all-start = ((bf16[4,72,192]{2,1,0:T(8,128)(2,1)}), bf16[4,72,192]{2,1,0:T(8,128)(2,1)S(1)}, u32[]{:S(2)}, u32[]{:S(2)}) async-start(bf16[4,72,192]{2,1,0:T(8,128)(2,1)} %get-tuple-element.85), calls=%async_computation | async-start | bytes 294912 | tf_op jit(solution)/shard_map/all_to_all | solution.py:685
  17.7 3.1 %collective-permute-start.3 = (bf16[56,768]{1,0:T(8,128)(2,1)}, bf16[56,768]{1,0:T(8,128)(2,1)S(1)}, u32[]{:S(2)}, u32[]{:S(2)}) collective-permute-start(bf16[56,768]{1,0:T(8,128)(2,1)} %get-tuple-element.86), channel_id=1, source_target_pairs={{0,0},{1,8},{2,16},{3,24},{4,4},{5,12},{6,20},{7,28},{8,1},{9,9},{... | collective-permute-start | bytes 258056 | tf_op jit(solution)/shard_map/ppermute | solution.py:626
  24.1 8.8 %all-gather = s32[12,3,128]{2,1,0:T(4,128)S(1)} all-gather(s32[3,3,128]{2,1,0:T(4,128)S(1)} %pad_add_fusion), channel_id=2, replica_groups=mesh['page'=8,'pb'=4] {'pb'}, dimensions={0}, use_global_device_ids=true | all-gather | bytes 23040 | tf_op jit(solution)/shard_map/all_gather | solution.py:693
  33.3 5.4 %collective-permute-start.6 = (bf16[128,768]{1,0:T(8,128)(2,1)S(1)}, bf16[128,768]{1,0:T(8,128)(2,1)S(1)}, u32[]{:S(2)}, u32[]{:S(2)}) collective-permute-start(bf16[128,768]{1,0:T(8,128)(2,1)S(1)} %constant_dynamic-update-slice_fusion), channel_id=1, source_target_pairs={{0,24},{1,25},{2,26},{3,27},{4,28},{5,29},{6,30},{7,31},{8,16},{9,... | collective-permute-start | bytes 589832 | tf_op jit(solution)/shard_map/ppermute | solution.py:599
  39.1 4.8 %collective-permute-done.6 = bf16[128,768]{1,0:T(8,128)(2,1)S(1)} collective-permute-done((bf16[128,768]{1,0:T(8,128)(2,1)S(1)}, bf16[128,768]{1,0:T(8,128)(2,1)S(1)}, u32[]{:S(2)}, u32[]{:S(2)}) %collective-permute-start.6) | collective-permute-done | bytes 196640 | tf_op jit(solution)/shard_map/ppermute | solution.py:599
  43.9 16.5 %collective-permute-done.5 = bf16[128,768]{1,0:T(8,128)(2,1)S(1)} collective-permute-done((bf16[128,768]{1,0:T(8,128)(2,1)S(1)}, bf16[128,768]{1,0:T(8,128)(2,1)S(1)}, u32[]{:S(2)}, u32[]{:S(2)}) %collective-permute-start.5) | collective-permute-done | bytes 196640 | tf_op jit(solution)/shard_map/ppermute | solution.py:599
  63.5 10.0 %fusion = (f32[3,512,384]{2,1,0:T(8,128)}, f32[3,512,384]{2,1,0:T(8,128)}) fusion(f32[3,512,192]{2,1,0:T(8,128)S(1)} %get-tuple-element.187, f32[3,512,192]{2,1,0:T(8,128)S(1)} %get-tuple-element.186), kind=kLoop, calls=%fused_computation.6 | loop fusion | flops 589824 | bytes 7077888 | tf_op jit(solution)/shard_map/cos | solution.py:702
  73.5 7.4 %collective-permute-done.7.theirs_ref = bf16[4,128,768]{2,1,0:T(8,128)(2,1)S(1)} collective-permute-done((bf16[4,128,768]{2,1,0:T(8,128)(2,1)S(1)}, bf16[4,128,768]{2,1,0:T(8,128)(2,1)S(1)}, u32[]{:S(2)}, u32[]{:S(2)}) %collective-permute-start.7) | collective-permute-done | bytes 786464 | tf_op jit(solution)/shard_map/ppermute | solution.py:599
  81.8 2.9 assemble.1
  85.8 23.1 %attend.1 = (bf16[3,512,576]{2,1,0:T(8,128)(2,1)}, bf16[3,3,512,512]{3,2,1,0:T(8,128)(2,1)}, f32[3,512,3]{2,1,0:T(8,128)}, bf16[4,3,64,384]{3,2,1,0:T(8,128)(2,1)}) custom-call(s32[1]{0:T(128)} %bitcast.5.me_ref, bf16[3,128,768]{2,1,0:T(8,128)(2,1)} %refs_0_.3, bf16[3,128,768]{2,1,0:T(8,128)(2,1)} %copy-done.19, bf16[3,128,768]{2,1,0:T(8,128)(2,1)} %copy-done.18, ...), custom_call_target="tpu_custom_call" | custom-call | flops 20000000000 | bytes 20000000 | tf_op jit(solution)/shard_map/attend/pallas_call | solution.py:256
  112.3 4.4 %collective-permute-done.10 = bf16[3,64,384]{2,1,0:T(8,128)(2,1)S(1)} collective-permute-done((bf16[3,64,384]{2,1,0:T(8,128)(2,1)S(1)}, bf16[3,64,384]{2,1,0:T(8,128)(2,1)S(1)}, u32[]{:S(2)}, u32[]{:S(2)}) %collective-permute-start.10) | collective-permute-done | bytes 147488 | tf_op jit(solution)/shard_map/ppermute | solution.py:585
  116.7 2.5 collective-permute-done.9
  119.3 3.4 %all-gather.4.cloned.1.call-done = bf16[7424,768]{1,0:T(8,128)(2,1)} async-done(((bf16[232,768]{1,0:T(8,128)(2,1)}), bf16[7424,768]{1,0:T(8,128)(2,1)}) %all-gather.4.cloned.1.call-update) | async-done | bytes 11403280 | tf_op jit(solution)/shard_map/all_gather | solution.py:689
  124.0 3.1 %fusion.30 = (bf16[32,24,768]{2,1,0:T(8,128)(2,1)S(1)}, bf16[32,24,768]{2,1,0:T(8,128)(2,1)S(1)}, bf16[32,24,768]{2,1,0:T(8,128)(2,1)S(1)}, bf16[32,24,768]{2,1,0:T(8,128)(2,1)S(1)}, bf16[32,24,768]{2,1,0:T(8,128)(2,1)S(1)}) fusion(bf16[32,232,768]{2,1,0:T(8,128)(2,1)} %bitcast.166), kind=kLoop, calls=%fused_computation.103 | loop fusion | bytes 11796480 | tf_op jit(solution)/shard_map/slice | solution.py:724
  127.1 2.5 pad_maximum_fusion.wi_ref
  129.6 25.7 %second_half.1 = (bf16[384,768]{1,0:T(8,128)(2,1)}, f32[384,768]{1,0:T(8,128)S(1)}, bf16[4,3,64,384]{3,2,1,0:T(8,128)(2,1)}, bf16[4,2,2,96,768]{4,3,2,1,0:T(8,12...) custom-call(s32[5]{0:T(128)S(1)} %copy-done, ...), custom_call_target="tpu_custom_call" | custom-call | flops 20000000000 | bytes 30000000 | tf_op jit(solution)/shard_map/second_half/pallas_call | solution.py:555
  157.0 4.3 %all-to-all-start.1 = ((bf16[4,3,64,384]{3,2,1,0:T(8,128)(2,1)}), bf16[4,3,64,384]{3,2,1,0:T(8,128)(2,1)}, u32[]{:S(2)}, u32[]{:S(2)}) async-start(bf16[4,3,64,384]{3,2,1,0:T(8,128)(2,1)} %get-tuple-element.99), calls=%async_computation.1 | async-start | bytes 1179648 | tf_op jit(solution)/shard_map/all_to_all | solution.py:733
  161.4 3.7 %collective-permute-done.11 = bf16[4,2,2,96,768]{4,3,2,1,0:T(8,128)(2,1)S(1)} collective-permute-done((bf16[4,2,2,96,768]{4,3,2,1,0:T(8,128)(2,1)}, bf16[4,2,2,96,768]{4,3,2,1,0:T(8,128)(2,1)S(1)}, u32[]{:S(2)}, u32[]{:S(2)}) %collective-permute-start.11) | collective-permute-done | bytes 2359328 | tf_op jit(solution)/shard_map/ppermute | solution.py:599
  165.1 3.9 %add_convert_fusion = bf16[4,2,2,96,768]{4,3,2,1,0:T(8,128)(2,1)} fusion(bf16[4,2,2,96,768]{4,3,2,1,0:T(8,128)(2,1)S(1)} %collective-permute-done.11, bf16[4,2,2,96,768]{4,3,2,1,0:T(8,128)(2,1)} %get-tuple-element.100), kind=kLoop, calls=%fused_computation.1 | loop fusion | flops 4718592 | bytes 7077888 | tf_op jit(solution)/shard_map/convert_element_type | solution.py:738
  169.0 2.9 fusion.2
  171.9 3.9 %all-to-all-start.2 = ((bf16[4,2,2,96,768]{4,3,2,1,0:T(8,128)(2,1)}), bf16[4,2,2,96,768]{4,3,2,1,0:T(8,128)(2,1)S(1)}, u32[]{:S(2)}, u32[]{:S(2)}) async-start(bf16[4,2,2,96,768]{4,3,2,1,0:T(8,128)(2,1)} %add_convert_fusion), calls=%async_computation.2 | async-start | bytes 4718592 | tf_op jit(solution)/shard_map/all_to_all | solution.py:612
  177.0 32.6 %attend_back.1 = (bf16[2,3,128,768]{3,2,1,0:T(8,128)(2,1)}, bf16[2,3,128,768]{3,2,1,0:T(8,128)(2,1)}, bf16[4,136,768]{2,1,0:T(8,128)(2,1)}, bf16[4,136,768]{2,1,0:T(8,128)(2,1)}) custom-call(s32[3]{0:T(128)} %pad_add_fusion.1.me_ref, bf16[3,128,768]{2,1,0:T(8,128)(2,1)} %refs_0_.3, bf16[3,128,768]{2,1,0:T(8,128)(2,1)} %copy-done.19, ...), custom_call_target="tpu_custom_call" | custom-call | flops 30000001024 | bytes 20000000 | tf_op jit(solution)/shard_map/attend_back/pallas_call | solution.py:373
  211.9 3.0 %fusion.3 = (bf16[5,4,24,768]{3,2,1,0:T(8,128)(2,1)S(1)}, f32[5,4,24,768]{3,2,1,0:T(8,128)}) fusion(bf16[5,2,2,4,24,768]{5,4,3,2,1,0:T(8,128)(2,1)} %collective-permute-done.12, bf16[5,2,4,24,768]{4,3,2,0,1:T(8,128)(2,1)S(1)} %collective-permute-done.13, bf16[5,2,2,4,24,768]{5,4,3,2,1,0:T(8,128)(2,1)S(1)} %copy-done.8), kind=kLoop, calls=%fused_computation.10 | loop fusion | flops 4055040 | bytes 6635520 | tf_op jit(solution)/shard_map/convert_element_type | solution.py:751
  215.0 17.7 %collective-permute-done.16 = bf16[5,4,24,768]{3,2,1,0:T(8,128)(2,1)S(1)} collective-permute-done((bf16[5,4,24,768]{3,2,1,0:T(8,128)(2,1)S(1)}, bf16[5,4,24,768]{3,2,1,0:T(8,128)(2,1)S(1)}, u32[]{:S(2)}, u32[]{:S(2)}) %collective-permute-start.16) | collective-permute-done | bytes 737312 | tf_op jit(solution)/shard_map/ppermute | solution.py:599
  235.1 3.0 %collective-permute-start.21 = (bf16[136,768]{1,0:T(8,128)(2,1)}, bf16[136,768]{1,0:T(8,128)(2,1)}, u32[]{:S(2)}, u32[]{:S(2)}) collective-permute-start(bf16[136,768]{1,0:T(8,128)(2,1)} %get-tuple-element.160), channel_id=1, source_target_pairs={{0,24},{1,25},{2,26},{3,27},{4,28},{5,29},{6,30},{7,31},{8,16},{9,... | collective-permute-start | bytes 626696 | tf_op jit(solution)/shard_map/ppermute | solution.py:599
  242.5 4.2 %all-to-all-start.3 = ((bf16[4,120,768]{2,1,0:T(8,128)(2,1)}), bf16[4,120,768]{2,1,0:T(8,128)(2,1)S(1)}, u32[]{:S(2)}, u32[]{:S(2)}) async-start(bf16[4,120,768]{2,1,0:T(8,128)(2,1)} %bitcast.58), calls=%async_computation.3 | async-start | bytes 1474560 | tf_op jit(solution)/shard_map/all_to_all | solution.py:612
  246.7 13.5 %collective-permute-done.20 = bf16[136,768]{1,0:T(8,128)(2,1)} collective-permute-done((bf16[136,768]{1,0:T(8,128)(2,1)}, bf16[136,768]{1,0:T(8,128)(2,1)}, u32[]{:S(2)}, u32[]{:S(2)}) %collective-permute-start.20) | collective-permute-done | bytes 208928 | tf_op jit(solution)/shard_map/ppermute | solution.py:599
  262.0 6.2 %collective-permute-start.23 = (bf16[136,192]{1,0:T(8,128)(2,1)S(1)}, bf16[136,192]{1,0:T(8,128)(2,1)S(1)}, u32[]{:S(2)}, u32[]{:S(2)}) collective-permute-start(bf16[136,192]{1,0:T(8,128)(2,1)S(1)} %get-tuple-element.173), channel_id=1, source_target_pairs={{0,1},{1,0},{2,3},{3,2},{4,5},{5,4},{6,7},{7,6},{8,9},{9,8},{10,11... | collective-permute-start | bytes 156680 | tf_op jit(solution)/shard_map/ppermute | solution.py:585
  272.0 4.2 %collective-permute-start.22 = (bf16[96,768]{1,0:T(8,128)(2,1)S(1)}, bf16[96,768]{1,0:T(8,128)(2,1)S(1)}, u32[]{:S(2)}, u32[]{:S(2)}) collective-permute-start(bf16[96,768]{1,0:T(8,128)(2,1)S(1)} %fusion.12), channel_id=1, source_target_pairs={{0,2},{1,3},{2,0},{3,1},{4,6},{5,7},{6,4},{7,5},{8,10},{9,11},{10,... | collective-permute-start | bytes 442376 | tf_op jit(solution)/shard_map/ppermute | solution.py:599
  276.2 2.4 fusion.4
  (141 shorter events, 38.1 us)
Async XLA Ops:
  7.2 115.5 %all-gather.4.cloned.1.call-start = ((), (), s32[]{:S(2)}) async-start(), calls=%async_computation.4 | async-start | bytes 11759616 | tf_op jit(solution)/shard_map/all_gather | solution.py:689
  11.3 50.4 %collective-permute-start.1 = (bf16[3,128,768]{2,1,0:T(8,128)(2,1)}, bf16[3,128,768]{2,1,0:T(8,128)(2,1)S(1)}, u32[]{:S(2)}, u32[]{:S(2)}) collective-permute-start(bf16[3,128,768]{2,1,0:T(8,128)(2,1)} %refs_0_.3), channel_id=1, source_target_pairs={{0,2},{1,3},{2,0},{3,1},{4,6},{5,7},{6,4},{7,5},{8,10},{9,11},{10,... | collective-permute-start | bytes 1769480 | tf_op jit(solution)/shard_map/ppermute | solution.py:585
  13.5 71.3 %collective-permute-start = (bf16[3,128,768]{2,1,0:T(8,128)(2,1)}, bf16[3,128,768]{2,1,0:T(8,128)(2,1)S(1)}, u32[]{:S(2)}, u32[]{:S(2)}) collective-permute-start(bf16[3,128,768]{2,1,0:T(8,128)(2,1)} %refs_0_.3), channel_id=1, source_target_pairs={{0,1},{1,0},{2,3},{3,2},{4,5},{5,4},{6,7},{7,6},{8,9},{9,8},{10,11... | collective-permute-start | bytes 1769480 | tf_op jit(solution)/shard_map/ppermute | solution.py:585
  14.4 18.6 %all-to-all-start = ((bf16[4,72,192]{2,1,0:T(8,128)(2,1)}), bf16[4,72,192]{2,1,0:T(8,128)(2,1)S(1)}, u32[]{:S(2)}, u32[]{:S(2)}) async-start(bf16[4,72,192]{2,1,0:T(8,128)(2,1)} %get-tuple-element.85), calls=%async_computation | async-start | bytes 294912 | tf_op jit(solution)/shard_map/all_to_all | solution.py:685
  17.7 15.5 %collective-permute-start.3 = (bf16[56,768]{1,0:T(8,128)(2,1)}, bf16[56,768]{1,0:T(8,128)(2,1)S(1)}, u32[]{:S(2)}, u32[]{:S(2)}) collective-permute-start(bf16[56,768]{1,0:T(8,128)(2,1)} %get-tuple-element.86), channel_id=1, source_target_pairs={{0,0},{1,8},{2,16},{3,24},{4,4},{5,12},{6,20},{7,28},{8,1},{9,9},{... | collective-permute-start | bytes 258056 | tf_op jit(solution)/shard_map/ppermute | solution.py:626
  33.3 10.6 %collective-permute-start.6 = (bf16[128,768]{1,0:T(8,128)(2,1)S(1)}, bf16[128,768]{1,0:T(8,128)(2,1)S(1)}, u32[]{:S(2)}, u32[]{:S(2)}) collective-permute-start(bf16[128,768]{1,0:T(8,128)(2,1)S(1)} %constant_dynamic-update-slice_fusion), channel_id=1, source_target_pairs={{0,24},{1,25},{2,26},{3,27},{4,28},{5,29},{6,30},{7,31},{8,16},{9,... | collective-permute-start | bytes 589832 | tf_op jit(solution)/shard_map/ppermute | solution.py:599
  38.7 21.7 %collective-permute-start.5 = (bf16[128,768]{1,0:T(8,128)(2,1)S(1)}, bf16[128,768]{1,0:T(8,128)(2,1)S(1)}, u32[]{:S(2)}, u32[]{:S(2)}) collective-permute-start(bf16[128,768]{1,0:T(8,128)(2,1)S(1)} %constant_dynamic-update-slice_fusion), channel_id=1, source_target_pairs={{0,16},{1,17},{2,18},{3,19},{4,20},{5,21},{6,22},{7,23},{8,24},{9,... | collective-permute-start | bytes 589832 | tf_op jit(solution)/shard_map/ppermute | solution.py:599
  38.7 21.7 %collective-permute-start.4 = (bf16[128,768]{1,0:T(8,128)(2,1)S(1)}, bf16[128,768]{1,0:T(8,128)(2,1)S(1)}, u32[]{:S(2)}, u32[]{:S(2)}) collective-permute-start(bf16[128,768]{1,0:T(8,128)(2,1)S(1)} %constant_dynamic-update-slice_fusion), channel_id=1, source_target_pairs={{0,8},{1,9},{2,10},{3,11},{4,12},{5,13},{6,14},{7,15},{8,0},{9,1},... | collective-permute-start | bytes 589832 | tf_op jit(solution)/shard_map/ppermute | solution.py:599
  60.5 20.4 %collective-permute-start.7 = (bf16[4,128,768]{2,1,0:T(8,128)(2,1)S(1)}, bf16[4,128,768]{2,1,0:T(8,128)(2,1)S(1)}, u32[]{:S(2)}, u32[]{:S(2)}) collective-permute-start(bf16[4,128,768]{2,1,0:T(8,128)(2,1)S(1)} %pad_maximum_fusion.2.mine_ref), channel_id=1, source_target_pairs={{0,4},{1,5},{2,6},{3,7},{4,0},{5,1},{6,2},{7,3},{8,12},{9,13},{10,... | collective-permute-start | bytes 2359304 | tf_op jit(solution)/shard_map/ppermute | solution.py:599
  61.7 23.0 %collective-permute-start.2 = (bf16[3,128,768]{2,1,0:T(8,128)(2,1)S(1)}, bf16[3,128,768]{2,1,0:T(8,128)(2,1)S(1)}, u32[]{:S(2)}, u32[]{:S(2)}) collective-permute-start(bf16[3,128,768]{2,1,0:T(8,128)(2,1)S(1)} %collective-permute-done.1.refs_2_), channel_id=1, source_target_pairs={{0,1},{1,0},{2,3},{3,2},{4,5},{5,4},{6,7},{7,6},{8,9},{9,8},{10,11... | collective-permute-start | bytes 1769480 | tf_op jit(solution)/shard_map/ppermute | solution.py:585
  110.0 6.6 %collective-permute-start.10 = (bf16[3,64,384]{2,1,0:T(8,128)(2,1)S(1)}, bf16[3,64,384]{2,1,0:T(8,128)(2,1)S(1)}, u32[]{:S(2)}, u32[]{:S(2)}) collective-permute-start(bf16[3,64,384]{2,1,0:T(8,128)(2,1)S(1)} %get-tuple-element.164), channel_id=1, source_target_pairs={{0,3},{1,2},{2,1},{3,0},{4,7},{5,6},{6,5},{7,4},{8,11},{9,10},{10,... | collective-permute-start | bytes 442376 | tf_op jit(solution)/shard_map/ppermute | solution.py:585
  111.8 7.4 %collective-permute-start.9 = (bf16[3,64,384]{2,1,0:T(8,128)(2,1)S(1)}, bf16[3,64,384]{2,1,0:T(8,128)(2,1)S(1)}, u32[]{:S(2)}, u32[]{:S(2)}) collective-permute-start(bf16[3,64,384]{2,1,0:T(8,128)(2,1)S(1)} %get-tuple-element.165), channel_id=1, source_target_pairs={{0,2},{1,3},{2,0},{3,1},{4,6},{5,7},{6,4},{7,5},{8,10},{9,11},{10,... | collective-permute-start | bytes 442376 | tf_op jit(solution)/shard_map/ppermute | solution.py:585
  111.8 7.3 %collective-permute-start.8 = (bf16[3,64,384]{2,1,0:T(8,128)(2,1)S(1)}, bf16[3,64,384]{2,1,0:T(8,128)(2,1)S(1)}, u32[]{:S(2)}, u32[]{:S(2)}) collective-permute-start(bf16[3,64,384]{2,1,0:T(8,128)(2,1)S(1)} %get-tuple-element.166), channel_id=1, source_target_pairs={{0,1},{1,0},{2,3},{3,2},{4,5},{5,4},{6,7},{7,6},{8,9},{9,8},{10,11... | collective-permute-start | bytes 442376 | tf_op jit(solution)/shard_map/ppermute | solution.py:585
  155.9 13.1 %collective-permute-start.12 = (bf16[5,2,2,4,24,768]{5,4,3,2,1,0:T(8,128)(2,1)}, bf16[5,2,2,4,24,768]{5,4,3,2,1,0:T(8,128)(2,1)}, u32[]{:S(2)}, u32[]{:S(2)}) collective-permute-start(bf16[5,2,2,4,24,768]{5,4,3,2,1,0:T(8,128)(2,1)} %get-tuple-element.103), channel_id=1, source_target_pairs={{0,1},{1,0},{2,3},{3,2},{4,5},{5,4},{6,7},{7,6},{8,9},{9,8},{10,11... | collective-permute-start | bytes 8847368 | tf_op jit(solution)/shard_map/ppermute | solution.py:599
  156.2 8.9 %collective-permute-start.11 = (bf16[4,2,2,96,768]{4,3,2,1,0:T(8,128)(2,1)}, bf16[4,2,2,96,768]{4,3,2,1,0:T(8,128)(2,1)S(1)}, u32[]{:S(2)}, u32[]{:S(2)}) collective-permute-start(bf16[4,2,2,96,768]{4,3,2,1,0:T(8,128)(2,1)} %get-tuple-element.101), channel_id=1, source_target_pairs={{0,1},{1,0},{2,3},{3,2},{4,5},{5,4},{6,7},{7,6},{8,9},{9,8},{10,11... | collective-permute-start | bytes 7077896 | tf_op jit(solution)/shard_map/ppermute | solution.py:599
  157.0 14.9 %all-to-all-start.1 = ((bf16[4,3,64,384]{3,2,1,0:T(8,128)(2,1)}), bf16[4,3,64,384]{3,2,1,0:T(8,128)(2,1)}, u32[]{:S(2)}, u32[]{:S(2)}) async-start(bf16[4,3,64,384]{3,2,1,0:T(8,128)(2,1)} %get-tuple-element.99), calls=%async_computation.1 | async-start | bytes 1179648 | tf_op jit(solution)/shard_map/all_to_all | solution.py:733
  171.9 66.8 %all-to-all-start.2 = ((bf16[4,2,2,96,768]{4,3,2,1,0:T(8,128)(2,1)}), bf16[4,2,2,96,768]{4,3,2,1,0:T(8,128)(2,1)S(1)}, u32[]{:S(2)}, u32[]{:S(2)}) async-start(bf16[4,2,2,96,768]{4,3,2,1,0:T(8,128)(2,1)} %add_convert_fusion), calls=%async_computation.2 | async-start | bytes 4718592 | tf_op jit(solution)/shard_map/all_to_all | solution.py:612
  175.8 33.9 %collective-permute-start.13 = (bf16[5,2,4,24,768]{4,3,2,0,1:T(8,128)(2,1)}, bf16[5,2,4,24,768]{4,3,2,0,1:T(8,128)(2,1)S(1)}, u32[]{:S(2)}, u32[]{:S(2)}) collective-permute-start(bf16[5,2,4,24,768]{4,3,2,0,1:T(8,128)(2,1)} %fusion.2), channel_id=1, source_target_pairs={{0,4},{1,5},{2,6},{3,7},{4,0},{5,1},{6,2},{7,3},{8,12},{9,13},{10,... | collective-permute-start | bytes 4423688 | tf_op jit(solution)/shard_map/ppermute | solution.py:599
  209.7 23.0 %collective-permute-start.15 = (bf16[2,3,128,768]{3,2,1,0:T(8,128)(2,1)}, bf16[2,3,128,768]{3,2,1,0:T(8,128)(2,1)S(1)}, u32[]{:S(2)}, u32[]{:S(2)}) collective-permute-start(bf16[2,3,128,768]{3,2,1,0:T(8,128)(2,1)} %get-tuple-element.113), channel_id=1, source_target_pairs={{0,1},{1,0},{2,3},{3,2},{4,5},{5,4},{6,7},{7,6},{8,9},{9,8},{10,11... | collective-permute-start | bytes 3538952 | tf_op jit(solution)/shard_map/ppermute | solution.py:599
  210.7 22.0 %collective-permute-start.14 = (bf16[4,136,768]{2,1,0:T(8,128)(2,1)}, bf16[4,136,768]{2,1,0:T(8,128)(2,1)S(1)}, u32[]{:S(2)}, u32[]{:S(2)}) collective-permute-start(bf16[4,136,768]{2,1,0:T(8,128)(2,1)} %get-tuple-element.111), channel_id=1, source_target_pairs={{0,4},{1,5},{2,6},{3,7},{4,0},{5,1},{6,2},{7,3},{8,12},{9,13},{10,... | collective-permute-start | bytes 2506760 | tf_op jit(solution)/shard_map/ppermute | solution.py:599
  214.9 17.8 %collective-permute-start.16 = (bf16[5,4,24,768]{3,2,1,0:T(8,128)(2,1)S(1)}, bf16[5,4,24,768]{3,2,1,0:T(8,128)(2,1)S(1)}, u32[]{:S(2)}, u32[]{:S(2)}) collective-permute-start(bf16[5,4,24,768]{3,2,1,0:T(8,128)(2,1)S(1)} %get-tuple-element.154), channel_id=1, source_target_pairs={{0,2},{1,3},{2,0},{3,1},{4,6},{5,7},{6,4},{7,5},{8,10},{9,11},{10,... | collective-permute-start | bytes 2211848 | tf_op jit(solution)/shard_map/ppermute | solution.py:599
  233.9 26.3 %collective-permute-start.17 = (bf16[3,128,768]{2,1,0:T(8,128)(2,1)}, bf16[3,128,768]{2,1,0:T(8,128)(2,1)}, u32[]{:S(2)}, u32[]{:S(2)}) collective-permute-start(bf16[3,128,768]{2,1,0:T(8,128)(2,1)} %fusion.6), channel_id=1, source_target_pairs={{0,2},{1,3},{2,0},{3,1},{4,6},{5,7},{6,4},{7,5},{8,10},{9,11},{10,... | collective-permute-start | bytes 1769480 | tf_op jit(solution)/shard_map/ppermute | solution.py:599
  235.1 11.6 %collective-permute-start.21 = (bf16[136,768]{1,0:T(8,128)(2,1)}, bf16[136,768]{1,0:T(8,128)(2,1)}, u32[]{:S(2)}, u32[]{:S(2)}) collective-permute-start(bf16[136,768]{1,0:T(8,128)(2,1)} %get-tuple-element.160), channel_id=1, source_target_pairs={{0,24},{1,25},{2,26},{3,27},{4,28},{5,29},{6,30},{7,31},{8,16},{9,... | collective-permute-start | bytes 626696 | tf_op jit(solution)/shard_map/ppermute | solution.py:599
  238.1 22.1 %collective-permute-start.20 = (bf16[136,768]{1,0:T(8,128)(2,1)}, bf16[136,768]{1,0:T(8,128)(2,1)}, u32[]{:S(2)}, u32[]{:S(2)}) collective-permute-start(bf16[136,768]{1,0:T(8,128)(2,1)} %get-tuple-element.161), channel_id=1, source_target_pairs={{0,16},{1,17},{2,18},{3,19},{4,20},{5,21},{6,22},{7,23},{8,24},{9,... | collective-permute-start | bytes 626696 | tf_op jit(solution)/shard_map/ppermute | solution.py:599
  238.1 22.1 %collective-permute-start.19 = (bf16[136,768]{1,0:T(8,128)(2,1)}, bf16[136,768]{1,0:T(8,128)(2,1)}, u32[]{:S(2)}, u32[]{:S(2)}) collective-permute-start(bf16[136,768]{1,0:T(8,128)(2,1)} %get-tuple-element.162), channel_id=1, source_target_pairs={{0,8},{1,9},{2,10},{3,11},{4,12},{5,13},{6,14},{7,15},{8,0},{9,1},... | collective-permute-start | bytes 626696 | tf_op jit(solution)/shard_map/ppermute | solution.py:599
  239.9 20.3 %collective-permute-start.18 = (bf16[2,96,768]{2,1,0:T(8,128)(2,1)}, bf16[2,96,768]{2,1,0:T(8,128)(2,1)S(1)}, u32[]{:S(2)}, u32[]{:S(2)}) collective-permute-start(bf16[2,96,768]{2,1,0:T(8,128)(2,1)} %get-tuple-element.158), channel_id=1, source_target_pairs={{0,4},{1,5},{2,6},{3,7},{4,0},{5,1},{6,2},{7,3},{8,12},{9,13},{10,... | collective-permute-start | bytes 884744 | tf_op jit(solution)/shard_map/ppermute | solution.py:599
  242.5 38.4 %all-to-all-start.3 = ((bf16[4,120,768]{2,1,0:T(8,128)(2,1)}), bf16[4,120,768]{2,1,0:T(8,128)(2,1)S(1)}, u32[]{:S(2)}, u32[]{:S(2)}) async-start(bf16[4,120,768]{2,1,0:T(8,128)(2,1)} %bitcast.58), calls=%async_computation.3 | async-start | bytes 1474560 | tf_op jit(solution)/shard_map/all_to_all | solution.py:612
  262.0 16.6 %collective-permute-start.23 = (bf16[136,192]{1,0:T(8,128)(2,1)S(1)}, bf16[136,192]{1,0:T(8,128)(2,1)S(1)}, u32[]{:S(2)}, u32[]{:S(2)}) collective-permute-start(bf16[136,192]{1,0:T(8,128)(2,1)S(1)} %get-tuple-element.173), channel_id=1, source_target_pairs={{0,1},{1,0},{2,3},{3,2},{4,5},{5,4},{6,7},{7,6},{8,9},{9,8},{10,11... | collective-permute-start | bytes 156680 | tf_op jit(solution)/shard_map/ppermute | solution.py:585
  268.2 10.4 %collective-permute-start.24 = (bf16[136,192]{1,0:T(8,128)(2,1)S(1)}, bf16[136,192]{1,0:T(8,128)(2,1)S(1)}, u32[]{:S(2)}, u32[]{:S(2)}) collective-permute-start(bf16[136,192]{1,0:T(8,128)(2,1)S(1)} %get-tuple-element.174), channel_id=1, source_target_pairs={{0,2},{1,3},{2,0},{3,1},{4,6},{5,7},{6,4},{7,5},{8,10},{9,11},{10,... | collective-permute-start | bytes 156680 | tf_op jit(solution)/shard_map/ppermute | solution.py:585
  269.6 9.0 %collective-permute-start.25 = (bf16[136,192]{1,0:T(8,128)(2,1)S(1)}, bf16[136,192]{1,0:T(8,128)(2,1)S(1)}, u32[]{:S(2)}, u32[]{:S(2)}) collective-permute-start(bf16[136,192]{1,0:T(8,128)(2,1)S(1)} %get-tuple-element.175), channel_id=1, source_target_pairs={{0,3},{1,2},{2,1},{3,0},{4,7},{5,6},{6,5},{7,4},{8,11},{9,10},{10,... | collective-permute-start | bytes 156680 | tf_op jit(solution)/shard_map/ppermute | solution.py:585
  269.9 8.7 %collective-permute-start.26 = (bf16[64,768]{1,0:T(8,128)(2,1)S(1)}, bf16[64,768]{1,0:T(8,128)(2,1)S(1)}, u32[]{:S(2)}, u32[]{:S(2)}) collective-permute-start(bf16[64,768]{1,0:T(8,128)(2,1)S(1)} %slice.292), channel_id=1, source_target_pairs={{0,0},{1,8},{2,16},{3,24},{4,4},{5,12},{6,20},{7,28},{8,1},{9,9},{... | collective-permute-start | bytes 294920 | tf_op jit(solution)/shard_map/ppermute | solution.py:626
  272.0 8.2 %collective-permute-start.22 = (bf16[96,768]{1,0:T(8,128)(2,1)S(1)}, bf16[96,768]{1,0:T(8,128)(2,1)S(1)}, u32[]{:S(2)}, u32[]{:S(2)}) collective-permute-start(bf16[96,768]{1,0:T(8,128)(2,1)S(1)} %fusion.12), channel_id=1, source_target_pairs={{0,2},{1,3},{2,0},{3,1},{4,6},{5,7},{6,4},{7,5},{8,10},{9,11},{10,... | collective-permute-start | bytes 442376 | tf_op jit(solution)/shard_map/ppermute | solution.py:599
  (21 other events, 162.6 us)
Sparse Core Ops, SparseCore 0:
  11.5 111.1 all-gather.3
